TPU v7x, 256 devices: a whole 4x4x8 slice. The times are simulated.
256 devices in a mesh: grp: 16 (over x_hi, y, core), loc: 16 (over z, x_lo).
Axes of the slice: x: 4 (x_hi: 2, x_lo: 2; x = x_hi * 2 + x_lo), y: 4, z: 8, core: 2. Of those that a mesh axis runs over, the one named last changes fastest.
Arguments:
- queries: bfloat16 [65536, 2048], P(('grp', 'loc')), may hold values from -5 to 5
- keys: bfloat16 [65536, 2048], P(('grp', 'loc')), may hold values from -5 to 5
- values: bfloat16 [65536, 2048], P(('grp', 'loc')), may hold values from -6 to 6
- grad_out: bfloat16 [65536, 2048], P(('grp', 'loc')), may hold values from -48 to 48
Outputs:
- attended: bfloat16 [65536, 2048], P(('grp', 'loc'))
- grad_queries: bfloat16 [65536, 2048], P(('grp', 'loc'))
- grad_keys: bfloat16 [65536, 2048], P(('grp', 'loc'))
- grad_values: bfloat16 [65536, 2048], P(('grp', 'loc'))
All inputs are finite; a program needn't handle non-finite values.
Results may differ from a plain program's by a relative error of at most 0.02.
Values may be sent and summed in bfloat16 or wider, within the bound.
No kernel may reach another device: no remote copies, remote signals or barrier semaphores. Data moves between devices by JAX's collectives and lax.ppermute only.
A program may use at most 192 MiB of HBM per device.

v0:
```python
import math

import jax
import jax.numpy as jnp
from jax import lax
from jax.sharding import PartitionSpec as P

HEADS = 16
HDIM = 128
BLK = 128
P2 = 64
P3 = 256


NEG_BIG = -1e30


def passed_along(value, axis, steps):
    count = lax.axis_size(axis)
    initial, last = (max(0, -steps), min(count, count - steps))
    return lax.ppermute(value, axis, [(source, source + steps) for source in range(initial, last)])


def pool_runs(tokens_in, run_len, factor):
    dims_in = tokens_in.shape
    grouped = tokens_in.reshape(
        dims_in[:-2] + (dims_in[-2] // run_len, run_len, dims_in[-1])
    ).astype(jnp.float32)
    return (jnp.sum(grouped, axis=-2) / factor).astype(jnp.bfloat16)


def block_terms(query_blk, key_set, value_set, allowed, grad_blk):
    row_count = query_blk.shape[0]
    key_count = key_set.shape[0]
    feat_width = query_blk.shape[1]
    score_scale = 1.0 / math.sqrt(HDIM)
    query_h = query_blk.reshape(row_count, HEADS, HDIM)
    key_h = key_set.reshape(key_count, HEADS, HDIM)
    value_h = value_set.reshape(key_count, HEADS, HDIM)
    grad_h = grad_blk.reshape(row_count, HEADS, HDIM)
    scores = (
        jnp.einsum("qhd,khd->hqk", query_h, key_h, preferred_element_type=jnp.float32) * score_scale
    )
    scores = jnp.where(allowed[None, :, :], scores, NEG_BIG)
    summit = jnp.max(scores, axis=2, keepdims=True)
    expo_terms = jnp.exp(scores - summit)
    totals = jnp.sum(expo_terms, axis=2, keepdims=True)
    mixed_sum = jnp.einsum(
        "hqk,khd->qhd", expo_terms.astype(jnp.bfloat16), value_h, preferred_element_type=jnp.float32
    )
    attended = (mixed_sum / jnp.transpose(totals, (1, 0, 2))).astype(jnp.bfloat16)
    deltas = jnp.sum(grad_h.astype(jnp.float32) * attended.astype(jnp.float32), axis=2)
    weights = expo_terms / totals
    grad_value = jnp.einsum(
        "hqk,qhd->khd", weights.astype(jnp.bfloat16), grad_h, preferred_element_type=jnp.float32
    )
    dot_grad = jnp.einsum("qhd,khd->hqk", grad_h, value_h, preferred_element_type=jnp.float32)
    dscore = (weights * (dot_grad - jnp.transpose(deltas)[:, :, None]) * score_scale).astype(
        jnp.bfloat16
    )
    grad_query = jnp.einsum(
        "hqk,khd->qhd", dscore, key_h, preferred_element_type=jnp.float32
    ).astype(jnp.bfloat16)
    grad_key = jnp.einsum("hqk,qhd->khd", dscore, query_h, preferred_element_type=jnp.float32)
    return (
        attended.reshape(row_count, feat_width),
        grad_query.reshape(row_count, feat_width),
        grad_key.reshape(key_count, feat_width),
        grad_value.reshape(key_count, feat_width),
        summit[:, :, 0],
        totals[:, :, 0],
        jnp.transpose(deltas),
    )


def per_device(queries, keys, values, grad_out):
    tok_rows, feat_width = queries.shape
    blocks = tok_rows // BLK
    loc_count = lax.axis_size("loc")
    grp_index = lax.axis_index("grp")
    loc_index = lax.axis_index("loc")
    seq_base = (grp_index * loc_count + loc_index) * tok_rows
    group_len = loc_count * tok_rows
    per_group = group_len // P2
    last_rows = jnp.stack([keys[tok_rows - BLK :], values[tok_rows - BLK :]])
    prior_rows = passed_along(last_rows, ("grp", "loc"), 1)
    pooled = pool_runs(jnp.stack([keys, values]), P2, math.sqrt(P2))
    second = lax.all_gather(pooled, "loc", axis=1, tiled=True)
    third_set = lax.all_gather(pool_runs(pooled, 4, 2.0), ("grp", "loc"), axis=1, tiled=True)
    third_count = third_set.shape[1]
    third_group = jnp.arange(third_count, dtype=jnp.int32) * P3 // group_len
    entry_end = (jnp.arange(per_group, dtype=jnp.int32) + 1) * P2
    fine_off = jnp.arange(2 * BLK, dtype=jnp.int32)
    query_off = jnp.arange(BLK, dtype=jnp.int32)
    pool_keys = jnp.concatenate([second[0], third_set[0]], axis=0)
    pool_values = jnp.concatenate([second[1], third_set[1]], axis=0)
    every_k = jnp.concatenate([prior_rows[0], keys], axis=0)
    every_v = jnp.concatenate([prior_rows[1], values], axis=0)
    window_k = jnp.concatenate(
        [
            every_k[:tok_rows].reshape(blocks, BLK, feat_width),
            every_k[BLK:].reshape(blocks, BLK, feat_width),
        ],
        axis=1,
    )
    window_v = jnp.concatenate(
        [
            every_v[:tok_rows].reshape(blocks, BLK, feat_width),
            every_v[BLK:].reshape(blocks, BLK, feat_width),
        ],
        axis=1,
    )

    def one_block(pieces):
        query_blk, win_k, win_v, grad_blk, block_idx = pieces
        blk_start = seq_base + block_idx * BLK
        query_pos = blk_start + query_off
        key_pos = blk_start - BLK + fine_off
        fine_ok = (key_pos[None, :] <= query_pos[:, None]) & (key_pos[None, :] >= 0)
        second_ok = grp_index * group_len + entry_end <= blk_start - BLK
        third_ok = third_group < grp_index
        allowed = jnp.concatenate(
            [
                fine_ok,
                jnp.broadcast_to(second_ok[None, :], (BLK, per_group)),
                jnp.broadcast_to(third_ok[None, :], (BLK, third_count)),
            ],
            axis=1,
        )
        key_set = jnp.concatenate([win_k, pool_keys], axis=0)
        value_set = jnp.concatenate([win_v, pool_values], axis=0)
        return block_terms(query_blk, key_set, value_set, allowed, grad_blk)

    attended, grad_query, grad_key, grad_value, summits, totals, deltas = lax.map(
        one_block,
        (
            queries.reshape(blocks, BLK, feat_width),
            window_k,
            window_v,
            grad_out.reshape(blocks, BLK, feat_width),
            jnp.arange(blocks, dtype=jnp.int32),
        ),
    )
    returned = passed_along(jnp.stack([grad_key[0, :BLK], grad_value[0, :BLK]]), ("grp", "loc"), -1)
    fine_k = (
        grad_key[:, BLK : 2 * BLK]
        + jnp.concatenate([grad_key[1:, :BLK], returned[0][None]], axis=0)
    ).reshape(tok_rows, feat_width)
    fine_v = (
        grad_value[:, BLK : 2 * BLK]
        + jnp.concatenate([grad_value[1:, :BLK], returned[1][None]], axis=0)
    ).reshape(tok_rows, feat_width)
    two_edge = 2 * BLK + per_group
    part_two = jnp.stack(
        [
            jnp.sum(grad_key[:, 2 * BLK : two_edge], axis=0),
            jnp.sum(grad_value[:, 2 * BLK : two_edge], axis=0),
        ]
    )
    part_three = jnp.stack(
        [jnp.sum(grad_key[:, two_edge:], axis=0), jnp.sum(grad_value[:, two_edge:], axis=0)]
    )
    mine_three = lax.psum_scatter(part_three, ("grp", "loc"), scatter_dimension=1, tiled=True)
    lifted = jnp.repeat(mine_three / 2.0, 4, axis=1)
    total_two = lax.psum_scatter(part_two, "loc", scatter_dimension=1, tiled=True) + lifted
    spread = jnp.repeat(total_two / math.sqrt(P2), P2, axis=1)
    grad_keys = (fine_k + spread[0]).astype(jnp.bfloat16)
    grad_values = (fine_v + spread[1]).astype(jnp.bfloat16)
    return (
        attended.reshape(tok_rows, feat_width),
        grad_query.reshape(tok_rows, feat_width),
        grad_keys,
        grad_values,
    )


def solution(mesh):
    return jax.shard_map(
        per_device,
        mesh=mesh,
        in_specs=(
            P(("grp", "loc"), None),
            P(("grp", "loc"), None),
            P(("grp", "loc"), None),
            P(("grp", "loc"), None),
        ),
        out_specs=(
            P(("grp", "loc"), None),
            P(("grp", "loc"), None),
            P(("grp", "loc"), None),
            P(("grp", "loc"), None),
        ),
        check_vma=False,
    )
```

profile of v0, /device:TPU:2, one launch (start us, length us, event | category | flops | bytes accessed | tf_op | source)
XLA Modules:
  0.0 1341.4 jit_solution(14488358167163401209)
XLA Ops:
  7.2 2.0 convert_reduce_fusion
  9.9 1.3 slice_bitcast_fusion.2
  12.3 3.8 collective-permute-start
  16.1 55.6 %all_gather.6 = bf16[2,64,2048]{2,0,1:T(2,128)(2,1)S(1)} all-gather(bf16[2,4,2048]{2,0,1:T(2,128)(2,1)S(1)} %copy.103), channel_id=1, replica_groups=mesh['grp'=16,'loc'=16] {'loc'}, dimensions={1}, use_global_device_ids=true | all-gather | bytes 557056 | tf_op jit(solution)/shard_map/all_gather | solution.py:88
  73.5 1.3 slice_bitcast_fusion
  75.0 1.4 pad_maximum_fusion.9
  76.4 1.6 pad_maximum_fusion.10
  78.0 638.3 %all-gather.3.cloned.1.call-done = bf16[2,524288]{1,0:T(2,128)(2,1)} async-done(((bf16[2,2048]{1,0:T(2,128)(2,1)}), bf16[2,524288]{1,0:T(2,128)(2,1)}) %all-gather.3.cloned.1.call-update) | async-done | bytes 2097168 | tf_op jit(solution)/shard_map/all_gather | solution.py:89
  716.3 24.5 %slice_reduce_fusion.2 = (bf16[524288]{0:T(1024)(128)(2,1)}, bf16[524288]{0:T(1024)(128)(2,1)S(1)}) fusion(bf16[2,524288]{1,0:T(2,128)(2,1)} %all-gather.3.cloned.1.call-done), kind=kLoop, calls=%fused_computation.61 | loop fusion | bytes 4194304 | tf_op jit(solution)/shard_map/slice | solution.py:95
  741.3 1.3 copy.107
  742.6 1.5 squeeze.36
  744.7 147.5 %while.19 = (s32[]{:T(128)}, bf16[2,128,2048]{2,1,0:T(8,128)(2,1)}, bf16[2,128,2048]{2,1,0:T(8,128)(2,1)}, f32[2,576,2048]{2,1,0:T(8,128)}, f32[2,576,2048]{2,1,...) while((s32[]{:T(128)}, bf16[2,128,2048]{2,1,0:T(8,128)(2,1)}, ...), condition=%wide.region_6.7_spmd.clone, body=%wide.region_2.6_spmd.clone.sunk | while | flops 1870609792 | bytes 214777040 | solution.py:134
  757.7 1.5 constant_dynamic-slice_fusion.8
  761.3 1.1 constant_dynamic-slice_fusion.9
  762.7 1.3 copy.154
  764.8 1.3 constant_dynamic-slice_fusion.10
  767.3 2.5 fusion.81
  769.9 2.2 copy-done
  773.0 1.4 copy.157
  774.5 1.4 constant_dynamic-slice_fusion.11
  777.1 5.9 multiply_reduce_fusion.2
  783.1 3.3 multiply_convert_fusion.5
  787.6 1.2 copy.161
  789.9 3.7 fusion.83
  793.6 5.0 copy.162
  798.6 6.0 broadcast_in_dim.159
  805.3 4.9 copy.163
  810.2 5.9 broadcast_in_dim.160
  816.1 8.8 constant_dynamic-update-slice_fusion.7
  824.9 1.5 constant_dynamic-slice_fusion.8
  828.6 1.1 constant_dynamic-slice_fusion.9
  829.9 1.3 copy.154
  832.0 1.3 constant_dynamic-slice_fusion.10
  834.5 2.5 fusion.81
  837.1 2.2 copy-done
  840.2 1.4 copy.157
  841.7 1.4 constant_dynamic-slice_fusion.11
  844.3 5.9 multiply_reduce_fusion.2
  850.3 3.3 multiply_convert_fusion.5
  854.8 1.2 copy.161
  857.1 3.7 fusion.83
  860.8 5.0 copy.162
  865.8 6.0 broadcast_in_dim.159
  872.6 4.9 copy.163
  877.4 5.9 broadcast_in_dim.160
  883.3 8.8 constant_dynamic-update-slice_fusion.7
  892.2 2.7 slice_reduce_fusion
  894.9 1.4 stack.50
  896.4 2.7 slice_reduce_fusion.1
  899.1 1.4 stack.49
  900.5 5.8 pad_maximum_fusion.8
  906.4 1.7 fusion.44
  908.1 1.7 fusion.45
  909.8 1.5 pad_maximum_fusion.11
  911.3 5.3 collective-permute-start.1
  916.6 1.3 slice_reduce_fusion.4
  918.0 1.3 slice_reduce_fusion.5
  921.7 262.8 %all-reduce.7.cloned.1.call-done = f32[2,256,2048]{2,0,1:T(2,128)} async-done(((f32[2,256,2048]{2,0,1:T(2,128)}), f32[2,256,2048]{2,0,1:T(2,128)}) %all-reduce.7.cloned.1.call-update) | async-done | bytes 4194320
  1185.2 140.5 %all-reduce.5.cloned.1.call-done = f32[2,64,2048]{2,1,0:T(8,128)} async-done(((f32[2,64,2048]{2,1,0:T(8,128)}), f32[2,64,2048]{2,1,0:T(8,128)}) %all-reduce.5.cloned.1.call-update) | async-done | bytes 1048592
  1326.7 1.7 fusion.46
  1328.4 1.9 maximum_add_fusion
  1330.3 1.2 fusion.41
  1331.4 1.9 maximum_add_fusion.1
  1333.3 1.2 fusion.40
  (156 shorter events, 26.1 us)
Async XLA Ops:
  7.2 709.1 %all-gather.3.cloned.1.call-start = ((), (), s32[]{:S(2)}) async-start(), calls=%async_computation | async-start | bytes 2105344 | tf_op jit(solution)/shard_map/all_gather | solution.py:89
  9.9 1174.6 %all-reduce.7.cloned.1.call-start = ((), (), s32[]{:S(2)}) async-start(), calls=%async_computation.2 | async-start | bytes 8388608
  11.2 63.5 %copy-start.12 = (bf16[256,2048]{1,0:T(8,128)(2,1)S(1)}, bf16[256,2048]{1,0:T(8,128)(2,1)}, u32[]{:S(2)}) copy-start(bf16[256,2048]{1,0:T(8,128)(2,1)} %param.8) | copy-start | bytes 3145732
  12.3 61.2 %collective-permute-start = (bf16[2,128,2048]{2,1,0:T(8,128)(2,1)}, bf16[2,128,2048]{2,1,0:T(8,128)(2,1)}, u32[]{:S(2)}, u32[]{:S(2)}) collective-permute-start(bf16[2,128,2048]{2,1,0:T(8,128)(2,1)} %pad_maximum_fusion.14), channel_id=1, source_target_pairs={{0,1},{1,2},{2,3},{3,4},{4,5},{5,6},{6,7},{7,8},{8,9},{9,10},{10,1... | collective-permute-start | bytes 3145736 | tf_op jit(solution)/shard_map/ppermute | solution.py:21
  71.7 3.1 copy-start.13
  757.7 7.1 copy-start.4
  757.7 8.4 copy-start.14
  759.5 23.5 %copy-start.11 = (bf16[1,128,2048]{1,2,0:T(8,128)(2,1)}, bf16[1,128,2048]{1,2,0:T(8,128)(2,1)S(1)}, u32[]{:S(2)}) copy-start(bf16[1,128,2048]{1,2,0:T(8,128)(2,1)S(1)} %copy.152) | copy-start | bytes 1572868 | tf_op jit(solution)/shard_map/while
  762.7 4.6 copy-start.1
  767.3 2.5 copy-start.7
  769.8 2.2 copy-start
  769.8 3.1 copy-start.3
  769.9 4.5 copy-start.16
  774.4 8.6 copy-start.18
  776.4 6.6 slice-start
  777.1 5.9 copy-start.10
  777.1 5.9 slice-start.1
  777.1 5.9 copy-start.9
  783.0 3.3 copy-start.6
  783.1 3.3 copy-start.8
  783.1 3.3 copy-start.17
  798.6 6.0 copy-start.2
  816.1 8.8 copy-start.5
  816.1 8.8 copy-start.15
  824.9 7.1 copy-start.4
  824.9 8.4 copy-start.14
  826.7 23.5 %copy-start.11 = (bf16[1,128,2048]{1,2,0:T(8,128)(2,1)}, bf16[1,128,2048]{1,2,0:T(8,128)(2,1)S(1)}, u32[]{:S(2)}) copy-start(bf16[1,128,2048]{1,2,0:T(8,128)(2,1)S(1)} %copy.152) | copy-start | bytes 1572868 | tf_op jit(solution)/shard_map/while
  829.9 4.6 copy-start.1
  834.5 2.5 copy-start.7
  837.1 2.2 copy-start
  837.1 3.1 copy-start.3
  837.1 4.5 copy-start.16
  841.7 8.6 copy-start.18
  843.6 6.6 slice-start
  844.3 5.9 copy-start.10
  844.3 5.9 slice-start.1
  844.3 5.9 copy-start.9
  850.3 3.3 copy-start.6
  850.3 3.3 copy-start.8
  850.3 3.3 copy-start.17
  865.8 6.0 copy-start.2
  883.3 8.8 copy-start.5
  883.3 8.8 copy-start.15
  906.4 419.4 %all-reduce.5.cloned.1.call-start = ((), (), s32[]{:S(2)}) async-start(), calls=%async_computation.1 | async-start | bytes 2097152
  911.3 9.1 copy-start.19
  911.3 415.4 %collective-permute-start.1 = (f32[2,128,2048]{2,1,0:T(8,128)}, f32[2,128,2048]{2,1,0:T(8,128)}, u32[]{:S(2)}, u32[]{:S(2)}) collective-permute-start(f32[2,128,2048]{2,1,0:T(8,128)} %pad_maximum_fusion.11), channel_id=1, source_target_pairs={{1,0},{2,1},{3,2},{4,3},{5,4},{6,5},{7,6},{8,7},{9,8},{10,9},{11,1... | collective-permute-start | bytes 6291464 | tf_op jit(solution)/shard_map/ppermute | solution.py:21
Sparse Core Ops, SparseCore 0:
  10.4 705.7 all-gather.2
  906.5 277.9 all-reduce.6
  1187.9 137.8 all-reduce.4
where the time goes:
time: 1350 us; the launch traced here: 1340 us
  waiting for transfers between devices  1040 us (77%)
  local copies, waits for them, and re-layouts  137 us (10%)
  blocking collectives  55.6 us (4%)
  matrix products  34.3 us (3%)
  other arithmetic  33.8 us (3%)
  loops' own time  15.1 us (1%)
  between operations  15 us (1%)
    all_gather x1, waiting for transfers between devices, per_device(): lax.all_gather(pool_runs(pooled, 4, 2.0), ('grp', 'loc'), axis=1, tiled=T...  638 us
    unnamed x5, waiting for transfers between devices  403 us
    all_gather x1, blocking collectives, per_device(): second = lax.all_gather(pooled, 'loc', axis=1, tiled=True)  55.6 us
  transfers between devices with their start and end apart: 5, of which 3 were waited for; matrix products, arithmetic and copies ran while one was open for 1% of the time, Pallas kernels for 0%

commit v1 on v0

v1 whole, which is shorter than its diff:
```python
import math

import jax
import jax.numpy as jnp
import numpy as np
from jax import lax
from jax.experimental import pallas as pl
from jax.experimental.pallas import tpu as pltpu
from jax.sharding import Mesh, PartitionSpec as P

HEADS = 16
HDIM = 128
BLK = 128
P2 = 64
FEAT = HEADS * HDIM
NEG_BIG = -1e30
LOG2E = math.log2(math.e)
SCALE = 1.0 / math.sqrt(HDIM)

NXH, NY, NC, NZ, NXL = 2, 4, 2, 8, 2
AXES = ("xh", "y", "c", "z", "xl")
N2 = NZ * NXL * 4
N3G = NZ * NXL
N3 = N3G * NXH * NY * NC
NP = N2 + N3
HPB = 4


def nt(a, b):
    return lax.dot_general(a, b, (((1,), (1,)), ((), ())), preferred_element_type=jnp.float32)


def nn(a, b):
    return lax.dot_general(a, b, (((1,), (0,)), ((), ())), preferred_element_type=jnp.float32)


def tn(a, b):
    return lax.dot_general(a, b, (((0,), (0,)), ((), ())), preferred_element_type=jnp.float32)


def one_head(bias_ref, seg, refs, outs):
    q_ref, k_ref, v_ref, g_ref, prior_x_ref, prior_z_ref, pk2_ref, pv2_ref = refs[:8]
    thirds = refs[8:]
    att_ref, dq_ref, dk_ref, dv_ref, dprior_ref, g2_ref, near_ref, far_ref = outs
    q = q_ref[:, seg]
    k = k_ref[:, seg]
    v = v_ref[:, seg]
    g = g_ref[:, seg]
    prior_k = prior_x_ref[0, :, seg] + prior_z_ref[0, :, seg]
    prior_v = prior_x_ref[1, :, seg] + prior_z_ref[1, :, seg]
    pk = jnp.concatenate(
        [pk2_ref[:, seg]] + [t[s, 0, :, seg] for t in thirds for s in range(NXH)], axis=0
    )
    pv = jnp.concatenate(
        [pv2_ref[:, seg]] + [t[s, 1, :, seg] for t in thirds for s in range(NXH)], axis=0
    )
    c2 = SCALE * LOG2E
    key_i = lax.broadcasted_iota(jnp.int32, (BLK, BLK), 0)
    qry_i = lax.broadcasted_iota(jnp.int32, (BLK, BLK), 1)
    causal = key_i <= qry_i
    q0, q1 = q[:BLK], q[BLK:]
    g0, g1 = g[:BLK], g[BLK:]
    k0, k1 = k[:BLK], k[BLK:]
    v0, v1 = v[:BLK], v[BLK:]

    sp = nt(pk, q) * c2 + bias_ref[BLK:, :]
    s_prior = nt(prior_k, q0) * c2 + bias_ref[:BLK, :BLK]
    s_k0 = nt(k0, q) * c2
    s00 = jnp.where(causal, s_k0[:, :BLK], NEG_BIG)
    s01 = s_k0[:, BLK:]
    s11 = jnp.where(causal, nt(k1, q1) * c2, NEG_BIG)

    fine = ((s_prior, s00), (s01, s11))
    fine_k = ((prior_v, v0), (v0, v1))
    expo, invs, atts, deltas = [], [], [], []
    for b in range(2):
        cols = slice(b * BLK, (b + 1) * BLK)
        sa, sb = fine[b]
        spb = sp[:, cols]
        top = jnp.maximum(
            jnp.max(spb, axis=0, keepdims=True), jnp.max(jnp.maximum(sa, sb), axis=0, keepdims=True)
        )
        ea = jnp.exp2(sa - top)
        eb = jnp.exp2(sb - top)
        ep = jnp.exp2(spb - top)
        tot = jnp.sum(ea + eb, axis=0, keepdims=True) + jnp.sum(ep, axis=0, keepdims=True)
        inv = 1.0 / tot
        invs.append(inv)
        expo.append((ea, eb, ep))
    ep_all = jnp.concatenate(
        [expo[0][2].astype(jnp.bfloat16), expo[1][2].astype(jnp.bfloat16)], axis=1
    )
    mixed_p = tn(ep_all, pv)
    g32 = g.astype(jnp.float32)
    for b in range(2):
        rows = slice(b * BLK, (b + 1) * BLK)
        va, vb = fine_k[b]
        ea, eb, _ = expo[b]
        mixed = mixed_p[rows] + tn(ea.astype(jnp.bfloat16), va) + tn(eb.astype(jnp.bfloat16), vb)
        inv_col = jnp.transpose(jnp.broadcast_to(invs[b], (8, BLK)))[:, 0:1]
        att = (mixed * inv_col).astype(jnp.bfloat16)
        att_ref[rows, seg] = att
        delta_col = jnp.sum(g32[rows] * att.astype(jnp.float32), axis=1, keepdims=True)
        deltas.append(jnp.transpose(jnp.broadcast_to(delta_col, (BLK, BLK)))[0:1, :])

    dp = nt(pv, g)
    d_prior = nt(prior_v, g0)
    d_k0 = nt(v0, g)
    d11 = nt(v1, g1)
    dots = ((d_prior, d_k0[:, :BLK]), (d_k0[:, BLK:], d11))
    ws, ds = [], []
    for b in range(2):
        cols = slice(b * BLK, (b + 1) * BLK)
        wts = [e * invs[b] for e in expo[b]]
        dot_b = dots[b] + (dp[:, cols],)
        ws.append([w.astype(jnp.bfloat16) for w in wts])
        ds.append(
            [(w * SCALE * (d - deltas[b])).astype(jnp.bfloat16) for w, d in zip(wts, dot_b)]
        )
    wp = jnp.concatenate([ws[0][2], ws[1][2]], axis=1)
    dsp = jnp.concatenate([ds[0][2], ds[1][2]], axis=1)
    wk0 = jnp.concatenate([ws[0][1], ws[1][0]], axis=1)
    dsk0 = jnp.concatenate([ds[0][1], ds[1][0]], axis=1)

    dq = tn(dsp, pk)
    dq0 = dq[:BLK] + tn(ds[0][0], prior_k) + tn(ds[0][1], k0)
    dq1 = dq[BLK:] + tn(ds[1][0], k0) + tn(ds[1][1], k1)
    dq_ref[:BLK, seg] = dq0.astype(jnp.bfloat16)
    dq_ref[BLK:, seg] = dq1.astype(jnp.bfloat16)

    dprior_ref[0, :, seg] = nn(ds[0][0], q0).astype(jnp.bfloat16)
    dprior_ref[1, :, seg] = nn(ws[0][0], g0).astype(jnp.bfloat16)
    dk_ref[:BLK, seg] = nn(dsk0, q)
    dk_ref[BLK:, seg] = nn(ds[1][1], q1)
    dv_ref[:BLK, seg] = nn(wk0, g)
    dv_ref[BLK:, seg] = nn(ws[1][1], g1)
    gkp = nn(dsp, q)
    gvp = nn(wp, g)
    for kv, part in enumerate((gkp, gvp)):
        for s in range(NZ):
            g2_ref[s, kv, :, seg] = part[s * 8 : s * 8 + 8]
        for s in range(2 * NY * NXH):
            lo = N2 + s * N3G
            ref = near_ref if s < NY * NXH else far_ref
            ref[s // NXH % NY, s % NXH, kv, :, seg] = part[lo : lo + N3G].astype(jnp.bfloat16)


def attn_kernel(bias_ref, *refs):
    for h in range(HPB):
        seg = slice(h * HDIM, (h + 1) * HDIM)
        one_head(bias_ref, seg, refs[:16], refs[16:])


def cols(width, *lead):
    zeros = (0,) * len(lead)
    return pl.BlockSpec(lead + (width,), lambda i: zeros + (i,))


def attention(bias, q, k, v, g, prior_x, prior_z, pk2, pv2, thirds):
    width = HPB * HDIM
    rows = q.shape[0]
    shape = jax.ShapeDtypeStruct
    row_spec = cols(width, rows)
    sums_spec = cols(width, NY, NXH, 2, N3G)
    return pl.pallas_call(
        attn_kernel,
        grid=(FEAT // width,),
        in_specs=[
            pl.BlockSpec((BLK + NP, 2 * BLK), lambda i: (0, 0)),
            row_spec, row_spec, row_spec, row_spec,
            cols(width, 2, BLK), cols(width, 2, BLK), cols(width, N2), cols(width, N2),
        ] + [cols(width, NXH, 2, N3G)] * 8,
        out_specs=[
            row_spec, row_spec, row_spec, row_spec,
            cols(width, 2, BLK), cols(width, NZ, 2, 8), sums_spec, sums_spec,
        ],
        out_shape=[
            shape((rows, FEAT), jnp.bfloat16),
            shape((rows, FEAT), jnp.bfloat16),
            shape((rows, FEAT), jnp.float32),
            shape((rows, FEAT), jnp.float32),
            shape((2, BLK, FEAT), jnp.bfloat16),
            shape((NZ, 2, 8, FEAT), jnp.float32),
            shape((NY, NXH, 2, N3G, FEAT), jnp.bfloat16),
            shape((NY, NXH, 2, N3G, FEAT), jnp.bfloat16),
        ],
        compiler_params=pltpu.CompilerParams(vmem_limit_bytes=48 * 1024 * 1024),
        cost_estimate=pl.CostEstimate(
            flops=6 * 2 * 2 * BLK * 576 * FEAT, bytes_accessed=20 << 20, transcendentals=0
        ),
    )(bias, q, k, v, g, prior_x, prior_z, pk2, pv2, *thirds)


def pool_kernel(k_ref, v_ref, pooled_ref, last_ref):
    for kv, ref in ((0, k_ref), (1, v_ref)):
        last_ref[kv] = ref[BLK:, :]
        for e in range(4):
            run = ref[e * P2 : (e + 1) * P2, :].astype(jnp.float32)
            total = jnp.sum(run, axis=0, keepdims=True) * (1.0 / math.sqrt(P2))
            pooled_ref[kv, e : e + 1, :] = total.astype(jnp.bfloat16)


def pool(k, v):
    width = 512
    rows = k.shape[0]
    shape = jax.ShapeDtypeStruct
    return pl.pallas_call(
        pool_kernel,
        grid=(FEAT // width,),
        in_specs=[cols(width, rows)] * 2,
        out_specs=[cols(width, 2, 4), cols(width, 2, BLK)],
        out_shape=[
            shape((2, 4, FEAT), jnp.bfloat16),
            shape((2, BLK, FEAT), jnp.bfloat16),
        ],
        compiler_params=pltpu.CompilerParams(vmem_limit_bytes=32 * 1024 * 1024),
        cost_estimate=pl.CostEstimate(flops=1 << 20, bytes_accessed=3 << 20, transcendentals=0),
    )(k, v)


def gathered_kernel(*refs):
    pieces, (pk_ref, pv_ref, third_ref) = refs[:NZ], refs[NZ:]
    for kv, out in ((0, pk_ref), (1, pv_ref)):
        parts = [p[kv].astype(jnp.float32) for p in pieces]
        out[...] = jnp.concatenate(parts, axis=0).astype(jnp.bfloat16)
        sums = [
            jnp.sum(p[lo : lo + 4], axis=0, keepdims=True) * 0.5 for p in parts for lo in (0, 4)
        ]
        third_ref[0, kv] = jnp.concatenate(sums, axis=0).astype(jnp.bfloat16)


def gathered(pieces):
    width = 1024
    shape = jax.ShapeDtypeStruct
    return pl.pallas_call(
        gathered_kernel,
        grid=(FEAT // width,),
        in_specs=[cols(width, 2, 8)] * NZ,
        out_specs=[cols(width, N2), cols(width, N2), cols(width, 1, 2, N3G)],
        out_shape=[
            shape((N2, FEAT), jnp.bfloat16),
            shape((N2, FEAT), jnp.bfloat16),
            shape((NXH, 2, N3G, FEAT), jnp.bfloat16),
        ],
        compiler_params=pltpu.CompilerParams(vmem_limit_bytes=32 * 1024 * 1024),
        cost_estimate=pl.CostEstimate(flops=1 << 20, bytes_accessed=1 << 20, transcendentals=0),
    )(*pieces)


def lifted_kernel(g2_ref, mine_ref, other_ref, *outs):
    for kv in range(2):
        third = (mine_ref[kv] + other_ref[kv].astype(jnp.float32)) * 0.5
        for s in range(NZ):
            lift = jnp.concatenate(
                [jnp.broadcast_to(third[s * 2 + i : s * 2 + i + 1], (4, third.shape[1])) for i in range(2)],
                axis=0,
            )
            outs[s][kv] = (g2_ref[s, kv] + lift).astype(outs[s].dtype)


def lifted(g2, mine, other):
    width = 1024
    shape = jax.ShapeDtypeStruct
    return pl.pallas_call(
        lifted_kernel,
        grid=(FEAT // width,),
        in_specs=[cols(width, NZ, 2, 8), cols(width, 2, N3G), cols(width, 2, N3G)],
        out_specs=[cols(width, 2, 8)] * NZ,
        out_shape=[
            shape((2, 8, FEAT), jnp.float32 if s == 0 else jnp.bfloat16) for s in range(NZ)
        ],
        compiler_params=pltpu.CompilerParams(vmem_limit_bytes=32 * 1024 * 1024),
        cost_estimate=pl.CostEstimate(flops=1 << 20, bytes_accessed=2 << 20, transcendentals=0),
    )(g2, mine, other)


def finish_kernel(dk_ref, dv_ref, back_x_ref, back_z_ref, two_ref, gk_ref, gv_ref):
    for kv, src, dst in ((0, dk_ref, gk_ref), (1, dv_ref, gv_ref)):
        for part in range(4):
            lo = part * P2
            spread = two_ref[kv, part : part + 1, :]
            val = src[lo : lo + P2, :] + spread
            if part >= 2:
                rows = slice(lo - BLK, lo - BLK + P2)
                back = back_x_ref[kv, rows, :] + back_z_ref[kv, rows, :]
                val = val + back.astype(jnp.float32)
            dst[lo : lo + P2, :] = val.astype(jnp.bfloat16)


def finish(dk, dv, back_x, back_z, two):
    rows = dk.shape[0]
    width = 512
    shape = jax.ShapeDtypeStruct
    return pl.pallas_call(
        finish_kernel,
        grid=(FEAT // width,),
        in_specs=[cols(width, rows)] * 2 + [cols(width, 2, BLK)] * 2 + [cols(width, 2, 4)],
        out_specs=[cols(width, rows)] * 2,
        out_shape=[shape((rows, FEAT), jnp.bfloat16)] * 2,
        compiler_params=pltpu.CompilerParams(vmem_limit_bytes=48 * 1024 * 1024),
        cost_estimate=pl.CostEstimate(flops=1 << 20, bytes_accessed=7 << 20, transcendentals=0),
    )(dk, dv, back_x, back_z, two)


def ring(value, axis, size, step):
    return lax.ppermute(value, axis, [(i, (i + step) % size) for i in range(size)])


def bf(x):
    return x.astype(jnp.bfloat16)


def f32(x):
    return x.astype(jnp.float32)


def per_device(queries, keys, values, grad_out):
    xh, y, c, z, xl = (lax.axis_index(a) for a in AXES)
    group = xh * (NY * NC) + y * NC + c
    shard = z * NXL + xl
    count = NXH * NY * NC * NZ * NXL

    pooled, last = pool(keys, values)
    pair = jnp.concatenate([pooled, ring(pooled, "xl", NXL, 1)], axis=1)
    last, pair = lax.optimization_barrier((last, pair))
    prior_x = lax.ppermute(last, AXES, [(i, i + 1) for i in range(0, count - 1, 2)])
    pieces = [pair] + [ring(pair, "z", NZ, s) for s in range(1, NZ)]
    pk2, pv2, third = gathered(pieces)
    own_third = third[0]
    prior_x, last, own_third = lax.optimization_barrier((prior_x, last, own_third))
    prior_z = lax.ppermute(last, AXES, [(i, i + 1) for i in range(1, count - 1, 2)])
    third = third.at[1].set(ring(own_third, "xh", NXH, 1))
    thirds = [third] + [ring(third, "y", NY, s) for s in range(1, NY)]
    thirds = thirds + [ring(t, "c", NC, 1) for t in thirds]

    r2 = jnp.arange(N2, dtype=jnp.int32)
    from_shard = ((z - r2 // 8) % NZ) * NXL + (xl + r2 // 4) % NXL
    entry = from_shard * 4 + r2 % 4
    ok2 = entry[:, None] < (4 * shard - 2 + 2 * jnp.arange(2, dtype=jnp.int32))[None, :]
    r3 = jnp.arange(N3, dtype=jnp.int32)
    per_xh, per_y = N3G, N3G * NXH
    per_c = per_y * NY
    from_group = (
        ((xh + r3 // per_xh) % NXH) * (NY * NC)
        + ((y - (r3 // per_y) % NY) % NY) * NC
        + (c + r3 // per_c) % NC
    )
    ok3 = jnp.broadcast_to((from_group < group)[:, None], (N3, 2))
    ok_prior = jnp.broadcast_to((group * (NZ * NXL) + shard) > 0, (BLK, 2))
    allowed = jnp.concatenate([ok_prior, ok2, ok3], axis=0)
    bias = jnp.repeat(jnp.where(allowed, 0.0, NEG_BIG).astype(jnp.float32), BLK, axis=1)

    attended, grad_q, dk, dv, dprior, g2, near, far = attention(
        bias, queries, keys, values, grad_out, prior_x, prior_z, pk2, pv2, thirds
    )

    back_z = lax.ppermute(dprior, AXES, [(i + 1, i) for i in range(1, count - 1, 2)])

    far = ring(far, "c", NC, 1)
    s3 = [f32(near[s]) + f32(far[s]) for s in range(NY)]
    t3 = s3[0]
    for s in range(1, NY):
        t3 = t3 + f32(ring(bf(s3[s]), "y", NY, -s))
    other = ring(bf(t3[1]), "xh", NXH, 1)
    dprior, other = lax.optimization_barrier((dprior, other))
    back_x = lax.ppermute(dprior, AXES, [(i + 1, i) for i in range(0, count - 1, 2)])
    parts = lifted(g2, t3[0], other)
    two = parts[0]
    for s in range(1, NZ):
        two = two + f32(ring(parts[s], "z", NZ, -s))
    back_z, two = lax.optimization_barrier((back_z, two))
    two = two[:, :4] + f32(ring(bf(two[:, 4:]), "xl", NXL, 1))
    two = two / math.sqrt(P2)
    grad_k, grad_v = finish(dk, dv, back_x, back_z, two)
    return attended, grad_q, grad_k, grad_v


def solution(mesh):
    fine_mesh = Mesh(np.asarray(mesh.devices).reshape(NXH, NY, NC, NZ, NXL), AXES)
    spec = P(AXES, None)
    return jax.shard_map(
        per_device,
        mesh=fine_mesh,
        in_specs=(spec,) * 4,
        out_specs=(spec,) * 4,
        check_vma=False,
    )
```

time: 1350 us -> 182 us (0.13)
  waiting for transfers between devices: 1040 us -> 58.8 us
  local copies, waits for them, and re-layouts: 137 us -> 4.95 us
  starting transfers between devices: 9.24 us -> 87 us
  blocking collectives: 55.6 us -> 0 us
  matrix products: 34.3 us -> 0 us
  other arithmetic: 33.8 us -> 0.66 us
  Pallas kernels: 0 us -> 26.9 us
  loops' own time: 15.1 us -> 0 us
  between operations: 15 us -> 0.91 us
    all_gather x1 -> x0, waiting for transfers between devices: 638 us -> none  [per_device(): lax.all_gather(pool_runs(pooled, 4, 2.0), ('grp', 'loc'), axis=1, tiled=T...]
    unnamed x5 -> x0, waiting for transfers between devices: 403 us -> none
    ppermute x2 -> x33, starting transfers between devices: 9.12 us -> 87 us  [the longest x29 63.8 us: ring(): lax.ppermute(value, axis, [(i, (i + step) % size) for i in range(size)])]
    ppermute x2 -> x33, waiting for transfers between devices: 0.01 us -> 58.8 us  [the longest x29 57.7 us: ring(): lax.ppermute(value, axis, [(i, (i + step) % size) for i in range(size)])]
    all_gather x1 -> x0, blocking collectives: 55.6 us -> none  [per_device(): second = lax.all_gather(pooled, 'loc', axis=1, tiled=True)]
    dot_general x12 -> x0, matrix products: 34.3 us -> none  [the longest x2 11.8 us: block_terms(): jnp.einsum('hqk,khd->qhd', expo_terms.astype(jnp.bfloat16), value_h, pref...]
    slice x6 -> x1, local copies, waits for them, and re-layouts: 30.3 us -> 0.02 us  [per_device(): two = two[:, :4] + f32(ring(bf(two[:, 4:]), 'xl', NXL, 1))]
    pallas_call x0 -> x5, Pallas kernels: none -> 26.9 us  [the longest x1 21 us: attention(): pl.pallas_call(attn_kernel, grid=(FEAT // width,), in_specs=[pl.BlockSpec...]
  transfers between devices with their start and end apart: 5 -> 33, of which waited for: 3 -> 15; matrix products, arithmetic and copies ran while one was open for 1% -> 2% of each run, Pallas kernels for 0% -> 1%
where the time goes in v1:
time: 182 us; the launch traced here: 179 us
  starting transfers between devices  87 us (48%)
  waiting for transfers between devices  58.8 us (32%)
  Pallas kernels  26.9 us (15%)
  local copies, waits for them, and re-layouts  4.95 us (3%)
    ppermute x29, starting transfers between devices, ring(): lax.ppermute(value, axis, [(i, (i + step) % size) for i in range(size)])  63.8 us
    ppermute x29, waiting for transfers between devices, ring(): lax.ppermute(value, axis, [(i, (i + step) % size) for i in range(size)])  57.7 us
    pallas_call x1, Pallas kernels, attention(): pl.pallas_call(attn_kernel, grid=(FEAT // width,), in_specs=[pl.BlockSpec...  21 us
    ppermute x1, starting transfers between devices, per_device(): lax.ppermute(dprior, AXES, [(i + 1, i) for i in range(0, count - 1, 2)])  15.1 us
    ppermute x1, starting transfers between devices, per_device(): lax.ppermute(last, AXES, [(i, i + 1) for i in range(1, count - 1, 2)])  5.38 us
    pallas_call x1, Pallas kernels, finish(): pl.pallas_call(finish_kernel, grid=(FEAT // width,), in_specs=[cols(width...  3.92 us
  transfers between devices with their start and end apart: 33, of which 15 were waited for; matrix products, arithmetic and copies ran while one was open for 2% of the time, Pallas kernels for 1%

profile of v1, /device:TPU:2, one launch (start us, length us, event | category | flops | bytes accessed | tf_op | source)
XLA Modules:
  0.0 179.3 jit_solution(11855827982637700655)
XLA Ops:
  0.6 0.0 copy-start.1
  0.6 1.2 copy-done.1
  1.9 1.2 copy-done.2
  3.1 0.8 shard_map.75
  3.9 2.4 %collective-permute-start = (bf16[2,4,2048]{2,1,0:T(4,128)(2,1)S(1)}, bf16[2,4,2048]{2,1,0:T(4,128)(2,1)S(1)}, u32[]{:S(2)}, u32[]{:S(2)}) collective-permute-start(bf16[2,4,2048]{2,1,0:T(4,128)(2,1)S(1)} %get-tuple-element.49), channel_id=1, source_target_pairs={{0,1},{1,0},{2,3},{3,2},{4,5},{5,4},{6,7},{7,6},{8,9},{9,8},{10,11... | collective-permute-start | bytes 98312 | tf_op jit(solution)/shard_map/ppermute | solution.py:306
  6.3 1.9 %collective-permute-done = bf16[2,4,2048]{2,1,0:T(4,128)(2,1)S(1)} collective-permute-done((bf16[2,4,2048]{2,1,0:T(4,128)(2,1)S(1)}, bf16[2,4,2048]{2,1,0:T(4,128)(2,1)S(1)}, u32[]{:S(2)}, u32[]{:S(2)}) %collective-permute-start) | collective-permute-done | bytes 32800 | tf_op jit(solution)/shard_map/ppermute | solution.py:306
  8.2 1.3 collective-permute-start.1
  9.5 5.7 %collective-permute-start.8 = (bf16[2,8,2048]{2,1,0:T(8,128)(2,1)S(1)}, bf16[2,8,2048]{2,1,0:T(8,128)(2,1)S(1)}, u32[]{:S(2)}, u32[]{:S(2)}) collective-permute-start(bf16[2,8,2048]{2,1,0:T(8,128)(2,1)S(1)} %pad_maximum_fusion.refs_0_), channel_id=1, source_target_pairs={{0,14},{2,0},{4,2},{6,4},{8,6},{10,8},{12,10},{14,12},{1,15},{3,1}... | collective-permute-start | bytes 196616 | tf_op jit(solution)/shard_map/ppermute | solution.py:306
  15.2 1.5 collective-permute-start.7
  16.6 0.4 collective-permute-start.6
  17.1 5.0 %collective-permute-start.5 = (bf16[2,8,2048]{2,1,0:T(8,128)(2,1)S(1)}, bf16[2,8,2048]{2,1,0:T(8,128)(2,1)S(1)}, u32[]{:S(2)}, u32[]{:S(2)}) collective-permute-start(bf16[2,8,2048]{2,1,0:T(8,128)(2,1)S(1)} %pad_maximum_fusion.refs_0_), channel_id=1, source_target_pairs={{0,8},{2,10},{4,12},{6,14},{8,0},{10,2},{12,4},{14,6},{1,9},{3,11}... | collective-permute-start | bytes 196616 | tf_op jit(solution)/shard_map/ppermute | solution.py:306
  22.1 0.0 collective-permute-start.4
  22.1 0.0 collective-permute-done.7.refs_6_
  22.1 2.5 %collective-permute-start.3 = (bf16[2,8,2048]{2,1,0:T(8,128)(2,1)S(1)}, bf16[2,8,2048]{2,1,0:T(8,128)(2,1)S(1)}, u32[]{:S(2)}, u32[]{:S(2)}) collective-permute-start(bf16[2,8,2048]{2,1,0:T(8,128)(2,1)S(1)} %pad_maximum_fusion.refs_0_), channel_id=1, source_target_pairs={{0,4},{2,6},{4,8},{6,10},{8,12},{10,14},{12,0},{14,2},{1,5},{3,7},... | collective-permute-start | bytes 196616 | tf_op jit(solution)/shard_map/ppermute | solution.py:306
  24.6 1.1 collective-permute-done.6.refs_5_
  25.7 0.8 collective-permute-start.2
  26.5 1.2 collective-permute-done.5.refs_4_
  27.7 3.5 %collective-permute-done.4.refs_3_ = bf16[2,8,2048]{2,1,0:T(8,128)(2,1)S(1)} collective-permute-done((bf16[2,8,2048]{2,1,0:T(8,128)(2,1)S(1)}, bf16[2,8,2048]{2,1,0:T(8,128)(2,1)S(1)}, u32[]{:S(2)}, u32[]{:S(2)}) %collective-permute-start.4) | collective-permute-done | bytes 65568 | tf_op jit(solution)/shard_map/ppermute | solution.py:306
  31.2 2.7 %collective-permute-done.3.refs_2_ = bf16[2,8,2048]{2,1,0:T(8,128)(2,1)S(1)} collective-permute-done((bf16[2,8,2048]{2,1,0:T(8,128)(2,1)S(1)}, bf16[2,8,2048]{2,1,0:T(8,128)(2,1)S(1)}, u32[]{:S(2)}, u32[]{:S(2)}) %collective-permute-start.3) | collective-permute-done | bytes 65568 | tf_op jit(solution)/shard_map/ppermute | solution.py:306
  33.9 0.0 collective-permute-done.2.refs_1_
  33.9 0.8 shard_map.76
  34.7 0.0 copy-start.3
  34.7 2.2 %collective-permute-start.10 = (bf16[2,16,2048]{2,1,0:T(8,128)(2,1)S(1)}, bf16[2,16,2048]{2,1,0:T(8,128)(2,1)S(1)}, u32[]{:S(2)}, u32[]{:S(2)}) collective-permute-start(bf16[2,16,2048]{2,1,0:T(8,128)(2,1)S(1)} %slice_bitcast_fusion.1), channel_id=1, source_target_pairs={{0,128},{128,0},{1,129},{129,1},{2,130},{130,2},{3,131},{131,3},{4... | collective-permute-start | bytes 393224 | tf_op jit(solution)/shard_map/ppermute | solution.py:306
  37.0 5.4 %collective-permute-start.9 = (bf16[2,128,2048]{2,1,0:T(8,128)(2,1)S(1)}, bf16[2,128,2048]{2,1,0:T(8,128)(2,1)}, u32[]{:S(2)}, u32[]{:S(2)}) collective-permute-start(bf16[2,128,2048]{2,1,0:T(8,128)(2,1)S(1)} %get-tuple-element.54), channel_id=1, source_target_pairs={{1,2},{3,4},{5,6},{7,8},{9,10},{11,12},{13,14},{15,16},{17,18},{19... | collective-permute-start | bytes 3145736 | tf_op jit(solution)/shard_map/ppermute | solution.py:331
  42.3 0.0 collective-permute-done.10
  42.4 3.1 %collective-permute-start.13 = (bf16[2,2,16,2048]{3,2,1,0:T(8,128)(2,1)S(1)}, bf16[2,2,16,2048]{3,2,1,0:T(8,128)(2,1)S(1)}, u32[]{:S(2)}, u32[]{:S(2)}) collective-permute-start(bf16[2,2,16,2048]{3,2,1,0:T(8,128)(2,1)S(1)} %bitcast_dynamic-update-slice_fusion.refs_8_), channel_id=1, source_target_pairs={{0,96},{32,0},{64,32},{96,64},{1,97},{33,1},{65,33},{97,65},{2,98}... | collective-permute-start | bytes 786440 | tf_op jit(solution)/shard_map/ppermute | solution.py:306
  45.5 0.6 collective-permute-start.12
  46.1 1.0 collective-permute-start.11
  47.1 0.1 broadcast_compare_fusion
  47.1 0.0 collective-permute-start.14
  47.2 7.7 %collective-permute-done.13.refs_11_ = bf16[2,2,16,2048]{3,2,1,0:T(8,128)(2,1)S(1)} collective-permute-done((bf16[2,2,16,2048]{3,2,1,0:T(8,128)(2,1)S(1)}, bf16[2,2,16,2048]{3,2,1,0:T(8,128)(2,1)S(1)}, u32[]{:S(2)}, u32[]{:S(2)}) %collective-permute-start.13) | collective-permute-done | bytes 262176 | tf_op jit(solution)/shard_map/ppermute | solution.py:306
  54.8 1.0 collective-permute-done.12.refs_10_
  55.8 2.7 %collective-permute-done.11.refs_9_ = bf16[2,2,16,2048]{3,2,1,0:T(8,128)(2,1)S(1)} collective-permute-done((bf16[2,2,16,2048]{3,2,1,0:T(8,128)(2,1)S(1)}, bf16[2,2,16,2048]{3,2,1,0:T(8,128)(2,1)S(1)}, u32[]{:S(2)}, u32[]{:S(2)}) %collective-permute-start.11) | collective-permute-done | bytes 262176 | tf_op jit(solution)/shard_map/ppermute | solution.py:306
  58.5 0.0 collective-permute-start.15
  58.6 0.1 pad.6.clone
  58.7 0.8 copy.8
  59.5 1.5 broadcast_in_dim.26
  61.0 0.0 collective-permute-done.14.refs_12_
  61.1 1.1 collective-permute-done.9.refs_5_
  62.2 21.0 %shard_map.77 = (bf16[256,2048]{1,0:T(8,128)(2,1)}, bf16[256,2048]{1,0:T(8,128)(2,1)}, f32[256,2048]{1,0:T(8,128)}, f32[256,2048]{1,0:T(8,128)}, bf16[2,128,2048...) custom-call(f32[448,256]{1,0:T(8,128)S(1)} %bitcast.24, ...), custom_call_target="tpu_custom_call" | custom-call | flops 3623878656 | bytes 20971520 | tf_op jit(solution)/shard_map/pallas_call | solution.py:165
  83.2 0.0 collective-permute-start.18
  83.2 2.9 %collective-permute-done.18 = bf16[4,2,2,16,2048]{4,3,2,1,0:T(8,128)(2,1)S(1)} collective-permute-done((bf16[4,2,2,16,2048]{4,3,2,1,0:T(8,128)(2,1)}, bf16[4,2,2,16,2048]{4,3,2,1,0:T(8,128)(2,1)S(1)}, u32[]{:S(2)}, u32[]{:S(2)}) %collective-permute-start.18) | collective-permute-done | bytes 1048608 | tf_op jit(solution)/shard_map/ppermute | solution.py:306
  86.1 0.3 fusion.2
  86.3 3.1 %collective-permute-start.19 = (bf16[2,2,16,2048]{3,2,1,0:T(8,128)(2,1)S(1)}, bf16[2,2,16,2048]{3,2,1,0:T(8,128)(2,1)S(1)}, u32[]{:S(2)}, u32[]{:S(2)}) collective-permute-start(bf16[2,2,16,2048]{3,2,1,0:T(8,128)(2,1)S(1)} %get-tuple-element.80), channel_id=1, source_target_pairs={{0,96},{32,0},{64,32},{96,64},{1,97},{33,1},{65,33},{97,65},{2,98}... | collective-permute-start | bytes 786440 | tf_op jit(solution)/shard_map/ppermute | solution.py:306
  89.4 2.2 %collective-permute-start.20 = (bf16[2,2,16,2048]{3,2,1,0:T(8,128)(2,1)S(1)}, bf16[2,2,16,2048]{3,2,1,0:T(8,128)(2,1)S(1)}, u32[]{:S(2)}, u32[]{:S(2)}) collective-permute-start(bf16[2,2,16,2048]{3,2,1,0:T(8,128)(2,1)S(1)} %get-tuple-element.82), channel_id=1, source_target_pairs={{0,64},{32,96},{64,0},{96,32},{1,65},{33,97},{65,1},{97,33},{2,66}... | collective-permute-start | bytes 786440 | tf_op jit(solution)/shard_map/ppermute | solution.py:306
  91.6 1.4 collective-permute-start.24
  93.1 7.9 %collective-permute-done.19 = bf16[2,2,16,2048]{3,2,1,0:T(8,128)(2,1)S(1)} collective-permute-done((bf16[2,2,16,2048]{3,2,1,0:T(8,128)(2,1)S(1)}, bf16[2,2,16,2048]{3,2,1,0:T(8,128)(2,1)S(1)}, u32[]{:S(2)}, u32[]{:S(2)}) %collective-permute-start.19) | collective-permute-done | bytes 262176 | tf_op jit(solution)/shard_map/ppermute | solution.py:306
  100.9 3.4 %collective-permute-done.21 = bf16[2,2,16,2048]{3,2,1,0:T(8,128)(2,1)S(1)} collective-permute-done((bf16[2,2,16,2048]{3,2,1,0:T(8,128)(2,1)S(1)}, bf16[2,2,16,2048]{3,2,1,0:T(8,128)(2,1)S(1)}, u32[]{:S(2)}, u32[]{:S(2)}) %collective-permute-start.21) | collective-permute-done | bytes 262176 | tf_op jit(solution)/shard_map/ppermute | solution.py:306
  104.3 0.2 fusion.1
  104.5 0.6 collective-permute-start.22
  105.2 5.9 %collective-permute-done.22.other_ref = bf16[2,16,2048]{2,1,0:T(8,128)(2,1)S(1)} collective-permute-done((bf16[2,16,2048]{2,1,0:T(8,128)(2,1)S(1)}, bf16[2,16,2048]{2,1,0:T(8,128)(2,1)S(1)}, u32[]{:S(2)}, u32[]{:S(2)}) %collective-permute-start.22) | collective-permute-done | bytes 131104 | tf_op jit(solution)/shard_map/ppermute | solution.py:306
  111.1 0.4 shard_map.78
  111.5 21.0 %collective-permute-start.25 = (bf16[2,8,2048]{2,1,0:T(8,128)(2,1)S(1)}, bf16[2,8,2048]{2,1,0:T(8,128)(2,1)S(1)}, u32[]{:S(2)}, u32[]{:S(2)}) collective-permute-start(bf16[2,8,2048]{2,1,0:T(8,128)(2,1)S(1)} %get-tuple-element.69), channel_id=1, source_target_pairs={{0,14},{2,0},{4,2},{6,4},{8,6},{10,8},{12,10},{14,12},{1,15},{3,1}... | collective-permute-start | bytes 196616 | tf_op jit(solution)/shard_map/ppermute | solution.py:306
  132.5 1.4 collective-permute-start.27
  133.9 4.6 %collective-permute-start.28 = (bf16[2,8,2048]{2,1,0:T(8,128)(2,1)S(1)}, bf16[2,8,2048]{2,1,0:T(8,128)(2,1)S(1)}, u32[]{:S(2)}, u32[]{:S(2)}) collective-permute-start(bf16[2,8,2048]{2,1,0:T(8,128)(2,1)S(1)} %get-tuple-element.72), channel_id=1, source_target_pairs={{0,8},{2,10},{4,12},{6,14},{8,0},{10,2},{12,4},{14,6},{1,9},{3,11}... | collective-permute-start | bytes 196616 | tf_op jit(solution)/shard_map/ppermute | solution.py:306
  138.5 15.1 %collective-permute-start.23 = (bf16[2,128,2048]{2,1,0:T(8,128)(2,1)S(1)}, bf16[2,128,2048]{2,1,0:T(8,128)(2,1)S(1)}, u32[]{:S(2)}, u32[]{:S(2)}) collective-permute-start(bf16[2,128,2048]{2,1,0:T(8,128)(2,1)S(1)} %get-tuple-element.65), channel_id=1, source_target_pairs={{1,0},{3,2},{5,4},{7,6},{9,8},{11,10},{13,12},{15,14},{17,16},{19,... | collective-permute-start | bytes 3145736 | tf_op jit(solution)/shard_map/ppermute | solution.py:366
  153.6 0.3 collective-permute-start.29
  154.0 2.8 %collective-permute-start.30 = (bf16[2,8,2048]{2,1,0:T(8,128)(2,1)S(1)}, bf16[2,8,2048]{2,1,0:T(8,128)(2,1)S(1)}, u32[]{:S(2)}, u32[]{:S(2)}) collective-permute-start(bf16[2,8,2048]{2,1,0:T(8,128)(2,1)S(1)} %get-tuple-element.74), channel_id=1, source_target_pairs={{0,4},{2,6},{4,8},{6,10},{8,12},{10,14},{12,0},{14,2},{1,5},{3,7},... | collective-permute-start | bytes 196616 | tf_op jit(solution)/shard_map/ppermute | solution.py:306
  156.8 1.5 collective-permute-start.31
  158.3 5.3 %collective-permute-done.29 = bf16[2,8,2048]{2,1,0:T(8,128)(2,1)S(1)} collective-permute-done((bf16[2,8,2048]{2,1,0:T(8,128)(2,1)S(1)}, bf16[2,8,2048]{2,1,0:T(8,128)(2,1)S(1)}, u32[]{:S(2)}, u32[]{:S(2)}) %collective-permute-start.29) | collective-permute-done | bytes 65568 | tf_op jit(solution)/shard_map/ppermute | solution.py:306
  163.6 0.1 convert_add_fusion
  163.7 1.1 collective-permute-start.32
  164.7 10.6 %collective-permute-done.32 = bf16[2,4,2048]{2,1,0:T(4,128)(2,1)S(1)} collective-permute-done((bf16[2,4,2048]{2,1,0:T(4,128)(2,1)S(1)}, bf16[2,4,2048]{2,1,0:T(4,128)(2,1)S(1)}, u32[]{:S(2)}, u32[]{:S(2)}) %collective-permute-start.32) | collective-permute-done | bytes 32800 | tf_op jit(solution)/shard_map/ppermute | solution.py:306
  175.4 3.9 %shard_map.79 = (bf16[256,2048]{1,0:T(8,128)(2,1)}, bf16[256,2048]{1,0:T(8,128)(2,1)}) custom-call(f32[256,2048]{1,0:T(8,128)S(1)} %copy-done, f32[256,2048]{1,0:T(8,128)} %get-tuple-element.61.dv_ref, bf16[2,128,2048]{2,1,0:T(8,128)(2,1)S(1)} %collective-permute-done.23.back_x_ref, bf16[2,128,2048]{2,1,0:T(8,128)(2,1)S(1)} %collective-permute-done.24.back_z_ref, ...), custom_call_target="tpu_custom_call" | custom-call | flops 1048576 | bytes 7340032 | tf_op jit(solution)/shard_map/pallas_call | solution.py:294
  (36 shorter events, 0.3 us)
Async XLA Ops:
  0.6 1.2 copy-start.1
  1.9 1.2 copy-start.2
  3.9 4.3 %collective-permute-start = (bf16[2,4,2048]{2,1,0:T(4,128)(2,1)S(1)}, bf16[2,4,2048]{2,1,0:T(4,128)(2,1)S(1)}, u32[]{:S(2)}, u32[]{:S(2)}) collective-permute-start(bf16[2,4,2048]{2,1,0:T(4,128)(2,1)S(1)} %get-tuple-element.49), channel_id=1, source_target_pairs={{0,1},{1,0},{2,3},{3,2},{4,5},{5,4},{6,7},{7,6},{8,9},{9,8},{10,11... | collective-permute-start | bytes 98312 | tf_op jit(solution)/shard_map/ppermute | solution.py:306
  8.2 26.5 %collective-permute-start.1 = (bf16[2,128,2048]{2,1,0:T(8,128)(2,1)S(1)}, bf16[2,128,2048]{2,1,0:T(8,128)(2,1)S(1)}, u32[]{:S(2)}, u32[]{:S(2)}) collective-permute-start(bf16[2,128,2048]{2,1,0:T(8,128)(2,1)S(1)} %get-tuple-element.54), channel_id=1, source_target_pairs={{0,1},{2,3},{4,5},{6,7},{8,9},{10,11},{12,13},{14,15},{16,17},{18,... | collective-permute-start | bytes 3145736 | tf_op jit(solution)/shard_map/ppermute | solution.py:326
  9.5 12.6 %collective-permute-start.8 = (bf16[2,8,2048]{2,1,0:T(8,128)(2,1)S(1)}, bf16[2,8,2048]{2,1,0:T(8,128)(2,1)S(1)}, u32[]{:S(2)}, u32[]{:S(2)}) collective-permute-start(bf16[2,8,2048]{2,1,0:T(8,128)(2,1)S(1)} %pad_maximum_fusion.refs_0_), channel_id=1, source_target_pairs={{0,14},{2,0},{4,2},{6,4},{8,6},{10,8},{12,10},{14,12},{1,15},{3,1}... | collective-permute-start | bytes 196616 | tf_op jit(solution)/shard_map/ppermute | solution.py:306
  15.2 7.0 %collective-permute-start.7 = (bf16[2,8,2048]{2,1,0:T(8,128)(2,1)S(1)}, bf16[2,8,2048]{2,1,0:T(8,128)(2,1)S(1)}, u32[]{:S(2)}, u32[]{:S(2)}) collective-permute-start(bf16[2,8,2048]{2,1,0:T(8,128)(2,1)S(1)} %pad_maximum_fusion.refs_0_), channel_id=1, source_target_pairs={{0,12},{2,14},{4,0},{6,2},{8,4},{10,6},{12,8},{14,10},{1,13},{3,15... | collective-permute-start | bytes 196616 | tf_op jit(solution)/shard_map/ppermute | solution.py:306
  16.6 9.1 %collective-permute-start.6 = (bf16[2,8,2048]{2,1,0:T(8,128)(2,1)S(1)}, bf16[2,8,2048]{2,1,0:T(8,128)(2,1)S(1)}, u32[]{:S(2)}, u32[]{:S(2)}) collective-permute-start(bf16[2,8,2048]{2,1,0:T(8,128)(2,1)S(1)} %pad_maximum_fusion.refs_0_), channel_id=1, source_target_pairs={{0,10},{2,12},{4,14},{6,0},{8,2},{10,4},{12,6},{14,8},{1,11},{3,13... | collective-permute-start | bytes 196616 | tf_op jit(solution)/shard_map/ppermute | solution.py:306
  17.1 10.6 %collective-permute-start.5 = (bf16[2,8,2048]{2,1,0:T(8,128)(2,1)S(1)}, bf16[2,8,2048]{2,1,0:T(8,128)(2,1)S(1)}, u32[]{:S(2)}, u32[]{:S(2)}) collective-permute-start(bf16[2,8,2048]{2,1,0:T(8,128)(2,1)S(1)} %pad_maximum_fusion.refs_0_), channel_id=1, source_target_pairs={{0,8},{2,10},{4,12},{6,14},{8,0},{10,2},{12,4},{14,6},{1,9},{3,11}... | collective-permute-start | bytes 196616 | tf_op jit(solution)/shard_map/ppermute | solution.py:306
  22.1 9.0 %collective-permute-start.4 = (bf16[2,8,2048]{2,1,0:T(8,128)(2,1)S(1)}, bf16[2,8,2048]{2,1,0:T(8,128)(2,1)S(1)}, u32[]{:S(2)}, u32[]{:S(2)}) collective-permute-start(bf16[2,8,2048]{2,1,0:T(8,128)(2,1)S(1)} %pad_maximum_fusion.refs_0_), channel_id=1, source_target_pairs={{0,6},{2,8},{4,10},{6,12},{8,14},{10,0},{12,2},{14,4},{1,7},{3,9},... | collective-permute-start | bytes 196616 | tf_op jit(solution)/shard_map/ppermute | solution.py:306
  22.1 11.7 %collective-permute-start.3 = (bf16[2,8,2048]{2,1,0:T(8,128)(2,1)S(1)}, bf16[2,8,2048]{2,1,0:T(8,128)(2,1)S(1)}, u32[]{:S(2)}, u32[]{:S(2)}) collective-permute-start(bf16[2,8,2048]{2,1,0:T(8,128)(2,1)S(1)} %pad_maximum_fusion.refs_0_), channel_id=1, source_target_pairs={{0,4},{2,6},{4,8},{6,10},{8,12},{10,14},{12,0},{14,2},{1,5},{3,7},... | collective-permute-start | bytes 196616 | tf_op jit(solution)/shard_map/ppermute | solution.py:306
  25.7 8.1 %collective-permute-start.2 = (bf16[2,8,2048]{2,1,0:T(8,128)(2,1)S(1)}, bf16[2,8,2048]{2,1,0:T(8,128)(2,1)S(1)}, u32[]{:S(2)}, u32[]{:S(2)}) collective-permute-start(bf16[2,8,2048]{2,1,0:T(8,128)(2,1)S(1)} %pad_maximum_fusion.refs_0_), channel_id=1, source_target_pairs={{0,2},{2,4},{4,6},{6,8},{8,10},{10,12},{12,14},{14,0},{1,3},{3,5},... | collective-permute-start | bytes 196616 | tf_op jit(solution)/shard_map/ppermute | solution.py:306
  34.7 2.2 %copy-start.3 = (bf16[2,128,2048]{2,1,0:T(8,128)(2,1)}, bf16[2,128,2048]{2,1,0:T(8,128)(2,1)S(1)}, u32[]{:S(2)}) copy-start(bf16[2,128,2048]{2,1,0:T(8,128)(2,1)S(1)} %collective-permute-done.1.refs_4_) | copy-start | bytes 3145732
  34.7 7.6 %collective-permute-start.10 = (bf16[2,16,2048]{2,1,0:T(8,128)(2,1)S(1)}, bf16[2,16,2048]{2,1,0:T(8,128)(2,1)S(1)}, u32[]{:S(2)}, u32[]{:S(2)}) collective-permute-start(bf16[2,16,2048]{2,1,0:T(8,128)(2,1)S(1)} %slice_bitcast_fusion.1), channel_id=1, source_target_pairs={{0,128},{128,0},{1,129},{129,1},{2,130},{130,2},{3,131},{131,3},{4... | collective-permute-start | bytes 393224 | tf_op jit(solution)/shard_map/ppermute | solution.py:306
  37.0 25.2 %collective-permute-start.9 = (bf16[2,128,2048]{2,1,0:T(8,128)(2,1)S(1)}, bf16[2,128,2048]{2,1,0:T(8,128)(2,1)}, u32[]{:S(2)}, u32[]{:S(2)}) collective-permute-start(bf16[2,128,2048]{2,1,0:T(8,128)(2,1)S(1)} %get-tuple-element.54), channel_id=1, source_target_pairs={{1,2},{3,4},{5,6},{7,8},{9,10},{11,12},{13,14},{15,16},{17,18},{19... | collective-permute-start | bytes 3145736 | tf_op jit(solution)/shard_map/ppermute | solution.py:331
  42.4 12.5 %collective-permute-start.13 = (bf16[2,2,16,2048]{3,2,1,0:T(8,128)(2,1)S(1)}, bf16[2,2,16,2048]{3,2,1,0:T(8,128)(2,1)S(1)}, u32[]{:S(2)}, u32[]{:S(2)}) collective-permute-start(bf16[2,2,16,2048]{3,2,1,0:T(8,128)(2,1)S(1)} %bitcast_dynamic-update-slice_fusion.refs_8_), channel_id=1, source_target_pairs={{0,96},{32,0},{64,32},{96,64},{1,97},{33,1},{65,33},{97,65},{2,98}... | collective-permute-start | bytes 786440 | tf_op jit(solution)/shard_map/ppermute | solution.py:306
  45.5 10.4 %collective-permute-start.12 = (bf16[2,2,16,2048]{3,2,1,0:T(8,128)(2,1)S(1)}, bf16[2,2,16,2048]{3,2,1,0:T(8,128)(2,1)S(1)}, u32[]{:S(2)}, u32[]{:S(2)}) collective-permute-start(bf16[2,2,16,2048]{3,2,1,0:T(8,128)(2,1)S(1)} %bitcast_dynamic-update-slice_fusion.refs_8_), channel_id=1, source_target_pairs={{0,64},{32,96},{64,0},{96,32},{1,65},{33,97},{65,1},{97,33},{2,66}... | collective-permute-start | bytes 786440 | tf_op jit(solution)/shard_map/ppermute | solution.py:306
  46.1 12.4 %collective-permute-start.11 = (bf16[2,2,16,2048]{3,2,1,0:T(8,128)(2,1)S(1)}, bf16[2,2,16,2048]{3,2,1,0:T(8,128)(2,1)S(1)}, u32[]{:S(2)}, u32[]{:S(2)}) collective-permute-start(bf16[2,2,16,2048]{3,2,1,0:T(8,128)(2,1)S(1)} %bitcast_dynamic-update-slice_fusion.refs_8_), channel_id=1, source_target_pairs={{0,32},{32,64},{64,96},{96,0},{1,33},{33,65},{65,97},{97,1},{2,34}... | collective-permute-start | bytes 786440 | tf_op jit(solution)/shard_map/ppermute | solution.py:306
  47.1 13.9 %collective-permute-start.14 = (bf16[2,2,16,2048]{3,2,1,0:T(8,128)(2,1)S(1)}, bf16[2,2,16,2048]{3,2,1,0:T(8,128)(2,1)S(1)}, u32[]{:S(2)}, u32[]{:S(2)}) collective-permute-start(bf16[2,2,16,2048]{3,2,1,0:T(8,128)(2,1)S(1)} %bitcast_dynamic-update-slice_fusion.refs_8_), channel_id=1, source_target_pairs={{0,16},{16,0},{1,17},{17,1},{2,18},{18,2},{3,19},{19,3},{4,20},{20... | collective-permute-start | bytes 786440 | tf_op jit(solution)/shard_map/ppermute | solution.py:306
  54.8 6.2 %collective-permute-start.17 = (bf16[2,2,16,2048]{3,2,1,0:T(8,128)(2,1)S(1)}, bf16[2,2,16,2048]{3,2,1,0:T(8,128)(2,1)S(1)}, u32[]{:S(2)}, u32[]{:S(2)}) collective-permute-start(bf16[2,2,16,2048]{3,2,1,0:T(8,128)(2,1)S(1)} %collective-permute-done.13.refs_11_), channel_id=1, source_target_pairs={{0,16},{16,0},{1,17},{17,1},{2,18},{18,2},{3,19},{19,3},{4,20},{20... | collective-permute-start | bytes 786440 | tf_op jit(solution)/shard_map/ppermute | solution.py:306
  55.8 5.2 %collective-permute-start.16 = (bf16[2,2,16,2048]{3,2,1,0:T(8,128)(2,1)S(1)}, bf16[2,2,16,2048]{3,2,1,0:T(8,128)(2,1)S(1)}, u32[]{:S(2)}, u32[]{:S(2)}) collective-permute-start(bf16[2,2,16,2048]{3,2,1,0:T(8,128)(2,1)S(1)} %collective-permute-done.12.refs_10_), channel_id=1, source_target_pairs={{0,16},{16,0},{1,17},{17,1},{2,18},{18,2},{3,19},{19,3},{4,20},{20... | collective-permute-start | bytes 786440 | tf_op jit(solution)/shard_map/ppermute | solution.py:306
  58.5 2.5 %collective-permute-start.15 = (bf16[2,2,16,2048]{3,2,1,0:T(8,128)(2,1)S(1)}, bf16[2,2,16,2048]{3,2,1,0:T(8,128)(2,1)}, u32[]{:S(2)}, u32[]{:S(2)}) collective-permute-start(bf16[2,2,16,2048]{3,2,1,0:T(8,128)(2,1)S(1)} %collective-permute-done.11.refs_9_), channel_id=1, source_target_pairs={{0,16},{16,0},{1,17},{17,1},{2,18},{18,2},{3,19},{19,3},{4,20},{20... | collective-permute-start | bytes 786440 | tf_op jit(solution)/shard_map/ppermute | solution.py:306
  83.2 2.9 %collective-permute-start.18 = (bf16[4,2,2,16,2048]{4,3,2,1,0:T(8,128)(2,1)}, bf16[4,2,2,16,2048]{4,3,2,1,0:T(8,128)(2,1)S(1)}, u32[]{:S(2)}, u32[]{:S(2)}) collective-permute-start(bf16[4,2,2,16,2048]{4,3,2,1,0:T(8,128)(2,1)} %get-tuple-element.64), channel_id=1, source_target_pairs={{0,16},{16,0},{1,17},{17,1},{2,18},{18,2},{3,19},{19,3},{4,20},{20... | collective-permute-start | bytes 3145736 | tf_op jit(solution)/shard_map/ppermute | solution.py:306
  86.3 14.6 %collective-permute-start.19 = (bf16[2,2,16,2048]{3,2,1,0:T(8,128)(2,1)S(1)}, bf16[2,2,16,2048]{3,2,1,0:T(8,128)(2,1)S(1)}, u32[]{:S(2)}, u32[]{:S(2)}) collective-permute-start(bf16[2,2,16,2048]{3,2,1,0:T(8,128)(2,1)S(1)} %get-tuple-element.80), channel_id=1, source_target_pairs={{0,96},{32,0},{64,32},{96,64},{1,97},{33,1},{65,33},{97,65},{2,98}... | collective-permute-start | bytes 786440 | tf_op jit(solution)/shard_map/ppermute | solution.py:306
  89.4 14.9 %collective-permute-start.21 = (bf16[2,2,16,2048]{3,2,1,0:T(8,128)(2,1)S(1)}, bf16[2,2,16,2048]{3,2,1,0:T(8,128)(2,1)S(1)}, u32[]{:S(2)}, u32[]{:S(2)}) collective-permute-start(bf16[2,2,16,2048]{3,2,1,0:T(8,128)(2,1)S(1)} %get-tuple-element.81), channel_id=1, source_target_pairs={{0,32},{32,64},{64,96},{96,0},{1,33},{33,65},{65,97},{97,1},{2,34}... | collective-permute-start | bytes 786440 | tf_op jit(solution)/shard_map/ppermute | solution.py:306
  89.4 14.9 %collective-permute-start.20 = (bf16[2,2,16,2048]{3,2,1,0:T(8,128)(2,1)S(1)}, bf16[2,2,16,2048]{3,2,1,0:T(8,128)(2,1)S(1)}, u32[]{:S(2)}, u32[]{:S(2)}) collective-permute-start(bf16[2,2,16,2048]{3,2,1,0:T(8,128)(2,1)S(1)} %get-tuple-element.82), channel_id=1, source_target_pairs={{0,64},{32,96},{64,0},{96,32},{1,65},{33,97},{65,1},{97,33},{2,66}... | collective-permute-start | bytes 786440 | tf_op jit(solution)/shard_map/ppermute | solution.py:306
  91.6 83.8 %copy-start = (f32[256,2048]{1,0:T(8,128)S(1)}, f32[256,2048]{1,0:T(8,128)}, u32[]{:S(2)}) copy-start(f32[256,2048]{1,0:T(8,128)} %get-tuple-element.60.dk_ref) | copy-start | bytes 6291460
  91.6 72.0 %collective-permute-start.24 = (bf16[2,128,2048]{2,1,0:T(8,128)(2,1)S(1)}, bf16[2,128,2048]{2,1,0:T(8,128)(2,1)S(1)}, u32[]{:S(2)}, u32[]{:S(2)}) collective-permute-start(bf16[2,128,2048]{2,1,0:T(8,128)(2,1)S(1)} %get-tuple-element.65), channel_id=1, source_target_pairs={{2,1},{4,3},{6,5},{8,7},{10,9},{12,11},{14,13},{16,15},{18,17},{20... | collective-permute-start | bytes 3145736 | tf_op jit(solution)/shard_map/ppermute | solution.py:357
  104.5 6.6 %collective-permute-start.22 = (bf16[2,16,2048]{2,1,0:T(8,128)(2,1)S(1)}, bf16[2,16,2048]{2,1,0:T(8,128)(2,1)S(1)}, u32[]{:S(2)}, u32[]{:S(2)}) collective-permute-start(bf16[2,16,2048]{2,1,0:T(8,128)(2,1)S(1)} %fusion.5), channel_id=1, source_target_pairs={{0,128},{128,0},{1,129},{129,1},{2,130},{130,2},{3,131},{131,3},{4... | collective-permute-start | bytes 393224 | tf_op jit(solution)/shard_map/ppermute | solution.py:306
  111.5 27.0 %collective-permute-start.25 = (bf16[2,8,2048]{2,1,0:T(8,128)(2,1)S(1)}, bf16[2,8,2048]{2,1,0:T(8,128)(2,1)S(1)}, u32[]{:S(2)}, u32[]{:S(2)}) collective-permute-start(bf16[2,8,2048]{2,1,0:T(8,128)(2,1)S(1)} %get-tuple-element.69), channel_id=1, source_target_pairs={{0,14},{2,0},{4,2},{6,4},{8,6},{10,8},{12,10},{14,12},{1,15},{3,1}... | collective-permute-start | bytes 196616 | tf_op jit(solution)/shard_map/ppermute | solution.py:306
  132.5 21.2 %collective-permute-start.26 = (bf16[2,8,2048]{2,1,0:T(8,128)(2,1)S(1)}, bf16[2,8,2048]{2,1,0:T(8,128)(2,1)S(1)}, u32[]{:S(2)}, u32[]{:S(2)}) collective-permute-start(bf16[2,8,2048]{2,1,0:T(8,128)(2,1)S(1)} %get-tuple-element.70), channel_id=1, source_target_pairs={{0,12},{2,14},{4,0},{6,2},{8,4},{10,6},{12,8},{14,10},{1,13},{3,15... | collective-permute-start | bytes 196616 | tf_op jit(solution)/shard_map/ppermute | solution.py:306
  132.5 21.5 %collective-permute-start.27 = (bf16[2,8,2048]{2,1,0:T(8,128)(2,1)S(1)}, bf16[2,8,2048]{2,1,0:T(8,128)(2,1)S(1)}, u32[]{:S(2)}, u32[]{:S(2)}) collective-permute-start(bf16[2,8,2048]{2,1,0:T(8,128)(2,1)S(1)} %get-tuple-element.71), channel_id=1, source_target_pairs={{0,10},{2,12},{4,14},{6,0},{8,2},{10,4},{12,6},{14,8},{1,11},{3,13... | collective-permute-start | bytes 196616 | tf_op jit(solution)/shard_map/ppermute | solution.py:306
  133.9 22.9 %collective-permute-start.28 = (bf16[2,8,2048]{2,1,0:T(8,128)(2,1)S(1)}, bf16[2,8,2048]{2,1,0:T(8,128)(2,1)S(1)}, u32[]{:S(2)}, u32[]{:S(2)}) collective-permute-start(bf16[2,8,2048]{2,1,0:T(8,128)(2,1)S(1)} %get-tuple-element.72), channel_id=1, source_target_pairs={{0,8},{2,10},{4,12},{6,14},{8,0},{10,2},{12,4},{14,6},{1,9},{3,11}... | collective-permute-start | bytes 196616 | tf_op jit(solution)/shard_map/ppermute | solution.py:306
  138.5 36.9 %collective-permute-start.23 = (bf16[2,128,2048]{2,1,0:T(8,128)(2,1)S(1)}, bf16[2,128,2048]{2,1,0:T(8,128)(2,1)S(1)}, u32[]{:S(2)}, u32[]{:S(2)}) collective-permute-start(bf16[2,128,2048]{2,1,0:T(8,128)(2,1)S(1)} %get-tuple-element.65), channel_id=1, source_target_pairs={{1,0},{3,2},{5,4},{7,6},{9,8},{11,10},{13,12},{15,14},{17,16},{19,... | collective-permute-start | bytes 3145736 | tf_op jit(solution)/shard_map/ppermute | solution.py:366
  153.6 9.9 %collective-permute-start.29 = (bf16[2,8,2048]{2,1,0:T(8,128)(2,1)S(1)}, bf16[2,8,2048]{2,1,0:T(8,128)(2,1)S(1)}, u32[]{:S(2)}, u32[]{:S(2)}) collective-permute-start(bf16[2,8,2048]{2,1,0:T(8,128)(2,1)S(1)} %get-tuple-element.73), channel_id=1, source_target_pairs={{0,6},{2,8},{4,10},{6,12},{8,14},{10,0},{12,2},{14,4},{1,7},{3,9},... | collective-permute-start | bytes 196616 | tf_op jit(solution)/shard_map/ppermute | solution.py:306
  154.0 9.6 %collective-permute-start.30 = (bf16[2,8,2048]{2,1,0:T(8,128)(2,1)S(1)}, bf16[2,8,2048]{2,1,0:T(8,128)(2,1)S(1)}, u32[]{:S(2)}, u32[]{:S(2)}) collective-permute-start(bf16[2,8,2048]{2,1,0:T(8,128)(2,1)S(1)} %get-tuple-element.74), channel_id=1, source_target_pairs={{0,4},{2,6},{4,8},{6,10},{8,12},{10,14},{12,0},{14,2},{1,5},{3,7},... | collective-permute-start | bytes 196616 | tf_op jit(solution)/shard_map/ppermute | solution.py:306
  156.8 6.8 %collective-permute-start.31 = (bf16[2,8,2048]{2,1,0:T(8,128)(2,1)S(1)}, bf16[2,8,2048]{2,1,0:T(8,128)(2,1)S(1)}, u32[]{:S(2)}, u32[]{:S(2)}) collective-permute-start(bf16[2,8,2048]{2,1,0:T(8,128)(2,1)S(1)} %get-tuple-element.75), channel_id=1, source_target_pairs={{0,2},{2,4},{4,6},{6,8},{8,10},{10,12},{12,14},{14,0},{1,3},{3,5},... | collective-permute-start | bytes 196616 | tf_op jit(solution)/shard_map/ppermute | solution.py:306
  163.7 11.7 %collective-permute-start.32 = (bf16[2,4,2048]{2,1,0:T(4,128)(2,1)S(1)}, bf16[2,4,2048]{2,1,0:T(4,128)(2,1)S(1)}, u32[]{:S(2)}, u32[]{:S(2)}) collective-permute-start(bf16[2,4,2048]{2,1,0:T(4,128)(2,1)S(1)} %slice.101), channel_id=1, source_target_pairs={{0,1},{1,0},{2,3},{3,2},{4,5},{5,4},{6,7},{7,6},{8,9},{9,8},{10,11... | collective-permute-start | bytes 98312 | tf_op jit(solution)/shard_map/ppermute | solution.py:306

commit v2 on v1

v2 whole, which is shorter than its diff:
```python
import math

import jax
import jax.numpy as jnp
import numpy as np
from jax import lax
from jax.experimental import pallas as pl
from jax.experimental.pallas import tpu as pltpu
from jax.sharding import Mesh, PartitionSpec as P

HEADS = 16
HDIM = 128
BLK = 128
P2 = 64
FEAT = HEADS * HDIM
NEG_BIG = -1e30
LOG2E = math.log2(math.e)
SCALE = 1.0 / math.sqrt(HDIM)

NXH, NY, NC, NZ, NXL = 2, 4, 2, 8, 2
AXES = ("xh", "y", "c", "z", "xl")
N2 = NZ * NXL * 4
N3G = NZ * NXL
N3 = N3G * NXH * NY * NC
NP = N2 + N3
HPB = 4
Z_ORDER = (4, 5, 3, 6, 2, 7, 1)
Y_STEP = (0, 1, 3, 2)


def nt(a, b):
    return lax.dot_general(a, b, (((1,), (1,)), ((), ())), preferred_element_type=jnp.float32)


def nn(a, b):
    return lax.dot_general(a, b, (((1,), (0,)), ((), ())), preferred_element_type=jnp.float32)


def tn(a, b):
    return lax.dot_general(a, b, (((0,), (0,)), ((), ())), preferred_element_type=jnp.float32)


def one_head(odd, bias_ref, seg, refs, outs):
    q_ref, k_ref, v_ref, g_ref, across_ref, along_ref, pk2_ref, pv2_ref = refs[:8]
    thirds = refs[8:]
    att_ref, dq_ref, dk_ref, dv_ref, dprior_ref, g2_ref, near_ref, far_ref = outs
    q = q_ref[:, seg]
    k = k_ref[:, seg]
    v = v_ref[:, seg]
    g = g_ref[:, seg]
    prior_k = jnp.where(odd, across_ref[0, :, seg], along_ref[0, :, seg])
    prior_v = jnp.where(odd, across_ref[1, :, seg], along_ref[1, :, seg])
    pk = jnp.concatenate(
        [pk2_ref[:, seg]] + [t[s, 0, :, seg] for t in thirds for s in range(NXH)], axis=0
    )
    pv = jnp.concatenate(
        [pv2_ref[:, seg]] + [t[s, 1, :, seg] for t in thirds for s in range(NXH)], axis=0
    )
    c2 = SCALE * LOG2E
    key_i = lax.broadcasted_iota(jnp.int32, (BLK, BLK), 0)
    qry_i = lax.broadcasted_iota(jnp.int32, (BLK, BLK), 1)
    causal = key_i <= qry_i
    q0, q1 = q[:BLK], q[BLK:]
    g0, g1 = g[:BLK], g[BLK:]
    k0, k1 = k[:BLK], k[BLK:]
    v0, v1 = v[:BLK], v[BLK:]

    sp = nt(pk, q) * c2 + bias_ref[BLK:, :]
    s_prior = nt(prior_k, q0) * c2 + bias_ref[:BLK, :BLK]
    s_k0 = nt(k0, q) * c2
    s00 = jnp.where(causal, s_k0[:, :BLK], NEG_BIG)
    s01 = s_k0[:, BLK:]
    s11 = jnp.where(causal, nt(k1, q1) * c2, NEG_BIG)

    fine = ((s_prior, s00), (s01, s11))
    fine_k = ((prior_v, v0), (v0, v1))
    expo, invs, atts, deltas = [], [], [], []
    for b in range(2):
        cols = slice(b * BLK, (b + 1) * BLK)
        sa, sb = fine[b]
        spb = sp[:, cols]
        top = jnp.maximum(
            jnp.max(spb, axis=0, keepdims=True), jnp.max(jnp.maximum(sa, sb), axis=0, keepdims=True)
        )
        ea = jnp.exp2(sa - top)
        eb = jnp.exp2(sb - top)
        ep = jnp.exp2(spb - top)
        tot = jnp.sum(ea + eb, axis=0, keepdims=True) + jnp.sum(ep, axis=0, keepdims=True)
        inv = 1.0 / tot
        invs.append(inv)
        expo.append((ea, eb, ep))
    ea_all = [e[0].astype(jnp.bfloat16) for e in expo]
    eb_all = [e[1].astype(jnp.bfloat16) for e in expo]
    ep_all = jnp.concatenate([e[2].astype(jnp.bfloat16) for e in expo], axis=1)
    mixed = tn(pv, ep_all) + tn(v0, jnp.concatenate([eb_all[0], ea_all[1]], axis=1))
    edge = jnp.concatenate([tn(prior_v, ea_all[0]), tn(v1, eb_all[1])], axis=1)
    inv_all = jnp.concatenate(invs, axis=1)
    att_t = ((mixed + edge) * inv_all).astype(jnp.bfloat16)
    att_ref[:, seg] = jnp.transpose(att_t)
    g_t = jnp.transpose(g).astype(jnp.float32)
    delta_all = jnp.sum(g_t * att_t.astype(jnp.float32), axis=0, keepdims=True)
    deltas = [delta_all[:, :BLK], delta_all[:, BLK:]]

    dp = nt(pv, g)
    d_prior = nt(prior_v, g0)
    d_k0 = nt(v0, g)
    d11 = nt(v1, g1)
    dots = ((d_prior, d_k0[:, :BLK]), (d_k0[:, BLK:], d11))
    ws, ds = [], []
    for b in range(2):
        cols = slice(b * BLK, (b + 1) * BLK)
        wts = [e * invs[b] for e in expo[b]]
        dot_b = dots[b] + (dp[:, cols],)
        ws.append([w.astype(jnp.bfloat16) for w in wts])
        ds.append(
            [(w * SCALE * (d - deltas[b])).astype(jnp.bfloat16) for w, d in zip(wts, dot_b)]
        )
    wp = jnp.concatenate([ws[0][2], ws[1][2]], axis=1)
    dsp = jnp.concatenate([ds[0][2], ds[1][2]], axis=1)
    wk0 = jnp.concatenate([ws[0][1], ws[1][0]], axis=1)
    dsk0 = jnp.concatenate([ds[0][1], ds[1][0]], axis=1)

    dq_t = tn(pk, dsp) + tn(k0, dsk0)
    dq_t = dq_t + jnp.concatenate([tn(prior_k, ds[0][0]), tn(k1, ds[1][1])], axis=1)
    dq_ref[:, seg] = jnp.transpose(dq_t.astype(jnp.bfloat16))

    dprior_ref[0, :, seg] = nn(ds[0][0], q0).astype(jnp.bfloat16)
    dprior_ref[1, :, seg] = nn(ws[0][0], g0).astype(jnp.bfloat16)
    dk_ref[:BLK, seg] = nn(dsk0, q)
    dk_ref[BLK:, seg] = nn(ds[1][1], q1)
    dv_ref[:BLK, seg] = nn(wk0, g)
    dv_ref[BLK:, seg] = nn(ws[1][1], g1)
    gkp = nn(dsp, q)
    gvp = nn(wp, g)
    for kv, part in enumerate((gkp, gvp)):
        for s in range(NZ):
            g2_ref[s, kv, :, seg] = part[s * 8 : s * 8 + 8]
        for s in range(2 * NY * NXH):
            lo = N2 + s * N3G
            ref = near_ref if s < NY * NXH else far_ref
            ref[s // NXH % NY, s % NXH, kv, :, seg] = part[lo : lo + N3G].astype(jnp.bfloat16)


def fill_bias(place_ref, bias_ref):
    xh, y, c, z, xl = (place_ref[i] for i in range(5))
    group = xh * (NY * NC) + y * NC + c
    shard = z * NXL + xl
    first = (group * (NZ * NXL) + shard) == 0
    bias_ref[:BLK, :] = jnp.full((BLK, 2 * BLK), jnp.where(first, NEG_BIG, 0.0), jnp.float32)
    r2 = lax.broadcasted_iota(jnp.int32, (N2, 2 * BLK), 0)
    late = lax.broadcasted_iota(jnp.int32, (N2, 2 * BLK), 1) // BLK
    from_shard = ((z + NZ - r2 // 8) % NZ) * NXL + (xl + r2 // 4) % NXL
    ok2 = from_shard * 4 + r2 % 4 < 4 * shard - 2 + 2 * late
    bias_ref[BLK : BLK + N2, :] = jnp.where(ok2, 0.0, NEG_BIG)
    for s in range(2 * NY * NXH):
        of_xh = (xh + s % NXH) % NXH
        of_y = (y + NY - Y_STEP[s // NXH % NY]) % NY
        of_c = (c + s // (NXH * NY)) % NC
        ok3 = of_xh * (NY * NC) + of_y * NC + of_c < group
        lo = BLK + N2 + s * N3G
        bias_ref[lo : lo + N3G, :] = jnp.full(
            (N3G, 2 * BLK), jnp.where(ok3, 0.0, NEG_BIG), jnp.float32
        )


def attn_kernel(place_ref, *refs):
    bias_ref = refs[-1]

    @pl.when(pl.program_id(0) == 0)
    def _():
        fill_bias(place_ref, bias_ref)

    odd = place_ref[4] == 1
    for h in range(HPB):
        seg = slice(h * HDIM, (h + 1) * HDIM)
        one_head(odd, bias_ref, seg, refs[:16], refs[16:24])


def cols(width, *lead):
    zeros = (0,) * len(lead)
    return pl.BlockSpec(lead + (width,), lambda i: zeros + (i,))


def attention(place, q, k, v, g, across, along, pk2, pv2, thirds):
    width = HPB * HDIM
    rows = q.shape[0]
    shape = jax.ShapeDtypeStruct
    row_spec = cols(width, rows)
    sums_spec = cols(width, NY, NXH, 2, N3G)
    return pl.pallas_call(
        attn_kernel,
        grid=(FEAT // width,),
        in_specs=[
            pl.BlockSpec(memory_space=pltpu.SMEM),
            row_spec, row_spec, row_spec, row_spec,
            cols(width, 2, BLK), cols(width, 2, BLK), cols(width, N2), cols(width, N2),
        ] + [cols(width, NXH, 2, N3G)] * 8,
        out_specs=[
            row_spec, row_spec, row_spec, row_spec,
            cols(width, 2, BLK), cols(width, NZ, 2, 8), sums_spec, sums_spec,
        ],
        out_shape=[
            shape((rows, FEAT), jnp.bfloat16),
            shape((rows, FEAT), jnp.bfloat16),
            shape((rows, FEAT), jnp.float32),
            shape((rows, FEAT), jnp.float32),
            shape((2, BLK, FEAT), jnp.bfloat16),
            shape((NZ, 2, 8, FEAT), jnp.float32),
            shape((NY, NXH, 2, N3G, FEAT), jnp.bfloat16),
            shape((NY, NXH, 2, N3G, FEAT), jnp.bfloat16),
        ],
        scratch_shapes=[pltpu.VMEM((BLK + NP, 2 * BLK), jnp.float32)],
        compiler_params=pltpu.CompilerParams(vmem_limit_bytes=24 * 1024 * 1024),
        cost_estimate=pl.CostEstimate(
            flops=6 * 2 * 2 * BLK * 576 * FEAT, bytes_accessed=20 << 20, transcendentals=0
        ),
    )(place, q, k, v, g, across, along, pk2, pv2, *thirds)


def pool_kernel(k_ref, v_ref, pooled_ref):
    for kv, ref in ((0, k_ref), (1, v_ref)):
        for e in range(4):
            run = ref[e * P2 : (e + 1) * P2, :].astype(jnp.float32)
            total = jnp.sum(run, axis=0, keepdims=True) * (1.0 / math.sqrt(P2))
            pooled_ref[kv, e : e + 1, :] = total.astype(jnp.bfloat16)


def pool(k, v):
    width = 512
    return pl.pallas_call(
        pool_kernel,
        grid=(FEAT // width,),
        in_specs=[cols(width, k.shape[0])] * 2,
        out_specs=cols(width, 2, 4),
        out_shape=jax.ShapeDtypeStruct((2, 4, FEAT), jnp.bfloat16),
        compiler_params=pltpu.CompilerParams(vmem_limit_bytes=56 * 1024 * 1024),
        cost_estimate=pl.CostEstimate(flops=1 << 20, bytes_accessed=2 << 20, transcendentals=0),
    )(k, v)


def gathered_kernel(*refs):
    by_step = dict(zip((0,) + Z_ORDER[::-1], refs[:NZ]))
    pieces, (pk_ref, pv_ref, third_ref) = [by_step[s] for s in range(NZ)], refs[NZ:]
    for kv, out in ((0, pk_ref), (1, pv_ref)):
        parts = [p[kv].astype(jnp.float32) for p in pieces]
        out[...] = jnp.concatenate(parts, axis=0).astype(jnp.bfloat16)
        sums = [
            jnp.sum(p[lo : lo + 4], axis=0, keepdims=True) * 0.5 for p in parts for lo in (0, 4)
        ]
        third_ref[0, kv] = jnp.concatenate(sums, axis=0).astype(jnp.bfloat16)


def gathered(pieces):
    width = 1024
    shape = jax.ShapeDtypeStruct
    return pl.pallas_call(
        gathered_kernel,
        grid=(FEAT // width,),
        in_specs=[cols(width, 2, 8)] * NZ,
        out_specs=[cols(width, N2), cols(width, N2), cols(width, 1, 2, N3G)],
        out_shape=[
            shape((N2, FEAT), jnp.bfloat16),
            shape((N2, FEAT), jnp.bfloat16),
            shape((NXH, 2, N3G, FEAT), jnp.bfloat16),
        ],
        compiler_params=pltpu.CompilerParams(vmem_limit_bytes=32 * 1024 * 1024),
        cost_estimate=pl.CostEstimate(flops=1 << 20, bytes_accessed=1 << 20, transcendentals=0),
    )(*pieces)


def lifted_kernel(g2_ref, third_ref, *outs):
    for kv in range(2):
        for s in range(NZ):
            for i in range(NXL):
                row = slice(s * NXL + i, s * NXL + i + 1)
                lift = third_ref[0, kv, row, :] * 0.5
                part = g2_ref[s, kv, i * 4 : i * 4 + 4, :] + lift
                outs[s][kv * NXL + i] = part.astype(outs[s].dtype)
                rest = third_ref[1, kv, row, :]
                outs[s][4, kv * NXL + i : kv * NXL + i + 1, :] = rest.astype(outs[s].dtype)


def lifted(g2, third):
    width = 1024
    shape = jax.ShapeDtypeStruct
    return pl.pallas_call(
        lifted_kernel,
        grid=(FEAT // width,),
        in_specs=[cols(width, NZ, 2, 8), cols(width, NXH, 2, N3G)],
        out_specs=[cols(width, 5, 4)] * NZ,
        out_shape=[
            shape((5, 4, FEAT), jnp.float32 if s == 0 else jnp.bfloat16) for s in range(NZ)
        ],
        compiler_params=pltpu.CompilerParams(vmem_limit_bytes=24 * 1024 * 1024),
        cost_estimate=pl.CostEstimate(flops=1 << 20, bytes_accessed=2 << 20, transcendentals=0),
    )(g2, third)


def finish_kernel(dk_ref, dv_ref, back_ref, two_ref, gk_ref, gv_ref):
    for kv, src, dst in ((0, dk_ref, gk_ref), (1, dv_ref, gv_ref)):
        for part in range(4):
            lo = part * P2
            spread = two_ref[kv, part : part + 1, :]
            val = src[lo : lo + P2, :] + spread
            if part >= 2:
                rows = slice(lo - BLK, lo - BLK + P2)
                val = val + back_ref[kv, rows, :].astype(jnp.float32)
            dst[lo : lo + P2, :] = val.astype(jnp.bfloat16)


def finish(dk, dv, back, two):
    rows = dk.shape[0]
    width = 512
    shape = jax.ShapeDtypeStruct
    return pl.pallas_call(
        finish_kernel,
        grid=(FEAT // width,),
        in_specs=[cols(width, rows)] * 2 + [cols(width, 2, BLK), cols(width, 2, 4)],
        out_specs=[cols(width, rows)] * 2,
        out_shape=[shape((rows, FEAT), jnp.bfloat16)] * 2,
        compiler_params=pltpu.CompilerParams(vmem_limit_bytes=48 * 1024 * 1024),
        cost_estimate=pl.CostEstimate(flops=1 << 20, bytes_accessed=7 << 20, transcendentals=0),
    )(dk, dv, back, two)


def in_hbm(*values):
    return [pltpu.with_memory_space_constraint(v, pltpu.HBM) for v in values]


def ring(value, axis, size, step):
    return lax.ppermute(value, axis, [(i, (i + step) % size) for i in range(size)])


def bf(x):
    return x.astype(jnp.bfloat16)


def f32(x):
    return x.astype(jnp.float32)


def across_pairs(step=1):
    groups, shards = NXH * NY * NC, NZ * NXL
    pairs = []
    for g in range(groups):
        for shard in range(shards):
            even = shard % 2 == 0
            crosses = shard == (shards - 1 if step > 0 else shards - 2)
            to = g + step if crosses else g
            if 0 <= to < groups:
                pairs.append((g * shards + shard, to * shards + shard + (1 if even else -1)))
    return pairs


def along_pairs(step):
    groups, shards = NXH * NY * NC, NZ * NXL
    return [
        (g * shards + shard, g * shards + (shard + 2 * step) % shards)
        for g in range(groups)
        for shard in range(0, shards, 2)
    ]


def per_device(queries, keys, values, grad_out):
    xh, y, c, z, xl = (lax.axis_index(a) for a in AXES)

    pooled = pool(keys, values)
    last = jnp.stack([keys[BLK:], values[BLK:]])
    pair = jnp.concatenate([pooled, ring(pooled, "xl", NXL, 1)], axis=1)
    last, pair = lax.optimization_barrier((last, pair))
    across = lax.ppermute(last, AXES, across_pairs(1))
    pieces = [pair] + [ring(pair, "z", NZ, s) for s in Z_ORDER[::-1]]
    pk2, pv2, third = gathered(pieces)
    own_third = third[0]
    across, own_third = lax.optimization_barrier((across, own_third))
    along = lax.ppermute(across, AXES, along_pairs(1))
    third = third.at[1].set(ring(own_third, "xh", NXH, 1))
    thirds = [third] + [ring(third, "y", NY, s) for s in Y_STEP[1:]]
    thirds = thirds + [ring(t, "c", NC, 1) for t in thirds]

    place = jnp.stack([xh, y, c, z, xl]).astype(jnp.int32)

    attended, grad_q, dk, dv, dprior, g2, near, far = attention(
        place, *in_hbm(queries, keys, values, grad_out, across, along, pk2, pv2), in_hbm(*thirds)
    )

    count = NXH * NY * NC * NZ * NXL
    back = lax.ppermute(dprior, AXES, [(i + 1, i) for i in range(count - 1)])

    far = ring(far, "c", NC, 1)
    s3 = [f32(near[s]) + f32(far[s]) for s in range(NY)]
    t3 = s3[0]
    for s in (3, 1, 2):
        t3 = t3 + f32(ring(bf(s3[s]), "y", NY, -Y_STEP[s]))
    parts = lifted(g2, t3)
    two = parts[0]
    for s in Z_ORDER:
        two = two + f32(ring(parts[s], "z", NZ, -s))
    back, two = lax.optimization_barrier((back, two))
    near_third = ring(bf(two[4, 0::2]), "xh", NXH, 1)
    far_third = lax.ppermute(
        bf(two[4, 1::2]), ("xh", "xl"), [(0, 3), (1, 2), (2, 1), (3, 0)]
    )
    two = two[0:4:2] + f32(ring(bf(two[1:4:2]), "xl", NXL, 1))
    two = two + 0.5 * (f32(near_third) + f32(far_third))[:, None, :]
    two = two / math.sqrt(P2)
    grad_k, grad_v = finish(dk, dv, back, two)
    return attended, grad_q, grad_k, grad_v


def solution(mesh):
    fine_mesh = Mesh(np.asarray(mesh.devices).reshape(NXH, NY, NC, NZ, NXL), AXES)
    spec = P(AXES, None)
    return jax.shard_map(
        per_device,
        mesh=fine_mesh,
        in_specs=(spec,) * 4,
        out_specs=(spec,) * 4,
        check_vma=False,
    )
```

time: 182 us -> 149 us (0.82); the launches traced: 179 us -> 148 us
  waiting for transfers between devices: 58.8 us -> 37 us
  starting transfers between devices: 87 us -> 82.3 us
  Pallas kernels: 26.9 us -> 24.7 us
  local copies, waits for them, and re-layouts: 4.95 us -> 2.84 us
    ppermute x29, waiting for transfers between devices: 57.7 us -> 35.5 us  [ring(): lax.ppermute(value, axis, [(i, (i + step) % size) for i in range(size)])]
    ppermute x29, starting transfers between devices: 63.8 us -> 45.3 us  [ring(): lax.ppermute(value, axis, [(i, (i + step) % size) for i in range(size)])]
    ppermute x4, starting transfers between devices: 23.2 us -> 37 us  [the longest x1 17.8 us: per_device(): lax.ppermute(bf(two[4, 1::2]), ('xh', 'xl'), [(0, 3), (1, 2), (2, 1), (3,...]
    pallas_call x1, Pallas kernels: 21 us -> 17.3 us  [attention(): pl.pallas_call(attn_kernel, grid=(FEAT // width,), in_specs=[pl.BlockSpec...]
    pallas_call x1, Pallas kernels: 0.82 us -> 3.68 us  [pool(): pl.pallas_call(pool_kernel, grid=(FEAT // width,), in_specs=[cols(width,...]
  transfers between devices with their start and end apart: 33 -> 33, of which waited for: 15 -> 16; matrix products, arithmetic and copies ran while one was open for 2% -> 0% of each run, Pallas kernels for 1% -> 1%
where the time goes in v2:
time: 149 us; the launch traced here: 148 us
  starting transfers between devices  82.3 us (55%)
  waiting for transfers between devices  37 us (25%)
  Pallas kernels  24.7 us (17%)
  local copies, waits for them, and re-layouts  2.84 us (2%)
    ppermute x29, starting transfers between devices, ring(): lax.ppermute(value, axis, [(i, (i + step) % size) for i in range(size)])  45.3 us
    ppermute x29, waiting for transfers between devices, ring(): lax.ppermute(value, axis, [(i, (i + step) % size) for i in range(size)])  35.5 us
    ppermute x1, starting transfers between devices, per_device(): lax.ppermute(bf(two[4, 1::2]), ('xh', 'xl'), [(0, 3), (1, 2), (2, 1), (3,...  17.8 us
    pallas_call x1, Pallas kernels, attention(): pl.pallas_call(attn_kernel, grid=(FEAT // width,), in_specs=[pl.BlockSpec...  17.3 us
    ppermute x1, starting transfers between devices, per_device(): back = lax.ppermute(dprior, AXES, [(i + 1, i) for i in range(count - 1)])  14.6 us
    ppermute x1, starting transfers between devices, per_device(): across = lax.ppermute(last, AXES, across_pairs(1))  3.86 us
    pallas_call x1, Pallas kernels, pool(): pl.pallas_call(pool_kernel, grid=(FEAT // width,), in_specs=[cols(width,...  3.68 us
  transfers between devices with their start and end apart: 33, of which 16 were waited for; matrix products, arithmetic and copies ran while one was open for 0% of the time, Pallas kernels for 1%

profile of v2, /device:TPU:2, one launch (start us, length us, event | category | flops | bytes accessed | tf_op | source)
XLA Modules:
  0.0 148.5 jit_solution(3654162476611163901)
XLA Ops:
  0.6 0.0 copy-start.6
  0.6 0.0 copy-start.5
  0.7 3.7 %shard_map.75 = bf16[2,4,2048]{2,1,0:T(4,128)(2,1)} custom-call(bf16[256,2048]{1,0:T(8,128)(2,1)} %refs_1_.1, bf16[256,2048]{1,0:T(8,128)(2,1)} %refs_2_.1), custom_call_target="tpu_custom_call" | custom-call | flops 1048576 | bytes 2097152 | tf_op jit(solution)/shard_map/pallas_call | solution.py:230
  4.3 2.3 %collective-permute-start = (bf16[2,4,2048]{2,1,0:T(4,128)(2,1)}, bf16[2,4,2048]{2,1,0:T(4,128)(2,1)S(1)}, u32[]{:S(2)}, u32[]{:S(2)}) collective-permute-start(bf16[2,4,2048]{2,1,0:T(4,128)(2,1)} %shard_map.75), channel_id=1, source_target_pairs={{0,1},{1,0},{2,3},{3,2},{4,5},{5,4},{6,7},{7,6},{8,9},{9,8},{10,11... | collective-permute-start | bytes 98312 | tf_op jit(solution)/shard_map/ppermute | solution.py:331
  6.6 0.1 slice_bitcast_fusion
  6.7 0.1 pad_maximum_fusion
  6.8 2.0 %collective-permute-done = bf16[2,4,2048]{2,1,0:T(4,128)(2,1)S(1)} collective-permute-done((bf16[2,4,2048]{2,1,0:T(4,128)(2,1)}, bf16[2,4,2048]{2,1,0:T(4,128)(2,1)S(1)}, u32[]{:S(2)}, u32[]{:S(2)}) %collective-permute-start) | collective-permute-done | bytes 32800 | tf_op jit(solution)/shard_map/ppermute | solution.py:331
  8.8 3.9 %collective-permute-start.1 = (bf16[2,128,2048]{2,1,0:T(8,128)(2,1)S(1)}, bf16[2,128,2048]{2,1,0:T(8,128)(2,1)S(1)}, u32[]{:S(2)}, u32[]{:S(2)}) collective-permute-start(bf16[2,128,2048]{2,1,0:T(8,128)(2,1)S(1)} %pad_maximum_fusion), channel_id=1, source_target_pairs={{0,1},{1,0},{2,3},{3,2},{4,5},{5,4},{6,7},{7,6},{8,9},{9,8},{10,11... | collective-permute-start | bytes 3145736 | tf_op jit(solution)/shard_map/ppermute | solution.py:371
  12.7 5.5 %collective-permute-start.8 = (bf16[2,8,2048]{2,1,0:T(8,128)(2,1)S(1)}, bf16[2,8,2048]{2,1,0:T(8,128)(2,1)S(1)}, u32[]{:S(2)}, u32[]{:S(2)}) collective-permute-start(bf16[2,8,2048]{2,1,0:T(8,128)(2,1)S(1)} %pad_maximum_fusion.1.refs_0_), channel_id=1, source_target_pairs={{0,8},{2,10},{4,12},{6,14},{8,0},{10,2},{12,4},{14,6},{1,9},{3,11}... | collective-permute-start | bytes 196616 | tf_op jit(solution)/shard_map/ppermute | solution.py:331
  18.2 0.0 collective-permute-start.7
  18.2 3.8 %collective-permute-start.6 = (bf16[2,8,2048]{2,1,0:T(8,128)(2,1)S(1)}, bf16[2,8,2048]{2,1,0:T(8,128)(2,1)S(1)}, u32[]{:S(2)}, u32[]{:S(2)}) collective-permute-start(bf16[2,8,2048]{2,1,0:T(8,128)(2,1)S(1)} %pad_maximum_fusion.1.refs_0_), channel_id=1, source_target_pairs={{0,6},{2,8},{4,10},{6,12},{8,14},{10,0},{12,2},{14,4},{1,7},{3,9},... | collective-permute-start | bytes 196616 | tf_op jit(solution)/shard_map/ppermute | solution.py:331
  22.1 0.9 collective-permute-start.5
  22.9 2.1 %collective-permute-start.4 = (bf16[2,8,2048]{2,1,0:T(8,128)(2,1)S(1)}, bf16[2,8,2048]{2,1,0:T(8,128)(2,1)S(1)}, u32[]{:S(2)}, u32[]{:S(2)}) collective-permute-start(bf16[2,8,2048]{2,1,0:T(8,128)(2,1)S(1)} %pad_maximum_fusion.1.refs_0_), channel_id=1, source_target_pairs={{0,4},{2,6},{4,8},{6,10},{8,12},{10,14},{12,0},{14,2},{1,5},{3,7},... | collective-permute-start | bytes 196616 | tf_op jit(solution)/shard_map/ppermute | solution.py:331
  25.0 1.5 %collective-permute-done.7.refs_6_ = bf16[2,8,2048]{2,1,0:T(8,128)(2,1)S(1)} collective-permute-done((bf16[2,8,2048]{2,1,0:T(8,128)(2,1)S(1)}, bf16[2,8,2048]{2,1,0:T(8,128)(2,1)S(1)}, u32[]{:S(2)}, u32[]{:S(2)}) %collective-permute-start.7) | collective-permute-done | bytes 65568 | tf_op jit(solution)/shard_map/ppermute | solution.py:331
  26.5 3.4 %collective-permute-start.3 = (bf16[2,8,2048]{2,1,0:T(8,128)(2,1)S(1)}, bf16[2,8,2048]{2,1,0:T(8,128)(2,1)S(1)}, u32[]{:S(2)}, u32[]{:S(2)}) collective-permute-start(bf16[2,8,2048]{2,1,0:T(8,128)(2,1)S(1)} %pad_maximum_fusion.1.refs_0_), channel_id=1, source_target_pairs={{0,14},{2,0},{4,2},{6,4},{8,6},{10,8},{12,10},{14,12},{1,15},{3,1}... | collective-permute-start | bytes 196616 | tf_op jit(solution)/shard_map/ppermute | solution.py:331
  29.9 0.0 collective-permute-done.6.refs_5_
  29.9 0.0 collective-permute-start.2
  29.9 0.0 collective-permute-done.5.refs_4_
  29.9 1.9 %collective-permute-done.3.refs_2_ = bf16[2,8,2048]{2,1,0:T(8,128)(2,1)S(1)} collective-permute-done((bf16[2,8,2048]{2,1,0:T(8,128)(2,1)S(1)}, bf16[2,8,2048]{2,1,0:T(8,128)(2,1)S(1)}, u32[]{:S(2)}, u32[]{:S(2)}) %collective-permute-start.3) | collective-permute-done | bytes 65568 | tf_op jit(solution)/shard_map/ppermute | solution.py:331
  31.8 3.6 %collective-permute-done.2.refs_1_ = bf16[2,8,2048]{2,1,0:T(8,128)(2,1)S(1)} collective-permute-done((bf16[2,8,2048]{2,1,0:T(8,128)(2,1)S(1)}, bf16[2,8,2048]{2,1,0:T(8,128)(2,1)S(1)}, u32[]{:S(2)}, u32[]{:S(2)}) %collective-permute-start.2) | collective-permute-done | bytes 65568 | tf_op jit(solution)/shard_map/ppermute | solution.py:331
  35.4 0.8 shard_map.76
  36.3 0.0 copy-start.8
  36.3 2.4 %collective-permute-start.10 = (bf16[2,16,2048]{2,1,0:T(8,128)(2,1)S(1)}, bf16[2,16,2048]{2,1,0:T(8,128)(2,1)S(1)}, u32[]{:S(2)}, u32[]{:S(2)}) collective-permute-start(bf16[2,16,2048]{2,1,0:T(8,128)(2,1)S(1)} %slice_bitcast_fusion.2), channel_id=1, source_target_pairs={{0,128},{128,0},{1,129},{129,1},{2,130},{130,2},{3,131},{131,3},{4... | collective-permute-start | bytes 393224 | tf_op jit(solution)/shard_map/ppermute | solution.py:331
  38.6 0.7 collective-permute-start.9
  39.4 3.5 %collective-permute-done.10 = bf16[2,16,2048]{2,1,0:T(8,128)(2,1)S(1)} collective-permute-done((bf16[2,16,2048]{2,1,0:T(8,128)(2,1)S(1)}, bf16[2,16,2048]{2,1,0:T(8,128)(2,1)S(1)}, u32[]{:S(2)}, u32[]{:S(2)}) %collective-permute-start.10) | collective-permute-done | bytes 131104 | tf_op jit(solution)/shard_map/ppermute | solution.py:331
  42.8 3.1 %collective-permute-start.13 = (bf16[2,2,16,2048]{3,2,1,0:T(8,128)(2,1)S(1)}, bf16[2,2,16,2048]{3,2,1,0:T(8,128)(2,1)S(1)}, u32[]{:S(2)}, u32[]{:S(2)}) collective-permute-start(bf16[2,2,16,2048]{3,2,1,0:T(8,128)(2,1)S(1)} %bitcast_dynamic-update-slice_fusion.refs_8_), channel_id=1, source_target_pairs={{0,64},{32,96},{64,0},{96,32},{1,65},{33,97},{65,1},{97,33},{2,66}... | collective-permute-start | bytes 786440 | tf_op jit(solution)/shard_map/ppermute | solution.py:331
  45.9 1.3 collective-permute-start.12
  47.2 0.8 collective-permute-start.11
  48.0 0.0 collective-permute-start.14
  48.0 4.1 %collective-permute-done.13.refs_11_ = bf16[2,2,16,2048]{3,2,1,0:T(8,128)(2,1)S(1)} collective-permute-done((bf16[2,2,16,2048]{3,2,1,0:T(8,128)(2,1)S(1)}, bf16[2,2,16,2048]{3,2,1,0:T(8,128)(2,1)S(1)}, u32[]{:S(2)}, u32[]{:S(2)}) %collective-permute-start.13) | collective-permute-done | bytes 262176 | tf_op jit(solution)/shard_map/ppermute | solution.py:331
  52.1 3.0 %collective-permute-done.12.refs_10_ = bf16[2,2,16,2048]{3,2,1,0:T(8,128)(2,1)S(1)} collective-permute-done((bf16[2,2,16,2048]{3,2,1,0:T(8,128)(2,1)S(1)}, bf16[2,2,16,2048]{3,2,1,0:T(8,128)(2,1)S(1)}, u32[]{:S(2)}, u32[]{:S(2)}) %collective-permute-start.12) | collective-permute-done | bytes 262176 | tf_op jit(solution)/shard_map/ppermute | solution.py:331
  55.1 0.3 collective-permute-done.11.refs_9_
  55.4 0.5 collective-permute-start.15
  55.9 0.1 stack.32.place_ref
  56.0 0.0 collective-permute-done.14.refs_12_
  56.0 0.8 collective-permute-done.16.refs_14_
  56.8 0.4 collective-permute-done.15.refs_13_
  57.2 0.9 copy-done.9
  58.2 17.3 %shard_map.77 = (bf16[256,2048]{1,0:T(8,128)(2,1)}, bf16[256,2048]{1,0:T(8,128)(2,1)}, f32[256,2048]{1,0:T(8,128)S(1)}, f32[256,2048]{1,0:T(8,128)S(1)}, bf16[2,...) custom-call(s32[5]{0:T(128)S(1)} %stack.32.place_ref, ...), custom_call_target="tpu_custom_call" | custom-call | flops 3623878656 | bytes 20971520 | tf_op jit(solution)/shard_map/pallas_call | solution.py:190
  75.4 0.5 collective-permute-start.19
  75.9 2.3 %collective-permute-done.19 = bf16[4,2,2,16,2048]{4,3,2,1,0:T(8,128)(2,1)S(1)} collective-permute-done((bf16[4,2,2,16,2048]{4,3,2,1,0:T(8,128)(2,1)S(1)}, bf16[4,2,2,16,2048]{4,3,2,1,0:T(8,128)(2,1)S(1)}, u32[]{:S(2)}, u32[]{:S(2)}) %collective-permute-start.19) | collective-permute-done | bytes 1048608 | tf_op jit(solution)/shard_map/ppermute | solution.py:331
  78.2 0.3 fusion.2
  78.5 2.5 %collective-permute-start.20 = (bf16[2,2,16,2048]{3,2,1,0:T(8,128)(2,1)S(1)}, bf16[2,2,16,2048]{3,2,1,0:T(8,128)(2,1)S(1)}, u32[]{:S(2)}, u32[]{:S(2)}) collective-permute-start(bf16[2,2,16,2048]{3,2,1,0:T(8,128)(2,1)S(1)} %get-tuple-element.70), channel_id=1, source_target_pairs={{0,64},{32,96},{64,0},{96,32},{1,65},{33,97},{65,1},{97,33},{2,66}... | collective-permute-start | bytes 786440 | tf_op jit(solution)/shard_map/ppermute | solution.py:331
  81.0 1.0 collective-permute-start.22
  82.0 2.2 %collective-permute-start.21 = (bf16[2,2,16,2048]{3,2,1,0:T(8,128)(2,1)S(1)}, bf16[2,2,16,2048]{3,2,1,0:T(8,128)(2,1)S(1)}, u32[]{:S(2)}, u32[]{:S(2)}) collective-permute-start(bf16[2,2,16,2048]{3,2,1,0:T(8,128)(2,1)S(1)} %get-tuple-element.72), channel_id=1, source_target_pairs={{0,96},{32,0},{64,32},{96,64},{1,97},{33,1},{65,33},{97,65},{2,98}... | collective-permute-start | bytes 786440 | tf_op jit(solution)/shard_map/ppermute | solution.py:331
  84.2 14.6 %collective-permute-start.18 = (bf16[2,128,2048]{2,1,0:T(8,128)(2,1)S(1)}, bf16[2,128,2048]{2,1,0:T(8,128)(2,1)S(1)}, u32[]{:S(2)}, u32[]{:S(2)}) collective-permute-start(bf16[2,128,2048]{2,1,0:T(8,128)(2,1)S(1)} %get-tuple-element.54), channel_id=1, source_target_pairs={{1,0},{2,1},{3,2},{4,3},{5,4},{6,5},{7,6},{8,7},{9,8},{10,9},{11,1... | collective-permute-start | bytes 3145736 | tf_op jit(solution)/shard_map/ppermute | solution.py:388
  98.9 0.2 fusion.1.third_ref
  99.0 0.7 shard_map.78
  99.8 1.5 %collective-permute-start.23 = (bf16[5,4,2048]{2,1,0:T(4,128)(2,1)S(1)}, bf16[5,4,2048]{2,1,0:T(4,128)(2,1)S(1)}, u32[]{:S(2)}, u32[]{:S(2)}) collective-permute-start(bf16[5,4,2048]{2,1,0:T(4,128)(2,1)S(1)} %get-tuple-element.59), channel_id=1, source_target_pairs={{0,8},{2,10},{4,12},{6,14},{8,0},{10,2},{12,4},{14,6},{1,9},{3,11}... | collective-permute-start | bytes 245768 | tf_op jit(solution)/shard_map/ppermute | solution.py:331
  101.3 3.6 %collective-permute-start.24 = (bf16[5,4,2048]{2,1,0:T(4,128)(2,1)S(1)}, bf16[5,4,2048]{2,1,0:T(4,128)(2,1)S(1)}, u32[]{:S(2)}, u32[]{:S(2)}) collective-permute-start(bf16[5,4,2048]{2,1,0:T(4,128)(2,1)S(1)} %get-tuple-element.60), channel_id=1, source_target_pairs={{0,6},{2,8},{4,10},{6,12},{8,14},{10,0},{12,2},{14,4},{1,7},{3,9},... | collective-permute-start | bytes 245768 | tf_op jit(solution)/shard_map/ppermute | solution.py:331
  104.8 1.5 collective-permute-start.25
  106.3 1.7 %collective-permute-start.26 = (bf16[5,4,2048]{2,1,0:T(4,128)(2,1)S(1)}, bf16[5,4,2048]{2,1,0:T(4,128)(2,1)S(1)}, u32[]{:S(2)}, u32[]{:S(2)}) collective-permute-start(bf16[5,4,2048]{2,1,0:T(4,128)(2,1)S(1)} %get-tuple-element.62), channel_id=1, source_target_pairs={{0,4},{2,6},{4,8},{6,10},{8,12},{10,14},{12,0},{14,2},{1,5},{3,7},... | collective-permute-start | bytes 245768 | tf_op jit(solution)/shard_map/ppermute | solution.py:331
  108.0 3.1 %collective-permute-done.23 = bf16[5,4,2048]{2,1,0:T(4,128)(2,1)S(1)} collective-permute-done((bf16[5,4,2048]{2,1,0:T(4,128)(2,1)S(1)}, bf16[5,4,2048]{2,1,0:T(4,128)(2,1)S(1)}, u32[]{:S(2)}, u32[]{:S(2)}) %collective-permute-start.23) | collective-permute-done | bytes 81952 | tf_op jit(solution)/shard_map/ppermute | solution.py:331
  111.1 4.3 %collective-permute-done.24 = bf16[5,4,2048]{2,1,0:T(4,128)(2,1)S(1)} collective-permute-done((bf16[5,4,2048]{2,1,0:T(4,128)(2,1)S(1)}, bf16[5,4,2048]{2,1,0:T(4,128)(2,1)S(1)}, u32[]{:S(2)}, u32[]{:S(2)}) %collective-permute-start.24) | collective-permute-done | bytes 81952 | tf_op jit(solution)/shard_map/ppermute | solution.py:331
  115.4 3.2 %collective-permute-start.29 = (bf16[5,4,2048]{2,1,0:T(4,128)(2,1)S(1)}, bf16[5,4,2048]{2,1,0:T(4,128)(2,1)S(1)}, u32[]{:S(2)}, u32[]{:S(2)}) collective-permute-start(bf16[5,4,2048]{2,1,0:T(4,128)(2,1)S(1)} %get-tuple-element.65), channel_id=1, source_target_pairs={{0,14},{2,0},{4,2},{6,4},{8,6},{10,8},{12,10},{14,12},{1,15},{3,1}... | collective-permute-start | bytes 245768 | tf_op jit(solution)/shard_map/ppermute | solution.py:331
  118.6 2.4 %collective-permute-done.28 = bf16[5,4,2048]{2,1,0:T(4,128)(2,1)S(1)} collective-permute-done((bf16[5,4,2048]{2,1,0:T(4,128)(2,1)S(1)}, bf16[5,4,2048]{2,1,0:T(4,128)(2,1)S(1)}, u32[]{:S(2)}, u32[]{:S(2)}) %collective-permute-start.28) | collective-permute-done | bytes 81952 | tf_op jit(solution)/shard_map/ppermute | solution.py:331
  121.0 0.2 convert_add_fusion
  121.3 1.5 %collective-permute-start.31 = (bf16[2,2048]{1,0:T(2,128)(2,1)S(1)}, bf16[2,2048]{1,0:T(2,128)(2,1)S(1)}, u32[]{:S(2)}, u32[]{:S(2)}) collective-permute-start(bf16[2,2048]{1,0:T(2,128)(2,1)S(1)} %bitcast.28), channel_id=1, source_target_pairs={{0,128},{128,0},{1,129},{129,1},{2,130},{130,2},{3,131},{131,3},{4... | collective-permute-start | bytes 24584 | tf_op jit(solution)/shard_map/ppermute | solution.py:331
  122.8 17.8 %collective-permute-start.32 = (bf16[2,2048]{1,0:T(2,128)(2,1)S(1)}, bf16[2,2048]{1,0:T(2,128)(2,1)S(1)}, u32[]{:S(2)}, u32[]{:S(2)}) collective-permute-start(bf16[2,2048]{1,0:T(2,128)(2,1)S(1)} %bitcast.27), channel_id=1, source_target_pairs={{0,129},{1,128},{128,1},{129,0},{2,131},{3,130},{130,3},{131,2},{4... | collective-permute-start | bytes 24584 | tf_op jit(solution)/shard_map/ppermute | solution.py:401
  140.7 0.1 collective-permute-start.30
  140.8 1.5 %collective-permute-done.32 = bf16[2,2048]{1,0:T(2,128)(2,1)S(1)} collective-permute-done((bf16[2,2048]{1,0:T(2,128)(2,1)S(1)}, bf16[2,2048]{1,0:T(2,128)(2,1)S(1)}, u32[]{:S(2)}, u32[]{:S(2)}) %collective-permute-start.32) | collective-permute-done | bytes 8224 | tf_op jit(solution)/shard_map/ppermute | solution.py:401
  142.3 2.4 %collective-permute-done.30 = bf16[2,4,2048]{2,1,0:T(4,128)(2,1)S(1)} collective-permute-done((bf16[2,4,2048]{2,1,0:T(4,128)(2,1)S(1)}, bf16[2,4,2048]{2,1,0:T(4,128)(2,1)S(1)}, u32[]{:S(2)}, u32[]{:S(2)}) %collective-permute-start.30) | collective-permute-done | bytes 32800 | tf_op jit(solution)/shard_map/ppermute | solution.py:331
  144.7 1.6 %copy-done.1 = f32[256,2048]{1,0:T(8,128)S(1)} copy-done((f32[256,2048]{1,0:T(8,128)S(1)}, f32[256,2048]{1,0:T(8,128)}, u32[]{:S(2)}) %copy-start.1) | copy-done | bytes 2097176
  146.3 2.2 %shard_map.79 = (bf16[256,2048]{1,0:T(8,128)(2,1)}, bf16[256,2048]{1,0:T(8,128)(2,1)}) custom-call(f32[256,2048]{1,0:T(8,128)S(1)} %get-tuple-element.52.dk_ref, f32[256,2048]{1,0:T(8,128)S(1)} %copy-done.1, bf16[2,128,2048]{2,1,0:T(8,128)(2,1)S(1)} %collective-permute-done.18.back_ref, f32[2,4,2048]{2,1,0:T(4,128)S(1)} %add_multiply_fusion.two_ref), custom_call_target="tpu_custom_call" | custom-call | flops 1048576 | bytes 7340032 | tf_op jit(solution)/shard_map/pallas_call | solution.py:315
  (50 shorter events, 0.3 us)
Async XLA Ops:
  0.6 6.0 %copy-start.6 = (bf16[256,2048]{1,0:T(8,128)(2,1)S(1)}, bf16[256,2048]{1,0:T(8,128)(2,1)}, u32[]{:S(2)}) copy-start(bf16[256,2048]{1,0:T(8,128)(2,1)} %refs_2_.1) | copy-start | bytes 3145732
  0.6 6.0 %copy-start.5 = (bf16[256,2048]{1,0:T(8,128)(2,1)S(1)}, bf16[256,2048]{1,0:T(8,128)(2,1)}, u32[]{:S(2)}) copy-start(bf16[256,2048]{1,0:T(8,128)(2,1)} %refs_1_.1) | copy-start | bytes 3145732
  4.3 4.4 %copy-start.7 = (bf16[2,4,2048]{2,1,0:T(4,128)(2,1)S(1)}, bf16[2,4,2048]{2,1,0:T(4,128)(2,1)}, u32[]{:S(2)}) copy-start(bf16[2,4,2048]{2,1,0:T(4,128)(2,1)} %shard_map.75) | copy-start | bytes 98308
  4.3 4.4 %collective-permute-start = (bf16[2,4,2048]{2,1,0:T(4,128)(2,1)}, bf16[2,4,2048]{2,1,0:T(4,128)(2,1)S(1)}, u32[]{:S(2)}, u32[]{:S(2)}) collective-permute-start(bf16[2,4,2048]{2,1,0:T(4,128)(2,1)} %shard_map.75), channel_id=1, source_target_pairs={{0,1},{1,0},{2,3},{3,2},{4,5},{5,4},{6,7},{7,6},{8,9},{9,8},{10,11... | collective-permute-start | bytes 98312 | tf_op jit(solution)/shard_map/ppermute | solution.py:331
  8.8 27.4 %collective-permute-start.1 = (bf16[2,128,2048]{2,1,0:T(8,128)(2,1)S(1)}, bf16[2,128,2048]{2,1,0:T(8,128)(2,1)S(1)}, u32[]{:S(2)}, u32[]{:S(2)}) collective-permute-start(bf16[2,128,2048]{2,1,0:T(8,128)(2,1)S(1)} %pad_maximum_fusion), channel_id=1, source_target_pairs={{0,1},{1,0},{2,3},{3,2},{4,5},{5,4},{6,7},{7,6},{8,9},{9,8},{10,11... | collective-permute-start | bytes 3145736 | tf_op jit(solution)/shard_map/ppermute | solution.py:371
  12.7 10.2 %collective-permute-start.8 = (bf16[2,8,2048]{2,1,0:T(8,128)(2,1)S(1)}, bf16[2,8,2048]{2,1,0:T(8,128)(2,1)S(1)}, u32[]{:S(2)}, u32[]{:S(2)}) collective-permute-start(bf16[2,8,2048]{2,1,0:T(8,128)(2,1)S(1)} %pad_maximum_fusion.1.refs_0_), channel_id=1, source_target_pairs={{0,8},{2,10},{4,12},{6,14},{8,0},{10,2},{12,4},{14,6},{1,9},{3,11}... | collective-permute-start | bytes 196616 | tf_op jit(solution)/shard_map/ppermute | solution.py:331
  18.2 8.2 %collective-permute-start.7 = (bf16[2,8,2048]{2,1,0:T(8,128)(2,1)S(1)}, bf16[2,8,2048]{2,1,0:T(8,128)(2,1)S(1)}, u32[]{:S(2)}, u32[]{:S(2)}) collective-permute-start(bf16[2,8,2048]{2,1,0:T(8,128)(2,1)S(1)} %pad_maximum_fusion.1.refs_0_), channel_id=1, source_target_pairs={{0,10},{2,12},{4,14},{6,0},{8,2},{10,4},{12,6},{14,8},{1,11},{3,13... | collective-permute-start | bytes 196616 | tf_op jit(solution)/shard_map/ppermute | solution.py:331
  18.2 11.6 %collective-permute-start.6 = (bf16[2,8,2048]{2,1,0:T(8,128)(2,1)S(1)}, bf16[2,8,2048]{2,1,0:T(8,128)(2,1)S(1)}, u32[]{:S(2)}, u32[]{:S(2)}) collective-permute-start(bf16[2,8,2048]{2,1,0:T(8,128)(2,1)S(1)} %pad_maximum_fusion.1.refs_0_), channel_id=1, source_target_pairs={{0,6},{2,8},{4,10},{6,12},{8,14},{10,0},{12,2},{14,4},{1,7},{3,9},... | collective-permute-start | bytes 196616 | tf_op jit(solution)/shard_map/ppermute | solution.py:331
  22.1 7.8 %collective-permute-start.5 = (bf16[2,8,2048]{2,1,0:T(8,128)(2,1)S(1)}, bf16[2,8,2048]{2,1,0:T(8,128)(2,1)S(1)}, u32[]{:S(2)}, u32[]{:S(2)}) collective-permute-start(bf16[2,8,2048]{2,1,0:T(8,128)(2,1)S(1)} %pad_maximum_fusion.1.refs_0_), channel_id=1, source_target_pairs={{0,12},{2,14},{4,0},{6,2},{8,4},{10,6},{12,8},{14,10},{1,13},{3,15... | collective-permute-start | bytes 196616 | tf_op jit(solution)/shard_map/ppermute | solution.py:331
  22.9 7.0 %collective-permute-start.4 = (bf16[2,8,2048]{2,1,0:T(8,128)(2,1)S(1)}, bf16[2,8,2048]{2,1,0:T(8,128)(2,1)S(1)}, u32[]{:S(2)}, u32[]{:S(2)}) collective-permute-start(bf16[2,8,2048]{2,1,0:T(8,128)(2,1)S(1)} %pad_maximum_fusion.1.refs_0_), channel_id=1, source_target_pairs={{0,4},{2,6},{4,8},{6,10},{8,12},{10,14},{12,0},{14,2},{1,5},{3,7},... | collective-permute-start | bytes 196616 | tf_op jit(solution)/shard_map/ppermute | solution.py:331
  26.5 5.3 %collective-permute-start.3 = (bf16[2,8,2048]{2,1,0:T(8,128)(2,1)S(1)}, bf16[2,8,2048]{2,1,0:T(8,128)(2,1)S(1)}, u32[]{:S(2)}, u32[]{:S(2)}) collective-permute-start(bf16[2,8,2048]{2,1,0:T(8,128)(2,1)S(1)} %pad_maximum_fusion.1.refs_0_), channel_id=1, source_target_pairs={{0,14},{2,0},{4,2},{6,4},{8,6},{10,8},{12,10},{14,12},{1,15},{3,1}... | collective-permute-start | bytes 196616 | tf_op jit(solution)/shard_map/ppermute | solution.py:331
  29.9 5.5 %collective-permute-start.2 = (bf16[2,8,2048]{2,1,0:T(8,128)(2,1)S(1)}, bf16[2,8,2048]{2,1,0:T(8,128)(2,1)S(1)}, u32[]{:S(2)}, u32[]{:S(2)}) collective-permute-start(bf16[2,8,2048]{2,1,0:T(8,128)(2,1)S(1)} %pad_maximum_fusion.1.refs_0_), channel_id=1, source_target_pairs={{0,2},{2,4},{4,6},{6,8},{8,10},{10,12},{12,14},{14,0},{1,3},{3,5},... | collective-permute-start | bytes 196616 | tf_op jit(solution)/shard_map/ppermute | solution.py:331
  36.2 19.2 %copy-start.3 = (bf16[64,2048]{1,0:T(8,128)(2,1)}, bf16[64,2048]{1,0:T(8,128)(2,1)S(1)}, u32[]{:S(2)}) copy-start(bf16[64,2048]{1,0:T(8,128)(2,1)S(1)} %get-tuple-element.47.refs_6_) | copy-start | bytes 786436
  36.2 19.7 %copy-start.4 = (bf16[64,2048]{1,0:T(8,128)(2,1)}, bf16[64,2048]{1,0:T(8,128)(2,1)S(1)}, u32[]{:S(2)}) copy-start(bf16[64,2048]{1,0:T(8,128)(2,1)S(1)} %get-tuple-element.48.refs_7_) | copy-start | bytes 786436
  36.3 21.9 %copy-start.8 = (bf16[2,128,2048]{2,1,0:T(8,128)(2,1)}, bf16[2,128,2048]{2,1,0:T(8,128)(2,1)S(1)}, u32[]{:S(2)}) copy-start(bf16[2,128,2048]{2,1,0:T(8,128)(2,1)S(1)} %collective-permute-done.1.refs_4_) | copy-start | bytes 3145732
  36.3 6.6 %collective-permute-start.10 = (bf16[2,16,2048]{2,1,0:T(8,128)(2,1)S(1)}, bf16[2,16,2048]{2,1,0:T(8,128)(2,1)S(1)}, u32[]{:S(2)}, u32[]{:S(2)}) collective-permute-start(bf16[2,16,2048]{2,1,0:T(8,128)(2,1)S(1)} %slice_bitcast_fusion.2), channel_id=1, source_target_pairs={{0,128},{128,0},{1,129},{129,1},{2,130},{130,2},{3,131},{131,3},{4... | collective-permute-start | bytes 393224 | tf_op jit(solution)/shard_map/ppermute | solution.py:331
  38.6 18.5 %collective-permute-start.9 = (bf16[2,128,2048]{2,1,0:T(8,128)(2,1)S(1)}, bf16[2,128,2048]{2,1,0:T(8,128)(2,1)S(1)}, u32[]{:S(2)}, u32[]{:S(2)}) collective-permute-start(bf16[2,128,2048]{2,1,0:T(8,128)(2,1)S(1)} %collective-permute-done.1.refs_4_), channel_id=1, source_target_pairs={{0,2},{2,4},{4,6},{6,8},{8,10},{10,12},{12,14},{14,0},{16,18},{18,... | collective-permute-start | bytes 3145736 | tf_op jit(solution)/shard_map/ppermute | solution.py:376
  42.8 15.3 %copy-start.2 = (bf16[2,2,16,2048]{3,2,1,0:T(8,128)(2,1)}, bf16[2,2,16,2048]{3,2,1,0:T(8,128)(2,1)S(1)}, u32[]{:S(2)}) copy-start(bf16[2,2,16,2048]{3,2,1,0:T(8,128)(2,1)S(1)} %bitcast_dynamic-update-slice_fusion.refs_8_) | copy-start | bytes 786436
  42.8 9.2 %collective-permute-start.13 = (bf16[2,2,16,2048]{3,2,1,0:T(8,128)(2,1)S(1)}, bf16[2,2,16,2048]{3,2,1,0:T(8,128)(2,1)S(1)}, u32[]{:S(2)}, u32[]{:S(2)}) collective-permute-start(bf16[2,2,16,2048]{3,2,1,0:T(8,128)(2,1)S(1)} %bitcast_dynamic-update-slice_fusion.refs_8_), channel_id=1, source_target_pairs={{0,64},{32,96},{64,0},{96,32},{1,65},{33,97},{65,1},{97,33},{2,66}... | collective-permute-start | bytes 786440 | tf_op jit(solution)/shard_map/ppermute | solution.py:331
  45.9 9.2 %collective-permute-start.12 = (bf16[2,2,16,2048]{3,2,1,0:T(8,128)(2,1)S(1)}, bf16[2,2,16,2048]{3,2,1,0:T(8,128)(2,1)S(1)}, u32[]{:S(2)}, u32[]{:S(2)}) collective-permute-start(bf16[2,2,16,2048]{3,2,1,0:T(8,128)(2,1)S(1)} %bitcast_dynamic-update-slice_fusion.refs_8_), channel_id=1, source_target_pairs={{0,96},{32,0},{64,32},{96,64},{1,97},{33,1},{65,33},{97,65},{2,98}... | collective-permute-start | bytes 786440 | tf_op jit(solution)/shard_map/ppermute | solution.py:331
  47.2 8.2 %collective-permute-start.11 = (bf16[2,2,16,2048]{3,2,1,0:T(8,128)(2,1)S(1)}, bf16[2,2,16,2048]{3,2,1,0:T(8,128)(2,1)S(1)}, u32[]{:S(2)}, u32[]{:S(2)}) collective-permute-start(bf16[2,2,16,2048]{3,2,1,0:T(8,128)(2,1)S(1)} %bitcast_dynamic-update-slice_fusion.refs_8_), channel_id=1, source_target_pairs={{0,32},{32,64},{64,96},{96,0},{1,33},{33,65},{65,97},{97,1},{2,34}... | collective-permute-start | bytes 786440 | tf_op jit(solution)/shard_map/ppermute | solution.py:331
  48.0 8.0 %collective-permute-start.14 = (bf16[2,2,16,2048]{3,2,1,0:T(8,128)(2,1)S(1)}, bf16[2,2,16,2048]{3,2,1,0:T(8,128)(2,1)S(1)}, u32[]{:S(2)}, u32[]{:S(2)}) collective-permute-start(bf16[2,2,16,2048]{3,2,1,0:T(8,128)(2,1)S(1)} %bitcast_dynamic-update-slice_fusion.refs_8_), channel_id=1, source_target_pairs={{0,16},{16,0},{1,17},{17,1},{2,18},{18,2},{3,19},{19,3},{4,20},{20... | collective-permute-start | bytes 786440 | tf_op jit(solution)/shard_map/ppermute | solution.py:331
  52.1 5.1 %copy-start.10 = (bf16[2,2,16,2048]{3,2,1,0:T(8,128)(2,1)}, bf16[2,2,16,2048]{3,2,1,0:T(8,128)(2,1)S(1)}, u32[]{:S(2)}) copy-start(bf16[2,2,16,2048]{3,2,1,0:T(8,128)(2,1)S(1)} %collective-permute-done.13.refs_11_) | copy-start | bytes 786436
  52.1 3.9 %collective-permute-start.17 = (bf16[2,2,16,2048]{3,2,1,0:T(8,128)(2,1)S(1)}, bf16[2,2,16,2048]{3,2,1,0:T(8,128)(2,1)}, u32[]{:S(2)}, u32[]{:S(2)}) collective-permute-start(bf16[2,2,16,2048]{3,2,1,0:T(8,128)(2,1)S(1)} %collective-permute-done.13.refs_11_), channel_id=1, source_target_pairs={{0,16},{16,0},{1,17},{17,1},{2,18},{18,2},{3,19},{19,3},{4,20},{20... | collective-permute-start | bytes 786440 | tf_op jit(solution)/shard_map/ppermute | solution.py:331
  55.1 2.1 %copy-start.11 = (bf16[2,2,16,2048]{3,2,1,0:T(8,128)(2,1)}, bf16[2,2,16,2048]{3,2,1,0:T(8,128)(2,1)S(1)}, u32[]{:S(2)}) copy-start(bf16[2,2,16,2048]{3,2,1,0:T(8,128)(2,1)S(1)} %collective-permute-done.12.refs_10_) | copy-start | bytes 786436
  55.1 1.7 %collective-permute-start.16 = (bf16[2,2,16,2048]{3,2,1,0:T(8,128)(2,1)S(1)}, bf16[2,2,16,2048]{3,2,1,0:T(8,128)(2,1)}, u32[]{:S(2)}, u32[]{:S(2)}) collective-permute-start(bf16[2,2,16,2048]{3,2,1,0:T(8,128)(2,1)S(1)} %collective-permute-done.12.refs_10_), channel_id=1, source_target_pairs={{0,16},{16,0},{1,17},{17,1},{2,18},{18,2},{3,19},{19,3},{4,20},{20... | collective-permute-start | bytes 786440 | tf_op jit(solution)/shard_map/ppermute | solution.py:331
  55.4 1.8 %copy-start.12 = (bf16[2,2,16,2048]{3,2,1,0:T(8,128)(2,1)}, bf16[2,2,16,2048]{3,2,1,0:T(8,128)(2,1)S(1)}, u32[]{:S(2)}) copy-start(bf16[2,2,16,2048]{3,2,1,0:T(8,128)(2,1)S(1)} %collective-permute-done.11.refs_9_) | copy-start | bytes 786436
  55.4 1.8 %collective-permute-start.15 = (bf16[2,2,16,2048]{3,2,1,0:T(8,128)(2,1)S(1)}, bf16[2,2,16,2048]{3,2,1,0:T(8,128)(2,1)}, u32[]{:S(2)}, u32[]{:S(2)}) collective-permute-start(bf16[2,2,16,2048]{3,2,1,0:T(8,128)(2,1)S(1)} %collective-permute-done.11.refs_9_), channel_id=1, source_target_pairs={{0,16},{16,0},{1,17},{17,1},{2,18},{18,2},{3,19},{19,3},{4,20},{20... | collective-permute-start | bytes 786440 | tf_op jit(solution)/shard_map/ppermute | solution.py:331
  56.0 1.2 copy-start.13
  57.2 1.0 copy-start.9
  75.4 23.4 %copy-start = (f32[256,2048]{1,0:T(8,128)}, f32[256,2048]{1,0:T(8,128)S(1)}, u32[]{:S(2)}) copy-start(f32[256,2048]{1,0:T(8,128)S(1)} %get-tuple-element.53.dv_ref) | copy-start | bytes 6291460
  75.4 2.7 %collective-permute-start.19 = (bf16[4,2,2,16,2048]{4,3,2,1,0:T(8,128)(2,1)S(1)}, bf16[4,2,2,16,2048]{4,3,2,1,0:T(8,128)(2,1)S(1)}, u32[]{:S(2)}, u32[]{:S(2)}) collective-permute-start(bf16[4,2,2,16,2048]{4,3,2,1,0:T(8,128)(2,1)S(1)} %get-tuple-element.57), channel_id=1, source_target_pairs={{0,16},{16,0},{1,17},{17,1},{2,18},{18,2},{3,19},{19,3},{4,20},{20... | collective-permute-start | bytes 3145736 | tf_op jit(solution)/shard_map/ppermute | solution.py:331
  78.5 20.4 %collective-permute-start.20 = (bf16[2,2,16,2048]{3,2,1,0:T(8,128)(2,1)S(1)}, bf16[2,2,16,2048]{3,2,1,0:T(8,128)(2,1)S(1)}, u32[]{:S(2)}, u32[]{:S(2)}) collective-permute-start(bf16[2,2,16,2048]{3,2,1,0:T(8,128)(2,1)S(1)} %get-tuple-element.70), channel_id=1, source_target_pairs={{0,64},{32,96},{64,0},{96,32},{1,65},{33,97},{65,1},{97,33},{2,66}... | collective-permute-start | bytes 786440 | tf_op jit(solution)/shard_map/ppermute | solution.py:331
  81.0 17.9 %collective-permute-start.22 = (bf16[2,2,16,2048]{3,2,1,0:T(8,128)(2,1)S(1)}, bf16[2,2,16,2048]{3,2,1,0:T(8,128)(2,1)S(1)}, u32[]{:S(2)}, u32[]{:S(2)}) collective-permute-start(bf16[2,2,16,2048]{3,2,1,0:T(8,128)(2,1)S(1)} %get-tuple-element.71), channel_id=1, source_target_pairs={{0,32},{32,64},{64,96},{96,0},{1,33},{33,65},{65,97},{97,1},{2,34}... | collective-permute-start | bytes 786440 | tf_op jit(solution)/shard_map/ppermute | solution.py:331
  82.0 16.9 %collective-permute-start.21 = (bf16[2,2,16,2048]{3,2,1,0:T(8,128)(2,1)S(1)}, bf16[2,2,16,2048]{3,2,1,0:T(8,128)(2,1)S(1)}, u32[]{:S(2)}, u32[]{:S(2)}) collective-permute-start(bf16[2,2,16,2048]{3,2,1,0:T(8,128)(2,1)S(1)} %get-tuple-element.72), channel_id=1, source_target_pairs={{0,96},{32,0},{64,32},{96,64},{1,97},{33,1},{65,33},{97,65},{2,98}... | collective-permute-start | bytes 786440 | tf_op jit(solution)/shard_map/ppermute | solution.py:331
  84.2 37.0 %collective-permute-start.18 = (bf16[2,128,2048]{2,1,0:T(8,128)(2,1)S(1)}, bf16[2,128,2048]{2,1,0:T(8,128)(2,1)S(1)}, u32[]{:S(2)}, u32[]{:S(2)}) collective-permute-start(bf16[2,128,2048]{2,1,0:T(8,128)(2,1)S(1)} %get-tuple-element.54), channel_id=1, source_target_pairs={{1,0},{2,1},{3,2},{4,3},{5,4},{6,5},{7,6},{8,7},{9,8},{10,9},{11,1... | collective-permute-start | bytes 3145736 | tf_op jit(solution)/shard_map/ppermute | solution.py:388
  99.8 11.3 %collective-permute-start.23 = (bf16[5,4,2048]{2,1,0:T(4,128)(2,1)S(1)}, bf16[5,4,2048]{2,1,0:T(4,128)(2,1)S(1)}, u32[]{:S(2)}, u32[]{:S(2)}) collective-permute-start(bf16[5,4,2048]{2,1,0:T(4,128)(2,1)S(1)} %get-tuple-element.59), channel_id=1, source_target_pairs={{0,8},{2,10},{4,12},{6,14},{8,0},{10,2},{12,4},{14,6},{1,9},{3,11}... | collective-permute-start | bytes 245768 | tf_op jit(solution)/shard_map/ppermute | solution.py:331
  101.3 14.1 %collective-permute-start.24 = (bf16[5,4,2048]{2,1,0:T(4,128)(2,1)S(1)}, bf16[5,4,2048]{2,1,0:T(4,128)(2,1)S(1)}, u32[]{:S(2)}, u32[]{:S(2)}) collective-permute-start(bf16[5,4,2048]{2,1,0:T(4,128)(2,1)S(1)} %get-tuple-element.60), channel_id=1, source_target_pairs={{0,6},{2,8},{4,10},{6,12},{8,14},{10,0},{12,2},{14,4},{1,7},{3,9},... | collective-permute-start | bytes 245768 | tf_op jit(solution)/shard_map/ppermute | solution.py:331
  104.8 10.5 %collective-permute-start.25 = (bf16[5,4,2048]{2,1,0:T(4,128)(2,1)S(1)}, bf16[5,4,2048]{2,1,0:T(4,128)(2,1)S(1)}, u32[]{:S(2)}, u32[]{:S(2)}) collective-permute-start(bf16[5,4,2048]{2,1,0:T(4,128)(2,1)S(1)} %get-tuple-element.61), channel_id=1, source_target_pairs={{0,10},{2,12},{4,14},{6,0},{8,2},{10,4},{12,6},{14,8},{1,11},{3,13... | collective-permute-start | bytes 245768 | tf_op jit(solution)/shard_map/ppermute | solution.py:331
  106.3 12.3 %collective-permute-start.26 = (bf16[5,4,2048]{2,1,0:T(4,128)(2,1)S(1)}, bf16[5,4,2048]{2,1,0:T(4,128)(2,1)S(1)}, u32[]{:S(2)}, u32[]{:S(2)}) collective-permute-start(bf16[5,4,2048]{2,1,0:T(4,128)(2,1)S(1)} %get-tuple-element.62), channel_id=1, source_target_pairs={{0,4},{2,6},{4,8},{6,10},{8,12},{10,14},{12,0},{14,2},{1,5},{3,7},... | collective-permute-start | bytes 245768 | tf_op jit(solution)/shard_map/ppermute | solution.py:331
  111.1 7.5 %collective-permute-start.27 = (bf16[5,4,2048]{2,1,0:T(4,128)(2,1)S(1)}, bf16[5,4,2048]{2,1,0:T(4,128)(2,1)S(1)}, u32[]{:S(2)}, u32[]{:S(2)}) collective-permute-start(bf16[5,4,2048]{2,1,0:T(4,128)(2,1)S(1)} %get-tuple-element.63), channel_id=1, source_target_pairs={{0,12},{2,14},{4,0},{6,2},{8,4},{10,6},{12,8},{14,10},{1,13},{3,15... | collective-permute-start | bytes 245768 | tf_op jit(solution)/shard_map/ppermute | solution.py:331
  115.4 5.7 %collective-permute-start.28 = (bf16[5,4,2048]{2,1,0:T(4,128)(2,1)S(1)}, bf16[5,4,2048]{2,1,0:T(4,128)(2,1)S(1)}, u32[]{:S(2)}, u32[]{:S(2)}) collective-permute-start(bf16[5,4,2048]{2,1,0:T(4,128)(2,1)S(1)} %get-tuple-element.64), channel_id=1, source_target_pairs={{0,2},{2,4},{4,6},{6,8},{8,10},{10,12},{12,14},{14,0},{1,3},{3,5},... | collective-permute-start | bytes 245768 | tf_op jit(solution)/shard_map/ppermute | solution.py:331
  115.4 5.6 %collective-permute-start.29 = (bf16[5,4,2048]{2,1,0:T(4,128)(2,1)S(1)}, bf16[5,4,2048]{2,1,0:T(4,128)(2,1)S(1)}, u32[]{:S(2)}, u32[]{:S(2)}) collective-permute-start(bf16[5,4,2048]{2,1,0:T(4,128)(2,1)S(1)} %get-tuple-element.65), channel_id=1, source_target_pairs={{0,14},{2,0},{4,2},{6,4},{8,6},{10,8},{12,10},{14,12},{1,15},{3,1}... | collective-permute-start | bytes 245768 | tf_op jit(solution)/shard_map/ppermute | solution.py:331
  121.3 19.5 %collective-permute-start.31 = (bf16[2,2048]{1,0:T(2,128)(2,1)S(1)}, bf16[2,2048]{1,0:T(2,128)(2,1)S(1)}, u32[]{:S(2)}, u32[]{:S(2)}) collective-permute-start(bf16[2,2048]{1,0:T(2,128)(2,1)S(1)} %bitcast.28), channel_id=1, source_target_pairs={{0,128},{128,0},{1,129},{129,1},{2,130},{130,2},{3,131},{131,3},{4... | collective-permute-start | bytes 24584 | tf_op jit(solution)/shard_map/ppermute | solution.py:331
  122.8 19.5 %collective-permute-start.32 = (bf16[2,2048]{1,0:T(2,128)(2,1)S(1)}, bf16[2,2048]{1,0:T(2,128)(2,1)S(1)}, u32[]{:S(2)}, u32[]{:S(2)}) collective-permute-start(bf16[2,2048]{1,0:T(2,128)(2,1)S(1)} %bitcast.27), channel_id=1, source_target_pairs={{0,129},{1,128},{128,1},{129,0},{2,131},{3,130},{130,3},{131,2},{4... | collective-permute-start | bytes 24584 | tf_op jit(solution)/shard_map/ppermute | solution.py:401
  140.7 4.0 %collective-permute-start.30 = (bf16[2,4,2048]{2,1,0:T(4,128)(2,1)S(1)}, bf16[2,4,2048]{2,1,0:T(4,128)(2,1)S(1)}, u32[]{:S(2)}, u32[]{:S(2)}) collective-permute-start(bf16[2,4,2048]{2,1,0:T(4,128)(2,1)S(1)} %slice.85), channel_id=1, source_target_pairs={{0,1},{1,0},{2,3},{3,2},{4,5},{5,4},{6,7},{7,6},{8,9},{9,8},{10,11... | collective-permute-start | bytes 98312 | tf_op jit(solution)/shard_map/ppermute | solution.py:331
  144.7 1.6 %copy-start.1 = (f32[256,2048]{1,0:T(8,128)S(1)}, f32[256,2048]{1,0:T(8,128)}, u32[]{:S(2)}) copy-start(f32[256,2048]{1,0:T(8,128)} %copy-done) | copy-start | bytes 6291460

commit v3 on v2

--- a/solution.py
+++ b/solution.py
@@ -26,6 +26,7 @@
 HPB = 4
 Z_ORDER = (4, 5, 3, 6, 2, 7, 1)
 Y_STEP = (0, 1, 3, 2)
+DIAGONAL = ((0, 3), (1, 2), (2, 1), (3, 0))
 
 
 def nt(a, b):
@@ -40,16 +41,16 @@
     return lax.dot_general(a, b, (((0,), (0,)), ((), ())), preferred_element_type=jnp.float32)
 
 
-def one_head(odd, bias_ref, seg, refs, outs):
-    q_ref, k_ref, v_ref, g_ref, across_ref, along_ref, pk2_ref, pv2_ref = refs[:8]
-    thirds = refs[8:]
+def one_head(bias_ref, seg, refs, outs):
+    q_ref, k_ref, v_ref, g_ref, prior_ref, pk2_ref, pv2_ref = refs[:7]
+    thirds = refs[7:]
     att_ref, dq_ref, dk_ref, dv_ref, dprior_ref, g2_ref, near_ref, far_ref = outs
     q = q_ref[:, seg]
     k = k_ref[:, seg]
     v = v_ref[:, seg]
     g = g_ref[:, seg]
-    prior_k = jnp.where(odd, across_ref[0, :, seg], along_ref[0, :, seg])
-    prior_v = jnp.where(odd, across_ref[1, :, seg], along_ref[1, :, seg])
+    prior_k = prior_ref[0, :, seg]
+    prior_v = prior_ref[1, :, seg]
     pk = jnp.concatenate(
         [pk2_ref[:, seg]] + [t[s, 0, :, seg] for t in thirds for s in range(NXH)], axis=0
     )
@@ -126,10 +127,10 @@
 
     dprior_ref[0, :, seg] = nn(ds[0][0], q0).astype(jnp.bfloat16)
     dprior_ref[1, :, seg] = nn(ws[0][0], g0).astype(jnp.bfloat16)
-    dk_ref[:BLK, seg] = nn(dsk0, q)
-    dk_ref[BLK:, seg] = nn(ds[1][1], q1)
-    dv_ref[:BLK, seg] = nn(wk0, g)
-    dv_ref[BLK:, seg] = nn(ws[1][1], g1)
+    dk_ref[:BLK, seg] = nn(dsk0, q).astype(jnp.bfloat16)
+    dk_ref[BLK:, seg] = nn(ds[1][1], q1).astype(jnp.bfloat16)
+    dv_ref[:BLK, seg] = nn(wk0, g).astype(jnp.bfloat16)
+    dv_ref[BLK:, seg] = nn(ws[1][1], g1).astype(jnp.bfloat16)
     gkp = nn(dsp, q)
     gvp = nn(wp, g)
     for kv, part in enumerate((gkp, gvp)):
@@ -170,10 +171,9 @@
     def _():
         fill_bias(place_ref, bias_ref)
 
-    odd = place_ref[4] == 1
     for h in range(HPB):
         seg = slice(h * HDIM, (h + 1) * HDIM)
-        one_head(odd, bias_ref, seg, refs[:16], refs[16:24])
+        one_head(bias_ref, seg, refs[:15], refs[15:23])
 
 
 def cols(width, *lead):
@@ -181,7 +181,7 @@
     return pl.BlockSpec(lead + (width,), lambda i: zeros + (i,))
 
 
-def attention(place, q, k, v, g, across, along, pk2, pv2, thirds):
+def attention(place, q, k, v, g, prior, pk2, pv2, thirds):
     width = HPB * HDIM
     rows = q.shape[0]
     shape = jax.ShapeDtypeStruct
@@ -193,7 +193,7 @@
         in_specs=[
             pl.BlockSpec(memory_space=pltpu.SMEM),
             row_spec, row_spec, row_spec, row_spec,
-            cols(width, 2, BLK), cols(width, 2, BLK), cols(width, N2), cols(width, N2),
+            cols(width, 2, BLK), cols(width, N2), cols(width, N2),
         ] + [cols(width, NXH, 2, N3G)] * 8,
         out_specs=[
             row_spec, row_spec, row_spec, row_spec,
@@ -202,8 +202,8 @@
         out_shape=[
             shape((rows, FEAT), jnp.bfloat16),
             shape((rows, FEAT), jnp.bfloat16),
-            shape((rows, FEAT), jnp.float32),
-            shape((rows, FEAT), jnp.float32),
+            shape((rows, FEAT), jnp.bfloat16),
+            shape((rows, FEAT), jnp.bfloat16),
             shape((2, BLK, FEAT), jnp.bfloat16),
             shape((NZ, 2, 8, FEAT), jnp.float32),
             shape((NY, NXH, 2, N3G, FEAT), jnp.bfloat16),
@@ -214,40 +214,69 @@
         cost_estimate=pl.CostEstimate(
             flops=6 * 2 * 2 * BLK * 576 * FEAT, bytes_accessed=20 << 20, transcendentals=0
         ),
-    )(place, q, k, v, g, across, along, pk2, pv2, *thirds)
-
-
-def pool_kernel(k_ref, v_ref, pooled_ref):
+    )(place, q, k, v, g, prior, pk2, pv2, *thirds)
+
+
+def pool_kernel(k_ref, v_ref, pooled_ref, third_ref):
     for kv, ref in ((0, k_ref), (1, v_ref)):
+        third = jnp.zeros((1, ref.shape[1]), jnp.float32)
         for e in range(4):
             run = ref[e * P2 : (e + 1) * P2, :].astype(jnp.float32)
             total = jnp.sum(run, axis=0, keepdims=True) * (1.0 / math.sqrt(P2))
-            pooled_ref[kv, e : e + 1, :] = total.astype(jnp.bfloat16)
+            entry = total.astype(jnp.bfloat16)
+            pooled_ref[kv, e : e + 1, :] = entry
+            third = third + entry.astype(jnp.float32)
+        third_ref[kv : kv + 1, :] = (third * 0.5).astype(jnp.bfloat16)
 
 
 def pool(k, v):
     width = 512
+    shape = jax.ShapeDtypeStruct
     return pl.pallas_call(
         pool_kernel,
         grid=(FEAT // width,),
         in_specs=[cols(width, k.shape[0])] * 2,
-        out_specs=cols(width, 2, 4),
-        out_shape=jax.ShapeDtypeStruct((2, 4, FEAT), jnp.bfloat16),
-        compiler_params=pltpu.CompilerParams(vmem_limit_bytes=56 * 1024 * 1024),
+        out_specs=[cols(width, 2, 4), cols(width, 2)],
+        out_shape=[
+            shape((2, 4, FEAT), jnp.bfloat16),
+            shape((2, FEAT), jnp.bfloat16),
+        ],
+        compiler_params=pltpu.CompilerParams(vmem_limit_bytes=24 * 1024 * 1024),
         cost_estimate=pl.CostEstimate(flops=1 << 20, bytes_accessed=2 << 20, transcendentals=0),
     )(k, v)
+
+
+def joined_kernel(mine_ref, other_ref, near_ref, far_ref, out_ref):
+    for kv in range(2):
+        out_ref[kv * NXL] = mine_ref[kv]
+        out_ref[kv * NXL + 1] = other_ref[kv]
+        out_ref[4, kv * NXL : kv * NXL + 1, :] = near_ref[kv : kv + 1, :]
+        out_ref[4, kv * NXL + 1 : kv * NXL + 2, :] = far_ref[kv : kv + 1, :]
+
+
+def joined(mine, other, near, far):
+    width = FEAT
+    return pl.pallas_call(
+        joined_kernel,
+        grid=(1,),
+        in_specs=[cols(width, 2, 4), cols(width, 2, 4), cols(width, 2), cols(width, 2)],
+        out_specs=cols(width, 5, 4),
+        out_shape=jax.ShapeDtypeStruct((5, 4, FEAT), jnp.bfloat16),
+        compiler_params=pltpu.CompilerParams(vmem_limit_bytes=24 * 1024 * 1024),
+        cost_estimate=pl.CostEstimate(flops=1 << 10, bytes_accessed=1 << 18, transcendentals=0),
+    )(mine, other, near, far)
 
 
 def gathered_kernel(*refs):
     by_step = dict(zip((0,) + Z_ORDER[::-1], refs[:NZ]))
     pieces, (pk_ref, pv_ref, third_ref) = [by_step[s] for s in range(NZ)], refs[NZ:]
     for kv, out in ((0, pk_ref), (1, pv_ref)):
-        parts = [p[kv].astype(jnp.float32) for p in pieces]
-        out[...] = jnp.concatenate(parts, axis=0).astype(jnp.bfloat16)
-        sums = [
-            jnp.sum(p[lo : lo + 4], axis=0, keepdims=True) * 0.5 for p in parts for lo in (0, 4)
-        ]
+        runs = [p[kv * NXL + i].astype(jnp.float32) for p in pieces for i in range(NXL)]
+        out[...] = jnp.concatenate(runs, axis=0).astype(jnp.bfloat16)
+        sums = [jnp.sum(r, axis=0, keepdims=True) * 0.5 for r in runs]
         third_ref[0, kv] = jnp.concatenate(sums, axis=0).astype(jnp.bfloat16)
+        rest = [p[4, kv * NXL : kv * NXL + NXL, :].astype(jnp.float32) for p in pieces]
+        third_ref[1, kv] = jnp.concatenate(rest, axis=0).astype(jnp.bfloat16)
 
 
 def gathered(pieces):
@@ -256,11 +285,11 @@
     return pl.pallas_call(
         gathered_kernel,
         grid=(FEAT // width,),
-        in_specs=[cols(width, 2, 8)] * NZ,
-        out_specs=[cols(width, N2), cols(width, N2), cols(width, 1, 2, N3G)],
+        in_specs=[cols(width, 5, 4)] * NZ,
+        out_specs=[cols(width, N2), cols(width, N2), cols(width, NXH, 2, N3G)],
         out_shape=[
-            shape((N2, FEAT), jnp.bfloat16),
-            shape((N2, FEAT), jnp.bfloat16),
+            pltpu.HBM((N2, FEAT), jnp.bfloat16),
+            pltpu.HBM((N2, FEAT), jnp.bfloat16),
             shape((NXH, 2, N3G, FEAT), jnp.bfloat16),
         ],
         compiler_params=pltpu.CompilerParams(vmem_limit_bytes=32 * 1024 * 1024),
@@ -301,7 +330,7 @@
         for part in range(4):
             lo = part * P2
             spread = two_ref[kv, part : part + 1, :]
-            val = src[lo : lo + P2, :] + spread
+            val = src[lo : lo + P2, :].astype(jnp.float32) + spread
             if part >= 2:
                 rows = slice(lo - BLK, lo - BLK + P2)
                 val = val + back_ref[kv, rows, :].astype(jnp.float32)
@@ -339,49 +368,27 @@
     return x.astype(jnp.float32)
 
 
-def across_pairs(step=1):
-    groups, shards = NXH * NY * NC, NZ * NXL
-    pairs = []
-    for g in range(groups):
-        for shard in range(shards):
-            even = shard % 2 == 0
-            crosses = shard == (shards - 1 if step > 0 else shards - 2)
-            to = g + step if crosses else g
-            if 0 <= to < groups:
-                pairs.append((g * shards + shard, to * shards + shard + (1 if even else -1)))
-    return pairs
-
-
-def along_pairs(step):
-    groups, shards = NXH * NY * NC, NZ * NXL
-    return [
-        (g * shards + shard, g * shards + (shard + 2 * step) % shards)
-        for g in range(groups)
-        for shard in range(0, shards, 2)
-    ]
-
-
 def per_device(queries, keys, values, grad_out):
     xh, y, c, z, xl = (lax.axis_index(a) for a in AXES)
 
-    pooled = pool(keys, values)
-    last = jnp.stack([keys[BLK:], values[BLK:]])
-    pair = jnp.concatenate([pooled, ring(pooled, "xl", NXL, 1)], axis=1)
-    last, pair = lax.optimization_barrier((last, pair))
-    across = lax.ppermute(last, AXES, across_pairs(1))
+    pooled, own = pool(keys, values)
+    other = ring(pooled, "xl", NXL, 1)
+    near_own = ring(own, "xh", NXH, 1)
+    far_own = lax.ppermute(own, ("xh", "xl"), DIAGONAL)
+    pair = joined(pooled, other, near_own, far_own)
     pieces = [pair] + [ring(pair, "z", NZ, s) for s in Z_ORDER[::-1]]
     pk2, pv2, third = gathered(pieces)
-    own_third = third[0]
-    across, own_third = lax.optimization_barrier((across, own_third))
-    along = lax.ppermute(across, AXES, along_pairs(1))
-    third = third.at[1].set(ring(own_third, "xh", NXH, 1))
+    last = jnp.stack([keys[BLK:], values[BLK:]])
+    last, third = lax.optimization_barrier((last, third))
+    count = NXH * NY * NC * NZ * NXL
+    prior = lax.ppermute(last, AXES, [(i, i + 1) for i in range(count - 1)])
     thirds = [third] + [ring(third, "y", NY, s) for s in Y_STEP[1:]]
     thirds = thirds + [ring(t, "c", NC, 1) for t in thirds]
 
     place = jnp.stack([xh, y, c, z, xl]).astype(jnp.int32)
 
     attended, grad_q, dk, dv, dprior, g2, near, far = attention(
-        place, *in_hbm(queries, keys, values, grad_out, across, along, pk2, pv2), in_hbm(*thirds)
+        place, *in_hbm(queries, keys, values, grad_out, prior, pk2, pv2), in_hbm(*thirds)
     )
 
     count = NXH * NY * NC * NZ * NXL
@@ -392,14 +399,14 @@
     t3 = s3[0]
     for s in (3, 1, 2):
         t3 = t3 + f32(ring(bf(s3[s]), "y", NY, -Y_STEP[s]))
+    back, t3 = lax.optimization_barrier((back, t3))
     parts = lifted(g2, t3)
     two = parts[0]
     for s in Z_ORDER:
         two = two + f32(ring(parts[s], "z", NZ, -s))
-    back, two = lax.optimization_barrier((back, two))
     near_third = ring(bf(two[4, 0::2]), "xh", NXH, 1)
     far_third = lax.ppermute(
-        bf(two[4, 1::2]), ("xh", "xl"), [(0, 3), (1, 2), (2, 1), (3, 0)]
+        bf(two[4, 1::2]), ("xh", "xl"), DIAGONAL
     )
     two = two[0:4:2] + f32(ring(bf(two[1:4:2]), "xl", NXL, 1))
     two = two + 0.5 * (f32(near_third) + f32(far_third))[:, None, :]

time: 149 us -> 142 us (0.953)
  starting transfers between devices: 82.3 us -> 69.5 us
  waiting for transfers between devices: 37 us -> 45 us
  Pallas kernels: 24.7 us -> 22.1 us
    ppermute x3, starting transfers between devices: 22.4 us -> 5.57 us  [the longest x1 2.96 us: per_device(): prior = lax.ppermute(last, AXES, [(i, i + 1) for i in range(count - 1)])]
    ppermute x29, starting transfers between devices: 45.3 us -> 60.9 us  [ring(): lax.ppermute(value, axis, [(i, (i + step) % size) for i in range(size)])]
    ppermute x1, starting transfers between devices: 14.6 us -> 3.09 us  [per_device(): back = lax.ppermute(dprior, AXES, [(i + 1, i) for i in range(count - 1)])]
    ppermute x3, waiting for transfers between devices: 1.5 us -> 8.64 us  [the longest x1 5.66 us: per_device(): prior = lax.ppermute(last, AXES, [(i, i + 1) for i in range(count - 1)])]
    ppermute x1, waiting for transfers between devices: 0.01 us -> 5.46 us  [per_device(): back = lax.ppermute(dprior, AXES, [(i + 1, i) for i in range(count - 1)])]
    ppermute x29, waiting for transfers between devices: 35.5 us -> 30.9 us  [ring(): lax.ppermute(value, axis, [(i, (i + step) % size) for i in range(size)])]
    pallas_call x1, Pallas kernels: 3.68 us -> 0.76 us  [pool(): pl.pallas_call(pool_kernel, grid=(FEAT // width,), in_specs=[cols(width,...]
    unnamed x28 -> x18, local copies, waits for them, and re-layouts: 2.58 us -> 3.41 us
  transfers between devices with their start and end apart: 33 -> 33, of which waited for: 16 -> 21; matrix products, arithmetic and copies ran while one was open for 0% -> 0% of each run, Pallas kernels for 1% -> 0%
where the time goes in v3:
time: 142 us
  starting transfers between devices  69.5 us (49%)
  waiting for transfers between devices  45 us (32%)
  Pallas kernels  22.1 us (16%)
  local copies, waits for them, and re-layouts  3.65 us (3%)
    ppermute x29, starting transfers between devices, ring(): lax.ppermute(value, axis, [(i, (i + step) % size) for i in range(size)])  60.9 us
    ppermute x29, waiting for transfers between devices, ring(): lax.ppermute(value, axis, [(i, (i + step) % size) for i in range(size)])  30.9 us
    pallas_call x1, Pallas kernels, attention(): pl.pallas_call(attn_kernel, grid=(FEAT // width,), in_specs=[pl.BlockSpec...  17.1 us
    ppermute x1, waiting for transfers between devices, per_device(): prior = lax.ppermute(last, AXES, [(i, i + 1) for i in range(count - 1)])  5.66 us
    ppermute x1, waiting for transfers between devices, per_device(): back = lax.ppermute(dprior, AXES, [(i + 1, i) for i in range(count - 1)])  5.46 us
    unnamed x18, local copies, waits for them, and re-layouts  3.41 us
    ppermute x1, starting transfers between devices, per_device(): back = lax.ppermute(dprior, AXES, [(i + 1, i) for i in range(count - 1)])  3.09 us
    ppermute x1, starting transfers between devices, per_device(): prior = lax.ppermute(last, AXES, [(i, i + 1) for i in range(count - 1)])  2.96 us
  transfers between devices with their start and end apart: 33, of which 21 were waited for; matrix products, arithmetic and copies ran while one was open for 0% of the time, Pallas kernels for 0%

profile of v3, /device:TPU:2, one launch (start us, length us, event | category | flops | bytes accessed | tf_op | source)
XLA Modules:
  0.0 141.8 jit_solution(11409859249345355986)
XLA Ops:
  0.6 0.0 copy-start
  0.6 1.2 copy-done
  1.9 1.2 copy-done.2
  3.1 0.8 shard_map.75
  3.9 2.4 %collective-permute-start = (bf16[2,4,2048]{2,1,0:T(4,128)(2,1)S(1)}, bf16[2,4,2048]{2,1,0:T(4,128)(2,1)S(1)}, u32[]{:S(2)}, u32[]{:S(2)}) collective-permute-start(bf16[2,4,2048]{2,1,0:T(4,128)(2,1)S(1)} %get-tuple-element.31.mine_ref), channel_id=1, source_target_pairs={{0,1},{1,0},{2,3},{3,2},{4,5},{5,4},{6,7},{7,6},{8,9},{9,8},{10,11... | collective-permute-start | bytes 98312 | tf_op jit(solution)/shard_map/ppermute | solution.py:360
  6.2 0.4 collective-permute-start.2
  6.6 1.8 %collective-permute-start.1 = (bf16[2,2048]{1,0:T(2,128)(2,1)S(1)}, bf16[2,2048]{1,0:T(2,128)(2,1)S(1)}, u32[]{:S(2)}, u32[]{:S(2)}) collective-permute-start(bf16[2,2048]{1,0:T(2,128)(2,1)S(1)} %get-tuple-element.32), channel_id=1, source_target_pairs={{0,128},{128,0},{1,129},{129,1},{2,130},{130,2},{3,131},{131,3},{4... | collective-permute-start | bytes 24584 | tf_op jit(solution)/shard_map/ppermute | solution.py:360
  8.4 1.5 %collective-permute-done.2.far_ref = bf16[2,2048]{1,0:T(2,128)(2,1)S(1)} collective-permute-done((bf16[2,2048]{1,0:T(2,128)(2,1)S(1)}, bf16[2,2048]{1,0:T(2,128)(2,1)S(1)}, u32[]{:S(2)}, u32[]{:S(2)}) %collective-permute-start.2) | collective-permute-done | bytes 8224 | tf_op jit(solution)/shard_map/ppermute | solution.py:377
  9.9 1.9 %collective-permute-done.1.near_ref = bf16[2,2048]{1,0:T(2,128)(2,1)S(1)} collective-permute-done((bf16[2,2048]{1,0:T(2,128)(2,1)S(1)}, bf16[2,2048]{1,0:T(2,128)(2,1)S(1)}, u32[]{:S(2)}, u32[]{:S(2)}) %collective-permute-start.1) | collective-permute-done | bytes 8224 | tf_op jit(solution)/shard_map/ppermute | solution.py:360
  11.8 7.3 %collective-permute-start.9 = (bf16[5,4,2048]{2,1,0:T(4,128)(2,1)S(1)}, bf16[5,4,2048]{2,1,0:T(4,128)(2,1)S(1)}, u32[]{:S(2)}, u32[]{:S(2)}) collective-permute-start(bf16[5,4,2048]{2,1,0:T(4,128)(2,1)S(1)} %shard_map.76.refs_0_), channel_id=1, source_target_pairs={{0,8},{2,10},{4,12},{6,14},{8,0},{10,2},{12,4},{14,6},{1,9},{3,11}... | collective-permute-start | bytes 245768 | tf_op jit(solution)/shard_map/ppermute | solution.py:360
  19.1 0.1 slice_bitcast_fusion
  19.2 3.9 %collective-permute-start.7 = (bf16[5,4,2048]{2,1,0:T(4,128)(2,1)S(1)}, bf16[5,4,2048]{2,1,0:T(4,128)(2,1)S(1)}, u32[]{:S(2)}, u32[]{:S(2)}) collective-permute-start(bf16[5,4,2048]{2,1,0:T(4,128)(2,1)S(1)} %shard_map.76.refs_0_), channel_id=1, source_target_pairs={{0,6},{2,8},{4,10},{6,12},{8,14},{10,0},{12,2},{14,4},{1,7},{3,9},... | collective-permute-start | bytes 245768 | tf_op jit(solution)/shard_map/ppermute | solution.py:360
  23.1 0.9 collective-permute-start.6
  24.0 2.1 %collective-permute-start.5 = (bf16[5,4,2048]{2,1,0:T(4,128)(2,1)S(1)}, bf16[5,4,2048]{2,1,0:T(4,128)(2,1)S(1)}, u32[]{:S(2)}, u32[]{:S(2)}) collective-permute-start(bf16[5,4,2048]{2,1,0:T(4,128)(2,1)S(1)} %shard_map.76.refs_0_), channel_id=1, source_target_pairs={{0,4},{2,6},{4,8},{6,10},{8,12},{10,14},{12,0},{14,2},{1,5},{3,7},... | collective-permute-start | bytes 245768 | tf_op jit(solution)/shard_map/ppermute | solution.py:360
  26.0 2.5 %collective-permute-start.4 = (bf16[5,4,2048]{2,1,0:T(4,128)(2,1)S(1)}, bf16[5,4,2048]{2,1,0:T(4,128)(2,1)S(1)}, u32[]{:S(2)}, u32[]{:S(2)}) collective-permute-start(bf16[5,4,2048]{2,1,0:T(4,128)(2,1)S(1)} %shard_map.76.refs_0_), channel_id=1, source_target_pairs={{0,14},{2,0},{4,2},{6,4},{8,6},{10,8},{12,10},{14,12},{1,15},{3,1}... | collective-permute-start | bytes 245768 | tf_op jit(solution)/shard_map/ppermute | solution.py:360
  28.5 0.6 collective-permute-done.8.refs_6_
  29.1 1.4 collective-permute-start.3
  30.5 0.1 pad_maximum_fusion
  30.7 1.2 collective-permute-done.6.refs_4_
  31.8 0.4 collective-permute-done.5.refs_3_
  32.3 0.6 collective-permute-done.4.refs_2_
  32.9 1.9 %collective-permute-done.3.refs_1_ = bf16[5,4,2048]{2,1,0:T(4,128)(2,1)S(1)} collective-permute-done((bf16[5,4,2048]{2,1,0:T(4,128)(2,1)S(1)}, bf16[5,4,2048]{2,1,0:T(4,128)(2,1)S(1)}, u32[]{:S(2)}, u32[]{:S(2)}) %collective-permute-start.3) | collective-permute-done | bytes 81952 | tf_op jit(solution)/shard_map/ppermute | solution.py:360
  34.8 1.4 %shard_map.77 = (bf16[64,2048]{1,0:T(8,128)(2,1)}, bf16[64,2048]{1,0:T(8,128)(2,1)}, bf16[2,2,16,2048]{3,2,1,0:T(8,128)(2,1)S(1)}) custom-call(bf16[5,4,2048]{2,1,0:T(4,128)(2,1)S(1)} %shard_map.76.refs_0_, bf16[5,4,2048]{2,1,0:T(4,128)(2,1)S(1)} %collective-permute-done.3.refs_1_, bf16[5,4,2048]{2,1,0:T(4,128)(2,1)S(1)} %collective-permute-done.4.refs_2_, ...), custom_call_target="tpu_custom_call" | custom-call | flops 1048576 | bytes 1048576 | tf_op jit(solution)/shard_map/pallas_call | solution.py:285
  36.2 3.0 %collective-permute-start.10 = (bf16[2,128,2048]{2,1,0:T(8,128)(2,1)S(1)}, bf16[2,128,2048]{2,1,0:T(8,128)(2,1)S(1)}, u32[]{:S(2)}, u32[]{:S(2)}) collective-permute-start(bf16[2,128,2048]{2,1,0:T(8,128)(2,1)S(1)} %pad_maximum_fusion), channel_id=1, source_target_pairs={{0,1},{1,2},{2,3},{3,4},{4,5},{5,6},{6,7},{7,8},{8,9},{9,10},{10,1... | collective-permute-start | bytes 3145736 | tf_op jit(solution)/shard_map/ppermute | solution.py:384
  39.2 3.3 %collective-permute-start.13 = (bf16[2,2,16,2048]{3,2,1,0:T(8,128)(2,1)S(1)}, bf16[2,2,16,2048]{3,2,1,0:T(8,128)(2,1)S(1)}, u32[]{:S(2)}, u32[]{:S(2)}) collective-permute-start(bf16[2,2,16,2048]{3,2,1,0:T(8,128)(2,1)S(1)} %get-tuple-element.37.refs_7_), channel_id=1, source_target_pairs={{0,64},{32,96},{64,0},{96,32},{1,65},{33,97},{65,1},{97,33},{2,66}... | collective-permute-start | bytes 786440 | tf_op jit(solution)/shard_map/ppermute | solution.py:360
  42.5 1.1 collective-permute-start.12
  43.5 1.0 collective-permute-start.11
  44.5 5.4 %collective-permute-done.13.refs_10_ = bf16[2,2,16,2048]{3,2,1,0:T(8,128)(2,1)S(1)} collective-permute-done((bf16[2,2,16,2048]{3,2,1,0:T(8,128)(2,1)S(1)}, bf16[2,2,16,2048]{3,2,1,0:T(8,128)(2,1)S(1)}, u32[]{:S(2)}, u32[]{:S(2)}) %collective-permute-start.13) | collective-permute-done | bytes 262176 | tf_op jit(solution)/shard_map/ppermute | solution.py:360
  50.0 3.1 %collective-permute-done.12.refs_9_ = bf16[2,2,16,2048]{3,2,1,0:T(8,128)(2,1)S(1)} collective-permute-done((bf16[2,2,16,2048]{3,2,1,0:T(8,128)(2,1)S(1)}, bf16[2,2,16,2048]{3,2,1,0:T(8,128)(2,1)S(1)}, u32[]{:S(2)}, u32[]{:S(2)}) %collective-permute-start.12) | collective-permute-done | bytes 262176 | tf_op jit(solution)/shard_map/ppermute | solution.py:360
  53.1 0.5 collective-permute-start.15
  53.6 0.1 stack.32.place_ref
  53.6 1.1 collective-permute-done.16.refs_13_
  54.7 0.4 collective-permute-done.15.refs_12_
  55.1 5.7 %collective-permute-done.10.refs_4_ = bf16[2,128,2048]{2,1,0:T(8,128)(2,1)S(1)} collective-permute-done((bf16[2,128,2048]{2,1,0:T(8,128)(2,1)S(1)}, bf16[2,128,2048]{2,1,0:T(8,128)(2,1)S(1)}, u32[]{:S(2)}, u32[]{:S(2)}) %collective-permute-start.10) | collective-permute-done | bytes 1048608 | tf_op jit(solution)/shard_map/ppermute | solution.py:384
  60.8 0.9 copy-done.4
  61.7 17.1 %shard_map.78 = (bf16[256,2048]{1,0:T(8,128)(2,1)}, bf16[256,2048]{1,0:T(8,128)(2,1)}, bf16[256,2048]{1,0:T(8,128)(2,1)S(1)}, bf16[256,2048]{1,0:T(8,128)(2,1)S(...) custom-call(s32[5]{0:T(128)S(1)} %stack.32.place_ref, ...), custom_call_target="tpu_custom_call" | custom-call | flops 3623878656 | bytes 20971520 | tf_op jit(solution)/shard_map/pallas_call | solution.py:190
  78.8 0.1 collective-permute-start.19
  78.9 3.1 %collective-permute-start.18 = (bf16[2,128,2048]{2,1,0:T(8,128)(2,1)S(1)}, bf16[2,128,2048]{2,1,0:T(8,128)(2,1)S(1)}, u32[]{:S(2)}, u32[]{:S(2)}) collective-permute-start(bf16[2,128,2048]{2,1,0:T(8,128)(2,1)S(1)} %get-tuple-element.42), channel_id=1, source_target_pairs={{1,0},{2,1},{3,2},{4,3},{5,4},{6,5},{7,6},{8,7},{9,8},{10,9},{11,1... | collective-permute-start | bytes 3145736 | tf_op jit(solution)/shard_map/ppermute | solution.py:395
  82.0 0.3 fusion.2
  82.3 6.4 %collective-permute-start.20 = (bf16[2,2,16,2048]{3,2,1,0:T(8,128)(2,1)S(1)}, bf16[2,2,16,2048]{3,2,1,0:T(8,128)(2,1)S(1)}, u32[]{:S(2)}, u32[]{:S(2)}) collective-permute-start(bf16[2,2,16,2048]{3,2,1,0:T(8,128)(2,1)S(1)} %get-tuple-element.60), channel_id=1, source_target_pairs={{0,64},{32,96},{64,0},{96,32},{1,65},{33,97},{65,1},{97,33},{2,66}... | collective-permute-start | bytes 786440 | tf_op jit(solution)/shard_map/ppermute | solution.py:360
  88.7 1.0 collective-permute-start.22
  89.6 2.3 %collective-permute-start.21 = (bf16[2,2,16,2048]{3,2,1,0:T(8,128)(2,1)S(1)}, bf16[2,2,16,2048]{3,2,1,0:T(8,128)(2,1)S(1)}, u32[]{:S(2)}, u32[]{:S(2)}) collective-permute-start(bf16[2,2,16,2048]{3,2,1,0:T(8,128)(2,1)S(1)} %get-tuple-element.62), channel_id=1, source_target_pairs={{0,96},{32,0},{64,32},{96,64},{1,97},{33,1},{65,33},{97,65},{2,98}... | collective-permute-start | bytes 786440 | tf_op jit(solution)/shard_map/ppermute | solution.py:360
  91.9 3.9 %collective-permute-done.20 = bf16[2,2,16,2048]{3,2,1,0:T(8,128)(2,1)S(1)} collective-permute-done((bf16[2,2,16,2048]{3,2,1,0:T(8,128)(2,1)S(1)}, bf16[2,2,16,2048]{3,2,1,0:T(8,128)(2,1)S(1)}, u32[]{:S(2)}, u32[]{:S(2)}) %collective-permute-start.20) | collective-permute-done | bytes 262176 | tf_op jit(solution)/shard_map/ppermute | solution.py:360
  95.8 5.2 %collective-permute-done.22 = bf16[2,2,16,2048]{3,2,1,0:T(8,128)(2,1)S(1)} collective-permute-done((bf16[2,2,16,2048]{3,2,1,0:T(8,128)(2,1)S(1)}, bf16[2,2,16,2048]{3,2,1,0:T(8,128)(2,1)S(1)}, u32[]{:S(2)}, u32[]{:S(2)}) %collective-permute-start.22) | collective-permute-done | bytes 262176 | tf_op jit(solution)/shard_map/ppermute | solution.py:360
  101.0 0.7 collective-permute-done.21
  101.7 0.2 fusion.1.third_ref
  101.9 5.5 %collective-permute-done.18.back_ref = bf16[2,128,2048]{2,1,0:T(8,128)(2,1)S(1)} collective-permute-done((bf16[2,128,2048]{2,1,0:T(8,128)(2,1)S(1)}, bf16[2,128,2048]{2,1,0:T(8,128)(2,1)S(1)}, u32[]{:S(2)}, u32[]{:S(2)}) %collective-permute-start.18) | collective-permute-done | bytes 1048608 | tf_op jit(solution)/shard_map/ppermute | solution.py:395
  107.3 0.7 shard_map.79
  108.0 5.9 %collective-permute-start.23 = (bf16[5,4,2048]{2,1,0:T(4,128)(2,1)S(1)}, bf16[5,4,2048]{2,1,0:T(4,128)(2,1)S(1)}, u32[]{:S(2)}, u32[]{:S(2)}) collective-permute-start(bf16[5,4,2048]{2,1,0:T(4,128)(2,1)S(1)} %get-tuple-element.49), channel_id=1, source_target_pairs={{0,8},{2,10},{4,12},{6,14},{8,0},{10,2},{12,4},{14,6},{1,9},{3,11}... | collective-permute-start | bytes 245768 | tf_op jit(solution)/shard_map/ppermute | solution.py:360
  114.0 2.3 %collective-permute-start.24 = (bf16[5,4,2048]{2,1,0:T(4,128)(2,1)S(1)}, bf16[5,4,2048]{2,1,0:T(4,128)(2,1)S(1)}, u32[]{:S(2)}, u32[]{:S(2)}) collective-permute-start(bf16[5,4,2048]{2,1,0:T(4,128)(2,1)S(1)} %get-tuple-element.50), channel_id=1, source_target_pairs={{0,6},{2,8},{4,10},{6,12},{8,14},{10,0},{12,2},{14,4},{1,7},{3,9},... | collective-permute-start | bytes 245768 | tf_op jit(solution)/shard_map/ppermute | solution.py:360
  116.3 2.7 %collective-permute-start.25 = (bf16[5,4,2048]{2,1,0:T(4,128)(2,1)S(1)}, bf16[5,4,2048]{2,1,0:T(4,128)(2,1)S(1)}, u32[]{:S(2)}, u32[]{:S(2)}) collective-permute-start(bf16[5,4,2048]{2,1,0:T(4,128)(2,1)S(1)} %get-tuple-element.51), channel_id=1, source_target_pairs={{0,10},{2,12},{4,14},{6,0},{8,2},{10,4},{12,6},{14,8},{1,11},{3,13... | collective-permute-start | bytes 245768 | tf_op jit(solution)/shard_map/ppermute | solution.py:360
  119.0 0.8 collective-permute-start.26
  119.7 3.4 %collective-permute-start.27 = (bf16[5,4,2048]{2,1,0:T(4,128)(2,1)S(1)}, bf16[5,4,2048]{2,1,0:T(4,128)(2,1)S(1)}, u32[]{:S(2)}, u32[]{:S(2)}) collective-permute-start(bf16[5,4,2048]{2,1,0:T(4,128)(2,1)S(1)} %get-tuple-element.53), channel_id=1, source_target_pairs={{0,12},{2,14},{4,0},{6,2},{8,4},{10,6},{12,8},{14,10},{1,13},{3,15... | collective-permute-start | bytes 245768 | tf_op jit(solution)/shard_map/ppermute | solution.py:360
  123.1 4.2 %collective-permute-start.29 = (bf16[5,4,2048]{2,1,0:T(4,128)(2,1)S(1)}, bf16[5,4,2048]{2,1,0:T(4,128)(2,1)S(1)}, u32[]{:S(2)}, u32[]{:S(2)}) collective-permute-start(bf16[5,4,2048]{2,1,0:T(4,128)(2,1)S(1)} %get-tuple-element.55), channel_id=1, source_target_pairs={{0,14},{2,0},{4,2},{6,4},{8,6},{10,8},{12,10},{14,12},{1,15},{3,1}... | collective-permute-start | bytes 245768 | tf_op jit(solution)/shard_map/ppermute | solution.py:360
  127.4 0.3 collective-permute-done.26
  127.7 1.7 %collective-permute-done.27 = bf16[5,4,2048]{2,1,0:T(4,128)(2,1)S(1)} collective-permute-done((bf16[5,4,2048]{2,1,0:T(4,128)(2,1)S(1)}, bf16[5,4,2048]{2,1,0:T(4,128)(2,1)S(1)}, u32[]{:S(2)}, u32[]{:S(2)}) %collective-permute-start.27) | collective-permute-done | bytes 81952 | tf_op jit(solution)/shard_map/ppermute | solution.py:360
  129.3 0.1 collective-permute-done.29
  129.4 0.2 fusion.5
  129.7 3.8 %collective-permute-start.31 = (bf16[2,2048]{1,0:T(2,128)(2,1)S(1)}, bf16[2,2048]{1,0:T(2,128)(2,1)S(1)}, u32[]{:S(2)}, u32[]{:S(2)}) collective-permute-start(bf16[2,2048]{1,0:T(2,128)(2,1)S(1)} %bitcast.24), channel_id=1, source_target_pairs={{0,128},{128,0},{1,129},{129,1},{2,130},{130,2},{3,131},{131,3},{4... | collective-permute-start | bytes 24584 | tf_op jit(solution)/shard_map/ppermute | solution.py:360
  133.4 2.2 %collective-permute-start.32 = (bf16[2,2048]{1,0:T(2,128)(2,1)S(1)}, bf16[2,2048]{1,0:T(2,128)(2,1)S(1)}, u32[]{:S(2)}, u32[]{:S(2)}) collective-permute-start(bf16[2,2048]{1,0:T(2,128)(2,1)S(1)} %bitcast.23), channel_id=1, source_target_pairs={{0,129},{1,128},{128,1},{129,0},{2,131},{3,130},{130,3},{131,2},{4... | collective-permute-start | bytes 24584 | tf_op jit(solution)/shard_map/ppermute | solution.py:408
  135.7 0.1 collective-permute-start.30
  135.8 1.5 %collective-permute-done.32 = bf16[2,2048]{1,0:T(2,128)(2,1)S(1)} collective-permute-done((bf16[2,2048]{1,0:T(2,128)(2,1)S(1)}, bf16[2,2048]{1,0:T(2,128)(2,1)S(1)}, u32[]{:S(2)}, u32[]{:S(2)}) %collective-permute-start.32) | collective-permute-done | bytes 8224 | tf_op jit(solution)/shard_map/ppermute | solution.py:408
  137.3 2.4 %collective-permute-done.30 = bf16[2,4,2048]{2,1,0:T(4,128)(2,1)S(1)} collective-permute-done((bf16[2,4,2048]{2,1,0:T(4,128)(2,1)S(1)}, bf16[2,4,2048]{2,1,0:T(4,128)(2,1)S(1)}, u32[]{:S(2)}, u32[]{:S(2)}) %collective-permute-start.30) | collective-permute-done | bytes 32800 | tf_op jit(solution)/shard_map/ppermute | solution.py:360
  139.7 2.1 %shard_map.80 = (bf16[256,2048]{1,0:T(8,128)(2,1)}, bf16[256,2048]{1,0:T(8,128)(2,1)}) custom-call(bf16[256,2048]{1,0:T(8,128)(2,1)S(1)} %get-tuple-element.40.dk_ref, bf16[256,2048]{1,0:T(8,128)(2,1)S(1)} %get-tuple-element.41.dv_ref, bf16[2,128,2048]{2,1,0:T(8,128)(2,1)S(1)} %collective-permute-done.18.back_ref, f32[2,4,2048]{2,1,0:T(4,128)S(1)} %add_multiply_fusion.two_ref), custom_call_target="tpu_custom_call" | custom-call | flops 1048576 | bytes 7340032 | tf_op jit(solution)/shard_map/pallas_call | solution.py:344
  (37 shorter events, 0.2 us)
Async XLA Ops:
  0.6 1.2 copy-start
  1.9 1.2 copy-start.2
  3.1 16.0 %copy-start.1 = (bf16[256,2048]{1,0:T(8,128)(2,1)S(1)}, bf16[256,2048]{1,0:T(8,128)(2,1)}, u32[]{:S(2)}) copy-start(bf16[256,2048]{1,0:T(8,128)(2,1)} %refs_1_.1) | copy-start | bytes 3145732
  3.9 7.9 %collective-permute-start = (bf16[2,4,2048]{2,1,0:T(4,128)(2,1)S(1)}, bf16[2,4,2048]{2,1,0:T(4,128)(2,1)S(1)}, u32[]{:S(2)}, u32[]{:S(2)}) collective-permute-start(bf16[2,4,2048]{2,1,0:T(4,128)(2,1)S(1)} %get-tuple-element.31.mine_ref), channel_id=1, source_target_pairs={{0,1},{1,0},{2,3},{3,2},{4,5},{5,4},{6,7},{7,6},{8,9},{9,8},{10,11... | collective-permute-start | bytes 98312 | tf_op jit(solution)/shard_map/ppermute | solution.py:360
  6.2 3.7 %collective-permute-start.2 = (bf16[2,2048]{1,0:T(2,128)(2,1)S(1)}, bf16[2,2048]{1,0:T(2,128)(2,1)S(1)}, u32[]{:S(2)}, u32[]{:S(2)}) collective-permute-start(bf16[2,2048]{1,0:T(2,128)(2,1)S(1)} %get-tuple-element.32), channel_id=1, source_target_pairs={{0,129},{1,128},{128,1},{129,0},{2,131},{3,130},{130,3},{131,2},{4... | collective-permute-start | bytes 24584 | tf_op jit(solution)/shard_map/ppermute | solution.py:377
  6.6 5.2 %collective-permute-start.1 = (bf16[2,2048]{1,0:T(2,128)(2,1)S(1)}, bf16[2,2048]{1,0:T(2,128)(2,1)S(1)}, u32[]{:S(2)}, u32[]{:S(2)}) collective-permute-start(bf16[2,2048]{1,0:T(2,128)(2,1)S(1)} %get-tuple-element.32), channel_id=1, source_target_pairs={{0,128},{128,0},{1,129},{129,1},{2,130},{130,2},{3,131},{131,3},{4... | collective-permute-start | bytes 24584 | tf_op jit(solution)/shard_map/ppermute | solution.py:360
  11.8 14.2 %collective-permute-start.9 = (bf16[5,4,2048]{2,1,0:T(4,128)(2,1)S(1)}, bf16[5,4,2048]{2,1,0:T(4,128)(2,1)S(1)}, u32[]{:S(2)}, u32[]{:S(2)}) collective-permute-start(bf16[5,4,2048]{2,1,0:T(4,128)(2,1)S(1)} %shard_map.76.refs_0_), channel_id=1, source_target_pairs={{0,8},{2,10},{4,12},{6,14},{8,0},{10,2},{12,4},{14,6},{1,9},{3,11}... | collective-permute-start | bytes 245768 | tf_op jit(solution)/shard_map/ppermute | solution.py:360
  19.1 10.0 %collective-permute-start.8 = (bf16[5,4,2048]{2,1,0:T(4,128)(2,1)S(1)}, bf16[5,4,2048]{2,1,0:T(4,128)(2,1)S(1)}, u32[]{:S(2)}, u32[]{:S(2)}) collective-permute-start(bf16[5,4,2048]{2,1,0:T(4,128)(2,1)S(1)} %shard_map.76.refs_0_), channel_id=1, source_target_pairs={{0,10},{2,12},{4,14},{6,0},{8,2},{10,4},{12,6},{14,8},{1,11},{3,13... | collective-permute-start | bytes 245768 | tf_op jit(solution)/shard_map/ppermute | solution.py:360
  19.2 11.5 %collective-permute-start.7 = (bf16[5,4,2048]{2,1,0:T(4,128)(2,1)S(1)}, bf16[5,4,2048]{2,1,0:T(4,128)(2,1)S(1)}, u32[]{:S(2)}, u32[]{:S(2)}) collective-permute-start(bf16[5,4,2048]{2,1,0:T(4,128)(2,1)S(1)} %shard_map.76.refs_0_), channel_id=1, source_target_pairs={{0,6},{2,8},{4,10},{6,12},{8,14},{10,0},{12,2},{14,4},{1,7},{3,9},... | collective-permute-start | bytes 245768 | tf_op jit(solution)/shard_map/ppermute | solution.py:360
  23.1 8.8 %collective-permute-start.6 = (bf16[5,4,2048]{2,1,0:T(4,128)(2,1)S(1)}, bf16[5,4,2048]{2,1,0:T(4,128)(2,1)S(1)}, u32[]{:S(2)}, u32[]{:S(2)}) collective-permute-start(bf16[5,4,2048]{2,1,0:T(4,128)(2,1)S(1)} %shard_map.76.refs_0_), channel_id=1, source_target_pairs={{0,12},{2,14},{4,0},{6,2},{8,4},{10,6},{12,8},{14,10},{1,13},{3,15... | collective-permute-start | bytes 245768 | tf_op jit(solution)/shard_map/ppermute | solution.py:360
  24.0 8.3 %collective-permute-start.5 = (bf16[5,4,2048]{2,1,0:T(4,128)(2,1)S(1)}, bf16[5,4,2048]{2,1,0:T(4,128)(2,1)S(1)}, u32[]{:S(2)}, u32[]{:S(2)}) collective-permute-start(bf16[5,4,2048]{2,1,0:T(4,128)(2,1)S(1)} %shard_map.76.refs_0_), channel_id=1, source_target_pairs={{0,4},{2,6},{4,8},{6,10},{8,12},{10,14},{12,0},{14,2},{1,5},{3,7},... | collective-permute-start | bytes 245768 | tf_op jit(solution)/shard_map/ppermute | solution.py:360
  26.0 6.9 %collective-permute-start.4 = (bf16[5,4,2048]{2,1,0:T(4,128)(2,1)S(1)}, bf16[5,4,2048]{2,1,0:T(4,128)(2,1)S(1)}, u32[]{:S(2)}, u32[]{:S(2)}) collective-permute-start(bf16[5,4,2048]{2,1,0:T(4,128)(2,1)S(1)} %shard_map.76.refs_0_), channel_id=1, source_target_pairs={{0,14},{2,0},{4,2},{6,4},{8,6},{10,8},{12,10},{14,12},{1,15},{3,1}... | collective-permute-start | bytes 245768 | tf_op jit(solution)/shard_map/ppermute | solution.py:360
  29.1 5.7 %collective-permute-start.3 = (bf16[5,4,2048]{2,1,0:T(4,128)(2,1)S(1)}, bf16[5,4,2048]{2,1,0:T(4,128)(2,1)S(1)}, u32[]{:S(2)}, u32[]{:S(2)}) collective-permute-start(bf16[5,4,2048]{2,1,0:T(4,128)(2,1)S(1)} %shard_map.76.refs_0_), channel_id=1, source_target_pairs={{0,2},{2,4},{4,6},{6,8},{8,10},{10,12},{12,14},{14,0},{1,3},{3,5},... | collective-permute-start | bytes 245768 | tf_op jit(solution)/shard_map/ppermute | solution.py:360
  36.2 24.5 %copy-start.3 = (bf16[2,2,16,2048]{3,2,1,0:T(8,128)(2,1)}, bf16[2,2,16,2048]{3,2,1,0:T(8,128)(2,1)S(1)}, u32[]{:S(2)}) copy-start(bf16[2,2,16,2048]{3,2,1,0:T(8,128)(2,1)S(1)} %get-tuple-element.37.refs_7_) | copy-start | bytes 786436
  36.2 24.5 %collective-permute-start.10 = (bf16[2,128,2048]{2,1,0:T(8,128)(2,1)S(1)}, bf16[2,128,2048]{2,1,0:T(8,128)(2,1)S(1)}, u32[]{:S(2)}, u32[]{:S(2)}) collective-permute-start(bf16[2,128,2048]{2,1,0:T(8,128)(2,1)S(1)} %pad_maximum_fusion), channel_id=1, source_target_pairs={{0,1},{1,2},{2,3},{3,4},{4,5},{5,6},{6,7},{7,8},{8,9},{9,10},{10,1... | collective-permute-start | bytes 3145736 | tf_op jit(solution)/shard_map/ppermute | solution.py:384
  39.2 10.8 %collective-permute-start.13 = (bf16[2,2,16,2048]{3,2,1,0:T(8,128)(2,1)S(1)}, bf16[2,2,16,2048]{3,2,1,0:T(8,128)(2,1)S(1)}, u32[]{:S(2)}, u32[]{:S(2)}) collective-permute-start(bf16[2,2,16,2048]{3,2,1,0:T(8,128)(2,1)S(1)} %get-tuple-element.37.refs_7_), channel_id=1, source_target_pairs={{0,64},{32,96},{64,0},{96,32},{1,65},{33,97},{65,1},{97,33},{2,66}... | collective-permute-start | bytes 786440 | tf_op jit(solution)/shard_map/ppermute | solution.py:360
  42.5 10.6 %collective-permute-start.12 = (bf16[2,2,16,2048]{3,2,1,0:T(8,128)(2,1)S(1)}, bf16[2,2,16,2048]{3,2,1,0:T(8,128)(2,1)S(1)}, u32[]{:S(2)}, u32[]{:S(2)}) collective-permute-start(bf16[2,2,16,2048]{3,2,1,0:T(8,128)(2,1)S(1)} %get-tuple-element.37.refs_7_), channel_id=1, source_target_pairs={{0,96},{32,0},{64,32},{96,64},{1,97},{33,1},{65,33},{97,65},{2,98}... | collective-permute-start | bytes 786440 | tf_op jit(solution)/shard_map/ppermute | solution.py:360
  43.5 9.5 %collective-permute-start.11 = (bf16[2,2,16,2048]{3,2,1,0:T(8,128)(2,1)S(1)}, bf16[2,2,16,2048]{3,2,1,0:T(8,128)(2,1)S(1)}, u32[]{:S(2)}, u32[]{:S(2)}) collective-permute-start(bf16[2,2,16,2048]{3,2,1,0:T(8,128)(2,1)S(1)} %get-tuple-element.37.refs_7_), channel_id=1, source_target_pairs={{0,32},{32,64},{64,96},{96,0},{1,33},{33,65},{65,97},{97,1},{2,34}... | collective-permute-start | bytes 786440 | tf_op jit(solution)/shard_map/ppermute | solution.py:360
  44.5 9.1 %collective-permute-start.14 = (bf16[2,2,16,2048]{3,2,1,0:T(8,128)(2,1)S(1)}, bf16[2,2,16,2048]{3,2,1,0:T(8,128)(2,1)S(1)}, u32[]{:S(2)}, u32[]{:S(2)}) collective-permute-start(bf16[2,2,16,2048]{3,2,1,0:T(8,128)(2,1)S(1)} %get-tuple-element.37.refs_7_), channel_id=1, source_target_pairs={{0,16},{16,0},{1,17},{17,1},{2,18},{18,2},{3,19},{19,3},{4,20},{20... | collective-permute-start | bytes 786440 | tf_op jit(solution)/shard_map/ppermute | solution.py:360
  49.9 10.8 %copy-start.5 = (bf16[2,2,16,2048]{3,2,1,0:T(8,128)(2,1)}, bf16[2,2,16,2048]{3,2,1,0:T(8,128)(2,1)S(1)}, u32[]{:S(2)}) copy-start(bf16[2,2,16,2048]{3,2,1,0:T(8,128)(2,1)S(1)} %collective-permute-done.13.refs_10_) | copy-start | bytes 786436
  49.9 3.7 %collective-permute-start.17 = (bf16[2,2,16,2048]{3,2,1,0:T(8,128)(2,1)S(1)}, bf16[2,2,16,2048]{3,2,1,0:T(8,128)(2,1)}, u32[]{:S(2)}, u32[]{:S(2)}) collective-permute-start(bf16[2,2,16,2048]{3,2,1,0:T(8,128)(2,1)S(1)} %collective-permute-done.13.refs_10_), channel_id=1, source_target_pairs={{0,16},{16,0},{1,17},{17,1},{2,18},{18,2},{3,19},{19,3},{4,20},{20... | collective-permute-start | bytes 786440 | tf_op jit(solution)/shard_map/ppermute | solution.py:360
  53.0 7.7 %copy-start.6 = (bf16[2,2,16,2048]{3,2,1,0:T(8,128)(2,1)}, bf16[2,2,16,2048]{3,2,1,0:T(8,128)(2,1)S(1)}, u32[]{:S(2)}) copy-start(bf16[2,2,16,2048]{3,2,1,0:T(8,128)(2,1)S(1)} %collective-permute-done.12.refs_9_) | copy-start | bytes 786436
  53.0 1.7 %collective-permute-start.16 = (bf16[2,2,16,2048]{3,2,1,0:T(8,128)(2,1)S(1)}, bf16[2,2,16,2048]{3,2,1,0:T(8,128)(2,1)}, u32[]{:S(2)}, u32[]{:S(2)}) collective-permute-start(bf16[2,2,16,2048]{3,2,1,0:T(8,128)(2,1)S(1)} %collective-permute-done.12.refs_9_), channel_id=1, source_target_pairs={{0,16},{16,0},{1,17},{17,1},{2,18},{18,2},{3,19},{19,3},{4,20},{20... | collective-permute-start | bytes 786440 | tf_op jit(solution)/shard_map/ppermute | solution.py:360
  53.0 7.7 %copy-start.7 = (bf16[2,2,16,2048]{3,2,1,0:T(8,128)(2,1)}, bf16[2,2,16,2048]{3,2,1,0:T(8,128)(2,1)S(1)}, u32[]{:S(2)}) copy-start(bf16[2,2,16,2048]{3,2,1,0:T(8,128)(2,1)S(1)} %collective-permute-done.11.refs_8_) | copy-start | bytes 786436
  53.1 2.0 %collective-permute-start.15 = (bf16[2,2,16,2048]{3,2,1,0:T(8,128)(2,1)S(1)}, bf16[2,2,16,2048]{3,2,1,0:T(8,128)(2,1)}, u32[]{:S(2)}, u32[]{:S(2)}) collective-permute-start(bf16[2,2,16,2048]{3,2,1,0:T(8,128)(2,1)S(1)} %collective-permute-done.11.refs_8_), channel_id=1, source_target_pairs={{0,16},{16,0},{1,17},{17,1},{2,18},{18,2},{3,19},{19,3},{4,20},{20... | collective-permute-start | bytes 786440 | tf_op jit(solution)/shard_map/ppermute | solution.py:360
  53.6 7.1 %copy-start.8 = (bf16[2,2,16,2048]{3,2,1,0:T(8,128)(2,1)}, bf16[2,2,16,2048]{3,2,1,0:T(8,128)(2,1)S(1)}, u32[]{:S(2)}) copy-start(bf16[2,2,16,2048]{3,2,1,0:T(8,128)(2,1)S(1)} %collective-permute-done.14.refs_11_) | copy-start | bytes 786436
  60.7 1.0 copy-start.4
  78.8 3.2 %collective-permute-start.19 = (bf16[4,2,2,16,2048]{4,3,2,1,0:T(8,128)(2,1)S(1)}, bf16[4,2,2,16,2048]{4,3,2,1,0:T(8,128)(2,1)S(1)}, u32[]{:S(2)}, u32[]{:S(2)}) collective-permute-start(bf16[4,2,2,16,2048]{4,3,2,1,0:T(8,128)(2,1)S(1)} %get-tuple-element.44), channel_id=1, source_target_pairs={{0,16},{16,0},{1,17},{17,1},{2,18},{18,2},{3,19},{19,3},{4,20},{20... | collective-permute-start | bytes 3145736 | tf_op jit(solution)/shard_map/ppermute | solution.py:360
  78.9 28.4 %collective-permute-start.18 = (bf16[2,128,2048]{2,1,0:T(8,128)(2,1)S(1)}, bf16[2,128,2048]{2,1,0:T(8,128)(2,1)S(1)}, u32[]{:S(2)}, u32[]{:S(2)}) collective-permute-start(bf16[2,128,2048]{2,1,0:T(8,128)(2,1)S(1)} %get-tuple-element.42), channel_id=1, source_target_pairs={{1,0},{2,1},{3,2},{4,3},{5,4},{6,5},{7,6},{8,7},{9,8},{10,9},{11,1... | collective-permute-start | bytes 3145736 | tf_op jit(solution)/shard_map/ppermute | solution.py:395
  82.3 13.5 %collective-permute-start.20 = (bf16[2,2,16,2048]{3,2,1,0:T(8,128)(2,1)S(1)}, bf16[2,2,16,2048]{3,2,1,0:T(8,128)(2,1)S(1)}, u32[]{:S(2)}, u32[]{:S(2)}) collective-permute-start(bf16[2,2,16,2048]{3,2,1,0:T(8,128)(2,1)S(1)} %get-tuple-element.60), channel_id=1, source_target_pairs={{0,64},{32,96},{64,0},{96,32},{1,65},{33,97},{65,1},{97,33},{2,66}... | collective-permute-start | bytes 786440 | tf_op jit(solution)/shard_map/ppermute | solution.py:360
  88.7 12.3 %collective-permute-start.22 = (bf16[2,2,16,2048]{3,2,1,0:T(8,128)(2,1)S(1)}, bf16[2,2,16,2048]{3,2,1,0:T(8,128)(2,1)S(1)}, u32[]{:S(2)}, u32[]{:S(2)}) collective-permute-start(bf16[2,2,16,2048]{3,2,1,0:T(8,128)(2,1)S(1)} %get-tuple-element.61), channel_id=1, source_target_pairs={{0,32},{32,64},{64,96},{96,0},{1,33},{33,65},{65,97},{97,1},{2,34}... | collective-permute-start | bytes 786440 | tf_op jit(solution)/shard_map/ppermute | solution.py:360
  89.6 12.1 %collective-permute-start.21 = (bf16[2,2,16,2048]{3,2,1,0:T(8,128)(2,1)S(1)}, bf16[2,2,16,2048]{3,2,1,0:T(8,128)(2,1)S(1)}, u32[]{:S(2)}, u32[]{:S(2)}) collective-permute-start(bf16[2,2,16,2048]{3,2,1,0:T(8,128)(2,1)S(1)} %get-tuple-element.62), channel_id=1, source_target_pairs={{0,96},{32,0},{64,32},{96,64},{1,97},{33,1},{65,33},{97,65},{2,98}... | collective-permute-start | bytes 786440 | tf_op jit(solution)/shard_map/ppermute | solution.py:360
  108.0 15.1 %collective-permute-start.23 = (bf16[5,4,2048]{2,1,0:T(4,128)(2,1)S(1)}, bf16[5,4,2048]{2,1,0:T(4,128)(2,1)S(1)}, u32[]{:S(2)}, u32[]{:S(2)}) collective-permute-start(bf16[5,4,2048]{2,1,0:T(4,128)(2,1)S(1)} %get-tuple-element.49), channel_id=1, source_target_pairs={{0,8},{2,10},{4,12},{6,14},{8,0},{10,2},{12,4},{14,6},{1,9},{3,11}... | collective-permute-start | bytes 245768 | tf_op jit(solution)/shard_map/ppermute | solution.py:360
  114.0 9.2 %collective-permute-start.24 = (bf16[5,4,2048]{2,1,0:T(4,128)(2,1)S(1)}, bf16[5,4,2048]{2,1,0:T(4,128)(2,1)S(1)}, u32[]{:S(2)}, u32[]{:S(2)}) collective-permute-start(bf16[5,4,2048]{2,1,0:T(4,128)(2,1)S(1)} %get-tuple-element.50), channel_id=1, source_target_pairs={{0,6},{2,8},{4,10},{6,12},{8,14},{10,0},{12,2},{14,4},{1,7},{3,9},... | collective-permute-start | bytes 245768 | tf_op jit(solution)/shard_map/ppermute | solution.py:360
  116.3 11.1 %collective-permute-start.25 = (bf16[5,4,2048]{2,1,0:T(4,128)(2,1)S(1)}, bf16[5,4,2048]{2,1,0:T(4,128)(2,1)S(1)}, u32[]{:S(2)}, u32[]{:S(2)}) collective-permute-start(bf16[5,4,2048]{2,1,0:T(4,128)(2,1)S(1)} %get-tuple-element.51), channel_id=1, source_target_pairs={{0,10},{2,12},{4,14},{6,0},{8,2},{10,4},{12,6},{14,8},{1,11},{3,13... | collective-permute-start | bytes 245768 | tf_op jit(solution)/shard_map/ppermute | solution.py:360
  119.0 8.7 %collective-permute-start.26 = (bf16[5,4,2048]{2,1,0:T(4,128)(2,1)S(1)}, bf16[5,4,2048]{2,1,0:T(4,128)(2,1)S(1)}, u32[]{:S(2)}, u32[]{:S(2)}) collective-permute-start(bf16[5,4,2048]{2,1,0:T(4,128)(2,1)S(1)} %get-tuple-element.52), channel_id=1, source_target_pairs={{0,4},{2,6},{4,8},{6,10},{8,12},{10,14},{12,0},{14,2},{1,5},{3,7},... | collective-permute-start | bytes 245768 | tf_op jit(solution)/shard_map/ppermute | solution.py:360
  119.7 9.6 %collective-permute-start.27 = (bf16[5,4,2048]{2,1,0:T(4,128)(2,1)S(1)}, bf16[5,4,2048]{2,1,0:T(4,128)(2,1)S(1)}, u32[]{:S(2)}, u32[]{:S(2)}) collective-permute-start(bf16[5,4,2048]{2,1,0:T(4,128)(2,1)S(1)} %get-tuple-element.53), channel_id=1, source_target_pairs={{0,12},{2,14},{4,0},{6,2},{8,4},{10,6},{12,8},{14,10},{1,13},{3,15... | collective-permute-start | bytes 245768 | tf_op jit(solution)/shard_map/ppermute | solution.py:360
  123.1 6.2 %collective-permute-start.28 = (bf16[5,4,2048]{2,1,0:T(4,128)(2,1)S(1)}, bf16[5,4,2048]{2,1,0:T(4,128)(2,1)S(1)}, u32[]{:S(2)}, u32[]{:S(2)}) collective-permute-start(bf16[5,4,2048]{2,1,0:T(4,128)(2,1)S(1)} %get-tuple-element.54), channel_id=1, source_target_pairs={{0,2},{2,4},{4,6},{6,8},{8,10},{10,12},{12,14},{14,0},{1,3},{3,5},... | collective-permute-start | bytes 245768 | tf_op jit(solution)/shard_map/ppermute | solution.py:360
  123.1 6.3 %collective-permute-start.29 = (bf16[5,4,2048]{2,1,0:T(4,128)(2,1)S(1)}, bf16[5,4,2048]{2,1,0:T(4,128)(2,1)S(1)}, u32[]{:S(2)}, u32[]{:S(2)}) collective-permute-start(bf16[5,4,2048]{2,1,0:T(4,128)(2,1)S(1)} %get-tuple-element.55), channel_id=1, source_target_pairs={{0,14},{2,0},{4,2},{6,4},{8,6},{10,8},{12,10},{14,12},{1,15},{3,1}... | collective-permute-start | bytes 245768 | tf_op jit(solution)/shard_map/ppermute | solution.py:360
  129.7 6.1 %collective-permute-start.31 = (bf16[2,2048]{1,0:T(2,128)(2,1)S(1)}, bf16[2,2048]{1,0:T(2,128)(2,1)S(1)}, u32[]{:S(2)}, u32[]{:S(2)}) collective-permute-start(bf16[2,2048]{1,0:T(2,128)(2,1)S(1)} %bitcast.24), channel_id=1, source_target_pairs={{0,128},{128,0},{1,129},{129,1},{2,130},{130,2},{3,131},{131,3},{4... | collective-permute-start | bytes 24584 | tf_op jit(solution)/shard_map/ppermute | solution.py:360
  133.4 3.8 %collective-permute-start.32 = (bf16[2,2048]{1,0:T(2,128)(2,1)S(1)}, bf16[2,2048]{1,0:T(2,128)(2,1)S(1)}, u32[]{:S(2)}, u32[]{:S(2)}) collective-permute-start(bf16[2,2048]{1,0:T(2,128)(2,1)S(1)} %bitcast.23), channel_id=1, source_target_pairs={{0,129},{1,128},{128,1},{129,0},{2,131},{3,130},{130,3},{131,2},{4... | collective-permute-start | bytes 24584 | tf_op jit(solution)/shard_map/ppermute | solution.py:408
  135.7 4.0 %collective-permute-start.30 = (bf16[2,4,2048]{2,1,0:T(4,128)(2,1)S(1)}, bf16[2,4,2048]{2,1,0:T(4,128)(2,1)S(1)}, u32[]{:S(2)}, u32[]{:S(2)}) collective-permute-start(bf16[2,4,2048]{2,1,0:T(4,128)(2,1)S(1)} %slice.56), channel_id=1, source_target_pairs={{0,1},{1,0},{2,3},{3,2},{4,5},{5,4},{6,7},{7,6},{8,9},{9,8},{10,11... | collective-permute-start | bytes 98312 | tf_op jit(solution)/shard_map/ppermute | solution.py:360

commit v4 on v3

--- a/solution.py
+++ b/solution.py
@@ -44,7 +44,7 @@
 def one_head(bias_ref, seg, refs, outs):
     q_ref, k_ref, v_ref, g_ref, prior_ref, pk2_ref, pv2_ref = refs[:7]
     thirds = refs[7:]
-    att_ref, dq_ref, dk_ref, dv_ref, dprior_ref, g2_ref, near_ref, far_ref = outs
+    att_ref, dq_ref, dk_ref, dv_ref, g2_ref, near_ref, far_ref, dprior_ref = outs
     q = q_ref[:, seg]
     k = k_ref[:, seg]
     v = v_ref[:, seg]
@@ -173,48 +173,55 @@
 
     for h in range(HPB):
         seg = slice(h * HDIM, (h + 1) * HDIM)
-        one_head(bias_ref, seg, refs[:15], refs[15:23])
-
-
-def cols(width, *lead):
+        one_head(bias_ref, seg, refs[:15], refs[-9:-1])
+
+
+def cols(width, *lead, at=0):
     zeros = (0,) * len(lead)
-    return pl.BlockSpec(lead + (width,), lambda i: zeros + (i,))
-
-
-def attention(place, q, k, v, g, prior, pk2, pv2, thirds):
+    return pl.BlockSpec(lead + (width,), lambda i: zeros + (i + at,))
+
+
+def attention(half, place, q, k, v, g, prior, pk2, pv2, thirds, earlier):
     width = HPB * HDIM
     rows = q.shape[0]
+    steps = FEAT // width // 2
+    at = half * steps
     shape = jax.ShapeDtypeStruct
-    row_spec = cols(width, rows)
-    sums_spec = cols(width, NY, NXH, 2, N3G)
+    row_spec = cols(width, rows, at=at)
+    sums_spec = cols(width, NY, NXH, 2, N3G, at=at)
+    prior_spec = cols(width, 2, BLK)
+    first_alias = 8 + len(thirds)
     return pl.pallas_call(
         attn_kernel,
-        grid=(FEAT // width,),
+        grid=(steps,),
         in_specs=[
             pl.BlockSpec(memory_space=pltpu.SMEM),
             row_spec, row_spec, row_spec, row_spec,
-            cols(width, 2, BLK), cols(width, N2), cols(width, N2),
-        ] + [cols(width, NXH, 2, N3G)] * 8,
+            prior_spec, cols(width, N2, at=at), cols(width, N2, at=at),
+        ]
+        + [cols(width, NXH, 2, N3G, at=at)] * len(thirds)
+        + [pl.BlockSpec(memory_space=pl.ANY)] * len(earlier),
         out_specs=[
             row_spec, row_spec, row_spec, row_spec,
-            cols(width, 2, BLK), cols(width, NZ, 2, 8), sums_spec, sums_spec,
+            cols(width, NZ, 2, 8, at=at), sums_spec, sums_spec, prior_spec,
         ],
         out_shape=[
             shape((rows, FEAT), jnp.bfloat16),
             shape((rows, FEAT), jnp.bfloat16),
             shape((rows, FEAT), jnp.bfloat16),
             shape((rows, FEAT), jnp.bfloat16),
-            shape((2, BLK, FEAT), jnp.bfloat16),
             shape((NZ, 2, 8, FEAT), jnp.float32),
             shape((NY, NXH, 2, N3G, FEAT), jnp.bfloat16),
             shape((NY, NXH, 2, N3G, FEAT), jnp.bfloat16),
+            shape((2, BLK, FEAT // 2), jnp.bfloat16),
         ],
         scratch_shapes=[pltpu.VMEM((BLK + NP, 2 * BLK), jnp.float32)],
+        input_output_aliases={first_alias + i: i for i in range(len(earlier))},
         compiler_params=pltpu.CompilerParams(vmem_limit_bytes=24 * 1024 * 1024),
         cost_estimate=pl.CostEstimate(
-            flops=6 * 2 * 2 * BLK * 576 * FEAT, bytes_accessed=20 << 20, transcendentals=0
+            flops=6 * 2 * BLK * 576 * FEAT, bytes_accessed=10 << 20, transcendentals=0
         ),
-    )(place, q, k, v, g, prior, pk2, pv2, *thirds)
+    )(place, q, k, v, g, prior, pk2, pv2, *thirds, *earlier)
 
 
 def pool_kernel(k_ref, v_ref, pooled_ref, third_ref):
@@ -325,7 +332,8 @@
     )(g2, third)
 
 
-def finish_kernel(dk_ref, dv_ref, back_ref, two_ref, gk_ref, gv_ref):
+def finish_kernel(dk_ref, dv_ref, lo_ref, hi_ref, two_ref, gk_ref, gv_ref):
+    low = pl.program_id(0) < pl.num_programs(0) // 2
     for kv, src, dst in ((0, dk_ref, gk_ref), (1, dv_ref, gv_ref)):
         for part in range(4):
             lo = part * P2
@@ -333,23 +341,29 @@
             val = src[lo : lo + P2, :].astype(jnp.float32) + spread
             if part >= 2:
                 rows = slice(lo - BLK, lo - BLK + P2)
-                val = val + back_ref[kv, rows, :].astype(jnp.float32)
+                back = jnp.where(low, lo_ref[kv, rows, :], hi_ref[kv, rows, :])
+                val = val + back.astype(jnp.float32)
             dst[lo : lo + P2, :] = val.astype(jnp.bfloat16)
 
 
-def finish(dk, dv, back, two):
+def finish(dk, dv, back_lo, back_hi, two):
     rows = dk.shape[0]
     width = 512
+    half = FEAT // width // 2
     shape = jax.ShapeDtypeStruct
     return pl.pallas_call(
         finish_kernel,
         grid=(FEAT // width,),
-        in_specs=[cols(width, rows)] * 2 + [cols(width, 2, BLK), cols(width, 2, 4)],
+        in_specs=[cols(width, rows)] * 2 + [
+            pl.BlockSpec((2, BLK, width), lambda i: (0, 0, jnp.minimum(i, half - 1))),
+            pl.BlockSpec((2, BLK, width), lambda i: (0, 0, jnp.maximum(i - half, 0))),
+            cols(width, 2, 4),
+        ],
         out_specs=[cols(width, rows)] * 2,
         out_shape=[shape((rows, FEAT), jnp.bfloat16)] * 2,
         compiler_params=pltpu.CompilerParams(vmem_limit_bytes=48 * 1024 * 1024),
         cost_estimate=pl.CostEstimate(flops=1 << 20, bytes_accessed=7 << 20, transcendentals=0),
-    )(dk, dv, back, two)
+    )(dk, dv, back_lo, back_hi, two)
 
 
 def in_hbm(*values):
@@ -378,28 +392,33 @@
     pair = joined(pooled, other, near_own, far_own)
     pieces = [pair] + [ring(pair, "z", NZ, s) for s in Z_ORDER[::-1]]
     pk2, pv2, third = gathered(pieces)
-    last = jnp.stack([keys[BLK:], values[BLK:]])
-    last, third = lax.optimization_barrier((last, third))
+    mid = FEAT // 2
+    lasts = [
+        jnp.stack([keys[BLK:, lo : lo + mid], values[BLK:, lo : lo + mid]]) for lo in (0, mid)
+    ]
+    *lasts, third = lax.optimization_barrier((*lasts, third))
     count = NXH * NY * NC * NZ * NXL
-    prior = lax.ppermute(last, AXES, [(i, i + 1) for i in range(count - 1)])
+    priors = [lax.ppermute(x, AXES, [(i, i + 1) for i in range(count - 1)]) for x in lasts]
     thirds = [third] + [ring(third, "y", NY, s) for s in Y_STEP[1:]]
     thirds = thirds + [ring(t, "c", NC, 1) for t in thirds]
 
     place = jnp.stack([xh, y, c, z, xl]).astype(jnp.int32)
 
-    attended, grad_q, dk, dv, dprior, g2, near, far = attention(
-        place, *in_hbm(queries, keys, values, grad_out, prior, pk2, pv2), in_hbm(*thirds)
-    )
-
-    count = NXH * NY * NC * NZ * NXL
-    back = lax.ppermute(dprior, AXES, [(i + 1, i) for i in range(count - 1)])
-
+    fixed = in_hbm(queries, keys, values, grad_out)
+    pools = (*in_hbm(pk2, pv2), in_hbm(*thirds))
+    outs, backs = [], []
+    for half in range(2):
+        *outs, dprior = attention(half, place, *fixed, *in_hbm(priors[half]), *pools, outs)
+        backs.append(lax.ppermute(dprior, AXES, [(i + 1, i) for i in range(count - 1)]))
+    attended, grad_q, dk, dv, g2, near, far = outs
+
+    backs[0], far = lax.optimization_barrier((backs[0], far))
     far = ring(far, "c", NC, 1)
     s3 = [f32(near[s]) + f32(far[s]) for s in range(NY)]
     t3 = s3[0]
     for s in (3, 1, 2):
         t3 = t3 + f32(ring(bf(s3[s]), "y", NY, -Y_STEP[s]))
-    back, t3 = lax.optimization_barrier((back, t3))
+    *backs, t3 = lax.optimization_barrier((*backs, t3))
     parts = lifted(g2, t3)
     two = parts[0]
     for s in Z_ORDER:
@@ -411,7 +430,7 @@
     two = two[0:4:2] + f32(ring(bf(two[1:4:2]), "xl", NXL, 1))
     two = two + 0.5 * (f32(near_third) + f32(far_third))[:, None, :]
     two = two / math.sqrt(P2)
-    grad_k, grad_v = finish(dk, dv, back, two)
+    grad_k, grad_v = finish(dk, dv, *backs, two)
     return attended, grad_q, grad_k, grad_v
 
 

time: 142 us -> 140 us (0.986); the launches traced: 142 us -> 138 us
  waiting for transfers between devices: 45 us -> 35.1 us
  starting transfers between devices: 69.5 us -> 72 us
  Pallas kernels: 22.1 us -> 24.3 us
    ppermute x2 -> x4, starting transfers between devices: 6.05 us -> 13.5 us  [the longest x2 7.53 us: per_device(): lax.ppermute(x, AXES, [(i, i + 1) for i in range(count - 1)])]
    ppermute x29, waiting for transfers between devices: 30.9 us -> 24.3 us  [ring(): lax.ppermute(value, axis, [(i, (i + step) % size) for i in range(size)])]
    ppermute x29, starting transfers between devices: 60.9 us -> 55.5 us  [ring(): lax.ppermute(value, axis, [(i, (i + step) % size) for i in range(size)])]
    pallas_call x1 -> x2, Pallas kernels: 17.1 us -> 19.2 us  [attention(): pl.pallas_call(attn_kernel, grid=(steps,), in_specs=[pl.BlockSpec(memory_...]
    ppermute x1, waiting for transfers between devices: 1.48 us -> 0.01 us  [per_device(): far_own = lax.ppermute(own, ('xh', 'xl'), DIAGONAL)]
    ppermute x1, waiting for transfers between devices: 1.5 us -> 0.06 us  [per_device(): far_third = lax.ppermute(bf(two[4, 1::2]), ('xh', 'xl'), DIAGONAL)]
    unnamed x18 -> x24, local copies, waits for them, and re-layouts: 3.41 us -> 4.24 us
    ppermute x2 -> x4, waiting for transfers between devices: 11.1 us -> 10.7 us  [the longest x2 10.7 us: per_device(): lax.ppermute(dprior, AXES, [(i + 1, i) for i in range(count - 1)])]
  transfers between devices with their start and end apart: 33 -> 35, of which waited for: 21 -> 18; matrix products, arithmetic and copies ran while one was open for 0% -> 1% of each run, Pallas kernels for 0% -> 14%
where the time goes in v4:
time: 140 us; the launch traced here: 138 us
  starting transfers between devices  72 us (51%)
  waiting for transfers between devices  35.1 us (25%)
  Pallas kernels  24.3 us (17%)
  local copies, waits for them, and re-layouts  4.47 us (3%)
  other arithmetic  1.53 us (1%)
    ppermute x29, starting transfers between devices, ring(): lax.ppermute(value, axis, [(i, (i + step) % size) for i in range(size)])  55.5 us
    ppermute x29, waiting for transfers between devices, ring(): lax.ppermute(value, axis, [(i, (i + step) % size) for i in range(size)])  24.3 us
    pallas_call x2, Pallas kernels, attention(): pl.pallas_call(attn_kernel, grid=(steps,), in_specs=[pl.BlockSpec(memory_...  19.2 us
    ppermute x2, waiting for transfers between devices, per_device(): lax.ppermute(dprior, AXES, [(i + 1, i) for i in range(count - 1)])  10.7 us
    ppermute x2, starting transfers between devices, per_device(): lax.ppermute(x, AXES, [(i, i + 1) for i in range(count - 1)])  7.53 us
    ppermute x2, starting transfers between devices, per_device(): lax.ppermute(dprior, AXES, [(i + 1, i) for i in range(count - 1)])  5.93 us
    unnamed x24, local copies, waits for them, and re-layouts  4.24 us
  transfers between devices with their start and end apart: 35, of which 18 were waited for; matrix products, arithmetic and copies ran while one was open for 1% of the time, Pallas kernels for 14%

profile of v4, /device:TPU:2, one launch (start us, length us, event | category | flops | bytes accessed | tf_op | source)
XLA Modules:
  0.0 138.3 jit_solution(14622419746877716112)
XLA Ops:
  0.6 1.2 copy-done
  1.9 1.2 copy-done.1
  3.1 0.8 shard_map.75
  3.9 1.6 %collective-permute-start.2 = (bf16[2,2048]{1,0:T(2,128)(2,1)S(1)}, bf16[2,2048]{1,0:T(2,128)(2,1)S(1)}, u32[]{:S(2)}, u32[]{:S(2)}) collective-permute-start(bf16[2,2048]{1,0:T(2,128)(2,1)S(1)} %get-tuple-element.44), channel_id=1, source_target_pairs={{0,129},{1,128},{128,1},{129,0},{2,131},{3,130},{130,3},{131,2},{4... | collective-permute-start | bytes 24584 | tf_op jit(solution)/shard_map/ppermute | solution.py:391
  5.4 2.8 %collective-permute-start.1 = (bf16[2,2048]{1,0:T(2,128)(2,1)S(1)}, bf16[2,2048]{1,0:T(2,128)(2,1)S(1)}, u32[]{:S(2)}, u32[]{:S(2)}) collective-permute-start(bf16[2,2048]{1,0:T(2,128)(2,1)S(1)} %get-tuple-element.44), channel_id=1, source_target_pairs={{0,128},{128,0},{1,129},{129,1},{2,130},{130,2},{3,131},{131,3},{4... | collective-permute-start | bytes 24584 | tf_op jit(solution)/shard_map/ppermute | solution.py:374
  8.3 2.3 %collective-permute-done.1.near_ref = bf16[2,2048]{1,0:T(2,128)(2,1)S(1)} collective-permute-done((bf16[2,2048]{1,0:T(2,128)(2,1)S(1)}, bf16[2,2048]{1,0:T(2,128)(2,1)S(1)}, u32[]{:S(2)}, u32[]{:S(2)}) %collective-permute-start.1) | collective-permute-done | bytes 8224 | tf_op jit(solution)/shard_map/ppermute | solution.py:374
  10.6 1.6 %collective-permute-done.other_ref = bf16[2,4,2048]{2,1,0:T(4,128)(2,1)S(1)} collective-permute-done((bf16[2,4,2048]{2,1,0:T(4,128)(2,1)S(1)}, bf16[2,4,2048]{2,1,0:T(4,128)(2,1)S(1)}, u32[]{:S(2)}, u32[]{:S(2)}) %collective-permute-start) | collective-permute-done | bytes 32800 | tf_op jit(solution)/shard_map/ppermute | solution.py:374
  12.2 5.7 %collective-permute-start.9 = (bf16[5,4,2048]{2,1,0:T(4,128)(2,1)S(1)}, bf16[5,4,2048]{2,1,0:T(4,128)(2,1)S(1)}, u32[]{:S(2)}, u32[]{:S(2)}) collective-permute-start(bf16[5,4,2048]{2,1,0:T(4,128)(2,1)S(1)} %shard_map.76.refs_0_), channel_id=1, source_target_pairs={{0,8},{2,10},{4,12},{6,14},{8,0},{10,2},{12,4},{14,6},{1,9},{3,11}... | collective-permute-start | bytes 245768 | tf_op jit(solution)/shard_map/ppermute | solution.py:374
  17.9 3.9 %collective-permute-start.7 = (bf16[5,4,2048]{2,1,0:T(4,128)(2,1)S(1)}, bf16[5,4,2048]{2,1,0:T(4,128)(2,1)S(1)}, u32[]{:S(2)}, u32[]{:S(2)}) collective-permute-start(bf16[5,4,2048]{2,1,0:T(4,128)(2,1)S(1)} %shard_map.76.refs_0_), channel_id=1, source_target_pairs={{0,6},{2,8},{4,10},{6,12},{8,14},{10,0},{12,2},{14,4},{1,7},{3,9},... | collective-permute-start | bytes 245768 | tf_op jit(solution)/shard_map/ppermute | solution.py:374
  21.8 0.9 collective-permute-start.6
  22.7 2.1 %collective-permute-start.5 = (bf16[5,4,2048]{2,1,0:T(4,128)(2,1)S(1)}, bf16[5,4,2048]{2,1,0:T(4,128)(2,1)S(1)}, u32[]{:S(2)}, u32[]{:S(2)}) collective-permute-start(bf16[5,4,2048]{2,1,0:T(4,128)(2,1)S(1)} %shard_map.76.refs_0_), channel_id=1, source_target_pairs={{0,4},{2,6},{4,8},{6,10},{8,12},{10,14},{12,0},{14,2},{1,5},{3,7},... | collective-permute-start | bytes 245768 | tf_op jit(solution)/shard_map/ppermute | solution.py:374
  24.8 2.5 %collective-permute-start.4 = (bf16[5,4,2048]{2,1,0:T(4,128)(2,1)S(1)}, bf16[5,4,2048]{2,1,0:T(4,128)(2,1)S(1)}, u32[]{:S(2)}, u32[]{:S(2)}) collective-permute-start(bf16[5,4,2048]{2,1,0:T(4,128)(2,1)S(1)} %shard_map.76.refs_0_), channel_id=1, source_target_pairs={{0,14},{2,0},{4,2},{6,4},{8,6},{10,8},{12,10},{14,12},{1,15},{3,1}... | collective-permute-start | bytes 245768 | tf_op jit(solution)/shard_map/ppermute | solution.py:374
  27.3 0.8 collective-permute-done.8.refs_6_
  28.1 1.5 %collective-permute-start.3 = (bf16[5,4,2048]{2,1,0:T(4,128)(2,1)S(1)}, bf16[5,4,2048]{2,1,0:T(4,128)(2,1)S(1)}, u32[]{:S(2)}, u32[]{:S(2)}) collective-permute-start(bf16[5,4,2048]{2,1,0:T(4,128)(2,1)S(1)} %shard_map.76.refs_0_), channel_id=1, source_target_pairs={{0,2},{2,4},{4,6},{6,8},{8,10},{10,12},{12,14},{14,0},{1,3},{3,5},... | collective-permute-start | bytes 245768 | tf_op jit(solution)/shard_map/ppermute | solution.py:374
  29.6 0.9 pad_maximum_fusion
  30.5 0.5 collective-permute-done.6.refs_4_
  31.0 1.0 collective-permute-done.4.refs_2_
  32.0 1.8 %collective-permute-done.3.refs_1_ = bf16[5,4,2048]{2,1,0:T(4,128)(2,1)S(1)} collective-permute-done((bf16[5,4,2048]{2,1,0:T(4,128)(2,1)S(1)}, bf16[5,4,2048]{2,1,0:T(4,128)(2,1)S(1)}, u32[]{:S(2)}, u32[]{:S(2)}) %collective-permute-start.3) | collective-permute-done | bytes 81952 | tf_op jit(solution)/shard_map/ppermute | solution.py:374
  33.8 1.4 %shard_map.77 = (bf16[64,2048]{1,0:T(8,128)(2,1)}, bf16[64,2048]{1,0:T(8,128)(2,1)}, bf16[2,2,16,2048]{3,2,1,0:T(8,128)(2,1)S(1)}) custom-call(bf16[5,4,2048]{2,1,0:T(4,128)(2,1)S(1)} %shard_map.76.refs_0_, bf16[5,4,2048]{2,1,0:T(4,128)(2,1)S(1)} %collective-permute-done.3.refs_1_, bf16[5,4,2048]{2,1,0:T(4,128)(2,1)S(1)} %collective-permute-done.4.refs_2_, ...), custom_call_target="tpu_custom_call" | custom-call | flops 1048576 | bytes 1048576 | tf_op jit(solution)/shard_map/pallas_call | solution.py:292
  35.2 3.2 %collective-permute-start.13 = (bf16[2,2,16,2048]{3,2,1,0:T(8,128)(2,1)S(1)}, bf16[2,2,16,2048]{3,2,1,0:T(8,128)(2,1)S(1)}, u32[]{:S(2)}, u32[]{:S(2)}) collective-permute-start(bf16[2,2,16,2048]{3,2,1,0:T(8,128)(2,1)S(1)} %get-tuple-element.49.refs_7_), channel_id=1, source_target_pairs={{0,64},{32,96},{64,0},{96,32},{1,65},{33,97},{65,1},{97,33},{2,66}... | collective-permute-start | bytes 786440 | tf_op jit(solution)/shard_map/ppermute | solution.py:374
  38.4 1.1 collective-permute-start.12
  39.5 1.0 collective-permute-start.11
  40.4 3.4 %collective-permute-start.18 = (bf16[2,128,1024]{2,1,0:T(8,128)(2,1)S(1)}, bf16[2,128,1024]{2,1,0:T(8,128)(2,1)S(1)}, u32[]{:S(2)}, u32[]{:S(2)}) collective-permute-start(bf16[2,128,1024]{2,1,0:T(8,128)(2,1)S(1)} %get-tuple-element.50), channel_id=1, source_target_pairs={{0,1},{1,2},{2,3},{3,4},{4,5},{5,6},{6,7},{7,8},{8,9},{9,10},{10,1... | collective-permute-start | bytes 1572872 | tf_op jit(solution)/shard_map/ppermute | solution.py:401
  43.9 0.1 collective-permute-start.14
  44.0 1.2 collective-permute-done.13.refs_10_
  45.1 3.1 %collective-permute-done.12.refs_9_ = bf16[2,2,16,2048]{3,2,1,0:T(8,128)(2,1)S(1)} collective-permute-done((bf16[2,2,16,2048]{3,2,1,0:T(8,128)(2,1)S(1)}, bf16[2,2,16,2048]{3,2,1,0:T(8,128)(2,1)S(1)}, u32[]{:S(2)}, u32[]{:S(2)}) %collective-permute-start.12) | collective-permute-done | bytes 262176 | tf_op jit(solution)/shard_map/ppermute | solution.py:374
  48.2 0.2 collective-permute-done.11.refs_8_
  48.4 0.3 collective-permute-start.15
  48.8 0.1 stack.41.place_ref
  48.8 4.1 %collective-permute-start.10 = (bf16[2,128,1024]{2,1,0:T(8,128)(2,1)}, bf16[2,128,1024]{2,1,0:T(8,128)(2,1)S(1)}, u32[]{:S(2)}, u32[]{:S(2)}) collective-permute-start(bf16[2,128,1024]{2,1,0:T(8,128)(2,1)} %get-tuple-element.46), channel_id=1, source_target_pairs={{0,1},{1,2},{2,3},{3,4},{4,5},{5,6},{6,7},{7,8},{8,9},{9,10},{10,1... | collective-permute-start | bytes 1572872 | tf_op jit(solution)/shard_map/ppermute | solution.py:401
  53.1 0.6 copy-done.7
  53.7 0.1 copy-done.8
  53.8 0.1 copy-done.9
  53.9 0.1 copy-done.11
  54.1 9.6 %shard_map.78 = (bf16[256,2048]{1,0:T(8,128)(2,1)}, bf16[256,2048]{1,0:T(8,128)(2,1)}, bf16[256,2048]{1,0:T(8,128)(2,1)S(1)}, bf16[256,2048]{1,0:T(8,128)(2,1)S(...) custom-call(s32[5]{0:T(128)S(1)} %stack.41.place_ref, ...), custom_call_target="tpu_custom_call" | custom-call | flops 1811939328 | bytes 10485760 | tf_op jit(solution)/shard_map/pallas_call | solution.py:194
  63.7 1.9 %collective-permute-start.19 = (bf16[2,128,1024]{2,1,0:T(8,128)(2,1)S(1)}, bf16[2,128,1024]{2,1,0:T(8,128)(2,1)S(1)}, u32[]{:S(2)}, u32[]{:S(2)}) collective-permute-start(bf16[2,128,1024]{2,1,0:T(8,128)(2,1)S(1)} %get-tuple-element.62), channel_id=1, source_target_pairs={{1,0},{2,1},{3,2},{4,3},{5,4},{6,5},{7,6},{8,7},{9,8},{10,9},{11,1... | collective-permute-start | bytes 1572872 | tf_op jit(solution)/shard_map/ppermute | solution.py:412
  65.6 0.8 copy-done.10
  66.4 9.6 %shard_map.79 = (bf16[256,2048]{1,0:T(8,128)(2,1)}, bf16[256,2048]{1,0:T(8,128)(2,1)}, bf16[256,2048]{1,0:T(8,128)(2,1)S(1)}, bf16[256,2048]{1,0:T(8,128)(2,1)S(...) custom-call(s32[5]{0:T(128)S(1)} %stack.41.place_ref, ...), custom_call_target="tpu_custom_call", output_to_operand_aliasing={{0}: (16, {}), {1}: (17, {}), {2}: (18, {}), {3}: (19, {}),... | custom-call | flops 1811939328 | bytes 10485760 | tf_op jit(solution)/shard_map/pallas_call | solution.py:194
  76.0 4.3 %collective-permute-done.19.lo_ref = bf16[2,128,1024]{2,1,0:T(8,128)(2,1)S(1)} collective-permute-done((bf16[2,128,1024]{2,1,0:T(8,128)(2,1)S(1)}, bf16[2,128,1024]{2,1,0:T(8,128)(2,1)S(1)}, u32[]{:S(2)}, u32[]{:S(2)}) %collective-permute-start.19) | collective-permute-done | bytes 524320 | tf_op jit(solution)/shard_map/ppermute | solution.py:412
  80.3 2.7 %collective-permute-done.21 = bf16[4,2,2,16,2048]{4,3,2,1,0:T(8,128)(2,1)S(1)} collective-permute-done((bf16[4,2,2,16,2048]{4,3,2,1,0:T(8,128)(2,1)S(1)}, bf16[4,2,2,16,2048]{4,3,2,1,0:T(8,128)(2,1)S(1)}, u32[]{:S(2)}, u32[]{:S(2)}) %collective-permute-start.21) | collective-permute-done | bytes 1048608 | tf_op jit(solution)/shard_map/ppermute | solution.py:374
  83.0 0.3 fusion.2
  83.2 3.1 %collective-permute-start.22 = (bf16[2,2,16,2048]{3,2,1,0:T(8,128)(2,1)S(1)}, bf16[2,2,16,2048]{3,2,1,0:T(8,128)(2,1)S(1)}, u32[]{:S(2)}, u32[]{:S(2)}) collective-permute-start(bf16[2,2,16,2048]{3,2,1,0:T(8,128)(2,1)S(1)} %get-tuple-element.84), channel_id=1, source_target_pairs={{0,64},{32,96},{64,0},{96,32},{1,65},{33,97},{65,1},{97,33},{2,66}... | collective-permute-start | bytes 786440 | tf_op jit(solution)/shard_map/ppermute | solution.py:374
  86.3 0.5 collective-permute-start.24
  86.8 2.7 %collective-permute-start.23 = (bf16[2,2,16,2048]{3,2,1,0:T(8,128)(2,1)S(1)}, bf16[2,2,16,2048]{3,2,1,0:T(8,128)(2,1)S(1)}, u32[]{:S(2)}, u32[]{:S(2)}) collective-permute-start(bf16[2,2,16,2048]{3,2,1,0:T(8,128)(2,1)S(1)} %get-tuple-element.86), channel_id=1, source_target_pairs={{0,96},{32,0},{64,32},{96,64},{1,97},{33,1},{65,33},{97,65},{2,98}... | collective-permute-start | bytes 786440 | tf_op jit(solution)/shard_map/ppermute | solution.py:374
  89.5 4.0 %collective-permute-start.20 = (bf16[2,128,1024]{2,1,0:T(8,128)(2,1)S(1)}, bf16[2,128,1024]{2,1,0:T(8,128)(2,1)S(1)}, u32[]{:S(2)}, u32[]{:S(2)}) collective-permute-start(bf16[2,128,1024]{2,1,0:T(8,128)(2,1)S(1)} %get-tuple-element.65), channel_id=1, source_target_pairs={{1,0},{2,1},{3,2},{4,3},{5,4},{6,5},{7,6},{8,7},{9,8},{10,9},{11,1... | collective-permute-start | bytes 1572872 | tf_op jit(solution)/shard_map/ppermute | solution.py:412
  93.5 0.5 collective-permute-done.22
  94.0 4.8 %collective-permute-done.24 = bf16[2,2,16,2048]{3,2,1,0:T(8,128)(2,1)S(1)} collective-permute-done((bf16[2,2,16,2048]{3,2,1,0:T(8,128)(2,1)S(1)}, bf16[2,2,16,2048]{3,2,1,0:T(8,128)(2,1)S(1)}, u32[]{:S(2)}, u32[]{:S(2)}) %collective-permute-start.24) | collective-permute-done | bytes 262176 | tf_op jit(solution)/shard_map/ppermute | solution.py:374
  98.8 0.2 fusion.1.third_ref
  99.0 6.5 %collective-permute-done.20.hi_ref = bf16[2,128,1024]{2,1,0:T(8,128)(2,1)S(1)} collective-permute-done((bf16[2,128,1024]{2,1,0:T(8,128)(2,1)S(1)}, bf16[2,128,1024]{2,1,0:T(8,128)(2,1)S(1)}, u32[]{:S(2)}, u32[]{:S(2)}) %collective-permute-start.20) | collective-permute-done | bytes 524320 | tf_op jit(solution)/shard_map/ppermute | solution.py:412
  105.4 0.7 shard_map.80
  106.1 3.4 %collective-permute-start.25 = (bf16[5,4,2048]{2,1,0:T(4,128)(2,1)S(1)}, bf16[5,4,2048]{2,1,0:T(4,128)(2,1)S(1)}, u32[]{:S(2)}, u32[]{:S(2)}) collective-permute-start(bf16[5,4,2048]{2,1,0:T(4,128)(2,1)S(1)} %get-tuple-element.73), channel_id=1, source_target_pairs={{0,8},{2,10},{4,12},{6,14},{8,0},{10,2},{12,4},{14,6},{1,9},{3,11}... | collective-permute-start | bytes 245768 | tf_op jit(solution)/shard_map/ppermute | solution.py:374
  109.5 5.1 %collective-permute-start.26 = (bf16[5,4,2048]{2,1,0:T(4,128)(2,1)S(1)}, bf16[5,4,2048]{2,1,0:T(4,128)(2,1)S(1)}, u32[]{:S(2)}, u32[]{:S(2)}) collective-permute-start(bf16[5,4,2048]{2,1,0:T(4,128)(2,1)S(1)} %get-tuple-element.74), channel_id=1, source_target_pairs={{0,6},{2,8},{4,10},{6,12},{8,14},{10,0},{12,2},{14,4},{1,7},{3,9},... | collective-permute-start | bytes 245768 | tf_op jit(solution)/shard_map/ppermute | solution.py:374
  114.7 4.7 %collective-permute-start.28 = (bf16[5,4,2048]{2,1,0:T(4,128)(2,1)S(1)}, bf16[5,4,2048]{2,1,0:T(4,128)(2,1)S(1)}, u32[]{:S(2)}, u32[]{:S(2)}) collective-permute-start(bf16[5,4,2048]{2,1,0:T(4,128)(2,1)S(1)} %get-tuple-element.76), channel_id=1, source_target_pairs={{0,4},{2,6},{4,8},{6,10},{8,12},{10,14},{12,0},{14,2},{1,5},{3,7},... | collective-permute-start | bytes 245768 | tf_op jit(solution)/shard_map/ppermute | solution.py:374
  119.4 2.9 %collective-permute-start.30 = (bf16[5,4,2048]{2,1,0:T(4,128)(2,1)S(1)}, bf16[5,4,2048]{2,1,0:T(4,128)(2,1)S(1)}, u32[]{:S(2)}, u32[]{:S(2)}) collective-permute-start(bf16[5,4,2048]{2,1,0:T(4,128)(2,1)S(1)} %get-tuple-element.78), channel_id=1, source_target_pairs={{0,2},{2,4},{4,6},{6,8},{8,10},{10,12},{12,14},{14,0},{1,3},{3,5},... | collective-permute-start | bytes 245768 | tf_op jit(solution)/shard_map/ppermute | solution.py:374
  122.3 4.2 %collective-permute-start.31 = (bf16[5,4,2048]{2,1,0:T(4,128)(2,1)S(1)}, bf16[5,4,2048]{2,1,0:T(4,128)(2,1)S(1)}, u32[]{:S(2)}, u32[]{:S(2)}) collective-permute-start(bf16[5,4,2048]{2,1,0:T(4,128)(2,1)S(1)} %get-tuple-element.79), channel_id=1, source_target_pairs={{0,14},{2,0},{4,2},{6,4},{8,6},{10,8},{12,10},{14,12},{1,15},{3,1}... | collective-permute-start | bytes 245768 | tf_op jit(solution)/shard_map/ppermute | solution.py:374
  126.5 1.0 collective-permute-done.29
  127.5 1.1 collective-permute-done.31
  128.6 0.2 fusion.5
  128.8 1.7 %collective-permute-start.33 = (bf16[2,2048]{1,0:T(2,128)(2,1)S(1)}, bf16[2,2048]{1,0:T(2,128)(2,1)S(1)}, u32[]{:S(2)}, u32[]{:S(2)}) collective-permute-start(bf16[2,2048]{1,0:T(2,128)(2,1)S(1)} %bitcast.28), channel_id=1, source_target_pairs={{0,128},{128,0},{1,129},{129,1},{2,130},{130,2},{3,131},{131,3},{4... | collective-permute-start | bytes 24584 | tf_op jit(solution)/shard_map/ppermute | solution.py:374
  130.6 1.5 %collective-permute-start.34 = (bf16[2,2048]{1,0:T(2,128)(2,1)S(1)}, bf16[2,2048]{1,0:T(2,128)(2,1)S(1)}, u32[]{:S(2)}, u32[]{:S(2)}) collective-permute-start(bf16[2,2048]{1,0:T(2,128)(2,1)S(1)} %bitcast.27), channel_id=1, source_target_pairs={{0,129},{1,128},{128,1},{129,0},{2,131},{3,130},{130,3},{131,2},{4... | collective-permute-start | bytes 24584 | tf_op jit(solution)/shard_map/ppermute | solution.py:427
  132.1 2.1 %collective-permute-start.32 = (bf16[2,4,2048]{2,1,0:T(4,128)(2,1)S(1)}, bf16[2,4,2048]{2,1,0:T(4,128)(2,1)S(1)}, u32[]{:S(2)}, u32[]{:S(2)}) collective-permute-start(bf16[2,4,2048]{2,1,0:T(4,128)(2,1)S(1)} %slice.64), channel_id=1, source_target_pairs={{0,1},{1,0},{2,3},{3,2},{4,5},{5,4},{6,7},{7,6},{8,9},{9,8},{10,11... | collective-permute-start | bytes 98312 | tf_op jit(solution)/shard_map/ppermute | solution.py:374
  134.1 0.1 collective-permute-done.34
  134.2 1.9 %collective-permute-done.32 = bf16[2,4,2048]{2,1,0:T(4,128)(2,1)S(1)} collective-permute-done((bf16[2,4,2048]{2,1,0:T(4,128)(2,1)S(1)}, bf16[2,4,2048]{2,1,0:T(4,128)(2,1)S(1)}, u32[]{:S(2)}, u32[]{:S(2)}) %collective-permute-start.32) | collective-permute-done | bytes 32800 | tf_op jit(solution)/shard_map/ppermute | solution.py:374
  136.1 2.1 %shard_map.81 = (bf16[256,2048]{1,0:T(8,128)(2,1)}, bf16[256,2048]{1,0:T(8,128)(2,1)}) custom-call(bf16[256,2048]{1,0:T(8,128)(2,1)S(1)} %get-tuple-element.60.dk_ref, bf16[256,2048]{1,0:T(8,128)(2,1)S(1)} %get-tuple-element.61.dv_ref, bf16[2,128,1024]{2,1,0:T(8,128)(2,1)S(1)} %collective-permute-done.19.lo_ref, ...), custom_call_target="tpu_custom_call" | custom-call | flops 1048576 | bytes 7340032 | tf_op jit(solution)/shard_map/pallas_call | solution.py:354
  (49 shorter events, 0.3 us)
Async XLA Ops:
  0.6 1.2 copy-start
  1.9 1.2 copy-start.1
  3.9 4.5 %collective-permute-start.2 = (bf16[2,2048]{1,0:T(2,128)(2,1)S(1)}, bf16[2,2048]{1,0:T(2,128)(2,1)S(1)}, u32[]{:S(2)}, u32[]{:S(2)}) collective-permute-start(bf16[2,2048]{1,0:T(2,128)(2,1)S(1)} %get-tuple-element.44), channel_id=1, source_target_pairs={{0,129},{1,128},{128,1},{129,0},{2,131},{3,130},{130,3},{131,2},{4... | collective-permute-start | bytes 24584 | tf_op jit(solution)/shard_map/ppermute | solution.py:391
  5.4 5.2 %collective-permute-start.1 = (bf16[2,2048]{1,0:T(2,128)(2,1)S(1)}, bf16[2,2048]{1,0:T(2,128)(2,1)S(1)}, u32[]{:S(2)}, u32[]{:S(2)}) collective-permute-start(bf16[2,2048]{1,0:T(2,128)(2,1)S(1)} %get-tuple-element.44), channel_id=1, source_target_pairs={{0,128},{128,0},{1,129},{129,1},{2,130},{130,2},{3,131},{131,3},{4... | collective-permute-start | bytes 24584 | tf_op jit(solution)/shard_map/ppermute | solution.py:374
  8.3 3.9 %collective-permute-start = (bf16[2,4,2048]{2,1,0:T(4,128)(2,1)S(1)}, bf16[2,4,2048]{2,1,0:T(4,128)(2,1)S(1)}, u32[]{:S(2)}, u32[]{:S(2)}) collective-permute-start(bf16[2,4,2048]{2,1,0:T(4,128)(2,1)S(1)} %get-tuple-element.43.mine_ref), channel_id=1, source_target_pairs={{0,1},{1,0},{2,3},{3,2},{4,5},{5,4},{6,7},{7,6},{8,9},{9,8},{10,11... | collective-permute-start | bytes 98312 | tf_op jit(solution)/shard_map/ppermute | solution.py:374
  12.2 12.5 %collective-permute-start.9 = (bf16[5,4,2048]{2,1,0:T(4,128)(2,1)S(1)}, bf16[5,4,2048]{2,1,0:T(4,128)(2,1)S(1)}, u32[]{:S(2)}, u32[]{:S(2)}) collective-permute-start(bf16[5,4,2048]{2,1,0:T(4,128)(2,1)S(1)} %shard_map.76.refs_0_), channel_id=1, source_target_pairs={{0,8},{2,10},{4,12},{6,14},{8,0},{10,2},{12,4},{14,6},{1,9},{3,11}... | collective-permute-start | bytes 245768 | tf_op jit(solution)/shard_map/ppermute | solution.py:374
  17.9 10.2 %collective-permute-start.8 = (bf16[5,4,2048]{2,1,0:T(4,128)(2,1)S(1)}, bf16[5,4,2048]{2,1,0:T(4,128)(2,1)S(1)}, u32[]{:S(2)}, u32[]{:S(2)}) collective-permute-start(bf16[5,4,2048]{2,1,0:T(4,128)(2,1)S(1)} %shard_map.76.refs_0_), channel_id=1, source_target_pairs={{0,10},{2,12},{4,14},{6,0},{8,2},{10,4},{12,6},{14,8},{1,11},{3,13... | collective-permute-start | bytes 245768 | tf_op jit(solution)/shard_map/ppermute | solution.py:374
  17.9 12.6 %collective-permute-start.7 = (bf16[5,4,2048]{2,1,0:T(4,128)(2,1)S(1)}, bf16[5,4,2048]{2,1,0:T(4,128)(2,1)S(1)}, u32[]{:S(2)}, u32[]{:S(2)}) collective-permute-start(bf16[5,4,2048]{2,1,0:T(4,128)(2,1)S(1)} %shard_map.76.refs_0_), channel_id=1, source_target_pairs={{0,6},{2,8},{4,10},{6,12},{8,14},{10,0},{12,2},{14,4},{1,7},{3,9},... | collective-permute-start | bytes 245768 | tf_op jit(solution)/shard_map/ppermute | solution.py:374
  21.8 9.1 %collective-permute-start.6 = (bf16[5,4,2048]{2,1,0:T(4,128)(2,1)S(1)}, bf16[5,4,2048]{2,1,0:T(4,128)(2,1)S(1)}, u32[]{:S(2)}, u32[]{:S(2)}) collective-permute-start(bf16[5,4,2048]{2,1,0:T(4,128)(2,1)S(1)} %shard_map.76.refs_0_), channel_id=1, source_target_pairs={{0,12},{2,14},{4,0},{6,2},{8,4},{10,6},{12,8},{14,10},{1,13},{3,15... | collective-permute-start | bytes 245768 | tf_op jit(solution)/shard_map/ppermute | solution.py:374
  22.7 8.3 %collective-permute-start.5 = (bf16[5,4,2048]{2,1,0:T(4,128)(2,1)S(1)}, bf16[5,4,2048]{2,1,0:T(4,128)(2,1)S(1)}, u32[]{:S(2)}, u32[]{:S(2)}) collective-permute-start(bf16[5,4,2048]{2,1,0:T(4,128)(2,1)S(1)} %shard_map.76.refs_0_), channel_id=1, source_target_pairs={{0,4},{2,6},{4,8},{6,10},{8,12},{10,14},{12,0},{14,2},{1,5},{3,7},... | collective-permute-start | bytes 245768 | tf_op jit(solution)/shard_map/ppermute | solution.py:374
  24.8 7.2 %collective-permute-start.4 = (bf16[5,4,2048]{2,1,0:T(4,128)(2,1)S(1)}, bf16[5,4,2048]{2,1,0:T(4,128)(2,1)S(1)}, u32[]{:S(2)}, u32[]{:S(2)}) collective-permute-start(bf16[5,4,2048]{2,1,0:T(4,128)(2,1)S(1)} %shard_map.76.refs_0_), channel_id=1, source_target_pairs={{0,14},{2,0},{4,2},{6,4},{8,6},{10,8},{12,10},{14,12},{1,15},{3,1}... | collective-permute-start | bytes 245768 | tf_op jit(solution)/shard_map/ppermute | solution.py:374
  28.1 5.7 %collective-permute-start.3 = (bf16[5,4,2048]{2,1,0:T(4,128)(2,1)S(1)}, bf16[5,4,2048]{2,1,0:T(4,128)(2,1)S(1)}, u32[]{:S(2)}, u32[]{:S(2)}) collective-permute-start(bf16[5,4,2048]{2,1,0:T(4,128)(2,1)S(1)} %shard_map.76.refs_0_), channel_id=1, source_target_pairs={{0,2},{2,4},{4,6},{6,8},{8,10},{10,12},{12,14},{14,0},{1,3},{3,5},... | collective-permute-start | bytes 245768 | tf_op jit(solution)/shard_map/ppermute | solution.py:374
  35.2 18.8 %copy-start.2 = (bf16[2,2,16,2048]{3,2,1,0:T(8,128)(2,1)}, bf16[2,2,16,2048]{3,2,1,0:T(8,128)(2,1)S(1)}, u32[]{:S(2)}) copy-start(bf16[2,2,16,2048]{3,2,1,0:T(8,128)(2,1)S(1)} %get-tuple-element.49.refs_7_) | copy-start | bytes 786436
  35.2 9.9 %collective-permute-start.13 = (bf16[2,2,16,2048]{3,2,1,0:T(8,128)(2,1)S(1)}, bf16[2,2,16,2048]{3,2,1,0:T(8,128)(2,1)S(1)}, u32[]{:S(2)}, u32[]{:S(2)}) collective-permute-start(bf16[2,2,16,2048]{3,2,1,0:T(8,128)(2,1)S(1)} %get-tuple-element.49.refs_7_), channel_id=1, source_target_pairs={{0,64},{32,96},{64,0},{96,32},{1,65},{33,97},{65,1},{97,33},{2,66}... | collective-permute-start | bytes 786440 | tf_op jit(solution)/shard_map/ppermute | solution.py:374
  38.4 9.8 %collective-permute-start.12 = (bf16[2,2,16,2048]{3,2,1,0:T(8,128)(2,1)S(1)}, bf16[2,2,16,2048]{3,2,1,0:T(8,128)(2,1)S(1)}, u32[]{:S(2)}, u32[]{:S(2)}) collective-permute-start(bf16[2,2,16,2048]{3,2,1,0:T(8,128)(2,1)S(1)} %get-tuple-element.49.refs_7_), channel_id=1, source_target_pairs={{0,96},{32,0},{64,32},{96,64},{1,97},{33,1},{65,33},{97,65},{2,98}... | collective-permute-start | bytes 786440 | tf_op jit(solution)/shard_map/ppermute | solution.py:374
  39.5 9.0 %collective-permute-start.11 = (bf16[2,2,16,2048]{3,2,1,0:T(8,128)(2,1)S(1)}, bf16[2,2,16,2048]{3,2,1,0:T(8,128)(2,1)S(1)}, u32[]{:S(2)}, u32[]{:S(2)}) collective-permute-start(bf16[2,2,16,2048]{3,2,1,0:T(8,128)(2,1)S(1)} %get-tuple-element.49.refs_7_), channel_id=1, source_target_pairs={{0,32},{32,64},{64,96},{96,0},{1,33},{33,65},{65,97},{97,1},{2,34}... | collective-permute-start | bytes 786440 | tf_op jit(solution)/shard_map/ppermute | solution.py:374
  40.4 12.6 %collective-permute-start.18 = (bf16[2,128,1024]{2,1,0:T(8,128)(2,1)S(1)}, bf16[2,128,1024]{2,1,0:T(8,128)(2,1)S(1)}, u32[]{:S(2)}, u32[]{:S(2)}) collective-permute-start(bf16[2,128,1024]{2,1,0:T(8,128)(2,1)S(1)} %get-tuple-element.50), channel_id=1, source_target_pairs={{0,1},{1,2},{2,3},{3,4},{4,5},{5,6},{6,7},{7,8},{8,9},{9,10},{10,1... | collective-permute-start | bytes 1572872 | tf_op jit(solution)/shard_map/ppermute | solution.py:401
  43.9 5.0 %collective-permute-start.14 = (bf16[2,2,16,2048]{3,2,1,0:T(8,128)(2,1)S(1)}, bf16[2,2,16,2048]{3,2,1,0:T(8,128)(2,1)S(1)}, u32[]{:S(2)}, u32[]{:S(2)}) collective-permute-start(bf16[2,2,16,2048]{3,2,1,0:T(8,128)(2,1)S(1)} %get-tuple-element.49.refs_7_), channel_id=1, source_target_pairs={{0,16},{16,0},{1,17},{17,1},{2,18},{18,2},{3,19},{19,3},{4,20},{20... | collective-permute-start | bytes 786440 | tf_op jit(solution)/shard_map/ppermute | solution.py:374
  45.1 8.9 %copy-start.3 = (bf16[2,2,16,2048]{3,2,1,0:T(8,128)(2,1)}, bf16[2,2,16,2048]{3,2,1,0:T(8,128)(2,1)S(1)}, u32[]{:S(2)}) copy-start(bf16[2,2,16,2048]{3,2,1,0:T(8,128)(2,1)S(1)} %collective-permute-done.13.refs_10_) | copy-start | bytes 786436
  45.1 7.8 %collective-permute-start.17 = (bf16[2,2,16,2048]{3,2,1,0:T(8,128)(2,1)S(1)}, bf16[2,2,16,2048]{3,2,1,0:T(8,128)(2,1)S(1)}, u32[]{:S(2)}, u32[]{:S(2)}) collective-permute-start(bf16[2,2,16,2048]{3,2,1,0:T(8,128)(2,1)S(1)} %collective-permute-done.13.refs_10_), channel_id=1, source_target_pairs={{0,16},{16,0},{1,17},{17,1},{2,18},{18,2},{3,19},{19,3},{4,20},{20... | collective-permute-start | bytes 786440 | tf_op jit(solution)/shard_map/ppermute | solution.py:374
  48.2 5.8 %copy-start.4 = (bf16[2,2,16,2048]{3,2,1,0:T(8,128)(2,1)}, bf16[2,2,16,2048]{3,2,1,0:T(8,128)(2,1)S(1)}, u32[]{:S(2)}) copy-start(bf16[2,2,16,2048]{3,2,1,0:T(8,128)(2,1)S(1)} %collective-permute-done.12.refs_9_) | copy-start | bytes 786436
  48.2 4.8 %collective-permute-start.16 = (bf16[2,2,16,2048]{3,2,1,0:T(8,128)(2,1)S(1)}, bf16[2,2,16,2048]{3,2,1,0:T(8,128)(2,1)S(1)}, u32[]{:S(2)}, u32[]{:S(2)}) collective-permute-start(bf16[2,2,16,2048]{3,2,1,0:T(8,128)(2,1)S(1)} %collective-permute-done.12.refs_9_), channel_id=1, source_target_pairs={{0,16},{16,0},{1,17},{17,1},{2,18},{18,2},{3,19},{19,3},{4,20},{20... | collective-permute-start | bytes 786440 | tf_op jit(solution)/shard_map/ppermute | solution.py:374
  48.4 5.6 %copy-start.5 = (bf16[2,2,16,2048]{3,2,1,0:T(8,128)(2,1)}, bf16[2,2,16,2048]{3,2,1,0:T(8,128)(2,1)S(1)}, u32[]{:S(2)}) copy-start(bf16[2,2,16,2048]{3,2,1,0:T(8,128)(2,1)S(1)} %collective-permute-done.11.refs_8_) | copy-start | bytes 786436
  48.4 4.6 %collective-permute-start.15 = (bf16[2,2,16,2048]{3,2,1,0:T(8,128)(2,1)S(1)}, bf16[2,2,16,2048]{3,2,1,0:T(8,128)(2,1)S(1)}, u32[]{:S(2)}, u32[]{:S(2)}) collective-permute-start(bf16[2,2,16,2048]{3,2,1,0:T(8,128)(2,1)S(1)} %collective-permute-done.11.refs_8_), channel_id=1, source_target_pairs={{0,16},{16,0},{1,17},{17,1},{2,18},{18,2},{3,19},{19,3},{4,20},{20... | collective-permute-start | bytes 786440 | tf_op jit(solution)/shard_map/ppermute | solution.py:374
  48.8 5.2 %copy-start.6 = (bf16[2,2,16,2048]{3,2,1,0:T(8,128)(2,1)}, bf16[2,2,16,2048]{3,2,1,0:T(8,128)(2,1)S(1)}, u32[]{:S(2)}) copy-start(bf16[2,2,16,2048]{3,2,1,0:T(8,128)(2,1)S(1)} %collective-permute-done.14.refs_11_) | copy-start | bytes 786436
  48.8 16.8 %collective-permute-start.10 = (bf16[2,128,1024]{2,1,0:T(8,128)(2,1)}, bf16[2,128,1024]{2,1,0:T(8,128)(2,1)S(1)}, u32[]{:S(2)}, u32[]{:S(2)}) collective-permute-start(bf16[2,128,1024]{2,1,0:T(8,128)(2,1)} %get-tuple-element.46), channel_id=1, source_target_pairs={{0,1},{1,2},{2,3},{3,4},{4,5},{5,6},{6,7},{7,8},{8,9},{9,10},{10,1... | collective-permute-start | bytes 1572872 | tf_op jit(solution)/shard_map/ppermute | solution.py:401
  53.0 0.7 copy-start.7
  53.0 0.8 copy-start.8
  53.0 0.9 copy-start.9
  53.0 1.0 copy-start.11
  63.7 16.6 %collective-permute-start.19 = (bf16[2,128,1024]{2,1,0:T(8,128)(2,1)S(1)}, bf16[2,128,1024]{2,1,0:T(8,128)(2,1)S(1)}, u32[]{:S(2)}, u32[]{:S(2)}) collective-permute-start(bf16[2,128,1024]{2,1,0:T(8,128)(2,1)S(1)} %get-tuple-element.62), channel_id=1, source_target_pairs={{1,0},{2,1},{3,2},{4,3},{5,4},{6,5},{7,6},{8,7},{9,8},{10,9},{11,1... | collective-permute-start | bytes 1572872 | tf_op jit(solution)/shard_map/ppermute | solution.py:412
  65.6 0.8 copy-start.10
  80.3 2.7 %collective-permute-start.21 = (bf16[4,2,2,16,2048]{4,3,2,1,0:T(8,128)(2,1)S(1)}, bf16[4,2,2,16,2048]{4,3,2,1,0:T(8,128)(2,1)S(1)}, u32[]{:S(2)}, u32[]{:S(2)}) collective-permute-start(bf16[4,2,2,16,2048]{4,3,2,1,0:T(8,128)(2,1)S(1)} %get-tuple-element.67), channel_id=1, source_target_pairs={{0,16},{16,0},{1,17},{17,1},{2,18},{18,2},{3,19},{19,3},{4,20},{20... | collective-permute-start | bytes 3145736 | tf_op jit(solution)/shard_map/ppermute | solution.py:374
  83.2 10.8 %collective-permute-start.22 = (bf16[2,2,16,2048]{3,2,1,0:T(8,128)(2,1)S(1)}, bf16[2,2,16,2048]{3,2,1,0:T(8,128)(2,1)S(1)}, u32[]{:S(2)}, u32[]{:S(2)}) collective-permute-start(bf16[2,2,16,2048]{3,2,1,0:T(8,128)(2,1)S(1)} %get-tuple-element.84), channel_id=1, source_target_pairs={{0,64},{32,96},{64,0},{96,32},{1,65},{33,97},{65,1},{97,33},{2,66}... | collective-permute-start | bytes 786440 | tf_op jit(solution)/shard_map/ppermute | solution.py:374
  86.3 12.5 %collective-permute-start.24 = (bf16[2,2,16,2048]{3,2,1,0:T(8,128)(2,1)S(1)}, bf16[2,2,16,2048]{3,2,1,0:T(8,128)(2,1)S(1)}, u32[]{:S(2)}, u32[]{:S(2)}) collective-permute-start(bf16[2,2,16,2048]{3,2,1,0:T(8,128)(2,1)S(1)} %get-tuple-element.85), channel_id=1, source_target_pairs={{0,32},{32,64},{64,96},{96,0},{1,33},{33,65},{65,97},{97,1},{2,34}... | collective-permute-start | bytes 786440 | tf_op jit(solution)/shard_map/ppermute | solution.py:374
  86.8 12.0 %collective-permute-start.23 = (bf16[2,2,16,2048]{3,2,1,0:T(8,128)(2,1)S(1)}, bf16[2,2,16,2048]{3,2,1,0:T(8,128)(2,1)S(1)}, u32[]{:S(2)}, u32[]{:S(2)}) collective-permute-start(bf16[2,2,16,2048]{3,2,1,0:T(8,128)(2,1)S(1)} %get-tuple-element.86), channel_id=1, source_target_pairs={{0,96},{32,0},{64,32},{96,64},{1,97},{33,1},{65,33},{97,65},{2,98}... | collective-permute-start | bytes 786440 | tf_op jit(solution)/shard_map/ppermute | solution.py:374
  89.5 15.9 %collective-permute-start.20 = (bf16[2,128,1024]{2,1,0:T(8,128)(2,1)S(1)}, bf16[2,128,1024]{2,1,0:T(8,128)(2,1)S(1)}, u32[]{:S(2)}, u32[]{:S(2)}) collective-permute-start(bf16[2,128,1024]{2,1,0:T(8,128)(2,1)S(1)} %get-tuple-element.65), channel_id=1, source_target_pairs={{1,0},{2,1},{3,2},{4,3},{5,4},{6,5},{7,6},{8,7},{9,8},{10,9},{11,1... | collective-permute-start | bytes 1572872 | tf_op jit(solution)/shard_map/ppermute | solution.py:412
  106.1 13.3 %collective-permute-start.25 = (bf16[5,4,2048]{2,1,0:T(4,128)(2,1)S(1)}, bf16[5,4,2048]{2,1,0:T(4,128)(2,1)S(1)}, u32[]{:S(2)}, u32[]{:S(2)}) collective-permute-start(bf16[5,4,2048]{2,1,0:T(4,128)(2,1)S(1)} %get-tuple-element.73), channel_id=1, source_target_pairs={{0,8},{2,10},{4,12},{6,14},{8,0},{10,2},{12,4},{14,6},{1,9},{3,11}... | collective-permute-start | bytes 245768 | tf_op jit(solution)/shard_map/ppermute | solution.py:374
  109.5 12.8 %collective-permute-start.26 = (bf16[5,4,2048]{2,1,0:T(4,128)(2,1)S(1)}, bf16[5,4,2048]{2,1,0:T(4,128)(2,1)S(1)}, u32[]{:S(2)}, u32[]{:S(2)}) collective-permute-start(bf16[5,4,2048]{2,1,0:T(4,128)(2,1)S(1)} %get-tuple-element.74), channel_id=1, source_target_pairs={{0,6},{2,8},{4,10},{6,12},{8,14},{10,0},{12,2},{14,4},{1,7},{3,9},... | collective-permute-start | bytes 245768 | tf_op jit(solution)/shard_map/ppermute | solution.py:374
  114.7 11.9 %collective-permute-start.27 = (bf16[5,4,2048]{2,1,0:T(4,128)(2,1)S(1)}, bf16[5,4,2048]{2,1,0:T(4,128)(2,1)S(1)}, u32[]{:S(2)}, u32[]{:S(2)}) collective-permute-start(bf16[5,4,2048]{2,1,0:T(4,128)(2,1)S(1)} %get-tuple-element.75), channel_id=1, source_target_pairs={{0,10},{2,12},{4,14},{6,0},{8,2},{10,4},{12,6},{14,8},{1,11},{3,13... | collective-permute-start | bytes 245768 | tf_op jit(solution)/shard_map/ppermute | solution.py:374
  114.7 11.9 %collective-permute-start.28 = (bf16[5,4,2048]{2,1,0:T(4,128)(2,1)S(1)}, bf16[5,4,2048]{2,1,0:T(4,128)(2,1)S(1)}, u32[]{:S(2)}, u32[]{:S(2)}) collective-permute-start(bf16[5,4,2048]{2,1,0:T(4,128)(2,1)S(1)} %get-tuple-element.76), channel_id=1, source_target_pairs={{0,4},{2,6},{4,8},{6,10},{8,12},{10,14},{12,0},{14,2},{1,5},{3,7},... | collective-permute-start | bytes 245768 | tf_op jit(solution)/shard_map/ppermute | solution.py:374
  119.4 8.1 %collective-permute-start.29 = (bf16[5,4,2048]{2,1,0:T(4,128)(2,1)S(1)}, bf16[5,4,2048]{2,1,0:T(4,128)(2,1)S(1)}, u32[]{:S(2)}, u32[]{:S(2)}) collective-permute-start(bf16[5,4,2048]{2,1,0:T(4,128)(2,1)S(1)} %get-tuple-element.77), channel_id=1, source_target_pairs={{0,12},{2,14},{4,0},{6,2},{8,4},{10,6},{12,8},{14,10},{1,13},{3,15... | collective-permute-start | bytes 245768 | tf_op jit(solution)/shard_map/ppermute | solution.py:374
  119.4 8.1 %collective-permute-start.30 = (bf16[5,4,2048]{2,1,0:T(4,128)(2,1)S(1)}, bf16[5,4,2048]{2,1,0:T(4,128)(2,1)S(1)}, u32[]{:S(2)}, u32[]{:S(2)}) collective-permute-start(bf16[5,4,2048]{2,1,0:T(4,128)(2,1)S(1)} %get-tuple-element.78), channel_id=1, source_target_pairs={{0,2},{2,4},{4,6},{6,8},{8,10},{10,12},{12,14},{14,0},{1,3},{3,5},... | collective-permute-start | bytes 245768 | tf_op jit(solution)/shard_map/ppermute | solution.py:374
  122.3 6.3 %collective-permute-start.31 = (bf16[5,4,2048]{2,1,0:T(4,128)(2,1)S(1)}, bf16[5,4,2048]{2,1,0:T(4,128)(2,1)S(1)}, u32[]{:S(2)}, u32[]{:S(2)}) collective-permute-start(bf16[5,4,2048]{2,1,0:T(4,128)(2,1)S(1)} %get-tuple-element.79), channel_id=1, source_target_pairs={{0,14},{2,0},{4,2},{6,4},{8,6},{10,8},{12,10},{14,12},{1,15},{3,1}... | collective-permute-start | bytes 245768 | tf_op jit(solution)/shard_map/ppermute | solution.py:374
  128.8 5.3 %collective-permute-start.33 = (bf16[2,2048]{1,0:T(2,128)(2,1)S(1)}, bf16[2,2048]{1,0:T(2,128)(2,1)S(1)}, u32[]{:S(2)}, u32[]{:S(2)}) collective-permute-start(bf16[2,2048]{1,0:T(2,128)(2,1)S(1)} %bitcast.28), channel_id=1, source_target_pairs={{0,128},{128,0},{1,129},{129,1},{2,130},{130,2},{3,131},{131,3},{4... | collective-permute-start | bytes 24584 | tf_op jit(solution)/shard_map/ppermute | solution.py:374
  130.6 3.7 %collective-permute-start.34 = (bf16[2,2048]{1,0:T(2,128)(2,1)S(1)}, bf16[2,2048]{1,0:T(2,128)(2,1)S(1)}, u32[]{:S(2)}, u32[]{:S(2)}) collective-permute-start(bf16[2,2048]{1,0:T(2,128)(2,1)S(1)} %bitcast.27), channel_id=1, source_target_pairs={{0,129},{1,128},{128,1},{129,0},{2,131},{3,130},{130,3},{131,2},{4... | collective-permute-start | bytes 24584 | tf_op jit(solution)/shard_map/ppermute | solution.py:427
  132.1 4.0 %collective-permute-start.32 = (bf16[2,4,2048]{2,1,0:T(4,128)(2,1)S(1)}, bf16[2,4,2048]{2,1,0:T(4,128)(2,1)S(1)}, u32[]{:S(2)}, u32[]{:S(2)}) collective-permute-start(bf16[2,4,2048]{2,1,0:T(4,128)(2,1)S(1)} %slice.64), channel_id=1, source_target_pairs={{0,1},{1,0},{2,3},{3,2},{4,5},{5,4},{6,7},{7,6},{8,9},{9,8},{10,11... | collective-permute-start | bytes 98312 | tf_op jit(solution)/shard_map/ppermute | solution.py:374

commit v5 on v4

--- a/solution.py
+++ b/solution.py
@@ -408,7 +408,7 @@
     pools = (*in_hbm(pk2, pv2), in_hbm(*thirds))
     outs, backs = [], []
     for half in range(2):
-        *outs, dprior = attention(half, place, *fixed, *in_hbm(priors[half]), *pools, outs)
+        *outs, dprior = attention(half, place, *fixed, priors[half], *pools, outs)
         backs.append(lax.ppermute(dprior, AXES, [(i + 1, i) for i in range(count - 1)]))
     attended, grad_q, dk, dv, g2, near, far = outs
 

time: 140 us -> 140 us (level)
    unnamed x24 -> x20, local copies, waits for them, and re-layouts: 4.24 us -> 3.27 us
  transfers between devices with their start and end apart: 35 -> 35, of which waited for: 18 -> 17; matrix products, arithmetic and copies ran while one was open for 1% -> 1% of each run, Pallas kernels for 14% -> 14%
where the time goes in v5:
time: 140 us; the launch traced here: 138 us
  starting transfers between devices  72.4 us (52%)
  waiting for transfers between devices  35.5 us (25%)
  Pallas kernels  24.1 us (17%)
  local copies, waits for them, and re-layouts  3.5 us (2%)
  other arithmetic  1.53 us (1%)
    ppermute x29, starting transfers between devices, ring(): lax.ppermute(value, axis, [(i, (i + step) % size) for i in range(size)])  55.4 us
    ppermute x29, waiting for transfers between devices, ring(): lax.ppermute(value, axis, [(i, (i + step) % size) for i in range(size)])  24.3 us
    pallas_call x2, Pallas kernels, attention(): pl.pallas_call(attn_kernel, grid=(steps,), in_specs=[pl.BlockSpec(memory_...  19.1 us
    ppermute x2, waiting for transfers between devices, per_device(): lax.ppermute(dprior, AXES, [(i + 1, i) for i in range(count - 1)])  11.1 us
    ppermute x2, starting transfers between devices, per_device(): lax.ppermute(x, AXES, [(i, i + 1) for i in range(count - 1)])  7.53 us
    ppermute x2, starting transfers between devices, per_device(): lax.ppermute(dprior, AXES, [(i + 1, i) for i in range(count - 1)])  6.38 us
    unnamed x20, local copies, waits for them, and re-layouts  3.27 us
  transfers between devices with their start and end apart: 35, of which 17 were waited for; matrix products, arithmetic and copies ran while one was open for 1% of the time, Pallas kernels for 14%

profile of v5, /device:TPU:2, one launch (start us, length us, event | category | flops | bytes accessed | tf_op | source)
XLA Modules:
  0.0 138.0 jit_solution(6411087653802907879)
XLA Ops:
  0.6 0.0 copy-start
  0.6 1.2 copy-done
  1.9 1.2 copy-done.1
  3.1 0.8 shard_map.75
  3.9 1.6 %collective-permute-start.2 = (bf16[2,2048]{1,0:T(2,128)(2,1)S(1)}, bf16[2,2048]{1,0:T(2,128)(2,1)S(1)}, u32[]{:S(2)}, u32[]{:S(2)}) collective-permute-start(bf16[2,2048]{1,0:T(2,128)(2,1)S(1)} %get-tuple-element.44), channel_id=1, source_target_pairs={{0,129},{1,128},{128,1},{129,0},{2,131},{3,130},{130,3},{131,2},{4... | collective-permute-start | bytes 24584 | tf_op jit(solution)/shard_map/ppermute | solution.py:391
  5.4 2.8 %collective-permute-start.1 = (bf16[2,2048]{1,0:T(2,128)(2,1)S(1)}, bf16[2,2048]{1,0:T(2,128)(2,1)S(1)}, u32[]{:S(2)}, u32[]{:S(2)}) collective-permute-start(bf16[2,2048]{1,0:T(2,128)(2,1)S(1)} %get-tuple-element.44), channel_id=1, source_target_pairs={{0,128},{128,0},{1,129},{129,1},{2,130},{130,2},{3,131},{131,3},{4... | collective-permute-start | bytes 24584 | tf_op jit(solution)/shard_map/ppermute | solution.py:374
  8.3 2.3 %collective-permute-done.1.near_ref = bf16[2,2048]{1,0:T(2,128)(2,1)S(1)} collective-permute-done((bf16[2,2048]{1,0:T(2,128)(2,1)S(1)}, bf16[2,2048]{1,0:T(2,128)(2,1)S(1)}, u32[]{:S(2)}, u32[]{:S(2)}) %collective-permute-start.1) | collective-permute-done | bytes 8224 | tf_op jit(solution)/shard_map/ppermute | solution.py:374
  10.6 1.6 %collective-permute-done.other_ref = bf16[2,4,2048]{2,1,0:T(4,128)(2,1)S(1)} collective-permute-done((bf16[2,4,2048]{2,1,0:T(4,128)(2,1)S(1)}, bf16[2,4,2048]{2,1,0:T(4,128)(2,1)S(1)}, u32[]{:S(2)}, u32[]{:S(2)}) %collective-permute-start) | collective-permute-done | bytes 32800 | tf_op jit(solution)/shard_map/ppermute | solution.py:374
  12.2 5.7 %collective-permute-start.9 = (bf16[5,4,2048]{2,1,0:T(4,128)(2,1)S(1)}, bf16[5,4,2048]{2,1,0:T(4,128)(2,1)S(1)}, u32[]{:S(2)}, u32[]{:S(2)}) collective-permute-start(bf16[5,4,2048]{2,1,0:T(4,128)(2,1)S(1)} %shard_map.76.refs_0_), channel_id=1, source_target_pairs={{0,8},{2,10},{4,12},{6,14},{8,0},{10,2},{12,4},{14,6},{1,9},{3,11}... | collective-permute-start | bytes 245768 | tf_op jit(solution)/shard_map/ppermute | solution.py:374
  17.9 0.0 collective-permute-start.8
  17.9 3.9 %collective-permute-start.7 = (bf16[5,4,2048]{2,1,0:T(4,128)(2,1)S(1)}, bf16[5,4,2048]{2,1,0:T(4,128)(2,1)S(1)}, u32[]{:S(2)}, u32[]{:S(2)}) collective-permute-start(bf16[5,4,2048]{2,1,0:T(4,128)(2,1)S(1)} %shard_map.76.refs_0_), channel_id=1, source_target_pairs={{0,6},{2,8},{4,10},{6,12},{8,14},{10,0},{12,2},{14,4},{1,7},{3,9},... | collective-permute-start | bytes 245768 | tf_op jit(solution)/shard_map/ppermute | solution.py:374
  21.8 0.9 collective-permute-start.6
  22.7 2.1 %collective-permute-start.5 = (bf16[5,4,2048]{2,1,0:T(4,128)(2,1)S(1)}, bf16[5,4,2048]{2,1,0:T(4,128)(2,1)S(1)}, u32[]{:S(2)}, u32[]{:S(2)}) collective-permute-start(bf16[5,4,2048]{2,1,0:T(4,128)(2,1)S(1)} %shard_map.76.refs_0_), channel_id=1, source_target_pairs={{0,4},{2,6},{4,8},{6,10},{8,12},{10,14},{12,0},{14,2},{1,5},{3,7},... | collective-permute-start | bytes 245768 | tf_op jit(solution)/shard_map/ppermute | solution.py:374
  24.8 2.5 %collective-permute-start.4 = (bf16[5,4,2048]{2,1,0:T(4,128)(2,1)S(1)}, bf16[5,4,2048]{2,1,0:T(4,128)(2,1)S(1)}, u32[]{:S(2)}, u32[]{:S(2)}) collective-permute-start(bf16[5,4,2048]{2,1,0:T(4,128)(2,1)S(1)} %shard_map.76.refs_0_), channel_id=1, source_target_pairs={{0,14},{2,0},{4,2},{6,4},{8,6},{10,8},{12,10},{14,12},{1,15},{3,1}... | collective-permute-start | bytes 245768 | tf_op jit(solution)/shard_map/ppermute | solution.py:374
  27.3 0.8 collective-permute-done.8.refs_6_
  28.1 1.5 %collective-permute-start.3 = (bf16[5,4,2048]{2,1,0:T(4,128)(2,1)S(1)}, bf16[5,4,2048]{2,1,0:T(4,128)(2,1)S(1)}, u32[]{:S(2)}, u32[]{:S(2)}) collective-permute-start(bf16[5,4,2048]{2,1,0:T(4,128)(2,1)S(1)} %shard_map.76.refs_0_), channel_id=1, source_target_pairs={{0,2},{2,4},{4,6},{6,8},{8,10},{10,12},{12,14},{14,0},{1,3},{3,5},... | collective-permute-start | bytes 245768 | tf_op jit(solution)/shard_map/ppermute | solution.py:374
  29.6 0.9 pad_maximum_fusion
  30.5 0.5 collective-permute-done.6.refs_4_
  31.0 1.0 collective-permute-done.4.refs_2_
  32.0 1.8 %collective-permute-done.3.refs_1_ = bf16[5,4,2048]{2,1,0:T(4,128)(2,1)S(1)} collective-permute-done((bf16[5,4,2048]{2,1,0:T(4,128)(2,1)S(1)}, bf16[5,4,2048]{2,1,0:T(4,128)(2,1)S(1)}, u32[]{:S(2)}, u32[]{:S(2)}) %collective-permute-start.3) | collective-permute-done | bytes 81952 | tf_op jit(solution)/shard_map/ppermute | solution.py:374
  33.8 1.4 %shard_map.77 = (bf16[64,2048]{1,0:T(8,128)(2,1)}, bf16[64,2048]{1,0:T(8,128)(2,1)}, bf16[2,2,16,2048]{3,2,1,0:T(8,128)(2,1)S(1)}) custom-call(bf16[5,4,2048]{2,1,0:T(4,128)(2,1)S(1)} %shard_map.76.refs_0_, bf16[5,4,2048]{2,1,0:T(4,128)(2,1)S(1)} %collective-permute-done.3.refs_1_, bf16[5,4,2048]{2,1,0:T(4,128)(2,1)S(1)} %collective-permute-done.4.refs_2_, ...), custom_call_target="tpu_custom_call" | custom-call | flops 1048576 | bytes 1048576 | tf_op jit(solution)/shard_map/pallas_call | solution.py:292
  35.2 3.2 %collective-permute-start.13 = (bf16[2,2,16,2048]{3,2,1,0:T(8,128)(2,1)S(1)}, bf16[2,2,16,2048]{3,2,1,0:T(8,128)(2,1)S(1)}, u32[]{:S(2)}, u32[]{:S(2)}) collective-permute-start(bf16[2,2,16,2048]{3,2,1,0:T(8,128)(2,1)S(1)} %get-tuple-element.49.refs_7_), channel_id=1, source_target_pairs={{0,64},{32,96},{64,0},{96,32},{1,65},{33,97},{65,1},{97,33},{2,66}... | collective-permute-start | bytes 786440 | tf_op jit(solution)/shard_map/ppermute | solution.py:374
  38.4 1.1 collective-permute-start.12
  39.5 1.0 collective-permute-start.11
  40.4 3.4 %collective-permute-start.18 = (bf16[2,128,1024]{2,1,0:T(8,128)(2,1)S(1)}, bf16[2,128,1024]{2,1,0:T(8,128)(2,1)S(1)}, u32[]{:S(2)}, u32[]{:S(2)}) collective-permute-start(bf16[2,128,1024]{2,1,0:T(8,128)(2,1)S(1)} %get-tuple-element.50), channel_id=1, source_target_pairs={{0,1},{1,2},{2,3},{3,4},{4,5},{5,6},{6,7},{7,8},{8,9},{9,10},{10,1... | collective-permute-start | bytes 1572872 | tf_op jit(solution)/shard_map/ppermute | solution.py:401
  43.9 0.1 collective-permute-start.14
  44.0 1.2 collective-permute-done.13.refs_10_
  45.1 3.1 %collective-permute-done.12.refs_9_ = bf16[2,2,16,2048]{3,2,1,0:T(8,128)(2,1)S(1)} collective-permute-done((bf16[2,2,16,2048]{3,2,1,0:T(8,128)(2,1)S(1)}, bf16[2,2,16,2048]{3,2,1,0:T(8,128)(2,1)S(1)}, u32[]{:S(2)}, u32[]{:S(2)}) %collective-permute-start.12) | collective-permute-done | bytes 262176 | tf_op jit(solution)/shard_map/ppermute | solution.py:374
  48.2 0.2 collective-permute-done.11.refs_8_
  48.4 0.3 collective-permute-start.15
  48.7 0.1 stack.41.place_ref
  48.8 4.1 %collective-permute-start.10 = (bf16[2,128,1024]{2,1,0:T(8,128)(2,1)}, bf16[2,128,1024]{2,1,0:T(8,128)(2,1)S(1)}, u32[]{:S(2)}, u32[]{:S(2)}) collective-permute-start(bf16[2,128,1024]{2,1,0:T(8,128)(2,1)} %get-tuple-element.46), channel_id=1, source_target_pairs={{0,1},{1,2},{2,3},{3,4},{4,5},{5,6},{6,7},{7,8},{8,9},{9,10},{10,1... | collective-permute-start | bytes 1572872 | tf_op jit(solution)/shard_map/ppermute | solution.py:401
  53.1 0.6 copy-done.7
  53.7 0.1 copy-done.8
  53.8 0.1 copy-done.9
  53.9 9.5 %shard_map.78 = (bf16[256,2048]{1,0:T(8,128)(2,1)}, bf16[256,2048]{1,0:T(8,128)(2,1)}, bf16[256,2048]{1,0:T(8,128)(2,1)S(1)}, bf16[256,2048]{1,0:T(8,128)(2,1)S(...) custom-call(s32[5]{0:T(128)S(1)} %stack.41.place_ref, ...), custom_call_target="tpu_custom_call" | custom-call | flops 1811939328 | bytes 10485760 | tf_op jit(solution)/shard_map/pallas_call | solution.py:194
  63.4 1.9 %collective-permute-start.19 = (bf16[2,128,1024]{2,1,0:T(8,128)(2,1)S(1)}, bf16[2,128,1024]{2,1,0:T(8,128)(2,1)S(1)}, u32[]{:S(2)}, u32[]{:S(2)}) collective-permute-start(bf16[2,128,1024]{2,1,0:T(8,128)(2,1)S(1)} %get-tuple-element.62), channel_id=1, source_target_pairs={{1,0},{2,1},{3,2},{4,3},{5,4},{6,5},{7,6},{8,7},{9,8},{10,9},{11,1... | collective-permute-start | bytes 1572872 | tf_op jit(solution)/shard_map/ppermute | solution.py:412
  65.3 9.6 %shard_map.79 = (bf16[256,2048]{1,0:T(8,128)(2,1)}, bf16[256,2048]{1,0:T(8,128)(2,1)}, bf16[256,2048]{1,0:T(8,128)(2,1)S(1)}, bf16[256,2048]{1,0:T(8,128)(2,1)S(...) custom-call(s32[5]{0:T(128)S(1)} %stack.41.place_ref, ...), custom_call_target="tpu_custom_call", output_to_operand_aliasing={{0}: (16, {}), {1}: (17, {}), {2}: (18, {}), {3}: (19, {}),... | custom-call | flops 1811939328 | bytes 10485760 | tf_op jit(solution)/shard_map/pallas_call | solution.py:194
  74.9 5.1 %collective-permute-done.19.lo_ref = bf16[2,128,1024]{2,1,0:T(8,128)(2,1)S(1)} collective-permute-done((bf16[2,128,1024]{2,1,0:T(8,128)(2,1)S(1)}, bf16[2,128,1024]{2,1,0:T(8,128)(2,1)S(1)}, u32[]{:S(2)}, u32[]{:S(2)}) %collective-permute-start.19) | collective-permute-done | bytes 524320 | tf_op jit(solution)/shard_map/ppermute | solution.py:412
  80.0 2.7 %collective-permute-done.21 = bf16[4,2,2,16,2048]{4,3,2,1,0:T(8,128)(2,1)S(1)} collective-permute-done((bf16[4,2,2,16,2048]{4,3,2,1,0:T(8,128)(2,1)S(1)}, bf16[4,2,2,16,2048]{4,3,2,1,0:T(8,128)(2,1)S(1)}, u32[]{:S(2)}, u32[]{:S(2)}) %collective-permute-start.21) | collective-permute-done | bytes 1048608 | tf_op jit(solution)/shard_map/ppermute | solution.py:374
  82.7 0.3 fusion.2
  82.9 2.6 %collective-permute-start.22 = (bf16[2,2,16,2048]{3,2,1,0:T(8,128)(2,1)S(1)}, bf16[2,2,16,2048]{3,2,1,0:T(8,128)(2,1)S(1)}, u32[]{:S(2)}, u32[]{:S(2)}) collective-permute-start(bf16[2,2,16,2048]{3,2,1,0:T(8,128)(2,1)S(1)} %get-tuple-element.84), channel_id=1, source_target_pairs={{0,64},{32,96},{64,0},{96,32},{1,65},{33,97},{65,1},{97,33},{2,66}... | collective-permute-start | bytes 786440 | tf_op jit(solution)/shard_map/ppermute | solution.py:374
  85.5 1.0 collective-permute-start.24
  86.5 2.3 %collective-permute-start.23 = (bf16[2,2,16,2048]{3,2,1,0:T(8,128)(2,1)S(1)}, bf16[2,2,16,2048]{3,2,1,0:T(8,128)(2,1)S(1)}, u32[]{:S(2)}, u32[]{:S(2)}) collective-permute-start(bf16[2,2,16,2048]{3,2,1,0:T(8,128)(2,1)S(1)} %get-tuple-element.86), channel_id=1, source_target_pairs={{0,96},{32,0},{64,32},{96,64},{1,97},{33,1},{65,33},{97,65},{2,98}... | collective-permute-start | bytes 786440 | tf_op jit(solution)/shard_map/ppermute | solution.py:374
  88.8 4.5 %collective-permute-start.20 = (bf16[2,128,1024]{2,1,0:T(8,128)(2,1)S(1)}, bf16[2,128,1024]{2,1,0:T(8,128)(2,1)S(1)}, u32[]{:S(2)}, u32[]{:S(2)}) collective-permute-start(bf16[2,128,1024]{2,1,0:T(8,128)(2,1)S(1)} %get-tuple-element.65), channel_id=1, source_target_pairs={{1,0},{2,1},{3,2},{4,3},{5,4},{6,5},{7,6},{8,7},{9,8},{10,9},{11,1... | collective-permute-start | bytes 1572872 | tf_op jit(solution)/shard_map/ppermute | solution.py:412
  93.2 0.5 collective-permute-done.22
  93.7 4.8 %collective-permute-done.24 = bf16[2,2,16,2048]{3,2,1,0:T(8,128)(2,1)S(1)} collective-permute-done((bf16[2,2,16,2048]{3,2,1,0:T(8,128)(2,1)S(1)}, bf16[2,2,16,2048]{3,2,1,0:T(8,128)(2,1)S(1)}, u32[]{:S(2)}, u32[]{:S(2)}) %collective-permute-start.24) | collective-permute-done | bytes 262176 | tf_op jit(solution)/shard_map/ppermute | solution.py:374
  98.5 0.2 fusion.1.third_ref
  98.7 6.0 %collective-permute-done.20.hi_ref = bf16[2,128,1024]{2,1,0:T(8,128)(2,1)S(1)} collective-permute-done((bf16[2,128,1024]{2,1,0:T(8,128)(2,1)S(1)}, bf16[2,128,1024]{2,1,0:T(8,128)(2,1)S(1)}, u32[]{:S(2)}, u32[]{:S(2)}) %collective-permute-start.20) | collective-permute-done | bytes 524320 | tf_op jit(solution)/shard_map/ppermute | solution.py:412
  104.7 0.7 shard_map.80
  105.4 3.9 %collective-permute-start.25 = (bf16[5,4,2048]{2,1,0:T(4,128)(2,1)S(1)}, bf16[5,4,2048]{2,1,0:T(4,128)(2,1)S(1)}, u32[]{:S(2)}, u32[]{:S(2)}) collective-permute-start(bf16[5,4,2048]{2,1,0:T(4,128)(2,1)S(1)} %get-tuple-element.73), channel_id=1, source_target_pairs={{0,8},{2,10},{4,12},{6,14},{8,0},{10,2},{12,4},{14,6},{1,9},{3,11}... | collective-permute-start | bytes 245768 | tf_op jit(solution)/shard_map/ppermute | solution.py:374
  109.2 5.1 %collective-permute-start.26 = (bf16[5,4,2048]{2,1,0:T(4,128)(2,1)S(1)}, bf16[5,4,2048]{2,1,0:T(4,128)(2,1)S(1)}, u32[]{:S(2)}, u32[]{:S(2)}) collective-permute-start(bf16[5,4,2048]{2,1,0:T(4,128)(2,1)S(1)} %get-tuple-element.74), channel_id=1, source_target_pairs={{0,6},{2,8},{4,10},{6,12},{8,14},{10,0},{12,2},{14,4},{1,7},{3,9},... | collective-permute-start | bytes 245768 | tf_op jit(solution)/shard_map/ppermute | solution.py:374
  114.3 4.7 %collective-permute-start.28 = (bf16[5,4,2048]{2,1,0:T(4,128)(2,1)S(1)}, bf16[5,4,2048]{2,1,0:T(4,128)(2,1)S(1)}, u32[]{:S(2)}, u32[]{:S(2)}) collective-permute-start(bf16[5,4,2048]{2,1,0:T(4,128)(2,1)S(1)} %get-tuple-element.76), channel_id=1, source_target_pairs={{0,4},{2,6},{4,8},{6,10},{8,12},{10,14},{12,0},{14,2},{1,5},{3,7},... | collective-permute-start | bytes 245768 | tf_op jit(solution)/shard_map/ppermute | solution.py:374
  119.1 2.9 %collective-permute-start.30 = (bf16[5,4,2048]{2,1,0:T(4,128)(2,1)S(1)}, bf16[5,4,2048]{2,1,0:T(4,128)(2,1)S(1)}, u32[]{:S(2)}, u32[]{:S(2)}) collective-permute-start(bf16[5,4,2048]{2,1,0:T(4,128)(2,1)S(1)} %get-tuple-element.78), channel_id=1, source_target_pairs={{0,2},{2,4},{4,6},{6,8},{8,10},{10,12},{12,14},{14,0},{1,3},{3,5},... | collective-permute-start | bytes 245768 | tf_op jit(solution)/shard_map/ppermute | solution.py:374
  122.0 3.8 %collective-permute-start.31 = (bf16[5,4,2048]{2,1,0:T(4,128)(2,1)S(1)}, bf16[5,4,2048]{2,1,0:T(4,128)(2,1)S(1)}, u32[]{:S(2)}, u32[]{:S(2)}) collective-permute-start(bf16[5,4,2048]{2,1,0:T(4,128)(2,1)S(1)} %get-tuple-element.79), channel_id=1, source_target_pairs={{0,14},{2,0},{4,2},{6,4},{8,6},{10,8},{12,10},{14,12},{1,15},{3,1}... | collective-permute-start | bytes 245768 | tf_op jit(solution)/shard_map/ppermute | solution.py:374
  125.8 1.4 %collective-permute-done.29 = bf16[5,4,2048]{2,1,0:T(4,128)(2,1)S(1)} collective-permute-done((bf16[5,4,2048]{2,1,0:T(4,128)(2,1)S(1)}, bf16[5,4,2048]{2,1,0:T(4,128)(2,1)S(1)}, u32[]{:S(2)}, u32[]{:S(2)}) %collective-permute-start.29) | collective-permute-done | bytes 81952 | tf_op jit(solution)/shard_map/ppermute | solution.py:374
  127.2 0.6 collective-permute-done.31
  127.8 0.2 fusion.5
  128.1 2.1 %collective-permute-start.33 = (bf16[2,2048]{1,0:T(2,128)(2,1)S(1)}, bf16[2,2048]{1,0:T(2,128)(2,1)S(1)}, u32[]{:S(2)}, u32[]{:S(2)}) collective-permute-start(bf16[2,2048]{1,0:T(2,128)(2,1)S(1)} %bitcast.28), channel_id=1, source_target_pairs={{0,128},{128,0},{1,129},{129,1},{2,130},{130,2},{3,131},{131,3},{4... | collective-permute-start | bytes 24584 | tf_op jit(solution)/shard_map/ppermute | solution.py:374
  130.2 1.5 %collective-permute-start.34 = (bf16[2,2048]{1,0:T(2,128)(2,1)S(1)}, bf16[2,2048]{1,0:T(2,128)(2,1)S(1)}, u32[]{:S(2)}, u32[]{:S(2)}) collective-permute-start(bf16[2,2048]{1,0:T(2,128)(2,1)S(1)} %bitcast.27), channel_id=1, source_target_pairs={{0,129},{1,128},{128,1},{129,0},{2,131},{3,130},{130,3},{131,2},{4... | collective-permute-start | bytes 24584 | tf_op jit(solution)/shard_map/ppermute | solution.py:427
  131.8 2.1 %collective-permute-start.32 = (bf16[2,4,2048]{2,1,0:T(4,128)(2,1)S(1)}, bf16[2,4,2048]{2,1,0:T(4,128)(2,1)S(1)}, u32[]{:S(2)}, u32[]{:S(2)}) collective-permute-start(bf16[2,4,2048]{2,1,0:T(4,128)(2,1)S(1)} %slice.64), channel_id=1, source_target_pairs={{0,1},{1,0},{2,3},{3,2},{4,5},{5,4},{6,7},{7,6},{8,9},{9,8},{10,11... | collective-permute-start | bytes 98312 | tf_op jit(solution)/shard_map/ppermute | solution.py:374
  133.8 0.0 collective-permute-done.34
  133.9 1.9 %collective-permute-done.32 = bf16[2,4,2048]{2,1,0:T(4,128)(2,1)S(1)} collective-permute-done((bf16[2,4,2048]{2,1,0:T(4,128)(2,1)S(1)}, bf16[2,4,2048]{2,1,0:T(4,128)(2,1)S(1)}, u32[]{:S(2)}, u32[]{:S(2)}) %collective-permute-start.32) | collective-permute-done | bytes 32800 | tf_op jit(solution)/shard_map/ppermute | solution.py:374
  135.8 2.1 %shard_map.81 = (bf16[256,2048]{1,0:T(8,128)(2,1)}, bf16[256,2048]{1,0:T(8,128)(2,1)}) custom-call(bf16[256,2048]{1,0:T(8,128)(2,1)S(1)} %get-tuple-element.60.dk_ref, bf16[256,2048]{1,0:T(8,128)(2,1)S(1)} %get-tuple-element.61.dv_ref, bf16[2,128,1024]{2,1,0:T(8,128)(2,1)S(1)} %collective-permute-done.19.lo_ref, ...), custom_call_target="tpu_custom_call" | custom-call | flops 1048576 | bytes 7340032 | tf_op jit(solution)/shard_map/pallas_call | solution.py:354
  (45 shorter events, 0.3 us)
Async XLA Ops:
  0.6 1.2 copy-start
  1.9 1.2 copy-start.1
  3.9 4.5 %collective-permute-start.2 = (bf16[2,2048]{1,0:T(2,128)(2,1)S(1)}, bf16[2,2048]{1,0:T(2,128)(2,1)S(1)}, u32[]{:S(2)}, u32[]{:S(2)}) collective-permute-start(bf16[2,2048]{1,0:T(2,128)(2,1)S(1)} %get-tuple-element.44), channel_id=1, source_target_pairs={{0,129},{1,128},{128,1},{129,0},{2,131},{3,130},{130,3},{131,2},{4... | collective-permute-start | bytes 24584 | tf_op jit(solution)/shard_map/ppermute | solution.py:391
  5.4 5.2 %collective-permute-start.1 = (bf16[2,2048]{1,0:T(2,128)(2,1)S(1)}, bf16[2,2048]{1,0:T(2,128)(2,1)S(1)}, u32[]{:S(2)}, u32[]{:S(2)}) collective-permute-start(bf16[2,2048]{1,0:T(2,128)(2,1)S(1)} %get-tuple-element.44), channel_id=1, source_target_pairs={{0,128},{128,0},{1,129},{129,1},{2,130},{130,2},{3,131},{131,3},{4... | collective-permute-start | bytes 24584 | tf_op jit(solution)/shard_map/ppermute | solution.py:374
  8.3 3.9 %collective-permute-start = (bf16[2,4,2048]{2,1,0:T(4,128)(2,1)S(1)}, bf16[2,4,2048]{2,1,0:T(4,128)(2,1)S(1)}, u32[]{:S(2)}, u32[]{:S(2)}) collective-permute-start(bf16[2,4,2048]{2,1,0:T(4,128)(2,1)S(1)} %get-tuple-element.43.mine_ref), channel_id=1, source_target_pairs={{0,1},{1,0},{2,3},{3,2},{4,5},{5,4},{6,7},{7,6},{8,9},{9,8},{10,11... | collective-permute-start | bytes 98312 | tf_op jit(solution)/shard_map/ppermute | solution.py:374
  12.2 12.5 %collective-permute-start.9 = (bf16[5,4,2048]{2,1,0:T(4,128)(2,1)S(1)}, bf16[5,4,2048]{2,1,0:T(4,128)(2,1)S(1)}, u32[]{:S(2)}, u32[]{:S(2)}) collective-permute-start(bf16[5,4,2048]{2,1,0:T(4,128)(2,1)S(1)} %shard_map.76.refs_0_), channel_id=1, source_target_pairs={{0,8},{2,10},{4,12},{6,14},{8,0},{10,2},{12,4},{14,6},{1,9},{3,11}... | collective-permute-start | bytes 245768 | tf_op jit(solution)/shard_map/ppermute | solution.py:374
  17.9 10.2 %collective-permute-start.8 = (bf16[5,4,2048]{2,1,0:T(4,128)(2,1)S(1)}, bf16[5,4,2048]{2,1,0:T(4,128)(2,1)S(1)}, u32[]{:S(2)}, u32[]{:S(2)}) collective-permute-start(bf16[5,4,2048]{2,1,0:T(4,128)(2,1)S(1)} %shard_map.76.refs_0_), channel_id=1, source_target_pairs={{0,10},{2,12},{4,14},{6,0},{8,2},{10,4},{12,6},{14,8},{1,11},{3,13... | collective-permute-start | bytes 245768 | tf_op jit(solution)/shard_map/ppermute | solution.py:374
  17.9 12.6 %collective-permute-start.7 = (bf16[5,4,2048]{2,1,0:T(4,128)(2,1)S(1)}, bf16[5,4,2048]{2,1,0:T(4,128)(2,1)S(1)}, u32[]{:S(2)}, u32[]{:S(2)}) collective-permute-start(bf16[5,4,2048]{2,1,0:T(4,128)(2,1)S(1)} %shard_map.76.refs_0_), channel_id=1, source_target_pairs={{0,6},{2,8},{4,10},{6,12},{8,14},{10,0},{12,2},{14,4},{1,7},{3,9},... | collective-permute-start | bytes 245768 | tf_op jit(solution)/shard_map/ppermute | solution.py:374
  21.8 9.1 %collective-permute-start.6 = (bf16[5,4,2048]{2,1,0:T(4,128)(2,1)S(1)}, bf16[5,4,2048]{2,1,0:T(4,128)(2,1)S(1)}, u32[]{:S(2)}, u32[]{:S(2)}) collective-permute-start(bf16[5,4,2048]{2,1,0:T(4,128)(2,1)S(1)} %shard_map.76.refs_0_), channel_id=1, source_target_pairs={{0,12},{2,14},{4,0},{6,2},{8,4},{10,6},{12,8},{14,10},{1,13},{3,15... | collective-permute-start | bytes 245768 | tf_op jit(solution)/shard_map/ppermute | solution.py:374
  22.7 8.3 %collective-permute-start.5 = (bf16[5,4,2048]{2,1,0:T(4,128)(2,1)S(1)}, bf16[5,4,2048]{2,1,0:T(4,128)(2,1)S(1)}, u32[]{:S(2)}, u32[]{:S(2)}) collective-permute-start(bf16[5,4,2048]{2,1,0:T(4,128)(2,1)S(1)} %shard_map.76.refs_0_), channel_id=1, source_target_pairs={{0,4},{2,6},{4,8},{6,10},{8,12},{10,14},{12,0},{14,2},{1,5},{3,7},... | collective-permute-start | bytes 245768 | tf_op jit(solution)/shard_map/ppermute | solution.py:374
  24.8 7.2 %collective-permute-start.4 = (bf16[5,4,2048]{2,1,0:T(4,128)(2,1)S(1)}, bf16[5,4,2048]{2,1,0:T(4,128)(2,1)S(1)}, u32[]{:S(2)}, u32[]{:S(2)}) collective-permute-start(bf16[5,4,2048]{2,1,0:T(4,128)(2,1)S(1)} %shard_map.76.refs_0_), channel_id=1, source_target_pairs={{0,14},{2,0},{4,2},{6,4},{8,6},{10,8},{12,10},{14,12},{1,15},{3,1}... | collective-permute-start | bytes 245768 | tf_op jit(solution)/shard_map/ppermute | solution.py:374
  28.1 5.7 %collective-permute-start.3 = (bf16[5,4,2048]{2,1,0:T(4,128)(2,1)S(1)}, bf16[5,4,2048]{2,1,0:T(4,128)(2,1)S(1)}, u32[]{:S(2)}, u32[]{:S(2)}) collective-permute-start(bf16[5,4,2048]{2,1,0:T(4,128)(2,1)S(1)} %shard_map.76.refs_0_), channel_id=1, source_target_pairs={{0,2},{2,4},{4,6},{6,8},{8,10},{10,12},{12,14},{14,0},{1,3},{3,5},... | collective-permute-start | bytes 245768 | tf_op jit(solution)/shard_map/ppermute | solution.py:374
  35.2 18.6 %copy-start.2 = (bf16[2,2,16,2048]{3,2,1,0:T(8,128)(2,1)}, bf16[2,2,16,2048]{3,2,1,0:T(8,128)(2,1)S(1)}, u32[]{:S(2)}) copy-start(bf16[2,2,16,2048]{3,2,1,0:T(8,128)(2,1)S(1)} %get-tuple-element.49.refs_7_) | copy-start | bytes 786436
  35.2 9.9 %collective-permute-start.13 = (bf16[2,2,16,2048]{3,2,1,0:T(8,128)(2,1)S(1)}, bf16[2,2,16,2048]{3,2,1,0:T(8,128)(2,1)S(1)}, u32[]{:S(2)}, u32[]{:S(2)}) collective-permute-start(bf16[2,2,16,2048]{3,2,1,0:T(8,128)(2,1)S(1)} %get-tuple-element.49.refs_7_), channel_id=1, source_target_pairs={{0,64},{32,96},{64,0},{96,32},{1,65},{33,97},{65,1},{97,33},{2,66}... | collective-permute-start | bytes 786440 | tf_op jit(solution)/shard_map/ppermute | solution.py:374
  38.4 9.8 %collective-permute-start.12 = (bf16[2,2,16,2048]{3,2,1,0:T(8,128)(2,1)S(1)}, bf16[2,2,16,2048]{3,2,1,0:T(8,128)(2,1)S(1)}, u32[]{:S(2)}, u32[]{:S(2)}) collective-permute-start(bf16[2,2,16,2048]{3,2,1,0:T(8,128)(2,1)S(1)} %get-tuple-element.49.refs_7_), channel_id=1, source_target_pairs={{0,96},{32,0},{64,32},{96,64},{1,97},{33,1},{65,33},{97,65},{2,98}... | collective-permute-start | bytes 786440 | tf_op jit(solution)/shard_map/ppermute | solution.py:374
  39.5 9.0 %collective-permute-start.11 = (bf16[2,2,16,2048]{3,2,1,0:T(8,128)(2,1)S(1)}, bf16[2,2,16,2048]{3,2,1,0:T(8,128)(2,1)S(1)}, u32[]{:S(2)}, u32[]{:S(2)}) collective-permute-start(bf16[2,2,16,2048]{3,2,1,0:T(8,128)(2,1)S(1)} %get-tuple-element.49.refs_7_), channel_id=1, source_target_pairs={{0,32},{32,64},{64,96},{96,0},{1,33},{33,65},{65,97},{97,1},{2,34}... | collective-permute-start | bytes 786440 | tf_op jit(solution)/shard_map/ppermute | solution.py:374
  40.4 12.6 %collective-permute-start.18 = (bf16[2,128,1024]{2,1,0:T(8,128)(2,1)S(1)}, bf16[2,128,1024]{2,1,0:T(8,128)(2,1)S(1)}, u32[]{:S(2)}, u32[]{:S(2)}) collective-permute-start(bf16[2,128,1024]{2,1,0:T(8,128)(2,1)S(1)} %get-tuple-element.50), channel_id=1, source_target_pairs={{0,1},{1,2},{2,3},{3,4},{4,5},{5,6},{6,7},{7,8},{8,9},{9,10},{10,1... | collective-permute-start | bytes 1572872 | tf_op jit(solution)/shard_map/ppermute | solution.py:401
  43.9 5.0 %collective-permute-start.14 = (bf16[2,2,16,2048]{3,2,1,0:T(8,128)(2,1)S(1)}, bf16[2,2,16,2048]{3,2,1,0:T(8,128)(2,1)S(1)}, u32[]{:S(2)}, u32[]{:S(2)}) collective-permute-start(bf16[2,2,16,2048]{3,2,1,0:T(8,128)(2,1)S(1)} %get-tuple-element.49.refs_7_), channel_id=1, source_target_pairs={{0,16},{16,0},{1,17},{17,1},{2,18},{18,2},{3,19},{19,3},{4,20},{20... | collective-permute-start | bytes 786440 | tf_op jit(solution)/shard_map/ppermute | solution.py:374
  45.1 8.7 %copy-start.3 = (bf16[2,2,16,2048]{3,2,1,0:T(8,128)(2,1)}, bf16[2,2,16,2048]{3,2,1,0:T(8,128)(2,1)S(1)}, u32[]{:S(2)}) copy-start(bf16[2,2,16,2048]{3,2,1,0:T(8,128)(2,1)S(1)} %collective-permute-done.13.refs_10_) | copy-start | bytes 786436
  45.1 7.8 %collective-permute-start.17 = (bf16[2,2,16,2048]{3,2,1,0:T(8,128)(2,1)S(1)}, bf16[2,2,16,2048]{3,2,1,0:T(8,128)(2,1)S(1)}, u32[]{:S(2)}, u32[]{:S(2)}) collective-permute-start(bf16[2,2,16,2048]{3,2,1,0:T(8,128)(2,1)S(1)} %collective-permute-done.13.refs_10_), channel_id=1, source_target_pairs={{0,16},{16,0},{1,17},{17,1},{2,18},{18,2},{3,19},{19,3},{4,20},{20... | collective-permute-start | bytes 786440 | tf_op jit(solution)/shard_map/ppermute | solution.py:374
  48.2 5.6 %copy-start.4 = (bf16[2,2,16,2048]{3,2,1,0:T(8,128)(2,1)}, bf16[2,2,16,2048]{3,2,1,0:T(8,128)(2,1)S(1)}, u32[]{:S(2)}) copy-start(bf16[2,2,16,2048]{3,2,1,0:T(8,128)(2,1)S(1)} %collective-permute-done.12.refs_9_) | copy-start | bytes 786436
  48.2 4.8 %collective-permute-start.16 = (bf16[2,2,16,2048]{3,2,1,0:T(8,128)(2,1)S(1)}, bf16[2,2,16,2048]{3,2,1,0:T(8,128)(2,1)S(1)}, u32[]{:S(2)}, u32[]{:S(2)}) collective-permute-start(bf16[2,2,16,2048]{3,2,1,0:T(8,128)(2,1)S(1)} %collective-permute-done.12.refs_9_), channel_id=1, source_target_pairs={{0,16},{16,0},{1,17},{17,1},{2,18},{18,2},{3,19},{19,3},{4,20},{20... | collective-permute-start | bytes 786440 | tf_op jit(solution)/shard_map/ppermute | solution.py:374
  48.4 4.6 %copy-start.5 = (bf16[2,2,16,2048]{3,2,1,0:T(8,128)(2,1)}, bf16[2,2,16,2048]{3,2,1,0:T(8,128)(2,1)S(1)}, u32[]{:S(2)}) copy-start(bf16[2,2,16,2048]{3,2,1,0:T(8,128)(2,1)S(1)} %collective-permute-done.11.refs_8_) | copy-start | bytes 786436
  48.4 4.6 %collective-permute-start.15 = (bf16[2,2,16,2048]{3,2,1,0:T(8,128)(2,1)S(1)}, bf16[2,2,16,2048]{3,2,1,0:T(8,128)(2,1)S(1)}, u32[]{:S(2)}, u32[]{:S(2)}) collective-permute-start(bf16[2,2,16,2048]{3,2,1,0:T(8,128)(2,1)S(1)} %collective-permute-done.11.refs_8_), channel_id=1, source_target_pairs={{0,16},{16,0},{1,17},{17,1},{2,18},{18,2},{3,19},{19,3},{4,20},{20... | collective-permute-start | bytes 786440 | tf_op jit(solution)/shard_map/ppermute | solution.py:374
  48.8 4.2 %copy-start.6 = (bf16[2,2,16,2048]{3,2,1,0:T(8,128)(2,1)}, bf16[2,2,16,2048]{3,2,1,0:T(8,128)(2,1)S(1)}, u32[]{:S(2)}) copy-start(bf16[2,2,16,2048]{3,2,1,0:T(8,128)(2,1)S(1)} %collective-permute-done.14.refs_11_) | copy-start | bytes 786436
  48.8 16.5 %collective-permute-start.10 = (bf16[2,128,1024]{2,1,0:T(8,128)(2,1)}, bf16[2,128,1024]{2,1,0:T(8,128)(2,1)S(1)}, u32[]{:S(2)}, u32[]{:S(2)}) collective-permute-start(bf16[2,128,1024]{2,1,0:T(8,128)(2,1)} %get-tuple-element.46), channel_id=1, source_target_pairs={{0,1},{1,2},{2,3},{3,4},{4,5},{5,6},{6,7},{7,8},{8,9},{9,10},{10,1... | collective-permute-start | bytes 1572872 | tf_op jit(solution)/shard_map/ppermute | solution.py:401
  53.0 0.7 copy-start.7
  53.0 0.8 copy-start.8
  53.0 0.8 copy-start.9
  63.4 16.6 %collective-permute-start.19 = (bf16[2,128,1024]{2,1,0:T(8,128)(2,1)S(1)}, bf16[2,128,1024]{2,1,0:T(8,128)(2,1)S(1)}, u32[]{:S(2)}, u32[]{:S(2)}) collective-permute-start(bf16[2,128,1024]{2,1,0:T(8,128)(2,1)S(1)} %get-tuple-element.62), channel_id=1, source_target_pairs={{1,0},{2,1},{3,2},{4,3},{5,4},{6,5},{7,6},{8,7},{9,8},{10,9},{11,1... | collective-permute-start | bytes 1572872 | tf_op jit(solution)/shard_map/ppermute | solution.py:412
  80.0 2.7 %collective-permute-start.21 = (bf16[4,2,2,16,2048]{4,3,2,1,0:T(8,128)(2,1)S(1)}, bf16[4,2,2,16,2048]{4,3,2,1,0:T(8,128)(2,1)S(1)}, u32[]{:S(2)}, u32[]{:S(2)}) collective-permute-start(bf16[4,2,2,16,2048]{4,3,2,1,0:T(8,128)(2,1)S(1)} %get-tuple-element.67), channel_id=1, source_target_pairs={{0,16},{16,0},{1,17},{17,1},{2,18},{18,2},{3,19},{19,3},{4,20},{20... | collective-permute-start | bytes 3145736 | tf_op jit(solution)/shard_map/ppermute | solution.py:374
  82.9 10.8 %collective-permute-start.22 = (bf16[2,2,16,2048]{3,2,1,0:T(8,128)(2,1)S(1)}, bf16[2,2,16,2048]{3,2,1,0:T(8,128)(2,1)S(1)}, u32[]{:S(2)}, u32[]{:S(2)}) collective-permute-start(bf16[2,2,16,2048]{3,2,1,0:T(8,128)(2,1)S(1)} %get-tuple-element.84), channel_id=1, source_target_pairs={{0,64},{32,96},{64,0},{96,32},{1,65},{33,97},{65,1},{97,33},{2,66}... | collective-permute-start | bytes 786440 | tf_op jit(solution)/shard_map/ppermute | solution.py:374
  85.5 13.0 %collective-permute-start.24 = (bf16[2,2,16,2048]{3,2,1,0:T(8,128)(2,1)S(1)}, bf16[2,2,16,2048]{3,2,1,0:T(8,128)(2,1)S(1)}, u32[]{:S(2)}, u32[]{:S(2)}) collective-permute-start(bf16[2,2,16,2048]{3,2,1,0:T(8,128)(2,1)S(1)} %get-tuple-element.85), channel_id=1, source_target_pairs={{0,32},{32,64},{64,96},{96,0},{1,33},{33,65},{65,97},{97,1},{2,34}... | collective-permute-start | bytes 786440 | tf_op jit(solution)/shard_map/ppermute | solution.py:374
  86.5 12.0 %collective-permute-start.23 = (bf16[2,2,16,2048]{3,2,1,0:T(8,128)(2,1)S(1)}, bf16[2,2,16,2048]{3,2,1,0:T(8,128)(2,1)S(1)}, u32[]{:S(2)}, u32[]{:S(2)}) collective-permute-start(bf16[2,2,16,2048]{3,2,1,0:T(8,128)(2,1)S(1)} %get-tuple-element.86), channel_id=1, source_target_pairs={{0,96},{32,0},{64,32},{96,64},{1,97},{33,1},{65,33},{97,65},{2,98}... | collective-permute-start | bytes 786440 | tf_op jit(solution)/shard_map/ppermute | solution.py:374
  88.8 15.9 %collective-permute-start.20 = (bf16[2,128,1024]{2,1,0:T(8,128)(2,1)S(1)}, bf16[2,128,1024]{2,1,0:T(8,128)(2,1)S(1)}, u32[]{:S(2)}, u32[]{:S(2)}) collective-permute-start(bf16[2,128,1024]{2,1,0:T(8,128)(2,1)S(1)} %get-tuple-element.65), channel_id=1, source_target_pairs={{1,0},{2,1},{3,2},{4,3},{5,4},{6,5},{7,6},{8,7},{9,8},{10,9},{11,1... | collective-permute-start | bytes 1572872 | tf_op jit(solution)/shard_map/ppermute | solution.py:412
  105.4 13.7 %collective-permute-start.25 = (bf16[5,4,2048]{2,1,0:T(4,128)(2,1)S(1)}, bf16[5,4,2048]{2,1,0:T(4,128)(2,1)S(1)}, u32[]{:S(2)}, u32[]{:S(2)}) collective-permute-start(bf16[5,4,2048]{2,1,0:T(4,128)(2,1)S(1)} %get-tuple-element.73), channel_id=1, source_target_pairs={{0,8},{2,10},{4,12},{6,14},{8,0},{10,2},{12,4},{14,6},{1,9},{3,11}... | collective-permute-start | bytes 245768 | tf_op jit(solution)/shard_map/ppermute | solution.py:374
  109.2 12.8 %collective-permute-start.26 = (bf16[5,4,2048]{2,1,0:T(4,128)(2,1)S(1)}, bf16[5,4,2048]{2,1,0:T(4,128)(2,1)S(1)}, u32[]{:S(2)}, u32[]{:S(2)}) collective-permute-start(bf16[5,4,2048]{2,1,0:T(4,128)(2,1)S(1)} %get-tuple-element.74), channel_id=1, source_target_pairs={{0,6},{2,8},{4,10},{6,12},{8,14},{10,0},{12,2},{14,4},{1,7},{3,9},... | collective-permute-start | bytes 245768 | tf_op jit(solution)/shard_map/ppermute | solution.py:374
  114.3 11.4 %collective-permute-start.27 = (bf16[5,4,2048]{2,1,0:T(4,128)(2,1)S(1)}, bf16[5,4,2048]{2,1,0:T(4,128)(2,1)S(1)}, u32[]{:S(2)}, u32[]{:S(2)}) collective-permute-start(bf16[5,4,2048]{2,1,0:T(4,128)(2,1)S(1)} %get-tuple-element.75), channel_id=1, source_target_pairs={{0,10},{2,12},{4,14},{6,0},{8,2},{10,4},{12,6},{14,8},{1,11},{3,13... | collective-permute-start | bytes 245768 | tf_op jit(solution)/shard_map/ppermute | solution.py:374
  114.3 11.4 %collective-permute-start.28 = (bf16[5,4,2048]{2,1,0:T(4,128)(2,1)S(1)}, bf16[5,4,2048]{2,1,0:T(4,128)(2,1)S(1)}, u32[]{:S(2)}, u32[]{:S(2)}) collective-permute-start(bf16[5,4,2048]{2,1,0:T(4,128)(2,1)S(1)} %get-tuple-element.76), channel_id=1, source_target_pairs={{0,4},{2,6},{4,8},{6,10},{8,12},{10,14},{12,0},{14,2},{1,5},{3,7},... | collective-permute-start | bytes 245768 | tf_op jit(solution)/shard_map/ppermute | solution.py:374
  119.1 8.1 %collective-permute-start.29 = (bf16[5,4,2048]{2,1,0:T(4,128)(2,1)S(1)}, bf16[5,4,2048]{2,1,0:T(4,128)(2,1)S(1)}, u32[]{:S(2)}, u32[]{:S(2)}) collective-permute-start(bf16[5,4,2048]{2,1,0:T(4,128)(2,1)S(1)} %get-tuple-element.77), channel_id=1, source_target_pairs={{0,12},{2,14},{4,0},{6,2},{8,4},{10,6},{12,8},{14,10},{1,13},{3,15... | collective-permute-start | bytes 245768 | tf_op jit(solution)/shard_map/ppermute | solution.py:374
  119.1 8.1 %collective-permute-start.30 = (bf16[5,4,2048]{2,1,0:T(4,128)(2,1)S(1)}, bf16[5,4,2048]{2,1,0:T(4,128)(2,1)S(1)}, u32[]{:S(2)}, u32[]{:S(2)}) collective-permute-start(bf16[5,4,2048]{2,1,0:T(4,128)(2,1)S(1)} %get-tuple-element.78), channel_id=1, source_target_pairs={{0,2},{2,4},{4,6},{6,8},{8,10},{10,12},{12,14},{14,0},{1,3},{3,5},... | collective-permute-start | bytes 245768 | tf_op jit(solution)/shard_map/ppermute | solution.py:374
  122.0 5.8 %collective-permute-start.31 = (bf16[5,4,2048]{2,1,0:T(4,128)(2,1)S(1)}, bf16[5,4,2048]{2,1,0:T(4,128)(2,1)S(1)}, u32[]{:S(2)}, u32[]{:S(2)}) collective-permute-start(bf16[5,4,2048]{2,1,0:T(4,128)(2,1)S(1)} %get-tuple-element.79), channel_id=1, source_target_pairs={{0,14},{2,0},{4,2},{6,4},{8,6},{10,8},{12,10},{14,12},{1,15},{3,1}... | collective-permute-start | bytes 245768 | tf_op jit(solution)/shard_map/ppermute | solution.py:374
  128.1 5.7 %collective-permute-start.33 = (bf16[2,2048]{1,0:T(2,128)(2,1)S(1)}, bf16[2,2048]{1,0:T(2,128)(2,1)S(1)}, u32[]{:S(2)}, u32[]{:S(2)}) collective-permute-start(bf16[2,2048]{1,0:T(2,128)(2,1)S(1)} %bitcast.28), channel_id=1, source_target_pairs={{0,128},{128,0},{1,129},{129,1},{2,130},{130,2},{3,131},{131,3},{4... | collective-permute-start | bytes 24584 | tf_op jit(solution)/shard_map/ppermute | solution.py:374
  130.2 3.7 %collective-permute-start.34 = (bf16[2,2048]{1,0:T(2,128)(2,1)S(1)}, bf16[2,2048]{1,0:T(2,128)(2,1)S(1)}, u32[]{:S(2)}, u32[]{:S(2)}) collective-permute-start(bf16[2,2048]{1,0:T(2,128)(2,1)S(1)} %bitcast.27), channel_id=1, source_target_pairs={{0,129},{1,128},{128,1},{129,0},{2,131},{3,130},{130,3},{131,2},{4... | collective-permute-start | bytes 24584 | tf_op jit(solution)/shard_map/ppermute | solution.py:427
  131.8 4.0 %collective-permute-start.32 = (bf16[2,4,2048]{2,1,0:T(4,128)(2,1)S(1)}, bf16[2,4,2048]{2,1,0:T(4,128)(2,1)S(1)}, u32[]{:S(2)}, u32[]{:S(2)}) collective-permute-start(bf16[2,4,2048]{2,1,0:T(4,128)(2,1)S(1)} %slice.64), channel_id=1, source_target_pairs={{0,1},{1,0},{2,3},{3,2},{4,5},{5,4},{6,7},{7,6},{8,9},{9,8},{10,11... | collective-permute-start | bytes 98312 | tf_op jit(solution)/shard_map/ppermute | solution.py:374

commit v6 on v5

--- a/solution.py
+++ b/solution.py
@@ -44,7 +44,7 @@
 def one_head(bias_ref, seg, refs, outs):
     q_ref, k_ref, v_ref, g_ref, prior_ref, pk2_ref, pv2_ref = refs[:7]
     thirds = refs[7:]
-    att_ref, dq_ref, dk_ref, dv_ref, g2_ref, near_ref, far_ref, dprior_ref = outs
+    att_ref, dq_ref, dk_ref, dv_ref, g2_ref, near_ref, far_a_ref, far_b_ref, dprior_ref = outs
     q = q_ref[:, seg]
     k = k_ref[:, seg]
     v = v_ref[:, seg]
@@ -138,8 +138,12 @@
             g2_ref[s, kv, :, seg] = part[s * 8 : s * 8 + 8]
         for s in range(2 * NY * NXH):
             lo = N2 + s * N3G
-            ref = near_ref if s < NY * NXH else far_ref
-            ref[s // NXH % NY, s % NXH, kv, :, seg] = part[lo : lo + N3G].astype(jnp.bfloat16)
+            slot, value = s // NXH % NY, part[lo : lo + N3G].astype(jnp.bfloat16)
+            if s < NY * NXH:
+                near_ref[slot, s % NXH, kv, :, seg] = value
+            else:
+                ref = (far_a_ref, far_b_ref)[slot // 2]
+                ref[slot % 2, s % NXH, kv, :, seg] = value
 
 
 def fill_bias(place_ref, bias_ref):
@@ -173,7 +177,7 @@
 
     for h in range(HPB):
         seg = slice(h * HDIM, (h + 1) * HDIM)
-        one_head(bias_ref, seg, refs[:15], refs[-9:-1])
+        one_head(bias_ref, seg, refs[:15], refs[-10:-1])
 
 
 def cols(width, *lead, at=0):
@@ -189,6 +193,7 @@
     shape = jax.ShapeDtypeStruct
     row_spec = cols(width, rows, at=at)
     sums_spec = cols(width, NY, NXH, 2, N3G, at=at)
+    half_spec = cols(width, NY // 2, NXH, 2, N3G, at=at)
     prior_spec = cols(width, 2, BLK)
     first_alias = 8 + len(thirds)
     return pl.pallas_call(
@@ -203,7 +208,7 @@
         + [pl.BlockSpec(memory_space=pl.ANY)] * len(earlier),
         out_specs=[
             row_spec, row_spec, row_spec, row_spec,
-            cols(width, NZ, 2, 8, at=at), sums_spec, sums_spec, prior_spec,
+            cols(width, NZ, 2, 8, at=at), sums_spec, half_spec, half_spec, prior_spec,
         ],
         out_shape=[
             shape((rows, FEAT), jnp.bfloat16),
@@ -212,7 +217,8 @@
             shape((rows, FEAT), jnp.bfloat16),
             shape((NZ, 2, 8, FEAT), jnp.float32),
             shape((NY, NXH, 2, N3G, FEAT), jnp.bfloat16),
-            shape((NY, NXH, 2, N3G, FEAT), jnp.bfloat16),
+            shape((NY // 2, NXH, 2, N3G, FEAT), jnp.bfloat16),
+            shape((NY // 2, NXH, 2, N3G, FEAT), jnp.bfloat16),
             shape((2, BLK, FEAT // 2), jnp.bfloat16),
         ],
         scratch_shapes=[pltpu.VMEM((BLK + NP, 2 * BLK), jnp.float32)],
@@ -224,33 +230,11 @@
     )(place, q, k, v, g, prior, pk2, pv2, *thirds, *earlier)
 
 
-def pool_kernel(k_ref, v_ref, pooled_ref, third_ref):
-    for kv, ref in ((0, k_ref), (1, v_ref)):
-        third = jnp.zeros((1, ref.shape[1]), jnp.float32)
-        for e in range(4):
-            run = ref[e * P2 : (e + 1) * P2, :].astype(jnp.float32)
-            total = jnp.sum(run, axis=0, keepdims=True) * (1.0 / math.sqrt(P2))
-            entry = total.astype(jnp.bfloat16)
-            pooled_ref[kv, e : e + 1, :] = entry
-            third = third + entry.astype(jnp.float32)
-        third_ref[kv : kv + 1, :] = (third * 0.5).astype(jnp.bfloat16)
-
-
 def pool(k, v):
-    width = 512
-    shape = jax.ShapeDtypeStruct
-    return pl.pallas_call(
-        pool_kernel,
-        grid=(FEAT // width,),
-        in_specs=[cols(width, k.shape[0])] * 2,
-        out_specs=[cols(width, 2, 4), cols(width, 2)],
-        out_shape=[
-            shape((2, 4, FEAT), jnp.bfloat16),
-            shape((2, FEAT), jnp.bfloat16),
-        ],
-        compiler_params=pltpu.CompilerParams(vmem_limit_bytes=24 * 1024 * 1024),
-        cost_estimate=pl.CostEstimate(flops=1 << 20, bytes_accessed=2 << 20, transcendentals=0),
-    )(k, v)
+    runs = jnp.stack([k, v]).astype(jnp.float32).reshape(2, 4, P2, FEAT)
+    pooled = (jnp.sum(runs, axis=2) / math.sqrt(P2)).astype(jnp.bfloat16)
+    third = jnp.sum(pooled.astype(jnp.float32), axis=1) * 0.5
+    return pooled, third.astype(jnp.bfloat16)
 
 
 def joined_kernel(mine_ref, other_ref, near_ref, far_ref, out_ref):
@@ -410,10 +394,11 @@
     for half in range(2):
         *outs, dprior = attention(half, place, *fixed, priors[half], *pools, outs)
         backs.append(lax.ppermute(dprior, AXES, [(i + 1, i) for i in range(count - 1)]))
-    attended, grad_q, dk, dv, g2, near, far = outs
-
-    backs[0], far = lax.optimization_barrier((backs[0], far))
-    far = ring(far, "c", NC, 1)
+    attended, grad_q, dk, dv, g2, near, far_a, far_b = outs
+
+    backs[0], far_a = lax.optimization_barrier((backs[0], far_a))
+    far_a, far_b = ring(far_a, "c", NC, 1), ring(far_b, "c", NC, 1)
+    far = [far_a[0], far_a[1], far_b[0], far_b[1]]
     s3 = [f32(near[s]) + f32(far[s]) for s in range(NY)]
     t3 = s3[0]
     for s in (3, 1, 2):

time: 140 us -> 140 us (level)
  waiting for transfers between devices: 35.5 us -> 32.9 us
  other arithmetic: 1.53 us -> 3.67 us
  starting transfers between devices: 72.4 us -> 74.3 us
    ppermute x29 -> x30, starting transfers between devices: 55.4 us -> 58 us  [ring(): lax.ppermute(value, axis, [(i, (i + step) % size) for i in range(size)])]
    reduce_sum x0 -> x2, other arithmetic: none -> 2.13 us  [the longest x1 2.07 us: pool(): pooled = (jnp.sum(runs, axis=2) / math.sqrt(P2)).astype(jnp.bfloat16)]
    ppermute x2, waiting for transfers between devices: 11.1 us -> 9.3 us  [per_device(): lax.ppermute(dprior, AXES, [(i + 1, i) for i in range(count - 1)])]
    unnamed x20 -> x22, local copies, waits for them, and re-layouts: 3.27 us -> 2.08 us
    ppermute x29 -> x30, waiting for transfers between devices: 24.3 us -> 23.4 us  [ring(): lax.ppermute(value, axis, [(i, (i + step) % size) for i in range(size)])]
  transfers between devices with their start and end apart: 35 -> 36, of which waited for: 17 -> 19; matrix products, arithmetic and copies ran while one was open for 1% -> 1% of each run, Pallas kernels for 14% -> 14%
where the time goes in v6:
time: 140 us; the launch traced here: 137 us
  starting transfers between devices  74.3 us (53%)
  waiting for transfers between devices  32.9 us (24%)
  Pallas kernels  23.4 us (17%)
  other arithmetic  3.67 us (3%)
  local copies, waits for them, and re-layouts  2.32 us (2%)
    ppermute x30, starting transfers between devices, ring(): lax.ppermute(value, axis, [(i, (i + step) % size) for i in range(size)])  58 us
    ppermute x30, waiting for transfers between devices, ring(): lax.ppermute(value, axis, [(i, (i + step) % size) for i in range(size)])  23.4 us
    pallas_call x2, Pallas kernels, attention(): pl.pallas_call(attn_kernel, grid=(steps,), in_specs=[pl.BlockSpec(memory_...  19.1 us
    ppermute x2, waiting for transfers between devices, per_device(): lax.ppermute(dprior, AXES, [(i + 1, i) for i in range(count - 1)])  9.3 us
    ppermute x2, starting transfers between devices, per_device(): lax.ppermute(x, AXES, [(i, i + 1) for i in range(count - 1)])  7.54 us
    ppermute x2, starting transfers between devices, per_device(): lax.ppermute(dprior, AXES, [(i + 1, i) for i in range(count - 1)])  5.94 us
  transfers between devices with their start and end apart: 36, of which 19 were waited for; matrix products, arithmetic and copies ran while one was open for 1% of the time, Pallas kernels for 14%

profile of v6, /device:TPU:2, one launch (start us, length us, event | category | flops | bytes accessed | tf_op | source)
XLA Modules:
  0.0 137.4 jit_solution(1687458564042674443)
XLA Ops:
  0.6 2.1 %convert_reduce_fusion = f32[2,4,2048]{2,1,0:T(4,128)S(1)} fusion(bf16[1,4,64,2048]{3,2,1,0:T(8,128)(2,1)} %bitcast.30, bf16[1,4,64,2048]{3,2,1,0:T(8,128)(2,1)} %bitcast.29), kind=kLoop, calls=%fused_computation | loop fusion | flops 3129344 | bytes 2162688 | tf_op jit(solution)/shard_map/reduce_sum | solution.py:235
  2.8 1.6 %collective-permute-start.2 = (bf16[2,2048]{1,0:T(2,128)(2,1)S(1)}, bf16[2,2048]{1,0:T(2,128)(2,1)S(1)}, u32[]{:S(2)}, u32[]{:S(2)}) collective-permute-start(bf16[2,2048]{1,0:T(2,128)(2,1)S(1)} %multiply_convert_fusion.1), channel_id=1, source_target_pairs={{0,129},{1,128},{128,1},{129,0},{2,131},{3,130},{130,3},{131,2},{4... | collective-permute-start | bytes 24584 | tf_op jit(solution)/shard_map/ppermute | solution.py:375
  4.4 2.8 %collective-permute-start.1 = (bf16[2,2048]{1,0:T(2,128)(2,1)S(1)}, bf16[2,2048]{1,0:T(2,128)(2,1)S(1)}, u32[]{:S(2)}, u32[]{:S(2)}) collective-permute-start(bf16[2,2048]{1,0:T(2,128)(2,1)S(1)} %multiply_convert_fusion.1), channel_id=1, source_target_pairs={{0,128},{128,0},{1,129},{129,1},{2,130},{130,2},{3,131},{131,3},{4... | collective-permute-start | bytes 24584 | tf_op jit(solution)/shard_map/ppermute | solution.py:358
  7.3 2.3 %collective-permute-done.1.near_ref = bf16[2,2048]{1,0:T(2,128)(2,1)S(1)} collective-permute-done((bf16[2,2048]{1,0:T(2,128)(2,1)S(1)}, bf16[2,2048]{1,0:T(2,128)(2,1)S(1)}, u32[]{:S(2)}, u32[]{:S(2)}) %collective-permute-start.1) | collective-permute-done | bytes 8224 | tf_op jit(solution)/shard_map/ppermute | solution.py:358
  9.5 1.6 %collective-permute-done.other_ref = bf16[2,4,2048]{2,1,0:T(4,128)(2,1)S(1)} collective-permute-done((bf16[2,4,2048]{2,1,0:T(4,128)(2,1)S(1)}, bf16[2,4,2048]{2,1,0:T(4,128)(2,1)S(1)}, u32[]{:S(2)}, u32[]{:S(2)}) %collective-permute-start) | collective-permute-done | bytes 32800 | tf_op jit(solution)/shard_map/ppermute | solution.py:358
  11.2 5.7 %collective-permute-start.9 = (bf16[5,4,2048]{2,1,0:T(4,128)(2,1)S(1)}, bf16[5,4,2048]{2,1,0:T(4,128)(2,1)S(1)}, u32[]{:S(2)}, u32[]{:S(2)}) collective-permute-start(bf16[5,4,2048]{2,1,0:T(4,128)(2,1)S(1)} %shard_map.75.refs_0_), channel_id=1, source_target_pairs={{0,8},{2,10},{4,12},{6,14},{8,0},{10,2},{12,4},{14,6},{1,9},{3,11}... | collective-permute-start | bytes 245768 | tf_op jit(solution)/shard_map/ppermute | solution.py:358
  16.9 3.9 %collective-permute-start.7 = (bf16[5,4,2048]{2,1,0:T(4,128)(2,1)S(1)}, bf16[5,4,2048]{2,1,0:T(4,128)(2,1)S(1)}, u32[]{:S(2)}, u32[]{:S(2)}) collective-permute-start(bf16[5,4,2048]{2,1,0:T(4,128)(2,1)S(1)} %shard_map.75.refs_0_), channel_id=1, source_target_pairs={{0,6},{2,8},{4,10},{6,12},{8,14},{10,0},{12,2},{14,4},{1,7},{3,9},... | collective-permute-start | bytes 245768 | tf_op jit(solution)/shard_map/ppermute | solution.py:358
  20.8 0.9 collective-permute-start.6
  21.7 2.1 %collective-permute-start.5 = (bf16[5,4,2048]{2,1,0:T(4,128)(2,1)S(1)}, bf16[5,4,2048]{2,1,0:T(4,128)(2,1)S(1)}, u32[]{:S(2)}, u32[]{:S(2)}) collective-permute-start(bf16[5,4,2048]{2,1,0:T(4,128)(2,1)S(1)} %shard_map.75.refs_0_), channel_id=1, source_target_pairs={{0,4},{2,6},{4,8},{6,10},{8,12},{10,14},{12,0},{14,2},{1,5},{3,7},... | collective-permute-start | bytes 245768 | tf_op jit(solution)/shard_map/ppermute | solution.py:358
  23.7 2.5 %collective-permute-start.4 = (bf16[5,4,2048]{2,1,0:T(4,128)(2,1)S(1)}, bf16[5,4,2048]{2,1,0:T(4,128)(2,1)S(1)}, u32[]{:S(2)}, u32[]{:S(2)}) collective-permute-start(bf16[5,4,2048]{2,1,0:T(4,128)(2,1)S(1)} %shard_map.75.refs_0_), channel_id=1, source_target_pairs={{0,14},{2,0},{4,2},{6,4},{8,6},{10,8},{12,10},{14,12},{1,15},{3,1}... | collective-permute-start | bytes 245768 | tf_op jit(solution)/shard_map/ppermute | solution.py:358
  26.3 0.8 collective-permute-done.8.refs_6_
  27.1 1.5 %collective-permute-start.3 = (bf16[5,4,2048]{2,1,0:T(4,128)(2,1)S(1)}, bf16[5,4,2048]{2,1,0:T(4,128)(2,1)S(1)}, u32[]{:S(2)}, u32[]{:S(2)}) collective-permute-start(bf16[5,4,2048]{2,1,0:T(4,128)(2,1)S(1)} %shard_map.75.refs_0_), channel_id=1, source_target_pairs={{0,2},{2,4},{4,6},{6,8},{8,10},{10,12},{12,14},{14,0},{1,3},{3,5},... | collective-permute-start | bytes 245768 | tf_op jit(solution)/shard_map/ppermute | solution.py:358
  28.6 0.9 pad_maximum_fusion
  29.5 0.5 collective-permute-done.6.refs_4_
  29.9 1.0 collective-permute-done.4.refs_2_
  30.9 1.8 %collective-permute-done.3.refs_1_ = bf16[5,4,2048]{2,1,0:T(4,128)(2,1)S(1)} collective-permute-done((bf16[5,4,2048]{2,1,0:T(4,128)(2,1)S(1)}, bf16[5,4,2048]{2,1,0:T(4,128)(2,1)S(1)}, u32[]{:S(2)}, u32[]{:S(2)}) %collective-permute-start.3) | collective-permute-done | bytes 81952 | tf_op jit(solution)/shard_map/ppermute | solution.py:358
  32.7 1.4 %shard_map.76 = (bf16[64,2048]{1,0:T(8,128)(2,1)}, bf16[64,2048]{1,0:T(8,128)(2,1)}, bf16[2,2,16,2048]{3,2,1,0:T(8,128)(2,1)S(1)}) custom-call(bf16[5,4,2048]{2,1,0:T(4,128)(2,1)S(1)} %shard_map.75.refs_0_, bf16[5,4,2048]{2,1,0:T(4,128)(2,1)S(1)} %collective-permute-done.3.refs_1_, bf16[5,4,2048]{2,1,0:T(4,128)(2,1)S(1)} %collective-permute-done.4.refs_2_, ...), custom_call_target="tpu_custom_call" | custom-call | flops 1048576 | bytes 1048576 | tf_op jit(solution)/shard_map/pallas_call | solution.py:276
  34.2 3.2 %collective-permute-start.13 = (bf16[2,2,16,2048]{3,2,1,0:T(8,128)(2,1)S(1)}, bf16[2,2,16,2048]{3,2,1,0:T(8,128)(2,1)S(1)}, u32[]{:S(2)}, u32[]{:S(2)}) collective-permute-start(bf16[2,2,16,2048]{3,2,1,0:T(8,128)(2,1)S(1)} %get-tuple-element.47.refs_7_), channel_id=1, source_target_pairs={{0,64},{32,96},{64,0},{96,32},{1,65},{33,97},{65,1},{97,33},{2,66}... | collective-permute-start | bytes 786440 | tf_op jit(solution)/shard_map/ppermute | solution.py:358
  37.3 1.1 collective-permute-start.12
  38.4 1.0 collective-permute-start.11
  39.4 3.4 %collective-permute-start.18 = (bf16[2,128,1024]{2,1,0:T(8,128)(2,1)S(1)}, bf16[2,128,1024]{2,1,0:T(8,128)(2,1)S(1)}, u32[]{:S(2)}, u32[]{:S(2)}) collective-permute-start(bf16[2,128,1024]{2,1,0:T(8,128)(2,1)S(1)} %get-tuple-element.48), channel_id=1, source_target_pairs={{0,1},{1,2},{2,3},{3,4},{4,5},{5,6},{6,7},{7,8},{8,9},{9,10},{10,1... | collective-permute-start | bytes 1572872 | tf_op jit(solution)/shard_map/ppermute | solution.py:385
  42.8 0.1 collective-permute-start.14
  42.9 1.2 collective-permute-done.13.refs_10_
  44.1 3.1 %collective-permute-done.12.refs_9_ = bf16[2,2,16,2048]{3,2,1,0:T(8,128)(2,1)S(1)} collective-permute-done((bf16[2,2,16,2048]{3,2,1,0:T(8,128)(2,1)S(1)}, bf16[2,2,16,2048]{3,2,1,0:T(8,128)(2,1)S(1)}, u32[]{:S(2)}, u32[]{:S(2)}) %collective-permute-start.12) | collective-permute-done | bytes 262176 | tf_op jit(solution)/shard_map/ppermute | solution.py:358
  47.2 0.2 collective-permute-done.11.refs_8_
  47.4 0.3 collective-permute-start.15
  47.7 4.1 %collective-permute-start.10 = (bf16[2,128,1024]{2,1,0:T(8,128)(2,1)}, bf16[2,128,1024]{2,1,0:T(8,128)(2,1)S(1)}, u32[]{:S(2)}, u32[]{:S(2)}) collective-permute-start(bf16[2,128,1024]{2,1,0:T(8,128)(2,1)} %get-tuple-element.44), channel_id=1, source_target_pairs={{0,1},{1,2},{2,3},{3,4},{4,5},{5,6},{6,7},{7,8},{8,9},{9,10},{10,1... | collective-permute-start | bytes 1572872 | tf_op jit(solution)/shard_map/ppermute | solution.py:385
  51.8 0.1 stack.50.place_ref
  52.0 0.8 copy-done.1
  52.8 0.1 copy-done.9
  52.9 0.1 copy-done.10
  53.0 1.0 copy-done.2
  54.0 9.5 %shard_map.77 = (bf16[256,2048]{1,0:T(8,128)(2,1)}, bf16[256,2048]{1,0:T(8,128)(2,1)}, bf16[256,2048]{1,0:T(8,128)(2,1)S(1)}, bf16[256,2048]{1,0:T(8,128)(2,1)S(...) custom-call(s32[5]{0:T(128)S(1)} %stack.50.place_ref, ...), custom_call_target="tpu_custom_call" | custom-call | flops 1811939328 | bytes 10485760 | tf_op jit(solution)/shard_map/pallas_call | solution.py:199
  63.5 1.9 %collective-permute-start.19 = (bf16[2,128,1024]{2,1,0:T(8,128)(2,1)S(1)}, bf16[2,128,1024]{2,1,0:T(8,128)(2,1)S(1)}, u32[]{:S(2)}, u32[]{:S(2)}) collective-permute-start(bf16[2,128,1024]{2,1,0:T(8,128)(2,1)S(1)} %get-tuple-element.61), channel_id=1, source_target_pairs={{1,0},{2,1},{3,2},{4,3},{5,4},{6,5},{7,6},{8,7},{9,8},{10,9},{11,1... | collective-permute-start | bytes 1572872 | tf_op jit(solution)/shard_map/ppermute | solution.py:396
  65.5 9.6 %shard_map.78 = (bf16[256,2048]{1,0:T(8,128)(2,1)}, bf16[256,2048]{1,0:T(8,128)(2,1)}, bf16[256,2048]{1,0:T(8,128)(2,1)S(1)}, bf16[256,2048]{1,0:T(8,128)(2,1)S(...) custom-call(s32[5]{0:T(128)S(1)} %stack.50.place_ref, ...), custom_call_target="tpu_custom_call", output_to_operand_aliasing={{0}: (16, {}), {1}: (17, {}), {2}: (18, {}), {3}: (19, {}),... | custom-call | flops 1811939328 | bytes 10485760 | tf_op jit(solution)/shard_map/pallas_call | solution.py:199
  75.1 2.2 %collective-permute-start.22 = (bf16[2,2,2,16,2048]{4,3,2,1,0:T(8,128)(2,1)S(1)}, bf16[2,2,2,16,2048]{4,3,2,1,0:T(8,128)(2,1)S(1)}, u32[]{:S(2)}, u32[]{:S(2)}) collective-permute-start(bf16[2,2,2,16,2048]{4,3,2,1,0:T(8,128)(2,1)S(1)} %get-tuple-element.67), channel_id=1, source_target_pairs={{0,16},{16,0},{1,17},{17,1},{2,18},{18,2},{3,19},{19,3},{4,20},{20... | collective-permute-start | bytes 1572872 | tf_op jit(solution)/shard_map/ppermute | solution.py:358
  77.3 2.8 %collective-permute-done.19.lo_ref = bf16[2,128,1024]{2,1,0:T(8,128)(2,1)S(1)} collective-permute-done((bf16[2,128,1024]{2,1,0:T(8,128)(2,1)S(1)}, bf16[2,128,1024]{2,1,0:T(8,128)(2,1)S(1)}, u32[]{:S(2)}, u32[]{:S(2)}) %collective-permute-start.19) | collective-permute-done | bytes 524320 | tf_op jit(solution)/shard_map/ppermute | solution.py:396
  80.2 1.9 %collective-permute-done.21 = bf16[2,2,2,16,2048]{4,3,2,1,0:T(8,128)(2,1)S(1)} collective-permute-done((bf16[2,2,2,16,2048]{4,3,2,1,0:T(8,128)(2,1)S(1)}, bf16[2,2,2,16,2048]{4,3,2,1,0:T(8,128)(2,1)S(1)}, u32[]{:S(2)}, u32[]{:S(2)}) %collective-permute-start.21) | collective-permute-done | bytes 524320 | tf_op jit(solution)/shard_map/ppermute | solution.py:358
  82.1 0.3 fusion.2
  82.3 3.1 %collective-permute-start.23 = (bf16[2,2,16,2048]{3,2,1,0:T(8,128)(2,1)S(1)}, bf16[2,2,16,2048]{3,2,1,0:T(8,128)(2,1)S(1)}, u32[]{:S(2)}, u32[]{:S(2)}) collective-permute-start(bf16[2,2,16,2048]{3,2,1,0:T(8,128)(2,1)S(1)} %get-tuple-element.86), channel_id=1, source_target_pairs={{0,64},{32,96},{64,0},{96,32},{1,65},{33,97},{65,1},{97,33},{2,66}... | collective-permute-start | bytes 786440 | tf_op jit(solution)/shard_map/ppermute | solution.py:358
  85.4 0.5 collective-permute-start.25
  85.9 2.7 %collective-permute-start.24 = (bf16[2,2,16,2048]{3,2,1,0:T(8,128)(2,1)S(1)}, bf16[2,2,16,2048]{3,2,1,0:T(8,128)(2,1)S(1)}, u32[]{:S(2)}, u32[]{:S(2)}) collective-permute-start(bf16[2,2,16,2048]{3,2,1,0:T(8,128)(2,1)S(1)} %get-tuple-element.88), channel_id=1, source_target_pairs={{0,96},{32,0},{64,32},{96,64},{1,97},{33,1},{65,33},{97,65},{2,98}... | collective-permute-start | bytes 786440 | tf_op jit(solution)/shard_map/ppermute | solution.py:358
  88.6 4.0 %collective-permute-start.20 = (bf16[2,128,1024]{2,1,0:T(8,128)(2,1)S(1)}, bf16[2,128,1024]{2,1,0:T(8,128)(2,1)S(1)}, u32[]{:S(2)}, u32[]{:S(2)}) collective-permute-start(bf16[2,128,1024]{2,1,0:T(8,128)(2,1)S(1)} %get-tuple-element.64), channel_id=1, source_target_pairs={{1,0},{2,1},{3,2},{4,3},{5,4},{6,5},{7,6},{8,7},{9,8},{10,9},{11,1... | collective-permute-start | bytes 1572872 | tf_op jit(solution)/shard_map/ppermute | solution.py:396
  92.7 0.5 collective-permute-done.23
  93.1 4.8 %collective-permute-done.25 = bf16[2,2,16,2048]{3,2,1,0:T(8,128)(2,1)S(1)} collective-permute-done((bf16[2,2,16,2048]{3,2,1,0:T(8,128)(2,1)S(1)}, bf16[2,2,16,2048]{3,2,1,0:T(8,128)(2,1)S(1)}, u32[]{:S(2)}, u32[]{:S(2)}) %collective-permute-start.25) | collective-permute-done | bytes 262176 | tf_op jit(solution)/shard_map/ppermute | solution.py:358
  97.9 0.2 fusion.1.third_ref
  98.1 6.5 %collective-permute-done.20.hi_ref = bf16[2,128,1024]{2,1,0:T(8,128)(2,1)S(1)} collective-permute-done((bf16[2,128,1024]{2,1,0:T(8,128)(2,1)S(1)}, bf16[2,128,1024]{2,1,0:T(8,128)(2,1)S(1)}, u32[]{:S(2)}, u32[]{:S(2)}) %collective-permute-start.20) | collective-permute-done | bytes 524320 | tf_op jit(solution)/shard_map/ppermute | solution.py:396
  104.5 0.7 shard_map.79
  105.2 3.6 %collective-permute-start.26 = (bf16[5,4,2048]{2,1,0:T(4,128)(2,1)S(1)}, bf16[5,4,2048]{2,1,0:T(4,128)(2,1)S(1)}, u32[]{:S(2)}, u32[]{:S(2)}) collective-permute-start(bf16[5,4,2048]{2,1,0:T(4,128)(2,1)S(1)} %get-tuple-element.73), channel_id=1, source_target_pairs={{0,8},{2,10},{4,12},{6,14},{8,0},{10,2},{12,4},{14,6},{1,9},{3,11}... | collective-permute-start | bytes 245768 | tf_op jit(solution)/shard_map/ppermute | solution.py:358
  108.9 4.9 %collective-permute-start.27 = (bf16[5,4,2048]{2,1,0:T(4,128)(2,1)S(1)}, bf16[5,4,2048]{2,1,0:T(4,128)(2,1)S(1)}, u32[]{:S(2)}, u32[]{:S(2)}) collective-permute-start(bf16[5,4,2048]{2,1,0:T(4,128)(2,1)S(1)} %get-tuple-element.74), channel_id=1, source_target_pairs={{0,6},{2,8},{4,10},{6,12},{8,14},{10,0},{12,2},{14,4},{1,7},{3,9},... | collective-permute-start | bytes 245768 | tf_op jit(solution)/shard_map/ppermute | solution.py:358
  113.8 0.1 collective-permute-start.28
  113.9 4.8 %collective-permute-start.29 = (bf16[5,4,2048]{2,1,0:T(4,128)(2,1)S(1)}, bf16[5,4,2048]{2,1,0:T(4,128)(2,1)S(1)}, u32[]{:S(2)}, u32[]{:S(2)}) collective-permute-start(bf16[5,4,2048]{2,1,0:T(4,128)(2,1)S(1)} %get-tuple-element.76), channel_id=1, source_target_pairs={{0,4},{2,6},{4,8},{6,10},{8,12},{10,14},{12,0},{14,2},{1,5},{3,7},... | collective-permute-start | bytes 245768 | tf_op jit(solution)/shard_map/ppermute | solution.py:358
  118.7 2.9 %collective-permute-start.31 = (bf16[5,4,2048]{2,1,0:T(4,128)(2,1)S(1)}, bf16[5,4,2048]{2,1,0:T(4,128)(2,1)S(1)}, u32[]{:S(2)}, u32[]{:S(2)}) collective-permute-start(bf16[5,4,2048]{2,1,0:T(4,128)(2,1)S(1)} %get-tuple-element.78), channel_id=1, source_target_pairs={{0,2},{2,4},{4,6},{6,8},{8,10},{10,12},{12,14},{14,0},{1,3},{3,5},... | collective-permute-start | bytes 245768 | tf_op jit(solution)/shard_map/ppermute | solution.py:358
  121.7 4.2 %collective-permute-start.32 = (bf16[5,4,2048]{2,1,0:T(4,128)(2,1)S(1)}, bf16[5,4,2048]{2,1,0:T(4,128)(2,1)S(1)}, u32[]{:S(2)}, u32[]{:S(2)}) collective-permute-start(bf16[5,4,2048]{2,1,0:T(4,128)(2,1)S(1)} %get-tuple-element.79), channel_id=1, source_target_pairs={{0,14},{2,0},{4,2},{6,4},{8,6},{10,8},{12,10},{14,12},{1,15},{3,1}... | collective-permute-start | bytes 245768 | tf_op jit(solution)/shard_map/ppermute | solution.py:358
  125.9 1.0 collective-permute-done.30
  126.9 1.1 collective-permute-done.32
  127.9 0.2 fusion.5
  128.2 1.8 %collective-permute-start.34 = (bf16[2,2048]{1,0:T(2,128)(2,1)S(1)}, bf16[2,2048]{1,0:T(2,128)(2,1)S(1)}, u32[]{:S(2)}, u32[]{:S(2)}) collective-permute-start(bf16[2,2048]{1,0:T(2,128)(2,1)S(1)} %bitcast.32), channel_id=1, source_target_pairs={{0,128},{128,0},{1,129},{129,1},{2,130},{130,2},{3,131},{131,3},{4... | collective-permute-start | bytes 24584 | tf_op jit(solution)/shard_map/ppermute | solution.py:358
  130.0 1.2 collective-permute-start.35
  131.2 2.1 %collective-permute-start.33 = (bf16[2,4,2048]{2,1,0:T(4,128)(2,1)S(1)}, bf16[2,4,2048]{2,1,0:T(4,128)(2,1)S(1)}, u32[]{:S(2)}, u32[]{:S(2)}) collective-permute-start(bf16[2,4,2048]{2,1,0:T(4,128)(2,1)S(1)} %slice.64), channel_id=1, source_target_pairs={{0,1},{1,0},{2,3},{3,2},{4,5},{5,4},{6,7},{7,6},{8,9},{9,8},{10,11... | collective-permute-start | bytes 98312 | tf_op jit(solution)/shard_map/ppermute | solution.py:358
  133.3 0.2 collective-permute-done.34
  133.4 0.2 collective-permute-done.35
  133.6 1.6 %collective-permute-done.33 = bf16[2,4,2048]{2,1,0:T(4,128)(2,1)S(1)} collective-permute-done((bf16[2,4,2048]{2,1,0:T(4,128)(2,1)S(1)}, bf16[2,4,2048]{2,1,0:T(4,128)(2,1)S(1)}, u32[]{:S(2)}, u32[]{:S(2)}) %collective-permute-start.33) | collective-permute-done | bytes 32800 | tf_op jit(solution)/shard_map/ppermute | solution.py:358
  135.2 2.1 %shard_map.80 = (bf16[256,2048]{1,0:T(8,128)(2,1)}, bf16[256,2048]{1,0:T(8,128)(2,1)}) custom-call(bf16[256,2048]{1,0:T(8,128)(2,1)S(1)} %get-tuple-element.59.dk_ref, bf16[256,2048]{1,0:T(8,128)(2,1)S(1)} %get-tuple-element.60.dv_ref, bf16[2,128,1024]{2,1,0:T(8,128)(2,1)S(1)} %collective-permute-done.19.lo_ref, ...), custom_call_target="tpu_custom_call" | custom-call | flops 1048576 | bytes 7340032 | tf_op jit(solution)/shard_map/pallas_call | solution.py:338
  (51 shorter events, 0.4 us)
Async XLA Ops:
  0.6 6.6 %copy-start.3 = (bf16[256,2048]{1,0:T(8,128)(2,1)S(1)}, bf16[256,2048]{1,0:T(8,128)(2,1)}, u32[]{:S(2)}) copy-start(bf16[256,2048]{1,0:T(8,128)(2,1)} %refs_1_.3) | copy-start | bytes 3145732
  2.7 14.1 %copy-start.4 = (bf16[256,2048]{1,0:T(8,128)(2,1)S(1)}, bf16[256,2048]{1,0:T(8,128)(2,1)}, u32[]{:S(2)}) copy-start(bf16[256,2048]{1,0:T(8,128)(2,1)} %refs_2_.3) | copy-start | bytes 3145732
  2.8 4.5 %collective-permute-start.2 = (bf16[2,2048]{1,0:T(2,128)(2,1)S(1)}, bf16[2,2048]{1,0:T(2,128)(2,1)S(1)}, u32[]{:S(2)}, u32[]{:S(2)}) collective-permute-start(bf16[2,2048]{1,0:T(2,128)(2,1)S(1)} %multiply_convert_fusion.1), channel_id=1, source_target_pairs={{0,129},{1,128},{128,1},{129,0},{2,131},{3,130},{130,3},{131,2},{4... | collective-permute-start | bytes 24584 | tf_op jit(solution)/shard_map/ppermute | solution.py:375
  4.4 5.2 %collective-permute-start.1 = (bf16[2,2048]{1,0:T(2,128)(2,1)S(1)}, bf16[2,2048]{1,0:T(2,128)(2,1)S(1)}, u32[]{:S(2)}, u32[]{:S(2)}) collective-permute-start(bf16[2,2048]{1,0:T(2,128)(2,1)S(1)} %multiply_convert_fusion.1), channel_id=1, source_target_pairs={{0,128},{128,0},{1,129},{129,1},{2,130},{130,2},{3,131},{131,3},{4... | collective-permute-start | bytes 24584 | tf_op jit(solution)/shard_map/ppermute | solution.py:358
  7.2 3.9 %collective-permute-start = (bf16[2,4,2048]{2,1,0:T(4,128)(2,1)S(1)}, bf16[2,4,2048]{2,1,0:T(4,128)(2,1)S(1)}, u32[]{:S(2)}, u32[]{:S(2)}) collective-permute-start(bf16[2,4,2048]{2,1,0:T(4,128)(2,1)S(1)} %get-tuple-element.85.mine_ref), channel_id=1, source_target_pairs={{0,1},{1,0},{2,3},{3,2},{4,5},{5,4},{6,7},{7,6},{8,9},{9,8},{10,11... | collective-permute-start | bytes 98312 | tf_op jit(solution)/shard_map/ppermute | solution.py:358
  11.2 12.5 %collective-permute-start.9 = (bf16[5,4,2048]{2,1,0:T(4,128)(2,1)S(1)}, bf16[5,4,2048]{2,1,0:T(4,128)(2,1)S(1)}, u32[]{:S(2)}, u32[]{:S(2)}) collective-permute-start(bf16[5,4,2048]{2,1,0:T(4,128)(2,1)S(1)} %shard_map.75.refs_0_), channel_id=1, source_target_pairs={{0,8},{2,10},{4,12},{6,14},{8,0},{10,2},{12,4},{14,6},{1,9},{3,11}... | collective-permute-start | bytes 245768 | tf_op jit(solution)/shard_map/ppermute | solution.py:358
  16.9 10.2 %collective-permute-start.8 = (bf16[5,4,2048]{2,1,0:T(4,128)(2,1)S(1)}, bf16[5,4,2048]{2,1,0:T(4,128)(2,1)S(1)}, u32[]{:S(2)}, u32[]{:S(2)}) collective-permute-start(bf16[5,4,2048]{2,1,0:T(4,128)(2,1)S(1)} %shard_map.75.refs_0_), channel_id=1, source_target_pairs={{0,10},{2,12},{4,14},{6,0},{8,2},{10,4},{12,6},{14,8},{1,11},{3,13... | collective-permute-start | bytes 245768 | tf_op jit(solution)/shard_map/ppermute | solution.py:358
  16.9 12.6 %collective-permute-start.7 = (bf16[5,4,2048]{2,1,0:T(4,128)(2,1)S(1)}, bf16[5,4,2048]{2,1,0:T(4,128)(2,1)S(1)}, u32[]{:S(2)}, u32[]{:S(2)}) collective-permute-start(bf16[5,4,2048]{2,1,0:T(4,128)(2,1)S(1)} %shard_map.75.refs_0_), channel_id=1, source_target_pairs={{0,6},{2,8},{4,10},{6,12},{8,14},{10,0},{12,2},{14,4},{1,7},{3,9},... | collective-permute-start | bytes 245768 | tf_op jit(solution)/shard_map/ppermute | solution.py:358
  20.8 9.1 %collective-permute-start.6 = (bf16[5,4,2048]{2,1,0:T(4,128)(2,1)S(1)}, bf16[5,4,2048]{2,1,0:T(4,128)(2,1)S(1)}, u32[]{:S(2)}, u32[]{:S(2)}) collective-permute-start(bf16[5,4,2048]{2,1,0:T(4,128)(2,1)S(1)} %shard_map.75.refs_0_), channel_id=1, source_target_pairs={{0,12},{2,14},{4,0},{6,2},{8,4},{10,6},{12,8},{14,10},{1,13},{3,15... | collective-permute-start | bytes 245768 | tf_op jit(solution)/shard_map/ppermute | solution.py:358
  21.7 8.3 %collective-permute-start.5 = (bf16[5,4,2048]{2,1,0:T(4,128)(2,1)S(1)}, bf16[5,4,2048]{2,1,0:T(4,128)(2,1)S(1)}, u32[]{:S(2)}, u32[]{:S(2)}) collective-permute-start(bf16[5,4,2048]{2,1,0:T(4,128)(2,1)S(1)} %shard_map.75.refs_0_), channel_id=1, source_target_pairs={{0,4},{2,6},{4,8},{6,10},{8,12},{10,14},{12,0},{14,2},{1,5},{3,7},... | collective-permute-start | bytes 245768 | tf_op jit(solution)/shard_map/ppermute | solution.py:358
  23.7 7.2 %collective-permute-start.4 = (bf16[5,4,2048]{2,1,0:T(4,128)(2,1)S(1)}, bf16[5,4,2048]{2,1,0:T(4,128)(2,1)S(1)}, u32[]{:S(2)}, u32[]{:S(2)}) collective-permute-start(bf16[5,4,2048]{2,1,0:T(4,128)(2,1)S(1)} %shard_map.75.refs_0_), channel_id=1, source_target_pairs={{0,14},{2,0},{4,2},{6,4},{8,6},{10,8},{12,10},{14,12},{1,15},{3,1}... | collective-permute-start | bytes 245768 | tf_op jit(solution)/shard_map/ppermute | solution.py:358
  27.1 5.7 %collective-permute-start.3 = (bf16[5,4,2048]{2,1,0:T(4,128)(2,1)S(1)}, bf16[5,4,2048]{2,1,0:T(4,128)(2,1)S(1)}, u32[]{:S(2)}, u32[]{:S(2)}) collective-permute-start(bf16[5,4,2048]{2,1,0:T(4,128)(2,1)S(1)} %shard_map.75.refs_0_), channel_id=1, source_target_pairs={{0,2},{2,4},{4,6},{6,8},{8,10},{10,12},{12,14},{14,0},{1,3},{3,5},... | collective-permute-start | bytes 245768 | tf_op jit(solution)/shard_map/ppermute | solution.py:358
  34.2 18.8 %copy-start = (bf16[2,2,16,2048]{3,2,1,0:T(8,128)(2,1)}, bf16[2,2,16,2048]{3,2,1,0:T(8,128)(2,1)S(1)}, u32[]{:S(2)}) copy-start(bf16[2,2,16,2048]{3,2,1,0:T(8,128)(2,1)S(1)} %get-tuple-element.47.refs_7_) | copy-start | bytes 786436
  34.2 9.9 %collective-permute-start.13 = (bf16[2,2,16,2048]{3,2,1,0:T(8,128)(2,1)S(1)}, bf16[2,2,16,2048]{3,2,1,0:T(8,128)(2,1)S(1)}, u32[]{:S(2)}, u32[]{:S(2)}) collective-permute-start(bf16[2,2,16,2048]{3,2,1,0:T(8,128)(2,1)S(1)} %get-tuple-element.47.refs_7_), channel_id=1, source_target_pairs={{0,64},{32,96},{64,0},{96,32},{1,65},{33,97},{65,1},{97,33},{2,66}... | collective-permute-start | bytes 786440 | tf_op jit(solution)/shard_map/ppermute | solution.py:358
  37.3 9.8 %collective-permute-start.12 = (bf16[2,2,16,2048]{3,2,1,0:T(8,128)(2,1)S(1)}, bf16[2,2,16,2048]{3,2,1,0:T(8,128)(2,1)S(1)}, u32[]{:S(2)}, u32[]{:S(2)}) collective-permute-start(bf16[2,2,16,2048]{3,2,1,0:T(8,128)(2,1)S(1)} %get-tuple-element.47.refs_7_), channel_id=1, source_target_pairs={{0,96},{32,0},{64,32},{96,64},{1,97},{33,1},{65,33},{97,65},{2,98}... | collective-permute-start | bytes 786440 | tf_op jit(solution)/shard_map/ppermute | solution.py:358
  38.4 9.0 %collective-permute-start.11 = (bf16[2,2,16,2048]{3,2,1,0:T(8,128)(2,1)S(1)}, bf16[2,2,16,2048]{3,2,1,0:T(8,128)(2,1)S(1)}, u32[]{:S(2)}, u32[]{:S(2)}) collective-permute-start(bf16[2,2,16,2048]{3,2,1,0:T(8,128)(2,1)S(1)} %get-tuple-element.47.refs_7_), channel_id=1, source_target_pairs={{0,32},{32,64},{64,96},{96,0},{1,33},{33,65},{65,97},{97,1},{2,34}... | collective-permute-start | bytes 786440 | tf_op jit(solution)/shard_map/ppermute | solution.py:358
  39.4 12.6 %collective-permute-start.18 = (bf16[2,128,1024]{2,1,0:T(8,128)(2,1)S(1)}, bf16[2,128,1024]{2,1,0:T(8,128)(2,1)S(1)}, u32[]{:S(2)}, u32[]{:S(2)}) collective-permute-start(bf16[2,128,1024]{2,1,0:T(8,128)(2,1)S(1)} %get-tuple-element.48), channel_id=1, source_target_pairs={{0,1},{1,2},{2,3},{3,4},{4,5},{5,6},{6,7},{7,8},{8,9},{9,10},{10,1... | collective-permute-start | bytes 1572872 | tf_op jit(solution)/shard_map/ppermute | solution.py:385
  42.8 4.9 %collective-permute-start.14 = (bf16[2,2,16,2048]{3,2,1,0:T(8,128)(2,1)S(1)}, bf16[2,2,16,2048]{3,2,1,0:T(8,128)(2,1)}, u32[]{:S(2)}, u32[]{:S(2)}) collective-permute-start(bf16[2,2,16,2048]{3,2,1,0:T(8,128)(2,1)S(1)} %get-tuple-element.47.refs_7_), channel_id=1, source_target_pairs={{0,16},{16,0},{1,17},{17,1},{2,18},{18,2},{3,19},{19,3},{4,20},{20... | collective-permute-start | bytes 786440 | tf_op jit(solution)/shard_map/ppermute | solution.py:358
  44.1 8.9 %copy-start.5 = (bf16[2,2,16,2048]{3,2,1,0:T(8,128)(2,1)}, bf16[2,2,16,2048]{3,2,1,0:T(8,128)(2,1)S(1)}, u32[]{:S(2)}) copy-start(bf16[2,2,16,2048]{3,2,1,0:T(8,128)(2,1)S(1)} %collective-permute-done.13.refs_10_) | copy-start | bytes 786436
  44.1 7.8 %collective-permute-start.17 = (bf16[2,2,16,2048]{3,2,1,0:T(8,128)(2,1)S(1)}, bf16[2,2,16,2048]{3,2,1,0:T(8,128)(2,1)S(1)}, u32[]{:S(2)}, u32[]{:S(2)}) collective-permute-start(bf16[2,2,16,2048]{3,2,1,0:T(8,128)(2,1)S(1)} %collective-permute-done.13.refs_10_), channel_id=1, source_target_pairs={{0,16},{16,0},{1,17},{17,1},{2,18},{18,2},{3,19},{19,3},{4,20},{20... | collective-permute-start | bytes 786440 | tf_op jit(solution)/shard_map/ppermute | solution.py:358
  47.2 5.8 %copy-start.6 = (bf16[2,2,16,2048]{3,2,1,0:T(8,128)(2,1)}, bf16[2,2,16,2048]{3,2,1,0:T(8,128)(2,1)S(1)}, u32[]{:S(2)}) copy-start(bf16[2,2,16,2048]{3,2,1,0:T(8,128)(2,1)S(1)} %collective-permute-done.12.refs_9_) | copy-start | bytes 786436
  47.2 4.7 %collective-permute-start.16 = (bf16[2,2,16,2048]{3,2,1,0:T(8,128)(2,1)S(1)}, bf16[2,2,16,2048]{3,2,1,0:T(8,128)(2,1)S(1)}, u32[]{:S(2)}, u32[]{:S(2)}) collective-permute-start(bf16[2,2,16,2048]{3,2,1,0:T(8,128)(2,1)S(1)} %collective-permute-done.12.refs_9_), channel_id=1, source_target_pairs={{0,16},{16,0},{1,17},{17,1},{2,18},{18,2},{3,19},{19,3},{4,20},{20... | collective-permute-start | bytes 786440 | tf_op jit(solution)/shard_map/ppermute | solution.py:358
  47.4 5.4 %copy-start.7 = (bf16[2,2,16,2048]{3,2,1,0:T(8,128)(2,1)}, bf16[2,2,16,2048]{3,2,1,0:T(8,128)(2,1)S(1)}, u32[]{:S(2)}) copy-start(bf16[2,2,16,2048]{3,2,1,0:T(8,128)(2,1)S(1)} %collective-permute-done.11.refs_8_) | copy-start | bytes 786436
  47.4 4.5 %collective-permute-start.15 = (bf16[2,2,16,2048]{3,2,1,0:T(8,128)(2,1)S(1)}, bf16[2,2,16,2048]{3,2,1,0:T(8,128)(2,1)S(1)}, u32[]{:S(2)}, u32[]{:S(2)}) collective-permute-start(bf16[2,2,16,2048]{3,2,1,0:T(8,128)(2,1)S(1)} %collective-permute-done.11.refs_8_), channel_id=1, source_target_pairs={{0,16},{16,0},{1,17},{17,1},{2,18},{18,2},{3,19},{19,3},{4,20},{20... | collective-permute-start | bytes 786440 | tf_op jit(solution)/shard_map/ppermute | solution.py:358
  47.7 17.8 %collective-permute-start.10 = (bf16[2,128,1024]{2,1,0:T(8,128)(2,1)}, bf16[2,128,1024]{2,1,0:T(8,128)(2,1)S(1)}, u32[]{:S(2)}, u32[]{:S(2)}) collective-permute-start(bf16[2,128,1024]{2,1,0:T(8,128)(2,1)} %get-tuple-element.44), channel_id=1, source_target_pairs={{0,1},{1,2},{2,3},{3,4},{4,5},{5,6},{6,7},{7,8},{8,9},{9,10},{10,1... | collective-permute-start | bytes 1572872 | tf_op jit(solution)/shard_map/ppermute | solution.py:385
  51.9 0.9 copy-start.8
  51.9 1.0 copy-start.9
  51.9 1.0 copy-start.10
  52.0 0.8 copy-start.1
  53.0 1.0 copy-start.2
  63.5 16.6 %collective-permute-start.19 = (bf16[2,128,1024]{2,1,0:T(8,128)(2,1)S(1)}, bf16[2,128,1024]{2,1,0:T(8,128)(2,1)S(1)}, u32[]{:S(2)}, u32[]{:S(2)}) collective-permute-start(bf16[2,128,1024]{2,1,0:T(8,128)(2,1)S(1)} %get-tuple-element.61), channel_id=1, source_target_pairs={{1,0},{2,1},{3,2},{4,3},{5,4},{6,5},{7,6},{8,7},{9,8},{10,9},{11,1... | collective-permute-start | bytes 1572872 | tf_op jit(solution)/shard_map/ppermute | solution.py:396
  75.1 5.0 %collective-permute-start.22 = (bf16[2,2,2,16,2048]{4,3,2,1,0:T(8,128)(2,1)S(1)}, bf16[2,2,2,16,2048]{4,3,2,1,0:T(8,128)(2,1)S(1)}, u32[]{:S(2)}, u32[]{:S(2)}) collective-permute-start(bf16[2,2,2,16,2048]{4,3,2,1,0:T(8,128)(2,1)S(1)} %get-tuple-element.67), channel_id=1, source_target_pairs={{0,16},{16,0},{1,17},{17,1},{2,18},{18,2},{3,19},{19,3},{4,20},{20... | collective-permute-start | bytes 1572872 | tf_op jit(solution)/shard_map/ppermute | solution.py:358
  80.2 1.9 %collective-permute-start.21 = (bf16[2,2,2,16,2048]{4,3,2,1,0:T(8,128)(2,1)S(1)}, bf16[2,2,2,16,2048]{4,3,2,1,0:T(8,128)(2,1)S(1)}, u32[]{:S(2)}, u32[]{:S(2)}) collective-permute-start(bf16[2,2,2,16,2048]{4,3,2,1,0:T(8,128)(2,1)S(1)} %get-tuple-element.66), channel_id=1, source_target_pairs={{0,16},{16,0},{1,17},{17,1},{2,18},{18,2},{3,19},{19,3},{4,20},{20... | collective-permute-start | bytes 1572872 | tf_op jit(solution)/shard_map/ppermute | solution.py:358
  82.3 10.8 %collective-permute-start.23 = (bf16[2,2,16,2048]{3,2,1,0:T(8,128)(2,1)S(1)}, bf16[2,2,16,2048]{3,2,1,0:T(8,128)(2,1)S(1)}, u32[]{:S(2)}, u32[]{:S(2)}) collective-permute-start(bf16[2,2,16,2048]{3,2,1,0:T(8,128)(2,1)S(1)} %get-tuple-element.86), channel_id=1, source_target_pairs={{0,64},{32,96},{64,0},{96,32},{1,65},{33,97},{65,1},{97,33},{2,66}... | collective-permute-start | bytes 786440 | tf_op jit(solution)/shard_map/ppermute | solution.py:358
  85.4 12.5 %collective-permute-start.25 = (bf16[2,2,16,2048]{3,2,1,0:T(8,128)(2,1)S(1)}, bf16[2,2,16,2048]{3,2,1,0:T(8,128)(2,1)S(1)}, u32[]{:S(2)}, u32[]{:S(2)}) collective-permute-start(bf16[2,2,16,2048]{3,2,1,0:T(8,128)(2,1)S(1)} %get-tuple-element.87), channel_id=1, source_target_pairs={{0,32},{32,64},{64,96},{96,0},{1,33},{33,65},{65,97},{97,1},{2,34}... | collective-permute-start | bytes 786440 | tf_op jit(solution)/shard_map/ppermute | solution.py:358
  85.9 12.0 %collective-permute-start.24 = (bf16[2,2,16,2048]{3,2,1,0:T(8,128)(2,1)S(1)}, bf16[2,2,16,2048]{3,2,1,0:T(8,128)(2,1)S(1)}, u32[]{:S(2)}, u32[]{:S(2)}) collective-permute-start(bf16[2,2,16,2048]{3,2,1,0:T(8,128)(2,1)S(1)} %get-tuple-element.88), channel_id=1, source_target_pairs={{0,96},{32,0},{64,32},{96,64},{1,97},{33,1},{65,33},{97,65},{2,98}... | collective-permute-start | bytes 786440 | tf_op jit(solution)/shard_map/ppermute | solution.py:358
  88.6 15.9 %collective-permute-start.20 = (bf16[2,128,1024]{2,1,0:T(8,128)(2,1)S(1)}, bf16[2,128,1024]{2,1,0:T(8,128)(2,1)S(1)}, u32[]{:S(2)}, u32[]{:S(2)}) collective-permute-start(bf16[2,128,1024]{2,1,0:T(8,128)(2,1)S(1)} %get-tuple-element.64), channel_id=1, source_target_pairs={{1,0},{2,1},{3,2},{4,3},{5,4},{6,5},{7,6},{8,7},{9,8},{10,9},{11,1... | collective-permute-start | bytes 1572872 | tf_op jit(solution)/shard_map/ppermute | solution.py:396
  105.2 13.5 %collective-permute-start.26 = (bf16[5,4,2048]{2,1,0:T(4,128)(2,1)S(1)}, bf16[5,4,2048]{2,1,0:T(4,128)(2,1)S(1)}, u32[]{:S(2)}, u32[]{:S(2)}) collective-permute-start(bf16[5,4,2048]{2,1,0:T(4,128)(2,1)S(1)} %get-tuple-element.73), channel_id=1, source_target_pairs={{0,8},{2,10},{4,12},{6,14},{8,0},{10,2},{12,4},{14,6},{1,9},{3,11}... | collective-permute-start | bytes 245768 | tf_op jit(solution)/shard_map/ppermute | solution.py:358
  108.9 12.8 %collective-permute-start.27 = (bf16[5,4,2048]{2,1,0:T(4,128)(2,1)S(1)}, bf16[5,4,2048]{2,1,0:T(4,128)(2,1)S(1)}, u32[]{:S(2)}, u32[]{:S(2)}) collective-permute-start(bf16[5,4,2048]{2,1,0:T(4,128)(2,1)S(1)} %get-tuple-element.74), channel_id=1, source_target_pairs={{0,6},{2,8},{4,10},{6,12},{8,14},{10,0},{12,2},{14,4},{1,7},{3,9},... | collective-permute-start | bytes 245768 | tf_op jit(solution)/shard_map/ppermute | solution.py:358
  113.8 12.1 %collective-permute-start.28 = (bf16[5,4,2048]{2,1,0:T(4,128)(2,1)S(1)}, bf16[5,4,2048]{2,1,0:T(4,128)(2,1)S(1)}, u32[]{:S(2)}, u32[]{:S(2)}) collective-permute-start(bf16[5,4,2048]{2,1,0:T(4,128)(2,1)S(1)} %get-tuple-element.75), channel_id=1, source_target_pairs={{0,10},{2,12},{4,14},{6,0},{8,2},{10,4},{12,6},{14,8},{1,11},{3,13... | collective-permute-start | bytes 245768 | tf_op jit(solution)/shard_map/ppermute | solution.py:358
  113.9 12.0 %collective-permute-start.29 = (bf16[5,4,2048]{2,1,0:T(4,128)(2,1)S(1)}, bf16[5,4,2048]{2,1,0:T(4,128)(2,1)S(1)}, u32[]{:S(2)}, u32[]{:S(2)}) collective-permute-start(bf16[5,4,2048]{2,1,0:T(4,128)(2,1)S(1)} %get-tuple-element.76), channel_id=1, source_target_pairs={{0,4},{2,6},{4,8},{6,10},{8,12},{10,14},{12,0},{14,2},{1,5},{3,7},... | collective-permute-start | bytes 245768 | tf_op jit(solution)/shard_map/ppermute | solution.py:358
  118.7 8.1 %collective-permute-start.30 = (bf16[5,4,2048]{2,1,0:T(4,128)(2,1)S(1)}, bf16[5,4,2048]{2,1,0:T(4,128)(2,1)S(1)}, u32[]{:S(2)}, u32[]{:S(2)}) collective-permute-start(bf16[5,4,2048]{2,1,0:T(4,128)(2,1)S(1)} %get-tuple-element.77), channel_id=1, source_target_pairs={{0,12},{2,14},{4,0},{6,2},{8,4},{10,6},{12,8},{14,10},{1,13},{3,15... | collective-permute-start | bytes 245768 | tf_op jit(solution)/shard_map/ppermute | solution.py:358
  118.7 8.1 %collective-permute-start.31 = (bf16[5,4,2048]{2,1,0:T(4,128)(2,1)S(1)}, bf16[5,4,2048]{2,1,0:T(4,128)(2,1)S(1)}, u32[]{:S(2)}, u32[]{:S(2)}) collective-permute-start(bf16[5,4,2048]{2,1,0:T(4,128)(2,1)S(1)} %get-tuple-element.78), channel_id=1, source_target_pairs={{0,2},{2,4},{4,6},{6,8},{8,10},{10,12},{12,14},{14,0},{1,3},{3,5},... | collective-permute-start | bytes 245768 | tf_op jit(solution)/shard_map/ppermute | solution.py:358
  121.7 6.3 %collective-permute-start.32 = (bf16[5,4,2048]{2,1,0:T(4,128)(2,1)S(1)}, bf16[5,4,2048]{2,1,0:T(4,128)(2,1)S(1)}, u32[]{:S(2)}, u32[]{:S(2)}) collective-permute-start(bf16[5,4,2048]{2,1,0:T(4,128)(2,1)S(1)} %get-tuple-element.79), channel_id=1, source_target_pairs={{0,14},{2,0},{4,2},{6,4},{8,6},{10,8},{12,10},{14,12},{1,15},{3,1}... | collective-permute-start | bytes 245768 | tf_op jit(solution)/shard_map/ppermute | solution.py:358
  128.2 5.2 %collective-permute-start.34 = (bf16[2,2048]{1,0:T(2,128)(2,1)S(1)}, bf16[2,2048]{1,0:T(2,128)(2,1)S(1)}, u32[]{:S(2)}, u32[]{:S(2)}) collective-permute-start(bf16[2,2048]{1,0:T(2,128)(2,1)S(1)} %bitcast.32), channel_id=1, source_target_pairs={{0,128},{128,0},{1,129},{129,1},{2,130},{130,2},{3,131},{131,3},{4... | collective-permute-start | bytes 24584 | tf_op jit(solution)/shard_map/ppermute | solution.py:358
  130.0 3.7 %collective-permute-start.35 = (bf16[2,2048]{1,0:T(2,128)(2,1)S(1)}, bf16[2,2048]{1,0:T(2,128)(2,1)S(1)}, u32[]{:S(2)}, u32[]{:S(2)}) collective-permute-start(bf16[2,2048]{1,0:T(2,128)(2,1)S(1)} %bitcast.31), channel_id=1, source_target_pairs={{0,129},{1,128},{128,1},{129,0},{2,131},{3,130},{130,3},{131,2},{4... | collective-permute-start | bytes 24584 | tf_op jit(solution)/shard_map/ppermute | solution.py:412
  131.2 4.0 %collective-permute-start.33 = (bf16[2,4,2048]{2,1,0:T(4,128)(2,1)S(1)}, bf16[2,4,2048]{2,1,0:T(4,128)(2,1)S(1)}, u32[]{:S(2)}, u32[]{:S(2)}) collective-permute-start(bf16[2,4,2048]{2,1,0:T(4,128)(2,1)S(1)} %slice.64), channel_id=1, source_target_pairs={{0,1},{1,0},{2,3},{3,2},{4,5},{5,4},{6,7},{7,6},{8,9},{9,8},{10,11... | collective-permute-start | bytes 98312 | tf_op jit(solution)/shard_map/ppermute | solution.py:358

commit v7 on v6

--- a/solution.py
+++ b/solution.py
@@ -24,7 +24,7 @@
 N3 = N3G * NXH * NY * NC
 NP = N2 + N3
 HPB = 4
-Z_ORDER = (4, 5, 3, 6, 2, 7, 1)
+Z_ORDER = (3, 5, 4, 2, 6, 1, 7)
 Y_STEP = (0, 1, 3, 2)
 DIAGONAL = ((0, 3), (1, 2), (2, 1), (3, 0))
 

time: 140 us -> 138 us (0.986); the launches traced: 137 us -> 138 us
  waiting for transfers between devices: 32.9 us -> 36 us
  starting transfers between devices: 74.3 us -> 72 us
    ppermute x2, starting transfers between devices: 7.54 us -> 10 us  [per_device(): lax.ppermute(x, AXES, [(i, i + 1) for i in range(count - 1)])]
    ppermute x30, waiting for transfers between devices: 23.4 us -> 25.7 us  [ring(): lax.ppermute(value, axis, [(i, (i + step) % size) for i in range(size)])]
    ppermute x2, starting transfers between devices: 5.94 us -> 3.93 us  [per_device(): lax.ppermute(dprior, AXES, [(i + 1, i) for i in range(count - 1)])]
    ppermute x30, starting transfers between devices: 58 us -> 56.4 us  [ring(): lax.ppermute(value, axis, [(i, (i + step) % size) for i in range(size)])]
where the time goes in v7:
time: 138 us
  starting transfers between devices  72 us (52%)
  waiting for transfers between devices  36 us (26%)
  Pallas kernels  23.4 us (17%)
  other arithmetic  3.67 us (3%)
  local copies, waits for them, and re-layouts  2.32 us (2%)
    ppermute x30, starting transfers between devices, ring(): lax.ppermute(value, axis, [(i, (i + step) % size) for i in range(size)])  56.4 us
    ppermute x30, waiting for transfers between devices, ring(): lax.ppermute(value, axis, [(i, (i + step) % size) for i in range(size)])  25.7 us
    pallas_call x2, Pallas kernels, attention(): pl.pallas_call(attn_kernel, grid=(steps,), in_specs=[pl.BlockSpec(memory_...  19.1 us
    ppermute x2, waiting for transfers between devices, per_device(): lax.ppermute(dprior, AXES, [(i + 1, i) for i in range(count - 1)])  10.2 us
    ppermute x2, starting transfers between devices, per_device(): lax.ppermute(x, AXES, [(i, i + 1) for i in range(count - 1)])  10 us
    ppermute x2, starting transfers between devices, per_device(): lax.ppermute(dprior, AXES, [(i + 1, i) for i in range(count - 1)])  3.93 us
  transfers between devices with their start and end apart: 36, of which 19 were waited for; matrix products, arithmetic and copies ran while one was open for 1% of the time, Pallas kernels for 14%

profile of v7, /device:TPU:2, one launch (start us, length us, event | category | flops | bytes accessed | tf_op | source)
XLA Modules:
  0.0 138.2 jit_solution(2122532882529874539)
XLA Ops:
  0.6 2.1 %convert_reduce_fusion = f32[2,4,2048]{2,1,0:T(4,128)S(1)} fusion(bf16[1,4,64,2048]{3,2,1,0:T(8,128)(2,1)} %bitcast.30, bf16[1,4,64,2048]{3,2,1,0:T(8,128)(2,1)} %bitcast.29), kind=kLoop, calls=%fused_computation | loop fusion | flops 3129344 | bytes 2162688 | tf_op jit(solution)/shard_map/reduce_sum | solution.py:235
  2.8 1.6 %collective-permute-start.2 = (bf16[2,2048]{1,0:T(2,128)(2,1)S(1)}, bf16[2,2048]{1,0:T(2,128)(2,1)S(1)}, u32[]{:S(2)}, u32[]{:S(2)}) collective-permute-start(bf16[2,2048]{1,0:T(2,128)(2,1)S(1)} %multiply_convert_fusion.1), channel_id=1, source_target_pairs={{0,129},{1,128},{128,1},{129,0},{2,131},{3,130},{130,3},{131,2},{4... | collective-permute-start | bytes 24584 | tf_op jit(solution)/shard_map/ppermute | solution.py:375
  4.4 2.8 %collective-permute-start.1 = (bf16[2,2048]{1,0:T(2,128)(2,1)S(1)}, bf16[2,2048]{1,0:T(2,128)(2,1)S(1)}, u32[]{:S(2)}, u32[]{:S(2)}) collective-permute-start(bf16[2,2048]{1,0:T(2,128)(2,1)S(1)} %multiply_convert_fusion.1), channel_id=1, source_target_pairs={{0,128},{128,0},{1,129},{129,1},{2,130},{130,2},{3,131},{131,3},{4... | collective-permute-start | bytes 24584 | tf_op jit(solution)/shard_map/ppermute | solution.py:358
  7.3 2.3 %collective-permute-done.1.near_ref = bf16[2,2048]{1,0:T(2,128)(2,1)S(1)} collective-permute-done((bf16[2,2048]{1,0:T(2,128)(2,1)S(1)}, bf16[2,2048]{1,0:T(2,128)(2,1)S(1)}, u32[]{:S(2)}, u32[]{:S(2)}) %collective-permute-start.1) | collective-permute-done | bytes 8224 | tf_op jit(solution)/shard_map/ppermute | solution.py:358
  9.5 1.6 %collective-permute-done.other_ref = bf16[2,4,2048]{2,1,0:T(4,128)(2,1)S(1)} collective-permute-done((bf16[2,4,2048]{2,1,0:T(4,128)(2,1)S(1)}, bf16[2,4,2048]{2,1,0:T(4,128)(2,1)S(1)}, u32[]{:S(2)}, u32[]{:S(2)}) %collective-permute-start) | collective-permute-done | bytes 32800 | tf_op jit(solution)/shard_map/ppermute | solution.py:358
  11.2 3.1 %collective-permute-start.9 = (bf16[5,4,2048]{2,1,0:T(4,128)(2,1)S(1)}, bf16[5,4,2048]{2,1,0:T(4,128)(2,1)S(1)}, u32[]{:S(2)}, u32[]{:S(2)}) collective-permute-start(bf16[5,4,2048]{2,1,0:T(4,128)(2,1)S(1)} %shard_map.75.refs_0_), channel_id=1, source_target_pairs={{0,6},{2,8},{4,10},{6,12},{8,14},{10,0},{12,2},{14,4},{1,7},{3,9},... | collective-permute-start | bytes 245768 | tf_op jit(solution)/shard_map/ppermute | solution.py:358
  14.3 2.2 %collective-permute-start.8 = (bf16[5,4,2048]{2,1,0:T(4,128)(2,1)S(1)}, bf16[5,4,2048]{2,1,0:T(4,128)(2,1)S(1)}, u32[]{:S(2)}, u32[]{:S(2)}) collective-permute-start(bf16[5,4,2048]{2,1,0:T(4,128)(2,1)S(1)} %shard_map.75.refs_0_), channel_id=1, source_target_pairs={{0,10},{2,12},{4,14},{6,0},{8,2},{10,4},{12,6},{14,8},{1,11},{3,13... | collective-permute-start | bytes 245768 | tf_op jit(solution)/shard_map/ppermute | solution.py:358
  16.5 5.5 %collective-permute-start.7 = (bf16[5,4,2048]{2,1,0:T(4,128)(2,1)S(1)}, bf16[5,4,2048]{2,1,0:T(4,128)(2,1)S(1)}, u32[]{:S(2)}, u32[]{:S(2)}) collective-permute-start(bf16[5,4,2048]{2,1,0:T(4,128)(2,1)S(1)} %shard_map.75.refs_0_), channel_id=1, source_target_pairs={{0,8},{2,10},{4,12},{6,14},{8,0},{10,2},{12,4},{14,6},{1,9},{3,11}... | collective-permute-start | bytes 245768 | tf_op jit(solution)/shard_map/ppermute | solution.py:358
  22.0 1.5 %collective-permute-start.6 = (bf16[5,4,2048]{2,1,0:T(4,128)(2,1)S(1)}, bf16[5,4,2048]{2,1,0:T(4,128)(2,1)S(1)}, u32[]{:S(2)}, u32[]{:S(2)}) collective-permute-start(bf16[5,4,2048]{2,1,0:T(4,128)(2,1)S(1)} %shard_map.75.refs_0_), channel_id=1, source_target_pairs={{0,4},{2,6},{4,8},{6,10},{8,12},{10,14},{12,0},{14,2},{1,5},{3,7},... | collective-permute-start | bytes 245768 | tf_op jit(solution)/shard_map/ppermute | solution.py:358
  23.5 2.7 %collective-permute-start.5 = (bf16[5,4,2048]{2,1,0:T(4,128)(2,1)S(1)}, bf16[5,4,2048]{2,1,0:T(4,128)(2,1)S(1)}, u32[]{:S(2)}, u32[]{:S(2)}) collective-permute-start(bf16[5,4,2048]{2,1,0:T(4,128)(2,1)S(1)} %shard_map.75.refs_0_), channel_id=1, source_target_pairs={{0,12},{2,14},{4,0},{6,2},{8,4},{10,6},{12,8},{14,10},{1,13},{3,15... | collective-permute-start | bytes 245768 | tf_op jit(solution)/shard_map/ppermute | solution.py:358
  26.2 1.0 collective-permute-start.4
  27.2 2.2 %collective-permute-start.3 = (bf16[5,4,2048]{2,1,0:T(4,128)(2,1)S(1)}, bf16[5,4,2048]{2,1,0:T(4,128)(2,1)S(1)}, u32[]{:S(2)}, u32[]{:S(2)}) collective-permute-start(bf16[5,4,2048]{2,1,0:T(4,128)(2,1)S(1)} %shard_map.75.refs_0_), channel_id=1, source_target_pairs={{0,14},{2,0},{4,2},{6,4},{8,6},{10,8},{12,10},{14,12},{1,15},{3,1}... | collective-permute-start | bytes 245768 | tf_op jit(solution)/shard_map/ppermute | solution.py:358
  29.4 0.9 pad_maximum_fusion
  30.3 1.2 collective-permute-done.5.refs_3_
  31.5 0.3 collective-permute-done.4.refs_2_
  31.8 2.4 %collective-permute-done.3.refs_1_ = bf16[5,4,2048]{2,1,0:T(4,128)(2,1)S(1)} collective-permute-done((bf16[5,4,2048]{2,1,0:T(4,128)(2,1)S(1)}, bf16[5,4,2048]{2,1,0:T(4,128)(2,1)S(1)}, u32[]{:S(2)}, u32[]{:S(2)}) %collective-permute-start.3) | collective-permute-done | bytes 81952 | tf_op jit(solution)/shard_map/ppermute | solution.py:358
  34.2 1.4 %shard_map.76 = (bf16[64,2048]{1,0:T(8,128)(2,1)}, bf16[64,2048]{1,0:T(8,128)(2,1)}, bf16[2,2,16,2048]{3,2,1,0:T(8,128)(2,1)S(1)}) custom-call(bf16[5,4,2048]{2,1,0:T(4,128)(2,1)S(1)} %shard_map.75.refs_0_, bf16[5,4,2048]{2,1,0:T(4,128)(2,1)S(1)} %collective-permute-done.3.refs_1_, bf16[5,4,2048]{2,1,0:T(4,128)(2,1)S(1)} %collective-permute-done.4.refs_2_, ...), custom_call_target="tpu_custom_call" | custom-call | flops 1048576 | bytes 1048576 | tf_op jit(solution)/shard_map/pallas_call | solution.py:276
  35.7 3.2 %collective-permute-start.13 = (bf16[2,2,16,2048]{3,2,1,0:T(8,128)(2,1)S(1)}, bf16[2,2,16,2048]{3,2,1,0:T(8,128)(2,1)S(1)}, u32[]{:S(2)}, u32[]{:S(2)}) collective-permute-start(bf16[2,2,16,2048]{3,2,1,0:T(8,128)(2,1)S(1)} %get-tuple-element.47.refs_7_), channel_id=1, source_target_pairs={{0,64},{32,96},{64,0},{96,32},{1,65},{33,97},{65,1},{97,33},{2,66}... | collective-permute-start | bytes 786440 | tf_op jit(solution)/shard_map/ppermute | solution.py:358
  38.8 1.1 collective-permute-start.12
  39.9 1.0 collective-permute-start.11
  40.9 5.2 %collective-permute-start.18 = (bf16[2,128,1024]{2,1,0:T(8,128)(2,1)S(1)}, bf16[2,128,1024]{2,1,0:T(8,128)(2,1)S(1)}, u32[]{:S(2)}, u32[]{:S(2)}) collective-permute-start(bf16[2,128,1024]{2,1,0:T(8,128)(2,1)S(1)} %get-tuple-element.48), channel_id=1, source_target_pairs={{0,1},{1,2},{2,3},{3,4},{4,5},{5,6},{6,7},{7,8},{8,9},{9,10},{10,1... | collective-permute-start | bytes 1572872 | tf_op jit(solution)/shard_map/ppermute | solution.py:385
  46.0 0.1 collective-permute-start.14
  46.2 0.5 collective-permute-start.17
  46.6 0.6 collective-permute-done.12.refs_9_
  47.3 0.2 collective-permute-done.11.refs_8_
  47.5 0.3 collective-permute-start.15
  47.8 4.9 %collective-permute-start.10 = (bf16[2,128,1024]{2,1,0:T(8,128)(2,1)}, bf16[2,128,1024]{2,1,0:T(8,128)(2,1)S(1)}, u32[]{:S(2)}, u32[]{:S(2)}) collective-permute-start(bf16[2,128,1024]{2,1,0:T(8,128)(2,1)} %get-tuple-element.44), channel_id=1, source_target_pairs={{0,1},{1,2},{2,3},{3,4},{4,5},{5,6},{6,7},{7,8},{8,9},{9,10},{10,1... | collective-permute-start | bytes 1572872 | tf_op jit(solution)/shard_map/ppermute | solution.py:385
  52.7 0.1 stack.50.place_ref
  52.8 0.8 copy-done.1
  53.7 0.1 copy-done.9
  53.8 0.1 copy-done.10
  53.9 1.0 copy-done.2
  54.9 9.5 %shard_map.77 = (bf16[256,2048]{1,0:T(8,128)(2,1)}, bf16[256,2048]{1,0:T(8,128)(2,1)}, bf16[256,2048]{1,0:T(8,128)(2,1)S(1)}, bf16[256,2048]{1,0:T(8,128)(2,1)S(...) custom-call(s32[5]{0:T(128)S(1)} %stack.50.place_ref, ...), custom_call_target="tpu_custom_call" | custom-call | flops 1811939328 | bytes 10485760 | tf_op jit(solution)/shard_map/pallas_call | solution.py:199
  64.4 1.9 %collective-permute-start.19 = (bf16[2,128,1024]{2,1,0:T(8,128)(2,1)S(1)}, bf16[2,128,1024]{2,1,0:T(8,128)(2,1)S(1)}, u32[]{:S(2)}, u32[]{:S(2)}) collective-permute-start(bf16[2,128,1024]{2,1,0:T(8,128)(2,1)S(1)} %get-tuple-element.61), channel_id=1, source_target_pairs={{1,0},{2,1},{3,2},{4,3},{5,4},{6,5},{7,6},{8,7},{9,8},{10,9},{11,1... | collective-permute-start | bytes 1572872 | tf_op jit(solution)/shard_map/ppermute | solution.py:396
  66.3 9.6 %shard_map.78 = (bf16[256,2048]{1,0:T(8,128)(2,1)}, bf16[256,2048]{1,0:T(8,128)(2,1)}, bf16[256,2048]{1,0:T(8,128)(2,1)S(1)}, bf16[256,2048]{1,0:T(8,128)(2,1)S(...) custom-call(s32[5]{0:T(128)S(1)} %stack.50.place_ref, ...), custom_call_target="tpu_custom_call", output_to_operand_aliasing={{0}: (16, {}), {1}: (17, {}), {2}: (18, {}), {3}: (19, {}),... | custom-call | flops 1811939328 | bytes 10485760 | tf_op jit(solution)/shard_map/pallas_call | solution.py:199
  76.0 1.2 collective-permute-start.22
  77.1 4.1 %collective-permute-done.19.lo_ref = bf16[2,128,1024]{2,1,0:T(8,128)(2,1)S(1)} collective-permute-done((bf16[2,128,1024]{2,1,0:T(8,128)(2,1)S(1)}, bf16[2,128,1024]{2,1,0:T(8,128)(2,1)S(1)}, u32[]{:S(2)}, u32[]{:S(2)}) %collective-permute-start.19) | collective-permute-done | bytes 524320 | tf_op jit(solution)/shard_map/ppermute | solution.py:396
  81.2 1.9 %collective-permute-done.21 = bf16[2,2,2,16,2048]{4,3,2,1,0:T(8,128)(2,1)S(1)} collective-permute-done((bf16[2,2,2,16,2048]{4,3,2,1,0:T(8,128)(2,1)S(1)}, bf16[2,2,2,16,2048]{4,3,2,1,0:T(8,128)(2,1)S(1)}, u32[]{:S(2)}, u32[]{:S(2)}) %collective-permute-start.21) | collective-permute-done | bytes 524320 | tf_op jit(solution)/shard_map/ppermute | solution.py:358
  83.1 0.3 fusion.2
  83.4 2.7 %collective-permute-start.23 = (bf16[2,2,16,2048]{3,2,1,0:T(8,128)(2,1)S(1)}, bf16[2,2,16,2048]{3,2,1,0:T(8,128)(2,1)S(1)}, u32[]{:S(2)}, u32[]{:S(2)}) collective-permute-start(bf16[2,2,16,2048]{3,2,1,0:T(8,128)(2,1)S(1)} %get-tuple-element.86), channel_id=1, source_target_pairs={{0,64},{32,96},{64,0},{96,32},{1,65},{33,97},{65,1},{97,33},{2,66}... | collective-permute-start | bytes 786440 | tf_op jit(solution)/shard_map/ppermute | solution.py:358
  86.1 0.5 collective-permute-start.25
  86.5 2.8 %collective-permute-start.24 = (bf16[2,2,16,2048]{3,2,1,0:T(8,128)(2,1)S(1)}, bf16[2,2,16,2048]{3,2,1,0:T(8,128)(2,1)S(1)}, u32[]{:S(2)}, u32[]{:S(2)}) collective-permute-start(bf16[2,2,16,2048]{3,2,1,0:T(8,128)(2,1)S(1)} %get-tuple-element.88), channel_id=1, source_target_pairs={{0,96},{32,0},{64,32},{96,64},{1,97},{33,1},{65,33},{97,65},{2,98}... | collective-permute-start | bytes 786440 | tf_op jit(solution)/shard_map/ppermute | solution.py:358
  89.3 2.0 %collective-permute-start.20 = (bf16[2,128,1024]{2,1,0:T(8,128)(2,1)S(1)}, bf16[2,128,1024]{2,1,0:T(8,128)(2,1)S(1)}, u32[]{:S(2)}, u32[]{:S(2)}) collective-permute-start(bf16[2,128,1024]{2,1,0:T(8,128)(2,1)S(1)} %get-tuple-element.64), channel_id=1, source_target_pairs={{1,0},{2,1},{3,2},{4,3},{5,4},{6,5},{7,6},{8,7},{9,8},{10,9},{11,1... | collective-permute-start | bytes 1572872 | tf_op jit(solution)/shard_map/ppermute | solution.py:396
  91.3 2.9 %collective-permute-done.23 = bf16[2,2,16,2048]{3,2,1,0:T(8,128)(2,1)S(1)} collective-permute-done((bf16[2,2,16,2048]{3,2,1,0:T(8,128)(2,1)S(1)}, bf16[2,2,16,2048]{3,2,1,0:T(8,128)(2,1)S(1)}, u32[]{:S(2)}, u32[]{:S(2)}) %collective-permute-start.23) | collective-permute-done | bytes 262176 | tf_op jit(solution)/shard_map/ppermute | solution.py:358
  94.2 4.8 %collective-permute-done.25 = bf16[2,2,16,2048]{3,2,1,0:T(8,128)(2,1)S(1)} collective-permute-done((bf16[2,2,16,2048]{3,2,1,0:T(8,128)(2,1)S(1)}, bf16[2,2,16,2048]{3,2,1,0:T(8,128)(2,1)S(1)}, u32[]{:S(2)}, u32[]{:S(2)}) %collective-permute-start.25) | collective-permute-done | bytes 262176 | tf_op jit(solution)/shard_map/ppermute | solution.py:358
  99.0 0.2 fusion.1.third_ref
  99.1 6.1 %collective-permute-done.20.hi_ref = bf16[2,128,1024]{2,1,0:T(8,128)(2,1)S(1)} collective-permute-done((bf16[2,128,1024]{2,1,0:T(8,128)(2,1)S(1)}, bf16[2,128,1024]{2,1,0:T(8,128)(2,1)S(1)}, u32[]{:S(2)}, u32[]{:S(2)}) %collective-permute-start.20) | collective-permute-done | bytes 524320 | tf_op jit(solution)/shard_map/ppermute | solution.py:396
  105.2 0.7 shard_map.79
  105.9 2.4 %collective-permute-start.26 = (bf16[5,4,2048]{2,1,0:T(4,128)(2,1)S(1)}, bf16[5,4,2048]{2,1,0:T(4,128)(2,1)S(1)}, u32[]{:S(2)}, u32[]{:S(2)}) collective-permute-start(bf16[5,4,2048]{2,1,0:T(4,128)(2,1)S(1)} %get-tuple-element.73), channel_id=1, source_target_pairs={{0,10},{2,12},{4,14},{6,0},{8,2},{10,4},{12,6},{14,8},{1,11},{3,13... | collective-permute-start | bytes 245768 | tf_op jit(solution)/shard_map/ppermute | solution.py:358
  108.3 3.3 %collective-permute-start.27 = (bf16[5,4,2048]{2,1,0:T(4,128)(2,1)S(1)}, bf16[5,4,2048]{2,1,0:T(4,128)(2,1)S(1)}, u32[]{:S(2)}, u32[]{:S(2)}) collective-permute-start(bf16[5,4,2048]{2,1,0:T(4,128)(2,1)S(1)} %get-tuple-element.74), channel_id=1, source_target_pairs={{0,6},{2,8},{4,10},{6,12},{8,14},{10,0},{12,2},{14,4},{1,7},{3,9},... | collective-permute-start | bytes 245768 | tf_op jit(solution)/shard_map/ppermute | solution.py:358
  111.6 2.5 %collective-permute-start.28 = (bf16[5,4,2048]{2,1,0:T(4,128)(2,1)S(1)}, bf16[5,4,2048]{2,1,0:T(4,128)(2,1)S(1)}, u32[]{:S(2)}, u32[]{:S(2)}) collective-permute-start(bf16[5,4,2048]{2,1,0:T(4,128)(2,1)S(1)} %get-tuple-element.75), channel_id=1, source_target_pairs={{0,8},{2,10},{4,12},{6,14},{8,0},{10,2},{12,4},{14,6},{1,9},{3,11}... | collective-permute-start | bytes 245768 | tf_op jit(solution)/shard_map/ppermute | solution.py:358
  114.0 3.9 %collective-permute-start.29 = (bf16[5,4,2048]{2,1,0:T(4,128)(2,1)S(1)}, bf16[5,4,2048]{2,1,0:T(4,128)(2,1)S(1)}, u32[]{:S(2)}, u32[]{:S(2)}) collective-permute-start(bf16[5,4,2048]{2,1,0:T(4,128)(2,1)S(1)} %get-tuple-element.76), channel_id=1, source_target_pairs={{0,12},{2,14},{4,0},{6,2},{8,4},{10,6},{12,8},{14,10},{1,13},{3,15... | collective-permute-start | bytes 245768 | tf_op jit(solution)/shard_map/ppermute | solution.py:358
  117.9 5.4 %collective-permute-start.31 = (bf16[5,4,2048]{2,1,0:T(4,128)(2,1)S(1)}, bf16[5,4,2048]{2,1,0:T(4,128)(2,1)S(1)}, u32[]{:S(2)}, u32[]{:S(2)}) collective-permute-start(bf16[5,4,2048]{2,1,0:T(4,128)(2,1)S(1)} %get-tuple-element.78), channel_id=1, source_target_pairs={{0,14},{2,0},{4,2},{6,4},{8,6},{10,8},{12,10},{14,12},{1,15},{3,1}... | collective-permute-start | bytes 245768 | tf_op jit(solution)/shard_map/ppermute | solution.py:358
  123.3 0.5 collective-permute-done.28
  123.8 0.7 collective-permute-done.30
  124.5 0.9 collective-permute-done.31
  125.4 3.6 %collective-permute-done.32 = bf16[5,4,2048]{2,1,0:T(4,128)(2,1)S(1)} collective-permute-done((bf16[5,4,2048]{2,1,0:T(4,128)(2,1)S(1)}, bf16[5,4,2048]{2,1,0:T(4,128)(2,1)S(1)}, u32[]{:S(2)}, u32[]{:S(2)}) %collective-permute-start.32) | collective-permute-done | bytes 81952 | tf_op jit(solution)/shard_map/ppermute | solution.py:358
  129.0 0.2 fusion.5
  129.2 1.7 %collective-permute-start.34 = (bf16[2,2048]{1,0:T(2,128)(2,1)S(1)}, bf16[2,2048]{1,0:T(2,128)(2,1)S(1)}, u32[]{:S(2)}, u32[]{:S(2)}) collective-permute-start(bf16[2,2048]{1,0:T(2,128)(2,1)S(1)} %bitcast.32), channel_id=1, source_target_pairs={{0,128},{128,0},{1,129},{129,1},{2,130},{130,2},{3,131},{131,3},{4... | collective-permute-start | bytes 24584 | tf_op jit(solution)/shard_map/ppermute | solution.py:358
  130.9 3.2 %collective-permute-start.33 = (bf16[2,4,2048]{2,1,0:T(4,128)(2,1)S(1)}, bf16[2,4,2048]{2,1,0:T(4,128)(2,1)S(1)}, u32[]{:S(2)}, u32[]{:S(2)}) collective-permute-start(bf16[2,4,2048]{2,1,0:T(4,128)(2,1)S(1)} %slice.64), channel_id=1, source_target_pairs={{0,1},{1,0},{2,3},{3,2},{4,5},{5,4},{6,7},{7,6},{8,9},{9,8},{10,11... | collective-permute-start | bytes 98312 | tf_op jit(solution)/shard_map/ppermute | solution.py:358
  134.1 0.4 collective-permute-done.34
  134.5 0.1 collective-permute-done.35
  134.6 1.4 %collective-permute-done.33 = bf16[2,4,2048]{2,1,0:T(4,128)(2,1)S(1)} collective-permute-done((bf16[2,4,2048]{2,1,0:T(4,128)(2,1)S(1)}, bf16[2,4,2048]{2,1,0:T(4,128)(2,1)S(1)}, u32[]{:S(2)}, u32[]{:S(2)}) %collective-permute-start.33) | collective-permute-done | bytes 32800 | tf_op jit(solution)/shard_map/ppermute | solution.py:358
  136.0 2.1 %shard_map.80 = (bf16[256,2048]{1,0:T(8,128)(2,1)}, bf16[256,2048]{1,0:T(8,128)(2,1)}) custom-call(bf16[256,2048]{1,0:T(8,128)(2,1)S(1)} %get-tuple-element.59.dk_ref, bf16[256,2048]{1,0:T(8,128)(2,1)S(1)} %get-tuple-element.60.dv_ref, bf16[2,128,1024]{2,1,0:T(8,128)(2,1)S(1)} %collective-permute-done.19.lo_ref, ...), custom_call_target="tpu_custom_call" | custom-call | flops 1048576 | bytes 7340032 | tf_op jit(solution)/shard_map/pallas_call | solution.py:338
  (51 shorter events, 0.4 us)
Async XLA Ops:
  0.6 6.6 %copy-start.3 = (bf16[256,2048]{1,0:T(8,128)(2,1)S(1)}, bf16[256,2048]{1,0:T(8,128)(2,1)}, u32[]{:S(2)}) copy-start(bf16[256,2048]{1,0:T(8,128)(2,1)} %refs_1_.3) | copy-start | bytes 3145732
  2.7 13.8 %copy-start.4 = (bf16[256,2048]{1,0:T(8,128)(2,1)S(1)}, bf16[256,2048]{1,0:T(8,128)(2,1)}, u32[]{:S(2)}) copy-start(bf16[256,2048]{1,0:T(8,128)(2,1)} %refs_2_.3) | copy-start | bytes 3145732
  2.8 4.5 %collective-permute-start.2 = (bf16[2,2048]{1,0:T(2,128)(2,1)S(1)}, bf16[2,2048]{1,0:T(2,128)(2,1)S(1)}, u32[]{:S(2)}, u32[]{:S(2)}) collective-permute-start(bf16[2,2048]{1,0:T(2,128)(2,1)S(1)} %multiply_convert_fusion.1), channel_id=1, source_target_pairs={{0,129},{1,128},{128,1},{129,0},{2,131},{3,130},{130,3},{131,2},{4... | collective-permute-start | bytes 24584 | tf_op jit(solution)/shard_map/ppermute | solution.py:375
  4.4 5.2 %collective-permute-start.1 = (bf16[2,2048]{1,0:T(2,128)(2,1)S(1)}, bf16[2,2048]{1,0:T(2,128)(2,1)S(1)}, u32[]{:S(2)}, u32[]{:S(2)}) collective-permute-start(bf16[2,2048]{1,0:T(2,128)(2,1)S(1)} %multiply_convert_fusion.1), channel_id=1, source_target_pairs={{0,128},{128,0},{1,129},{129,1},{2,130},{130,2},{3,131},{131,3},{4... | collective-permute-start | bytes 24584 | tf_op jit(solution)/shard_map/ppermute | solution.py:358
  7.2 3.9 %collective-permute-start = (bf16[2,4,2048]{2,1,0:T(4,128)(2,1)S(1)}, bf16[2,4,2048]{2,1,0:T(4,128)(2,1)S(1)}, u32[]{:S(2)}, u32[]{:S(2)}) collective-permute-start(bf16[2,4,2048]{2,1,0:T(4,128)(2,1)S(1)} %get-tuple-element.85.mine_ref), channel_id=1, source_target_pairs={{0,1},{1,0},{2,3},{3,2},{4,5},{5,4},{6,7},{7,6},{8,9},{9,8},{10,11... | collective-permute-start | bytes 98312 | tf_op jit(solution)/shard_map/ppermute | solution.py:358
  11.2 15.0 %collective-permute-start.9 = (bf16[5,4,2048]{2,1,0:T(4,128)(2,1)S(1)}, bf16[5,4,2048]{2,1,0:T(4,128)(2,1)S(1)}, u32[]{:S(2)}, u32[]{:S(2)}) collective-permute-start(bf16[5,4,2048]{2,1,0:T(4,128)(2,1)S(1)} %shard_map.75.refs_0_), channel_id=1, source_target_pairs={{0,6},{2,8},{4,10},{6,12},{8,14},{10,0},{12,2},{14,4},{1,7},{3,9},... | collective-permute-start | bytes 245768 | tf_op jit(solution)/shard_map/ppermute | solution.py:358
  14.3 12.9 %collective-permute-start.8 = (bf16[5,4,2048]{2,1,0:T(4,128)(2,1)S(1)}, bf16[5,4,2048]{2,1,0:T(4,128)(2,1)S(1)}, u32[]{:S(2)}, u32[]{:S(2)}) collective-permute-start(bf16[5,4,2048]{2,1,0:T(4,128)(2,1)S(1)} %shard_map.75.refs_0_), channel_id=1, source_target_pairs={{0,10},{2,12},{4,14},{6,0},{8,2},{10,4},{12,6},{14,8},{1,11},{3,13... | collective-permute-start | bytes 245768 | tf_op jit(solution)/shard_map/ppermute | solution.py:358
  16.5 13.7 %collective-permute-start.7 = (bf16[5,4,2048]{2,1,0:T(4,128)(2,1)S(1)}, bf16[5,4,2048]{2,1,0:T(4,128)(2,1)S(1)}, u32[]{:S(2)}, u32[]{:S(2)}) collective-permute-start(bf16[5,4,2048]{2,1,0:T(4,128)(2,1)S(1)} %shard_map.75.refs_0_), channel_id=1, source_target_pairs={{0,8},{2,10},{4,12},{6,14},{8,0},{10,2},{12,4},{14,6},{1,9},{3,11}... | collective-permute-start | bytes 245768 | tf_op jit(solution)/shard_map/ppermute | solution.py:358
  22.0 8.3 %collective-permute-start.6 = (bf16[5,4,2048]{2,1,0:T(4,128)(2,1)S(1)}, bf16[5,4,2048]{2,1,0:T(4,128)(2,1)S(1)}, u32[]{:S(2)}, u32[]{:S(2)}) collective-permute-start(bf16[5,4,2048]{2,1,0:T(4,128)(2,1)S(1)} %shard_map.75.refs_0_), channel_id=1, source_target_pairs={{0,4},{2,6},{4,8},{6,10},{8,12},{10,14},{12,0},{14,2},{1,5},{3,7},... | collective-permute-start | bytes 245768 | tf_op jit(solution)/shard_map/ppermute | solution.py:358
  23.5 8.0 %collective-permute-start.5 = (bf16[5,4,2048]{2,1,0:T(4,128)(2,1)S(1)}, bf16[5,4,2048]{2,1,0:T(4,128)(2,1)S(1)}, u32[]{:S(2)}, u32[]{:S(2)}) collective-permute-start(bf16[5,4,2048]{2,1,0:T(4,128)(2,1)S(1)} %shard_map.75.refs_0_), channel_id=1, source_target_pairs={{0,12},{2,14},{4,0},{6,2},{8,4},{10,6},{12,8},{14,10},{1,13},{3,15... | collective-permute-start | bytes 245768 | tf_op jit(solution)/shard_map/ppermute | solution.py:358
  26.2 5.7 %collective-permute-start.4 = (bf16[5,4,2048]{2,1,0:T(4,128)(2,1)S(1)}, bf16[5,4,2048]{2,1,0:T(4,128)(2,1)S(1)}, u32[]{:S(2)}, u32[]{:S(2)}) collective-permute-start(bf16[5,4,2048]{2,1,0:T(4,128)(2,1)S(1)} %shard_map.75.refs_0_), channel_id=1, source_target_pairs={{0,2},{2,4},{4,6},{6,8},{8,10},{10,12},{12,14},{14,0},{1,3},{3,5},... | collective-permute-start | bytes 245768 | tf_op jit(solution)/shard_map/ppermute | solution.py:358
  27.2 7.1 %collective-permute-start.3 = (bf16[5,4,2048]{2,1,0:T(4,128)(2,1)S(1)}, bf16[5,4,2048]{2,1,0:T(4,128)(2,1)S(1)}, u32[]{:S(2)}, u32[]{:S(2)}) collective-permute-start(bf16[5,4,2048]{2,1,0:T(4,128)(2,1)S(1)} %shard_map.75.refs_0_), channel_id=1, source_target_pairs={{0,14},{2,0},{4,2},{6,4},{8,6},{10,8},{12,10},{14,12},{1,15},{3,1}... | collective-permute-start | bytes 245768 | tf_op jit(solution)/shard_map/ppermute | solution.py:358
  35.7 18.2 %copy-start = (bf16[2,2,16,2048]{3,2,1,0:T(8,128)(2,1)}, bf16[2,2,16,2048]{3,2,1,0:T(8,128)(2,1)S(1)}, u32[]{:S(2)}) copy-start(bf16[2,2,16,2048]{3,2,1,0:T(8,128)(2,1)S(1)} %get-tuple-element.47.refs_7_) | copy-start | bytes 786436
  35.7 10.5 %collective-permute-start.13 = (bf16[2,2,16,2048]{3,2,1,0:T(8,128)(2,1)S(1)}, bf16[2,2,16,2048]{3,2,1,0:T(8,128)(2,1)S(1)}, u32[]{:S(2)}, u32[]{:S(2)}) collective-permute-start(bf16[2,2,16,2048]{3,2,1,0:T(8,128)(2,1)S(1)} %get-tuple-element.47.refs_7_), channel_id=1, source_target_pairs={{0,64},{32,96},{64,0},{96,32},{1,65},{33,97},{65,1},{97,33},{2,66}... | collective-permute-start | bytes 786440 | tf_op jit(solution)/shard_map/ppermute | solution.py:358
  38.8 8.4 %collective-permute-start.12 = (bf16[2,2,16,2048]{3,2,1,0:T(8,128)(2,1)S(1)}, bf16[2,2,16,2048]{3,2,1,0:T(8,128)(2,1)S(1)}, u32[]{:S(2)}, u32[]{:S(2)}) collective-permute-start(bf16[2,2,16,2048]{3,2,1,0:T(8,128)(2,1)S(1)} %get-tuple-element.47.refs_7_), channel_id=1, source_target_pairs={{0,96},{32,0},{64,32},{96,64},{1,97},{33,1},{65,33},{97,65},{2,98}... | collective-permute-start | bytes 786440 | tf_op jit(solution)/shard_map/ppermute | solution.py:358
  39.9 7.6 %collective-permute-start.11 = (bf16[2,2,16,2048]{3,2,1,0:T(8,128)(2,1)S(1)}, bf16[2,2,16,2048]{3,2,1,0:T(8,128)(2,1)S(1)}, u32[]{:S(2)}, u32[]{:S(2)}) collective-permute-start(bf16[2,2,16,2048]{3,2,1,0:T(8,128)(2,1)S(1)} %get-tuple-element.47.refs_7_), channel_id=1, source_target_pairs={{0,32},{32,64},{64,96},{96,0},{1,33},{33,65},{65,97},{97,1},{2,34}... | collective-permute-start | bytes 786440 | tf_op jit(solution)/shard_map/ppermute | solution.py:358
  40.9 11.9 %collective-permute-start.18 = (bf16[2,128,1024]{2,1,0:T(8,128)(2,1)S(1)}, bf16[2,128,1024]{2,1,0:T(8,128)(2,1)S(1)}, u32[]{:S(2)}, u32[]{:S(2)}) collective-permute-start(bf16[2,128,1024]{2,1,0:T(8,128)(2,1)S(1)} %get-tuple-element.48), channel_id=1, source_target_pairs={{0,1},{1,2},{2,3},{3,4},{4,5},{5,6},{6,7},{7,8},{8,9},{9,10},{10,1... | collective-permute-start | bytes 1572872 | tf_op jit(solution)/shard_map/ppermute | solution.py:385
  46.0 1.8 %collective-permute-start.14 = (bf16[2,2,16,2048]{3,2,1,0:T(8,128)(2,1)S(1)}, bf16[2,2,16,2048]{3,2,1,0:T(8,128)(2,1)}, u32[]{:S(2)}, u32[]{:S(2)}) collective-permute-start(bf16[2,2,16,2048]{3,2,1,0:T(8,128)(2,1)S(1)} %get-tuple-element.47.refs_7_), channel_id=1, source_target_pairs={{0,16},{16,0},{1,17},{17,1},{2,18},{18,2},{3,19},{19,3},{4,20},{20... | collective-permute-start | bytes 786440 | tf_op jit(solution)/shard_map/ppermute | solution.py:358
  46.2 7.7 %copy-start.5 = (bf16[2,2,16,2048]{3,2,1,0:T(8,128)(2,1)}, bf16[2,2,16,2048]{3,2,1,0:T(8,128)(2,1)S(1)}, u32[]{:S(2)}) copy-start(bf16[2,2,16,2048]{3,2,1,0:T(8,128)(2,1)S(1)} %collective-permute-done.13.refs_10_) | copy-start | bytes 786436
  46.2 6.6 %collective-permute-start.17 = (bf16[2,2,16,2048]{3,2,1,0:T(8,128)(2,1)S(1)}, bf16[2,2,16,2048]{3,2,1,0:T(8,128)(2,1)S(1)}, u32[]{:S(2)}, u32[]{:S(2)}) collective-permute-start(bf16[2,2,16,2048]{3,2,1,0:T(8,128)(2,1)S(1)} %collective-permute-done.13.refs_10_), channel_id=1, source_target_pairs={{0,16},{16,0},{1,17},{17,1},{2,18},{18,2},{3,19},{19,3},{4,20},{20... | collective-permute-start | bytes 786440 | tf_op jit(solution)/shard_map/ppermute | solution.py:358
  47.3 6.6 %copy-start.6 = (bf16[2,2,16,2048]{3,2,1,0:T(8,128)(2,1)}, bf16[2,2,16,2048]{3,2,1,0:T(8,128)(2,1)S(1)}, u32[]{:S(2)}) copy-start(bf16[2,2,16,2048]{3,2,1,0:T(8,128)(2,1)S(1)} %collective-permute-done.12.refs_9_) | copy-start | bytes 786436
  47.3 5.5 %collective-permute-start.16 = (bf16[2,2,16,2048]{3,2,1,0:T(8,128)(2,1)S(1)}, bf16[2,2,16,2048]{3,2,1,0:T(8,128)(2,1)S(1)}, u32[]{:S(2)}, u32[]{:S(2)}) collective-permute-start(bf16[2,2,16,2048]{3,2,1,0:T(8,128)(2,1)S(1)} %collective-permute-done.12.refs_9_), channel_id=1, source_target_pairs={{0,16},{16,0},{1,17},{17,1},{2,18},{18,2},{3,19},{19,3},{4,20},{20... | collective-permute-start | bytes 786440 | tf_op jit(solution)/shard_map/ppermute | solution.py:358
  47.5 6.2 %copy-start.7 = (bf16[2,2,16,2048]{3,2,1,0:T(8,128)(2,1)}, bf16[2,2,16,2048]{3,2,1,0:T(8,128)(2,1)S(1)}, u32[]{:S(2)}) copy-start(bf16[2,2,16,2048]{3,2,1,0:T(8,128)(2,1)S(1)} %collective-permute-done.11.refs_8_) | copy-start | bytes 786436
  47.5 5.3 %collective-permute-start.15 = (bf16[2,2,16,2048]{3,2,1,0:T(8,128)(2,1)S(1)}, bf16[2,2,16,2048]{3,2,1,0:T(8,128)(2,1)S(1)}, u32[]{:S(2)}, u32[]{:S(2)}) collective-permute-start(bf16[2,2,16,2048]{3,2,1,0:T(8,128)(2,1)S(1)} %collective-permute-done.11.refs_8_), channel_id=1, source_target_pairs={{0,16},{16,0},{1,17},{17,1},{2,18},{18,2},{3,19},{19,3},{4,20},{20... | collective-permute-start | bytes 786440 | tf_op jit(solution)/shard_map/ppermute | solution.py:358
  47.8 18.5 %collective-permute-start.10 = (bf16[2,128,1024]{2,1,0:T(8,128)(2,1)}, bf16[2,128,1024]{2,1,0:T(8,128)(2,1)S(1)}, u32[]{:S(2)}, u32[]{:S(2)}) collective-permute-start(bf16[2,128,1024]{2,1,0:T(8,128)(2,1)} %get-tuple-element.44), channel_id=1, source_target_pairs={{0,1},{1,2},{2,3},{3,4},{4,5},{5,6},{6,7},{7,8},{8,9},{9,10},{10,1... | collective-permute-start | bytes 1572872 | tf_op jit(solution)/shard_map/ppermute | solution.py:385
  52.8 0.9 copy-start.8
  52.8 1.0 copy-start.9
  52.8 1.0 copy-start.10
  52.8 0.8 copy-start.1
  53.8 1.0 copy-start.2
  64.4 16.8 %collective-permute-start.19 = (bf16[2,128,1024]{2,1,0:T(8,128)(2,1)S(1)}, bf16[2,128,1024]{2,1,0:T(8,128)(2,1)S(1)}, u32[]{:S(2)}, u32[]{:S(2)}) collective-permute-start(bf16[2,128,1024]{2,1,0:T(8,128)(2,1)S(1)} %get-tuple-element.61), channel_id=1, source_target_pairs={{1,0},{2,1},{3,2},{4,3},{5,4},{6,5},{7,6},{8,7},{9,8},{10,9},{11,1... | collective-permute-start | bytes 1572872 | tf_op jit(solution)/shard_map/ppermute | solution.py:396
  76.0 5.3 %collective-permute-start.22 = (bf16[2,2,2,16,2048]{4,3,2,1,0:T(8,128)(2,1)S(1)}, bf16[2,2,2,16,2048]{4,3,2,1,0:T(8,128)(2,1)S(1)}, u32[]{:S(2)}, u32[]{:S(2)}) collective-permute-start(bf16[2,2,2,16,2048]{4,3,2,1,0:T(8,128)(2,1)S(1)} %get-tuple-element.67), channel_id=1, source_target_pairs={{0,16},{16,0},{1,17},{17,1},{2,18},{18,2},{3,19},{19,3},{4,20},{20... | collective-permute-start | bytes 1572872 | tf_op jit(solution)/shard_map/ppermute | solution.py:358
  81.2 1.9 %collective-permute-start.21 = (bf16[2,2,2,16,2048]{4,3,2,1,0:T(8,128)(2,1)S(1)}, bf16[2,2,2,16,2048]{4,3,2,1,0:T(8,128)(2,1)S(1)}, u32[]{:S(2)}, u32[]{:S(2)}) collective-permute-start(bf16[2,2,2,16,2048]{4,3,2,1,0:T(8,128)(2,1)S(1)} %get-tuple-element.66), channel_id=1, source_target_pairs={{0,16},{16,0},{1,17},{17,1},{2,18},{18,2},{3,19},{19,3},{4,20},{20... | collective-permute-start | bytes 1572872 | tf_op jit(solution)/shard_map/ppermute | solution.py:358
  83.4 10.8 %collective-permute-start.23 = (bf16[2,2,16,2048]{3,2,1,0:T(8,128)(2,1)S(1)}, bf16[2,2,16,2048]{3,2,1,0:T(8,128)(2,1)S(1)}, u32[]{:S(2)}, u32[]{:S(2)}) collective-permute-start(bf16[2,2,16,2048]{3,2,1,0:T(8,128)(2,1)S(1)} %get-tuple-element.86), channel_id=1, source_target_pairs={{0,64},{32,96},{64,0},{96,32},{1,65},{33,97},{65,1},{97,33},{2,66}... | collective-permute-start | bytes 786440 | tf_op jit(solution)/shard_map/ppermute | solution.py:358
  86.1 12.9 %collective-permute-start.25 = (bf16[2,2,16,2048]{3,2,1,0:T(8,128)(2,1)S(1)}, bf16[2,2,16,2048]{3,2,1,0:T(8,128)(2,1)S(1)}, u32[]{:S(2)}, u32[]{:S(2)}) collective-permute-start(bf16[2,2,16,2048]{3,2,1,0:T(8,128)(2,1)S(1)} %get-tuple-element.87), channel_id=1, source_target_pairs={{0,32},{32,64},{64,96},{96,0},{1,33},{33,65},{65,97},{97,1},{2,34}... | collective-permute-start | bytes 786440 | tf_op jit(solution)/shard_map/ppermute | solution.py:358
  86.5 12.4 %collective-permute-start.24 = (bf16[2,2,16,2048]{3,2,1,0:T(8,128)(2,1)S(1)}, bf16[2,2,16,2048]{3,2,1,0:T(8,128)(2,1)S(1)}, u32[]{:S(2)}, u32[]{:S(2)}) collective-permute-start(bf16[2,2,16,2048]{3,2,1,0:T(8,128)(2,1)S(1)} %get-tuple-element.88), channel_id=1, source_target_pairs={{0,96},{32,0},{64,32},{96,64},{1,97},{33,1},{65,33},{97,65},{2,98}... | collective-permute-start | bytes 786440 | tf_op jit(solution)/shard_map/ppermute | solution.py:358
  89.3 15.9 %collective-permute-start.20 = (bf16[2,128,1024]{2,1,0:T(8,128)(2,1)S(1)}, bf16[2,128,1024]{2,1,0:T(8,128)(2,1)S(1)}, u32[]{:S(2)}, u32[]{:S(2)}) collective-permute-start(bf16[2,128,1024]{2,1,0:T(8,128)(2,1)S(1)} %get-tuple-element.64), channel_id=1, source_target_pairs={{1,0},{2,1},{3,2},{4,3},{5,4},{6,5},{7,6},{8,7},{9,8},{10,9},{11,1... | collective-permute-start | bytes 1572872 | tf_op jit(solution)/shard_map/ppermute | solution.py:396
  105.9 12.0 %collective-permute-start.26 = (bf16[5,4,2048]{2,1,0:T(4,128)(2,1)S(1)}, bf16[5,4,2048]{2,1,0:T(4,128)(2,1)S(1)}, u32[]{:S(2)}, u32[]{:S(2)}) collective-permute-start(bf16[5,4,2048]{2,1,0:T(4,128)(2,1)S(1)} %get-tuple-element.73), channel_id=1, source_target_pairs={{0,10},{2,12},{4,14},{6,0},{8,2},{10,4},{12,6},{14,8},{1,11},{3,13... | collective-permute-start | bytes 245768 | tf_op jit(solution)/shard_map/ppermute | solution.py:358
  108.3 15.1 %collective-permute-start.27 = (bf16[5,4,2048]{2,1,0:T(4,128)(2,1)S(1)}, bf16[5,4,2048]{2,1,0:T(4,128)(2,1)S(1)}, u32[]{:S(2)}, u32[]{:S(2)}) collective-permute-start(bf16[5,4,2048]{2,1,0:T(4,128)(2,1)S(1)} %get-tuple-element.74), channel_id=1, source_target_pairs={{0,6},{2,8},{4,10},{6,12},{8,14},{10,0},{12,2},{14,4},{1,7},{3,9},... | collective-permute-start | bytes 245768 | tf_op jit(solution)/shard_map/ppermute | solution.py:358
  111.6 12.2 %collective-permute-start.28 = (bf16[5,4,2048]{2,1,0:T(4,128)(2,1)S(1)}, bf16[5,4,2048]{2,1,0:T(4,128)(2,1)S(1)}, u32[]{:S(2)}, u32[]{:S(2)}) collective-permute-start(bf16[5,4,2048]{2,1,0:T(4,128)(2,1)S(1)} %get-tuple-element.75), channel_id=1, source_target_pairs={{0,8},{2,10},{4,12},{6,14},{8,0},{10,2},{12,4},{14,6},{1,9},{3,11}... | collective-permute-start | bytes 245768 | tf_op jit(solution)/shard_map/ppermute | solution.py:358
  114.0 9.8 %collective-permute-start.29 = (bf16[5,4,2048]{2,1,0:T(4,128)(2,1)S(1)}, bf16[5,4,2048]{2,1,0:T(4,128)(2,1)S(1)}, u32[]{:S(2)}, u32[]{:S(2)}) collective-permute-start(bf16[5,4,2048]{2,1,0:T(4,128)(2,1)S(1)} %get-tuple-element.76), channel_id=1, source_target_pairs={{0,12},{2,14},{4,0},{6,2},{8,4},{10,6},{12,8},{14,10},{1,13},{3,15... | collective-permute-start | bytes 245768 | tf_op jit(solution)/shard_map/ppermute | solution.py:358
  117.9 6.6 %collective-permute-start.30 = (bf16[5,4,2048]{2,1,0:T(4,128)(2,1)S(1)}, bf16[5,4,2048]{2,1,0:T(4,128)(2,1)S(1)}, u32[]{:S(2)}, u32[]{:S(2)}) collective-permute-start(bf16[5,4,2048]{2,1,0:T(4,128)(2,1)S(1)} %get-tuple-element.77), channel_id=1, source_target_pairs={{0,4},{2,6},{4,8},{6,10},{8,12},{10,14},{12,0},{14,2},{1,5},{3,7},... | collective-permute-start | bytes 245768 | tf_op jit(solution)/shard_map/ppermute | solution.py:358
  117.9 7.5 %collective-permute-start.31 = (bf16[5,4,2048]{2,1,0:T(4,128)(2,1)S(1)}, bf16[5,4,2048]{2,1,0:T(4,128)(2,1)S(1)}, u32[]{:S(2)}, u32[]{:S(2)}) collective-permute-start(bf16[5,4,2048]{2,1,0:T(4,128)(2,1)S(1)} %get-tuple-element.78), channel_id=1, source_target_pairs={{0,14},{2,0},{4,2},{6,4},{8,6},{10,8},{12,10},{14,12},{1,15},{3,1}... | collective-permute-start | bytes 245768 | tf_op jit(solution)/shard_map/ppermute | solution.py:358
  123.3 5.7 %collective-permute-start.32 = (bf16[5,4,2048]{2,1,0:T(4,128)(2,1)S(1)}, bf16[5,4,2048]{2,1,0:T(4,128)(2,1)S(1)}, u32[]{:S(2)}, u32[]{:S(2)}) collective-permute-start(bf16[5,4,2048]{2,1,0:T(4,128)(2,1)S(1)} %get-tuple-element.79), channel_id=1, source_target_pairs={{0,2},{2,4},{4,6},{6,8},{8,10},{10,12},{12,14},{14,0},{1,3},{3,5},... | collective-permute-start | bytes 245768 | tf_op jit(solution)/shard_map/ppermute | solution.py:358
  129.2 5.2 %collective-permute-start.34 = (bf16[2,2048]{1,0:T(2,128)(2,1)S(1)}, bf16[2,2048]{1,0:T(2,128)(2,1)S(1)}, u32[]{:S(2)}, u32[]{:S(2)}) collective-permute-start(bf16[2,2048]{1,0:T(2,128)(2,1)S(1)} %bitcast.32), channel_id=1, source_target_pairs={{0,128},{128,0},{1,129},{129,1},{2,130},{130,2},{3,131},{131,3},{4... | collective-permute-start | bytes 24584 | tf_op jit(solution)/shard_map/ppermute | solution.py:358
  130.9 3.7 %collective-permute-start.35 = (bf16[2,2048]{1,0:T(2,128)(2,1)S(1)}, bf16[2,2048]{1,0:T(2,128)(2,1)S(1)}, u32[]{:S(2)}, u32[]{:S(2)}) collective-permute-start(bf16[2,2048]{1,0:T(2,128)(2,1)S(1)} %bitcast.31), channel_id=1, source_target_pairs={{0,129},{1,128},{128,1},{129,0},{2,131},{3,130},{130,3},{131,2},{4... | collective-permute-start | bytes 24584 | tf_op jit(solution)/shard_map/ppermute | solution.py:412
  130.9 5.1 %collective-permute-start.33 = (bf16[2,4,2048]{2,1,0:T(4,128)(2,1)S(1)}, bf16[2,4,2048]{2,1,0:T(4,128)(2,1)S(1)}, u32[]{:S(2)}, u32[]{:S(2)}) collective-permute-start(bf16[2,4,2048]{2,1,0:T(4,128)(2,1)S(1)} %slice.64), channel_id=1, source_target_pairs={{0,1},{1,0},{2,3},{3,2},{4,5},{5,4},{6,7},{7,6},{8,9},{9,8},{10,11... | collective-permute-start | bytes 98312 | tf_op jit(solution)/shard_map/ppermute | solution.py:358
